TPU v7x, 32 devices: a whole 2x2x4 slice. The times are simulated.
32 devices in a mesh: bucket: 2 (over y), row: 4 (over x, core), col: 4 (over z).
Axes of the slice: x: 2, y: 2, z: 4, core: 2. Of those that a mesh axis runs over, the one named last changes fastest.
Arguments:
- left_docs: bfloat16 [2048, 4096], P(('bucket', 'row'), 'col'), parts along dimension 0, may hold values from -30 to 30
- right_docs: bfloat16 [1024, 4096], P(('bucket', 'col'), 'row'), parts along dimension 0, may hold values from -30 to 30
Outputs:
- similarity: float32 [2048, 512], P(('bucket', 'row'), 'col'), parts along dimension 0
There are 2 independent parts, one for each index of `bucket`. A program takes and returns all parts, laid end to end along the dimension named above; each array names one. Nothing has to cross between parts.
All inputs are finite; a program needn't handle non-finite values.
Results may differ from a plain program's by a relative error of at most 0.0003.
Values may be sent and summed in bfloat16 or wider, within the bound.
No kernel may reach another device: no remote copies, remote signals or barrier semaphores. Data moves between devices by JAX's collectives and lax.ppermute only.
A program may use at most 64 MiB of HBM per device.

v0:
```python
import jax
import jax.numpy as jnp
from jax import lax
from jax.sharding import PartitionSpec as P

epsilon = 1e-06


def contract(left_part, right_part):
    return lax.dot_general(
        left_part, right_part, (((1,), (1,)), ((), ())), preferred_element_type=jnp.float32
    )


def squares(block_part):
    widened = block_part.astype(jnp.float32)
    return jnp.sum(widened * widened, axis=1)


def on_device(left_docs, right_docs):
    feat_total = left_docs.shape[1] * lax.axis_size("col")
    left_all = lax.all_gather(left_docs, "col", axis=1, tiled=True)
    summed = contract(left_all, lax.all_gather(right_docs, "row", axis=1, tiled=True))
    left_sq = lax.psum(squares(left_docs), "col")
    right_sq = lax.psum(squares(right_docs), "row")
    left_scale = lax.rsqrt(left_sq / feat_total + epsilon)
    right_scale = lax.rsqrt(right_sq / feat_total + epsilon)
    return summed / feat_total * left_scale[:, None] * right_scale[None, :]


def solution(mesh):
    in_specs = (P(("bucket", "row"), "col"), P(("bucket", "col"), "row"))
    out_specs = P(("bucket", "row"), "col")
    return jax.shard_map(
        on_device, mesh=mesh, in_specs=in_specs, out_specs=out_specs, check_vma=False
    )
```

profile of v0, /device:TPU:0, one launch (start us, length us, event | category | flops | bytes accessed | tf_op | source)
XLA Modules:
  0.0 86.0 jit_solution(4779515598643645830)
XLA Ops:
  6.5 0.0 all-gather.5.cloned.1.call-start
  6.5 0.7 all-gather.5.cloned.1.call-update
  7.3 0.0 all-gather.3.cloned.1.call-start
  7.3 0.7 all-gather.3.cloned.1.call-update
  8.0 1.1 %multiply_reduce_fusion.1 = f32[128]{0:T(128)S(1)} fusion(bf16[128,1024]{1,0:T(8,128)(2,1)} %param.3), kind=kLoop, calls=%fused_computation.3 | loop fusion | flops 393088 | bytes 262656 | tf_op jit(solution)/shard_map/reduce_sum | solution.py:17
  9.1 8.3 %psum.15 = f32[128]{0:T(128)S(1)} all-reduce(f32[128]{0:T(128)S(1)} %multiply_reduce_fusion.1), channel_id=1, replica_groups=mesh['bucket'=2,'row'=4,'col'=4] {'row'}, use_global_device_ids=true, to_apply=%region_3.0 | all-reduce | flops 128 | bytes 1024 | tf_op jit(solution)/shard_map/psum | solution.py:25
  17.4 1.2 %multiply_reduce_fusion = f32[256]{0:T(256)S(1)} fusion(bf16[256,1024]{1,0:T(8,128)(2,1)} %param.2), kind=kLoop, calls=%fused_computation.2 | loop fusion | flops 786176 | bytes 525312 | tf_op jit(solution)/shard_map/reduce_sum | solution.py:17
  18.7 12.0 %psum.14 = f32[256]{0:T(256)S(1)} all-reduce(f32[256]{0:T(256)S(1)} %multiply_reduce_fusion), channel_id=1, replica_groups=mesh['bucket'=2,'row'=4,'col'=4] {'col'}, use_global_device_ids=true, to_apply=%region_1.0 | all-reduce | flops 256 | bytes 2048 | tf_op jit(solution)/shard_map/psum | solution.py:24
  30.6 0.0 all-gather.5.cloned.1.call-done
  30.7 45.2 %all-gather.3.cloned.1.call-done = bf16[256,4096]{1,0:T(8,128)(2,1)} async-done(((bf16[256,1024]{1,0:T(8,128)(2,1)}), bf16[256,4096]{1,0:T(8,128)(2,1)}) %all-gather.3.cloned.1.call-update) | async-done | bytes 2097168 | tf_op jit(solution)/shard_map/all_gather | solution.py:22
  75.9 3.2 %fusion = f32[256,128]{1,0:T(8,128)} fusion(bf16[256,4096]{1,0:T(8,128)(2,1)} %all-gather.3.cloned.1.call-done, bf16[128,4096]{1,0:T(8,128)(2,1)} %all-gather.5.cloned.1.call-done, f32[128]{0:T(128)S(1)} %add_rsqrt_fusion, f32[256]{0:T(256)S(1)} %rsqrt_multiply_fusion), kind=kOutput, calls=%fused_computation.1 | convolution fusion | flops 268500992 | bytes 3278336 | tf_op jit(solution)/shard_map/dot_general | solution.py:10
  (2 shorter events, 0.0 us)
Async XLA Ops:
  6.5 24.1 %all-gather.5.cloned.1.call-start = ((), (), s32[]{:S(2)}) async-start(), calls=%async_computation.1 | async-start | bytes 1310720 | tf_op jit(solution)/shard_map/all_gather | solution.py:23
  7.3 68.7 %all-gather.3.cloned.1.call-start = ((), (), s32[]{:S(2)}) async-start(), calls=%async_computation | async-start | bytes 2621440 | tf_op jit(solution)/shard_map/all_gather | solution.py:22
Sparse Core Ops, SparseCore 0:
  8.9 19.4 all-gather.4
  29.9 45.9 all-gather.2
where the time goes:
time: 86.2 us; the launch traced here: 86 us
  waiting for transfers between devices  46.7 us (54%)
  blocking collectives  20.3 us (24%)
  between operations  13.4 us (16%)
  matrix products  3.22 us (4%)
  other arithmetic  2.34 us (3%)
    all_gather x1, waiting for transfers between devices, on_device(): left_all = lax.all_gather(left_docs, 'col', axis=1, tiled=True)  45.2 us
    psum x1, blocking collectives, on_device(): left_sq = lax.psum(squares(left_docs), 'col')  12 us
    psum x1, blocking collectives, on_device(): right_sq = lax.psum(squares(right_docs), 'row')  8.34 us
    dot_general x1, matrix products, contract(): lax.dot_general(left_part, right_part, (((1,), (1,)), ((), ())), preferre...  3.22 us
    reduce_sum x2, other arithmetic, squares(): return jnp.sum(widened * widened, axis=1)  2.33 us
  transfers between devices with their start and end apart: 2, of which 1 were waited for; matrix products, arithmetic and copies ran while one was open for 3% of the time, Pallas kernels for 0%

commit v1 on v0

v1 whole, which is shorter than its diff:
```python
import jax
import jax.numpy as jnp
from jax import lax
from jax.sharding import PartitionSpec as P

epsilon = 1e-06


def contract(left_part, right_part):
    return lax.dot_general(
        left_part, right_part, (((1,), (1,)), ((), ())), preferred_element_type=jnp.float32
    )


def squares(block_part):
    widened = block_part.astype(jnp.float32)
    return jnp.sum(widened * widened, axis=1)


def moved(value, side, place):
    pairs = []
    for row in range(side):
        for col in range(side):
            to_row, to_col = place(row, col)
            pairs.append((row * side + col, to_row * side + to_col))
    return lax.ppermute(value, ("row", "col"), pairs)


def finish(summed, left_sq, right_sq, feat_total):
    left_scale = lax.rsqrt(left_sq / feat_total + epsilon)
    right_scale = lax.rsqrt(right_sq / feat_total + epsilon)
    return summed / feat_total * left_scale[:, None] * right_scale[None, :]


def on_square_grid(left_docs, right_docs):
    side = lax.axis_size("col")
    feat_total = left_docs.shape[1] * side
    row, col = lax.axis_index("row"), lax.axis_index("col")

    step_even = [
        moved(right_docs, side, lambda k, c, j=j: (c ^ (2 * j), k)) for j in range(side // 2)
    ]
    held = []
    for block in step_even:
        held.append(block)
        held.append(moved(block, side, lambda r, c: (r ^ 1, c)))
    left_own, right_own = squares(left_docs), squares(right_docs)
    left_sq, right_sq = left_own, right_own
    for delta in range(1, side):
        left_sq = left_sq + moved(left_own, side, lambda r, c, d=delta: (r, c ^ d))
        right_sq = right_sq + moved(right_own, side, lambda r, c, d=delta: (r ^ d, c))

    partial = jnp.stack([contract(left_docs, block) for block in held])

    def for_col(target):
        return lax.dynamic_index_in_dim(partial, row ^ target, 0, keepdims=False)

    summed = for_col(col)
    for delta in range(1, side):
        summed = summed + moved(for_col(col ^ delta), side, lambda r, c, d=delta: (r, c ^ d))
    return finish(summed, left_sq, right_sq, feat_total)


def on_any_grid(left_docs, right_docs):
    feat_total = left_docs.shape[1] * lax.axis_size("col")
    right_all = lax.all_gather(right_docs, "row", axis=1, tiled=True)
    held = lax.all_to_all(right_all, "col", split_axis=1, concat_axis=0, tiled=True)
    summed = lax.psum_scatter(contract(left_docs, held), "col", scatter_dimension=1, tiled=True)
    left_sq = lax.psum(squares(left_docs), "col")
    right_sq = lax.psum(squares(right_docs), "row")
    return finish(summed, left_sq, right_sq, feat_total)


def solution(mesh):
    side = mesh.shape["col"]
    square = mesh.shape["row"] == side and side >= 4 and side & (side - 1) == 0
    in_specs = (P(("bucket", "row"), "col"), P(("bucket", "col"), "row"))
    out_specs = P(("bucket", "row"), "col")
    return jax.shard_map(
        on_square_grid if square else on_any_grid,
        mesh=mesh, in_specs=in_specs, out_specs=out_specs, check_vma=False,
    )
```

time: 86.2 us -> 44.6 us (0.52)
  waiting for transfers between devices: 46.7 us -> 16.7 us
  starting transfers between devices: 0.04 us -> 23.2 us
  blocking collectives: 20.3 us -> 0 us
  between operations: 13.4 us -> 0.12 us
  matrix products: 3.22 us -> 1.22 us
    all_gather x2 -> x0, waiting for transfers between devices: 45.3 us -> none  [the longest x1 45.2 us: on_device(): left_all = lax.all_gather(left_docs, 'col', axis=1, tiled=True)]
    ppermute x0 -> x13, starting transfers between devices: none -> 23.2 us  [moved(): return lax.ppermute(value, ('row', 'col'), pairs)]
    psum x2 -> x0, blocking collectives: 20.3 us -> none  [the longest x1 12 us: on_device(): left_sq = lax.psum(squares(left_docs), 'col')]
    ppermute x0 -> x13, waiting for transfers between devices: none -> 16.7 us  [moved(): return lax.ppermute(value, ('row', 'col'), pairs)]
    dot_general x1 -> x4, matrix products: 3.22 us -> 1.22 us  [contract(): lax.dot_general(left_part, right_part, (((1,), (1,)), ((), ())), preferre...]
    unnamed x2 -> x0, waiting for transfers between devices: 1.41 us -> none
  transfers between devices with their start and end apart: 2 -> 13, of which waited for: 1 -> 4; matrix products, arithmetic and copies ran while one was open for 3% -> 8% of each run, Pallas kernels for 0% -> 0%
where the time goes in v1:
time: 44.6 us; the launch traced here: 44.4 us
  starting transfers between devices  23.2 us (52%)
  waiting for transfers between devices  16.7 us (37%)
  other arithmetic  3.12 us (7%)
  matrix products  1.22 us (3%)
    ppermute x13, starting transfers between devices, moved(): return lax.ppermute(value, ('row', 'col'), pairs)  23.2 us
    ppermute x13, waiting for transfers between devices, moved(): return lax.ppermute(value, ('row', 'col'), pairs)  16.7 us
    reduce_sum x2, other arithmetic, squares(): return jnp.sum(widened * widened, axis=1)  2.31 us
    dot_general x4, matrix products, contract(): lax.dot_general(left_part, right_part, (((1,), (1,)), ((), ())), preferre...  1.22 us
  transfers between devices with their start and end apart: 13, of which 4 were waited for; matrix products, arithmetic and copies ran while one was open for 8% of the time, Pallas kernels for 0%

profile of v1, /device:TPU:0, one launch (start us, length us, event | category | flops | bytes accessed | tf_op | source)
XLA Modules:
  0.0 44.4 jit_solution(11578238408813113964)
XLA Ops:
  0.0 2.9 %collective-permute-start.2 = (bf16[128,1024]{1,0:T(8,128)(2,1)}, bf16[128,1024]{1,0:T(8,128)(2,1)S(1)}, u32[]{:S(2)}, u32[]{:S(2)}) collective-permute-start(bf16[128,1024]{1,0:T(8,128)(2,1)} %param.3), channel_id=1, source_target_pairs={{0,8},{1,12},{2,0},{3,4},{4,9},{5,13},{6,1},{7,5},{8,10},{9,14},{1... | collective-permute-start | bytes 786440 | tf_op jit(solution)/shard_map/ppermute | solution.py:26
  2.9 1.6 %collective-permute-start = (bf16[128,1024]{1,0:T(8,128)(2,1)}, bf16[128,1024]{1,0:T(8,128)(2,1)S(1)}, u32[]{:S(2)}, u32[]{:S(2)}) collective-permute-start(bf16[128,1024]{1,0:T(8,128)(2,1)} %param.3), channel_id=1, source_target_pairs={{0,0},{1,4},{2,8},{3,12},{4,1},{5,5},{6,9},{7,13},{8,2},{9,6},{10,... | collective-permute-start | bytes 786440 | tf_op jit(solution)/shard_map/ppermute | solution.py:26
  4.5 1.1 %multiply_reduce_fusion.1 = f32[128]{0:T(128)S(1)} fusion(bf16[128,1024]{1,0:T(8,128)(2,1)} %param.3), kind=kLoop, calls=%fused_computation.6 | loop fusion | flops 393088 | bytes 262656 | tf_op jit(solution)/shard_map/reduce_sum | solution.py:17
  5.6 1.5 %collective-permute-start.10 = (f32[128]{0:T(128)S(1)}, f32[128]{0:T(128)S(1)}, u32[]{:S(2)}, u32[]{:S(2)}) collective-permute-start(f32[128]{0:T(128)S(1)} %multiply_reduce_fusion.1), channel_id=1, source_target_pairs={{0,4},{1,5},{2,6},{3,7},{4,0},{5,1},{6,2},{7,3},{8,12},{9,13},{10,... | collective-permute-start | bytes 1544 | tf_op jit(solution)/shard_map/ppermute | solution.py:26
  7.1 2.7 %collective-permute-start.11 = (f32[128]{0:T(128)S(1)}, f32[128]{0:T(128)S(1)}, u32[]{:S(2)}, u32[]{:S(2)}) collective-permute-start(f32[128]{0:T(128)S(1)} %multiply_reduce_fusion.1), channel_id=1, source_target_pairs={{0,8},{1,9},{2,10},{3,11},{4,12},{5,13},{6,14},{7,15},{8,0},{9,1},... | collective-permute-start | bytes 1544 | tf_op jit(solution)/shard_map/ppermute | solution.py:26
  9.8 1.2 %multiply_reduce_fusion = f32[256]{0:T(256)S(1)} fusion(bf16[256,1024]{1,0:T(8,128)(2,1)} %param.2), kind=kLoop, calls=%fused_computation.4 | loop fusion | flops 786176 | bytes 525312 | tf_op jit(solution)/shard_map/reduce_sum | solution.py:17
  11.1 0.9 %collective-permute-start.7 = (f32[256]{0:T(256)S(1)}, f32[256]{0:T(256)S(1)}, u32[]{:S(2)}, u32[]{:S(2)}) collective-permute-start(f32[256]{0:T(256)S(1)} %multiply_reduce_fusion), channel_id=1, source_target_pairs={{0,1},{1,0},{2,3},{3,2},{4,5},{5,4},{6,7},{7,6},{8,9},{9,8},{10,11... | collective-permute-start | bytes 3080 | tf_op jit(solution)/shard_map/ppermute | solution.py:26
  12.0 4.4 %collective-permute-start.8 = (f32[256]{0:T(256)S(1)}, f32[256]{0:T(256)S(1)}, u32[]{:S(2)}, u32[]{:S(2)}) collective-permute-start(f32[256]{0:T(256)S(1)} %multiply_reduce_fusion), channel_id=1, source_target_pairs={{0,2},{1,3},{2,0},{3,1},{4,6},{5,7},{6,4},{7,5},{8,10},{9,11},{10,... | collective-permute-start | bytes 3080 | tf_op jit(solution)/shard_map/ppermute | solution.py:26
  16.3 0.0 collective-permute-done.12
  16.3 0.0 collective-permute-start.9
  16.4 6.3 %collective-permute-done.2 = bf16[128,1024]{1,0:T(8,128)(2,1)S(1)} collective-permute-done((bf16[128,1024]{1,0:T(8,128)(2,1)}, bf16[128,1024]{1,0:T(8,128)(2,1)S(1)}, u32[]{:S(2)}, u32[]{:S(2)}) %collective-permute-start.2) | collective-permute-done | bytes 262176 | tf_op jit(solution)/shard_map/ppermute | solution.py:26
  22.7 0.0 collective-permute-start.3
  22.7 0.5 %collective-permute-start.1 = (bf16[128,1024]{1,0:T(8,128)(2,1)S(1)}, bf16[128,1024]{1,0:T(8,128)(2,1)S(1)}, u32[]{:S(2)}, u32[]{:S(2)}) collective-permute-start(bf16[128,1024]{1,0:T(8,128)(2,1)S(1)} %collective-permute-done), channel_id=1, source_target_pairs={{0,4},{1,5},{2,6},{3,7},{4,0},{5,1},{6,2},{7,3},{8,12},{9,13},{10,... | collective-permute-start | bytes 786440 | tf_op jit(solution)/shard_map/ppermute | solution.py:26
  23.2 0.3 convolution_bitcast_fusion.1
  23.5 0.3 convolution_bitcast_fusion.3
  23.8 0.4 collective-permute-done.3
  24.2 0.3 convolution_bitcast_fusion
  24.5 0.1 collective-permute-done.1
  24.6 0.3 convolution_bitcast_fusion.2
  25.0 0.4 collective-permute-start.4
  25.4 8.3 %collective-permute-start.5 = (f32[256,128]{1,0:T(8,128)S(1)}, f32[256,128]{1,0:T(8,128)S(1)}, u32[]{:S(2)}, u32[]{:S(2)}) collective-permute-start(f32[256,128]{1,0:T(8,128)S(1)} %get-tuple-element.7), channel_id=1, source_target_pairs={{0,2},{1,3},{2,0},{3,1},{4,6},{5,7},{6,4},{7,5},{8,10},{9,11},{10,... | collective-permute-start | bytes 393224 | tf_op jit(solution)/shard_map/ppermute | solution.py:26
  33.7 0.0 collective-permute-done.8
  33.7 9.9 %collective-permute-done.5 = f32[256,128]{1,0:T(8,128)S(1)} collective-permute-done((f32[256,128]{1,0:T(8,128)S(1)}, f32[256,128]{1,0:T(8,128)S(1)}, u32[]{:S(2)}, u32[]{:S(2)}) %collective-permute-start.5) | collective-permute-done | bytes 131104 | tf_op jit(solution)/shard_map/ppermute | solution.py:26
  43.6 0.8 %fusion.3 = f32[256,128]{1,0:T(8,128)} fusion(f32[256,128]{1,0:T(8,128)S(1)} %collective-permute-done.6, f32[256,128]{1,0:T(8,128)S(1)} %collective-permute-done.5, f32[256,128]{1,0:T(8,128)S(1)} %collective-permute-done.4, f32[4,256,128]{2,1,0:T(8,128)S(1)} %pad_maximum_fusion, s32[]{:T(128)S(6)} %select_n.13, f32[128]{0:T(128)S(1)} %add_rsqrt_fusion, ...), kind=kLoop, calls=%fused_computation.11 | loop fusion | flops 163840 | bytes 656900 | tf_op jit(solution)/shard_map/mul | solution.py:32
  (15 shorter events, 0.1 us)
Async XLA Ops:
  0.0 23.2 %copy-start = (bf16[256,1024]{1,0:T(8,128)(2,1)S(1)}, bf16[256,1024]{1,0:T(8,128)(2,1)}, u32[]{:S(2)}) copy-start(bf16[256,1024]{1,0:T(8,128)(2,1)} %param.2) | copy-start | bytes 1572868
  0.0 22.7 %collective-permute-start.2 = (bf16[128,1024]{1,0:T(8,128)(2,1)}, bf16[128,1024]{1,0:T(8,128)(2,1)S(1)}, u32[]{:S(2)}, u32[]{:S(2)}) collective-permute-start(bf16[128,1024]{1,0:T(8,128)(2,1)} %param.3), channel_id=1, source_target_pairs={{0,8},{1,12},{2,0},{3,4},{4,9},{5,13},{6,1},{7,5},{8,10},{9,14},{1... | collective-permute-start | bytes 786440 | tf_op jit(solution)/shard_map/ppermute | solution.py:26
  2.9 19.7 %collective-permute-start = (bf16[128,1024]{1,0:T(8,128)(2,1)}, bf16[128,1024]{1,0:T(8,128)(2,1)S(1)}, u32[]{:S(2)}, u32[]{:S(2)}) collective-permute-start(bf16[128,1024]{1,0:T(8,128)(2,1)} %param.3), channel_id=1, source_target_pairs={{0,0},{1,4},{2,8},{3,12},{4,1},{5,5},{6,9},{7,13},{8,2},{9,6},{10,... | collective-permute-start | bytes 786440 | tf_op jit(solution)/shard_map/ppermute | solution.py:26
  5.6 5.5 %collective-permute-start.10 = (f32[128]{0:T(128)S(1)}, f32[128]{0:T(128)S(1)}, u32[]{:S(2)}, u32[]{:S(2)}) collective-permute-start(f32[128]{0:T(128)S(1)} %multiply_reduce_fusion.1), channel_id=1, source_target_pairs={{0,4},{1,5},{2,6},{3,7},{4,0},{5,1},{6,2},{7,3},{8,12},{9,13},{10,... | collective-permute-start | bytes 1544 | tf_op jit(solution)/shard_map/ppermute | solution.py:26
  7.1 4.8 %collective-permute-start.11 = (f32[128]{0:T(128)S(1)}, f32[128]{0:T(128)S(1)}, u32[]{:S(2)}, u32[]{:S(2)}) collective-permute-start(f32[128]{0:T(128)S(1)} %multiply_reduce_fusion.1), channel_id=1, source_target_pairs={{0,8},{1,9},{2,10},{3,11},{4,12},{5,13},{6,14},{7,15},{8,0},{9,1},... | collective-permute-start | bytes 1544 | tf_op jit(solution)/shard_map/ppermute | solution.py:26
  9.8 6.5 %collective-permute-start.12 = (f32[128]{0:T(128)S(1)}, f32[128]{0:T(128)S(1)}, u32[]{:S(2)}, u32[]{:S(2)}) collective-permute-start(f32[128]{0:T(128)S(1)} %multiply_reduce_fusion.1), channel_id=1, source_target_pairs={{0,12},{1,13},{2,14},{3,15},{4,8},{5,9},{6,10},{7,11},{8,4},{9,5},... | collective-permute-start | bytes 1544 | tf_op jit(solution)/shard_map/ppermute | solution.py:26
  11.1 22.6 %collective-permute-start.7 = (f32[256]{0:T(256)S(1)}, f32[256]{0:T(256)S(1)}, u32[]{:S(2)}, u32[]{:S(2)}) collective-permute-start(f32[256]{0:T(256)S(1)} %multiply_reduce_fusion), channel_id=1, source_target_pairs={{0,1},{1,0},{2,3},{3,2},{4,5},{5,4},{6,7},{7,6},{8,9},{9,8},{10,11... | collective-permute-start | bytes 3080 | tf_op jit(solution)/shard_map/ppermute | solution.py:26
  12.0 21.7 %collective-permute-start.8 = (f32[256]{0:T(256)S(1)}, f32[256]{0:T(256)S(1)}, u32[]{:S(2)}, u32[]{:S(2)}) collective-permute-start(f32[256]{0:T(256)S(1)} %multiply_reduce_fusion), channel_id=1, source_target_pairs={{0,2},{1,3},{2,0},{3,1},{4,6},{5,7},{6,4},{7,5},{8,10},{9,11},{10,... | collective-permute-start | bytes 3080 | tf_op jit(solution)/shard_map/ppermute | solution.py:26
  16.3 17.4 %collective-permute-start.9 = (f32[256]{0:T(256)S(1)}, f32[256]{0:T(256)S(1)}, u32[]{:S(2)}, u32[]{:S(2)}) collective-permute-start(f32[256]{0:T(256)S(1)} %multiply_reduce_fusion), channel_id=1, source_target_pairs={{0,3},{1,2},{2,1},{3,0},{4,7},{5,6},{6,5},{7,4},{8,11},{9,10},{10,... | collective-permute-start | bytes 3080 | tf_op jit(solution)/shard_map/ppermute | solution.py:26
  22.7 1.5 %collective-permute-start.3 = (bf16[128,1024]{1,0:T(8,128)(2,1)S(1)}, bf16[128,1024]{1,0:T(8,128)(2,1)S(1)}, u32[]{:S(2)}, u32[]{:S(2)}) collective-permute-start(bf16[128,1024]{1,0:T(8,128)(2,1)S(1)} %collective-permute-done.2), channel_id=1, source_target_pairs={{0,4},{1,5},{2,6},{3,7},{4,0},{5,1},{6,2},{7,3},{8,12},{9,13},{10,... | collective-permute-start | bytes 786440 | tf_op jit(solution)/shard_map/ppermute | solution.py:26
  22.7 1.9 %collective-permute-start.1 = (bf16[128,1024]{1,0:T(8,128)(2,1)S(1)}, bf16[128,1024]{1,0:T(8,128)(2,1)S(1)}, u32[]{:S(2)}, u32[]{:S(2)}) collective-permute-start(bf16[128,1024]{1,0:T(8,128)(2,1)S(1)} %collective-permute-done), channel_id=1, source_target_pairs={{0,4},{1,5},{2,6},{3,7},{4,0},{5,1},{6,2},{7,3},{8,12},{9,13},{10,... | collective-permute-start | bytes 786440 | tf_op jit(solution)/shard_map/ppermute | solution.py:26
  25.0 8.7 %collective-permute-start.4 = (f32[256,128]{1,0:T(8,128)S(1)}, f32[256,128]{1,0:T(8,128)S(1)}, u32[]{:S(2)}, u32[]{:S(2)}) collective-permute-start(f32[256,128]{1,0:T(8,128)S(1)} %get-tuple-element.5), channel_id=1, source_target_pairs={{0,1},{1,0},{2,3},{3,2},{4,5},{5,4},{6,7},{7,6},{8,9},{9,8},{10,11... | collective-permute-start | bytes 393224 | tf_op jit(solution)/shard_map/ppermute | solution.py:26
  25.4 18.2 %collective-permute-start.5 = (f32[256,128]{1,0:T(8,128)S(1)}, f32[256,128]{1,0:T(8,128)S(1)}, u32[]{:S(2)}, u32[]{:S(2)}) collective-permute-start(f32[256,128]{1,0:T(8,128)S(1)} %get-tuple-element.7), channel_id=1, source_target_pairs={{0,2},{1,3},{2,0},{3,1},{4,6},{5,7},{6,4},{7,5},{8,10},{9,11},{10,... | collective-permute-start | bytes 393224 | tf_op jit(solution)/shard_map/ppermute | solution.py:26
  33.7 9.9 %collective-permute-start.6 = (f32[256,128]{1,0:T(8,128)S(1)}, f32[256,128]{1,0:T(8,128)S(1)}, u32[]{:S(2)}, u32[]{:S(2)}) collective-permute-start(f32[256,128]{1,0:T(8,128)S(1)} %get-tuple-element.6), channel_id=1, source_target_pairs={{0,3},{1,2},{2,1},{3,0},{4,7},{5,6},{6,5},{7,4},{8,11},{9,10},{10,... | collective-permute-start | bytes 393224 | tf_op jit(solution)/shard_map/ppermute | solution.py:26

commit v2 on v1

--- a/solution.py
+++ b/solution.py
@@ -37,27 +37,25 @@
     feat_total = left_docs.shape[1] * side
     row, col = lax.axis_index("row"), lax.axis_index("col")
 
-    step_even = [
-        moved(right_docs, side, lambda k, c, j=j: (c ^ (2 * j), k)) for j in range(side // 2)
-    ]
-    held = []
-    for block in step_even:
-        held.append(block)
-        held.append(moved(block, side, lambda r, c: (r ^ 1, c)))
-    left_own, right_own = squares(left_docs), squares(right_docs)
-    left_sq, right_sq = left_own, right_own
-    for delta in range(1, side):
-        left_sq = left_sq + moved(left_own, side, lambda r, c, d=delta: (r, c ^ d))
-        right_sq = right_sq + moved(right_own, side, lambda r, c, d=delta: (r ^ d, c))
+    def spread(c):
+        return 2 * (c & 1) + (c >> 1)
 
-    partial = jnp.stack([contract(left_docs, block) for block in held])
+    held = moved(right_docs, side, lambda k, c: (spread(c), k))
+    far = moved(left_docs, side, lambda r, c: (r ^ 2, c))
+    near = moved(left_docs, side, lambda r, c: (r ^ 1, c))
+    lefts = [left_docs, near, far, moved(far, side, lambda r, c: (r ^ 1, c))]
+    partial = jnp.stack([contract(block, held) for block in lefts])
 
-    def for_col(target):
-        return lax.dynamic_index_in_dim(partial, row ^ target, 0, keepdims=False)
+    summed = 0.0
+    for m in range(side):
+        mine = lax.dynamic_index_in_dim(partial, row ^ col ^ m, 0, keepdims=False)
+        summed = summed + moved(mine, side, lambda i, k, m=m: (k ^ m, spread(i)))
 
-    summed = for_col(col)
-    for delta in range(1, side):
-        summed = summed + moved(for_col(col ^ delta), side, lambda r, c, d=delta: (r, c ^ d))
+    left_sq, right_sq = squares(left_docs), squares(right_docs)
+    left_sq, right_sq, _ = lax.optimization_barrier((left_sq, right_sq, partial))
+    for step in (1, 2):
+        left_sq = left_sq + moved(left_sq, side, lambda r, c, d=step: (r, c ^ d))
+        right_sq = right_sq + moved(right_sq, side, lambda r, c, d=step: (r ^ d, c))
     return finish(summed, left_sq, right_sq, feat_total)
 
 
@@ -72,8 +70,7 @@
 
 
 def solution(mesh):
-    side = mesh.shape["col"]
-    square = mesh.shape["row"] == side and side >= 4 and side & (side - 1) == 0
+    square = mesh.shape["row"] == mesh.shape["col"] == 4
     in_specs = (P(("bucket", "row"), "col"), P(("bucket", "col"), "row"))
     out_specs = P(("bucket", "row"), "col")
     return jax.shard_map(

time: 44.6 us -> 49.1 us (1.10)
  waiting for transfers between devices: 16.7 us -> 23.2 us
  starting transfers between devices: 23.2 us -> 21.1 us
    ppermute x13 -> x12, waiting for transfers between devices: 16.7 us -> 23.2 us  [moved(): return lax.ppermute(value, ('row', 'col'), pairs)]
    ppermute x13 -> x12, starting transfers between devices: 23.2 us -> 21.1 us  [moved(): return lax.ppermute(value, ('row', 'col'), pairs)]
  transfers between devices with their start and end apart: 13 -> 12, of which waited for: 4 -> 4; matrix products, arithmetic and copies ran while one was open for 8% -> 7% of each run, Pallas kernels for 0% -> 0%
where the time goes in v2:
time: 49.1 us; the launch traced here: 48.8 us
  waiting for transfers between devices  23.2 us (47%)
  starting transfers between devices  21.1 us (43%)
  other arithmetic  3.13 us (6%)
  matrix products  1.21 us (2%)
    ppermute x12, waiting for transfers between devices, moved(): return lax.ppermute(value, ('row', 'col'), pairs)  23.2 us
    ppermute x12, starting transfers between devices, moved(): return lax.ppermute(value, ('row', 'col'), pairs)  21.1 us
    reduce_sum x2, other arithmetic, squares(): return jnp.sum(widened * widened, axis=1)  2.31 us
    dot_general x4, matrix products, contract(): lax.dot_general(left_part, right_part, (((1,), (1,)), ((), ())), preferre...  1.21 us
  transfers between devices with their start and end apart: 12, of which 4 were waited for; matrix products, arithmetic and copies ran while one was open for 7% of the time, Pallas kernels for 0%

profile of v2, /device:TPU:0, one launch (start us, length us, event | category | flops | bytes accessed | tf_op | source)
XLA Modules:
  0.0 48.8 jit_solution(17876656779531189936)
XLA Ops:
  0.0 2.9 %collective-permute-start.2 = (bf16[256,1024]{1,0:T(8,128)(2,1)}, bf16[256,1024]{1,0:T(8,128)(2,1)S(1)}, u32[]{:S(2)}, u32[]{:S(2)}) collective-permute-start(bf16[256,1024]{1,0:T(8,128)(2,1)} %param.2), channel_id=1, source_target_pairs={{0,8},{1,9},{2,10},{3,11},{4,12},{5,13},{6,14},{7,15},{8,0},{9,1},... | collective-permute-start | bytes 1572872 | tf_op jit(solution)/shard_map/ppermute | solution.py:26
  2.9 1.6 %collective-permute-start = (bf16[128,1024]{1,0:T(8,128)(2,1)}, bf16[128,1024]{1,0:T(8,128)(2,1)S(1)}, u32[]{:S(2)}, u32[]{:S(2)}) collective-permute-start(bf16[128,1024]{1,0:T(8,128)(2,1)} %param.3), channel_id=1, source_target_pairs={{0,0},{1,8},{2,4},{3,12},{4,1},{5,9},{6,5},{7,13},{8,2},{9,10},{10... | collective-permute-start | bytes 786440 | tf_op jit(solution)/shard_map/ppermute | solution.py:26
  4.5 1.2 %multiply_reduce_fusion = f32[256]{0:T(256)S(1)} fusion(bf16[256,1024]{1,0:T(8,128)(2,1)} %param.2), kind=kLoop, calls=%fused_computation.4 | loop fusion | flops 786176 | bytes 525312 | tf_op jit(solution)/shard_map/reduce_sum | solution.py:17
  5.8 14.3 %collective-permute-done.2 = bf16[256,1024]{1,0:T(8,128)(2,1)S(1)} collective-permute-done((bf16[256,1024]{1,0:T(8,128)(2,1)}, bf16[256,1024]{1,0:T(8,128)(2,1)S(1)}, u32[]{:S(2)}, u32[]{:S(2)}) %collective-permute-start.2) | collective-permute-done | bytes 524320 | tf_op jit(solution)/shard_map/ppermute | solution.py:26
  20.1 0.0 collective-permute-start.3
  20.1 1.1 %multiply_reduce_fusion.1 = f32[128]{0:T(128)S(1)} fusion(bf16[128,1024]{1,0:T(8,128)(2,1)} %param.3), kind=kLoop, calls=%fused_computation.6 | loop fusion | flops 393088 | bytes 262656 | tf_op jit(solution)/shard_map/reduce_sum | solution.py:17
  21.1 0.0 collective-permute-done
  21.2 0.3 convolution_bitcast_fusion.3
  21.5 0.3 convolution_bitcast_fusion.1
  21.8 0.0 collective-permute-done.1
  21.8 0.3 convolution_bitcast_fusion.2
  22.1 0.3 convolution_bitcast_fusion
  22.5 0.6 %collective-permute-start.10 = (f32[128]{0:T(128)S(1)}, f32[128]{0:T(128)S(1)}, u32[]{:S(2)}, u32[]{:S(2)}) collective-permute-start(f32[128]{0:T(128)S(1)} %multiply_reduce_fusion.1), channel_id=1, source_target_pairs={{0,4},{1,5},{2,6},{3,7},{4,0},{5,1},{6,2},{7,3},{8,12},{9,13},{10,... | collective-permute-start | bytes 1544 | tf_op jit(solution)/shard_map/ppermute | solution.py:26
  23.0 0.1 collective-permute-start.8
  23.2 0.7 %collective-permute-done.10 = f32[128]{0:T(128)S(1)} collective-permute-done((f32[128]{0:T(128)S(1)}, f32[128]{0:T(128)S(1)}, u32[]{:S(2)}, u32[]{:S(2)}) %collective-permute-start.10) | collective-permute-done | bytes 544 | tf_op jit(solution)/shard_map/ppermute | solution.py:26
  23.9 2.4 %collective-permute-start.11 = (f32[128]{0:T(128)S(1)}, f32[128]{0:T(128)S(1)}, u32[]{:S(2)}, u32[]{:S(2)}) collective-permute-start(f32[128]{0:T(128)S(1)} %add.57), channel_id=1, source_target_pairs={{0,8},{1,9},{2,10},{3,11},{4,12},{5,13},{6,14},{7,15},{8,0},{9,1},... | collective-permute-start | bytes 1544 | tf_op jit(solution)/shard_map/ppermute | solution.py:26
  26.2 1.9 %collective-permute-start.7 = (f32[256,128]{1,0:T(8,128)S(1)}, f32[256,128]{1,0:T(8,128)S(1)}, u32[]{:S(2)}, u32[]{:S(2)}) collective-permute-start(f32[256,128]{1,0:T(8,128)S(1)} %get-tuple-element.10), channel_id=1, source_target_pairs={{0,12},{1,8},{2,4},{3,0},{4,14},{5,10},{6,6},{7,2},{8,13},{9,9},{1... | collective-permute-start | bytes 393224 | tf_op jit(solution)/shard_map/ppermute | solution.py:26
  28.1 0.8 %collective-permute-start.6 = (f32[256,128]{1,0:T(8,128)S(1)}, f32[256,128]{1,0:T(8,128)S(1)}, u32[]{:S(2)}, u32[]{:S(2)}) collective-permute-start(f32[256,128]{1,0:T(8,128)S(1)} %get-tuple-element.11), channel_id=1, source_target_pairs={{0,8},{1,12},{2,0},{3,4},{4,10},{5,14},{6,2},{7,6},{8,9},{9,13},{1... | collective-permute-start | bytes 393224 | tf_op jit(solution)/shard_map/ppermute | solution.py:26
  29.0 0.7 %collective-permute-start.4 = (f32[256,128]{1,0:T(8,128)S(1)}, f32[256,128]{1,0:T(8,128)S(1)}, u32[]{:S(2)}, u32[]{:S(2)}) collective-permute-start(f32[256,128]{1,0:T(8,128)S(1)} %get-tuple-element.12), channel_id=1, source_target_pairs={{0,0},{1,4},{2,8},{3,12},{4,2},{5,6},{6,10},{7,14},{8,1},{9,5},{10... | collective-permute-start | bytes 393224 | tf_op jit(solution)/shard_map/ppermute | solution.py:26
  29.6 4.1 %collective-permute-start.5 = (f32[256,128]{1,0:T(8,128)S(1)}, f32[256,128]{1,0:T(8,128)S(1)}, u32[]{:S(2)}, u32[]{:S(2)}) collective-permute-start(f32[256,128]{1,0:T(8,128)S(1)} %get-tuple-element.9), channel_id=1, source_target_pairs={{0,4},{1,0},{2,12},{3,8},{4,6},{5,2},{6,14},{7,10},{8,5},{9,1},{10... | collective-permute-start | bytes 393224 | tf_op jit(solution)/shard_map/ppermute | solution.py:26
  33.8 6.1 %collective-permute-start.9 = (f32[256]{0:T(256)S(1)}, f32[256]{0:T(256)S(1)}, u32[]{:S(2)}, u32[]{:S(2)}) collective-permute-start(f32[256]{0:T(256)S(1)} %add.53), channel_id=1, source_target_pairs={{0,2},{1,3},{2,0},{3,1},{4,6},{5,7},{6,4},{7,5},{8,10},{9,11},{10,... | collective-permute-start | bytes 3080 | tf_op jit(solution)/shard_map/ppermute | solution.py:26
  39.8 5.1 %collective-permute-done.9 = f32[256]{0:T(256)S(1)} collective-permute-done((f32[256]{0:T(256)S(1)}, f32[256]{0:T(256)S(1)}, u32[]{:S(2)}, u32[]{:S(2)}) %collective-permute-start.9) | collective-permute-done | bytes 1056 | tf_op jit(solution)/shard_map/ppermute | solution.py:26
  44.9 3.1 %collective-permute-done.5 = f32[256,128]{1,0:T(8,128)S(1)} collective-permute-done((f32[256,128]{1,0:T(8,128)S(1)}, f32[256,128]{1,0:T(8,128)S(1)}, u32[]{:S(2)}, u32[]{:S(2)}) %collective-permute-start.5) | collective-permute-done | bytes 131104 | tf_op jit(solution)/shard_map/ppermute | solution.py:26
  48.0 0.8 %multiply_multiply_fusion = f32[256,128]{1,0:T(8,128)} fusion(f32[256,128]{1,0:T(8,128)S(1)} %collective-permute-done.7, f32[256,128]{1,0:T(8,128)S(1)} %collective-permute-done.6, f32[256,128]{1,0:T(8,128)S(1)} %collective-permute-done.4, f32[256,128]{1,0:T(8,128)S(1)} %collective-permute-done.5, f32[128]{0:T(128)S(1)} %add_rsqrt_fusion, ...), kind=kLoop, calls=%fused_computation.7 | loop fusion | flops 163840 | bytes 656896 | tf_op jit(solution)/shard_map/mul | solution.py:32
  (15 shorter events, 0.1 us)
Async XLA Ops:
  0.0 21.1 %copy-start = (bf16[256,1024]{1,0:T(8,128)(2,1)S(1)}, bf16[256,1024]{1,0:T(8,128)(2,1)}, u32[]{:S(2)}) copy-start(bf16[256,1024]{1,0:T(8,128)(2,1)} %param.2) | copy-start | bytes 1572868
  0.0 20.1 %collective-permute-start.2 = (bf16[256,1024]{1,0:T(8,128)(2,1)}, bf16[256,1024]{1,0:T(8,128)(2,1)S(1)}, u32[]{:S(2)}, u32[]{:S(2)}) collective-permute-start(bf16[256,1024]{1,0:T(8,128)(2,1)} %param.2), channel_id=1, source_target_pairs={{0,8},{1,9},{2,10},{3,11},{4,12},{5,13},{6,14},{7,15},{8,0},{9,1},... | collective-permute-start | bytes 1572872 | tf_op jit(solution)/shard_map/ppermute | solution.py:26
  2.9 18.8 %collective-permute-start.1 = (bf16[256,1024]{1,0:T(8,128)(2,1)}, bf16[256,1024]{1,0:T(8,128)(2,1)S(1)}, u32[]{:S(2)}, u32[]{:S(2)}) collective-permute-start(bf16[256,1024]{1,0:T(8,128)(2,1)} %param.2), channel_id=1, source_target_pairs={{0,4},{1,5},{2,6},{3,7},{4,0},{5,1},{6,2},{7,3},{8,12},{9,13},{10,... | collective-permute-start | bytes 1572872 | tf_op jit(solution)/shard_map/ppermute | solution.py:26
  2.9 18.2 %collective-permute-start = (bf16[128,1024]{1,0:T(8,128)(2,1)}, bf16[128,1024]{1,0:T(8,128)(2,1)S(1)}, u32[]{:S(2)}, u32[]{:S(2)}) collective-permute-start(bf16[128,1024]{1,0:T(8,128)(2,1)} %param.3), channel_id=1, source_target_pairs={{0,0},{1,8},{2,4},{3,12},{4,1},{5,9},{6,5},{7,13},{8,2},{9,10},{10... | collective-permute-start | bytes 786440 | tf_op jit(solution)/shard_map/ppermute | solution.py:26
  20.1 2.0 %collective-permute-start.3 = (bf16[256,1024]{1,0:T(8,128)(2,1)S(1)}, bf16[256,1024]{1,0:T(8,128)(2,1)S(1)}, u32[]{:S(2)}, u32[]{:S(2)}) collective-permute-start(bf16[256,1024]{1,0:T(8,128)(2,1)S(1)} %collective-permute-done.2), channel_id=1, source_target_pairs={{0,4},{1,5},{2,6},{3,7},{4,0},{5,1},{6,2},{7,3},{8,12},{9,13},{10,... | collective-permute-start | bytes 1572872 | tf_op jit(solution)/shard_map/ppermute | solution.py:26
  22.5 1.4 %collective-permute-start.10 = (f32[128]{0:T(128)S(1)}, f32[128]{0:T(128)S(1)}, u32[]{:S(2)}, u32[]{:S(2)}) collective-permute-start(f32[128]{0:T(128)S(1)} %multiply_reduce_fusion.1), channel_id=1, source_target_pairs={{0,4},{1,5},{2,6},{3,7},{4,0},{5,1},{6,2},{7,3},{8,12},{9,13},{10,... | collective-permute-start | bytes 1544 | tf_op jit(solution)/shard_map/ppermute | solution.py:26
  23.0 6.6 %collective-permute-start.8 = (f32[256]{0:T(256)S(1)}, f32[256]{0:T(256)S(1)}, u32[]{:S(2)}, u32[]{:S(2)}) collective-permute-start(f32[256]{0:T(256)S(1)} %multiply_reduce_fusion), channel_id=1, source_target_pairs={{0,1},{1,0},{2,3},{3,2},{4,5},{5,4},{6,7},{7,6},{8,9},{9,8},{10,11... | collective-permute-start | bytes 3080 | tf_op jit(solution)/shard_map/ppermute | solution.py:26
  23.9 9.9 %collective-permute-start.11 = (f32[128]{0:T(128)S(1)}, f32[128]{0:T(128)S(1)}, u32[]{:S(2)}, u32[]{:S(2)}) collective-permute-start(f32[128]{0:T(128)S(1)} %add.57), channel_id=1, source_target_pairs={{0,8},{1,9},{2,10},{3,11},{4,12},{5,13},{6,14},{7,15},{8,0},{9,1},... | collective-permute-start | bytes 1544 | tf_op jit(solution)/shard_map/ppermute | solution.py:26
  26.2 18.7 %collective-permute-start.7 = (f32[256,128]{1,0:T(8,128)S(1)}, f32[256,128]{1,0:T(8,128)S(1)}, u32[]{:S(2)}, u32[]{:S(2)}) collective-permute-start(f32[256,128]{1,0:T(8,128)S(1)} %get-tuple-element.10), channel_id=1, source_target_pairs={{0,12},{1,8},{2,4},{3,0},{4,14},{5,10},{6,6},{7,2},{8,13},{9,9},{1... | collective-permute-start | bytes 393224 | tf_op jit(solution)/shard_map/ppermute | solution.py:26
  28.1 16.8 %collective-permute-start.6 = (f32[256,128]{1,0:T(8,128)S(1)}, f32[256,128]{1,0:T(8,128)S(1)}, u32[]{:S(2)}, u32[]{:S(2)}) collective-permute-start(f32[256,128]{1,0:T(8,128)S(1)} %get-tuple-element.11), channel_id=1, source_target_pairs={{0,8},{1,12},{2,0},{3,4},{4,10},{5,14},{6,2},{7,6},{8,9},{9,13},{1... | collective-permute-start | bytes 393224 | tf_op jit(solution)/shard_map/ppermute | solution.py:26
  29.0 16.0 %collective-permute-start.4 = (f32[256,128]{1,0:T(8,128)S(1)}, f32[256,128]{1,0:T(8,128)S(1)}, u32[]{:S(2)}, u32[]{:S(2)}) collective-permute-start(f32[256,128]{1,0:T(8,128)S(1)} %get-tuple-element.12), channel_id=1, source_target_pairs={{0,0},{1,4},{2,8},{3,12},{4,2},{5,6},{6,10},{7,14},{8,1},{9,5},{10... | collective-permute-start | bytes 393224 | tf_op jit(solution)/shard_map/ppermute | solution.py:26
  29.6 18.4 %collective-permute-start.5 = (f32[256,128]{1,0:T(8,128)S(1)}, f32[256,128]{1,0:T(8,128)S(1)}, u32[]{:S(2)}, u32[]{:S(2)}) collective-permute-start(f32[256,128]{1,0:T(8,128)S(1)} %get-tuple-element.9), channel_id=1, source_target_pairs={{0,4},{1,0},{2,12},{3,8},{4,6},{5,2},{6,14},{7,10},{8,5},{9,1},{10... | collective-permute-start | bytes 393224 | tf_op jit(solution)/shard_map/ppermute | solution.py:26
  33.8 11.2 %collective-permute-start.9 = (f32[256]{0:T(256)S(1)}, f32[256]{0:T(256)S(1)}, u32[]{:S(2)}, u32[]{:S(2)}) collective-permute-start(f32[256]{0:T(256)S(1)} %add.53), channel_id=1, source_target_pairs={{0,2},{1,3},{2,0},{3,1},{4,6},{5,7},{6,4},{7,5},{8,10},{9,11},{10,... | collective-permute-start | bytes 3080 | tf_op jit(solution)/shard_map/ppermute | solution.py:26

commit v3 on v1

--- a/solution.py
+++ b/solution.py
@@ -35,7 +35,7 @@
 def on_square_grid(left_docs, right_docs):
     side = lax.axis_size("col")
     feat_total = left_docs.shape[1] * side
-    row, col = lax.axis_index("row"), lax.axis_index("col")
+    row = lax.axis_index("row")
 
     step_even = [
         moved(right_docs, side, lambda k, c, j=j: (c ^ (2 * j), k)) for j in range(side // 2)
@@ -51,13 +51,10 @@
         right_sq = right_sq + moved(right_own, side, lambda r, c, d=delta: (r ^ d, c))
 
     partial = jnp.stack([contract(left_docs, block) for block in held])
-
-    def for_col(target):
-        return lax.dynamic_index_in_dim(partial, row ^ target, 0, keepdims=False)
-
-    summed = for_col(col)
-    for delta in range(1, side):
-        summed = summed + moved(for_col(col ^ delta), side, lambda r, c, d=delta: (r, c ^ d))
+    partial = jnp.stack(
+        [lax.dynamic_index_in_dim(partial, row ^ c, 0, keepdims=False) for c in range(side)]
+    )
+    summed = jnp.sum(lax.all_to_all(partial, "col", split_axis=0, concat_axis=0), axis=0)
     return finish(summed, left_sq, right_sq, feat_total)
 
 

time: 44.6 us -> 51.9 us (1.16)
  waiting for transfers between devices: 16.7 us -> 26.1 us
  starting transfers between devices: 23.2 us -> 21.1 us
  other arithmetic: 3.12 us -> 1.99 us
  matrix products: 1.22 us -> 2.27 us
    ppermute x13 -> x10, starting transfers between devices: 23.2 us -> 11.5 us  [moved(): return lax.ppermute(value, ('row', 'col'), pairs)]
    all_to_all x0 -> x1, starting transfers between devices: none -> 9.62 us  [on_square_grid(): lax.all_to_all(partial, 'col', split_axis=0, concat_axis=0)]
    ppermute x13 -> x10, waiting for transfers between devices: 16.7 us -> 26.1 us  [moved(): return lax.ppermute(value, ('row', 'col'), pairs)]
    reduce_sum x2, other arithmetic: 2.31 us -> 0.31 us  [squares(): return jnp.sum(widened * widened, axis=1)]
    dot_general x4, matrix products: 1.22 us -> 2.27 us  [contract(): lax.dot_general(left_part, right_part, (((1,), (1,)), ((), ())), preferre...]
    another operation x0 -> x1, other arithmetic: none -> 0.83 us  [on_square_grid(): jnp.stack([lax.dynamic_index_in_dim(partial, row ^ c, 0, keepdims=False)...]
  transfers between devices with their start and end apart: 13 -> 11, of which waited for: 4 -> 3; matrix products, arithmetic and copies ran while one was open for 8% -> 4% of each run, Pallas kernels for 0% -> 0%
where the time goes in v3:
time: 51.9 us; the launch traced here: 51.6 us
  waiting for transfers between devices  26.1 us (50%)
  starting transfers between devices  21.1 us (41%)
  matrix products  2.27 us (4%)
  other arithmetic  1.99 us (4%)
    ppermute x10, waiting for transfers between devices, moved(): return lax.ppermute(value, ('row', 'col'), pairs)  26.1 us
    ppermute x10, starting transfers between devices, moved(): return lax.ppermute(value, ('row', 'col'), pairs)  11.5 us
    all_to_all x1, starting transfers between devices, on_square_grid(): lax.all_to_all(partial, 'col', split_axis=0, concat_axis=0)  9.62 us
    dot_general x4, matrix products, contract(): lax.dot_general(left_part, right_part, (((1,), (1,)), ((), ())), preferre...  2.27 us
  transfers between devices with their start and end apart: 11, of which 3 were waited for; matrix products, arithmetic and copies ran while one was open for 4% of the time, Pallas kernels for 0%

profile of v3, /device:TPU:0, one launch (start us, length us, event | category | flops | bytes accessed | tf_op | source)
XLA Modules:
  0.0 51.6 jit_solution(17059086904771918459)
XLA Ops:
  0.0 2.9 %collective-permute-start.2 = (bf16[128,1024]{1,0:T(8,128)(2,1)}, bf16[128,1024]{1,0:T(8,128)(2,1)S(1)}, u32[]{:S(2)}, u32[]{:S(2)}) collective-permute-start(bf16[128,1024]{1,0:T(8,128)(2,1)} %param.3), channel_id=1, source_target_pairs={{0,8},{1,12},{2,0},{3,4},{4,9},{5,13},{6,1},{7,5},{8,10},{9,14},{1... | collective-permute-start | bytes 786440 | tf_op jit(solution)/shard_map/ppermute | solution.py:26
  2.9 1.6 %collective-permute-start = (bf16[128,1024]{1,0:T(8,128)(2,1)}, bf16[128,1024]{1,0:T(8,128)(2,1)S(1)}, u32[]{:S(2)}, u32[]{:S(2)}) collective-permute-start(bf16[128,1024]{1,0:T(8,128)(2,1)} %param.3), channel_id=1, source_target_pairs={{0,0},{1,4},{2,8},{3,12},{4,1},{5,5},{6,9},{7,13},{8,2},{9,6},{10,... | collective-permute-start | bytes 786440 | tf_op jit(solution)/shard_map/ppermute | solution.py:26
  4.5 18.1 %collective-permute-done.2 = bf16[128,1024]{1,0:T(8,128)(2,1)S(1)} collective-permute-done((bf16[128,1024]{1,0:T(8,128)(2,1)}, bf16[128,1024]{1,0:T(8,128)(2,1)S(1)}, u32[]{:S(2)}, u32[]{:S(2)}) %collective-permute-start.2) | collective-permute-done | bytes 262176 | tf_op jit(solution)/shard_map/ppermute | solution.py:26
  22.6 0.0 collective-permute-start.3
  22.6 0.0 collective-permute-done
  22.6 0.5 collective-permute-start.1
  23.2 1.3 %convolution_bitcast_fusion.1 = f32[1,256,128]{2,1,0:T(8,128)S(1)} fusion(bf16[256,1024]{1,0:T(8,128)(2,1)} %param.2, bf16[128,1024]{1,0:T(8,128)(2,1)S(1)} %collective-permute-done.2), kind=kOutput, calls=%fused_computation.1 | convolution fusion | flops 67108864 | bytes 917504 | tf_op jit(solution)/shard_map/dot_general | solution.py:10
  24.5 0.3 convolution_bitcast_fusion.3
  24.8 0.0 collective-permute-done.3
  24.8 0.3 convolution_bitcast_fusion
  25.2 0.3 convolution_bitcast_fusion.2
  25.6 0.8 %pad_maximum_fusion.1 = f32[4,256,128]{2,1,0:T(8,128)} fusion(f32[1,256,128]{2,1,0:T(8,128)S(1)} %get-tuple-element.6, f32[1,256,128]{2,1,0:T(8,128)S(1)} %get-tuple-element.7, f32[1,256,128]{2,1,0:T(8,128)S(1)} %get-tuple-element.8, f32[1,256,128]{2,1,0:T(8,128)S(1)} %get-tuple-element.5), kind=kLoop, calls=%fused_computation.6 | loop fusion | flops 393216 | bytes 1048576 | tf_op jit(solution)/shard_map/stack | solution.py:54
  26.4 9.6 %all-to-all-start = ((f32[4,256,128]{2,1,0:T(8,128)}), f32[4,256,128]{2,1,0:T(8,128)S(1)}, u32[]{:S(2)}, u32[]{:S(2)}) async-start(f32[4,256,128]{2,1,0:T(8,128)} %pad_maximum_fusion.1), calls=%async_computation | async-start | bytes 1048576 | tf_op jit(solution)/shard_map/all_to_all | solution.py:57
  36.0 0.1 multiply_reduce_fusion.1
  36.2 0.1 collective-permute-start.7
  36.2 0.9 %collective-permute-start.8 = (f32[128]{0:T(128)S(1)}, f32[128]{0:T(128)S(1)}, u32[]{:S(2)}, u32[]{:S(2)}) collective-permute-start(f32[128]{0:T(128)S(1)} %multiply_reduce_fusion.1), channel_id=1, source_target_pairs={{0,8},{1,9},{2,10},{3,11},{4,12},{5,13},{6,14},{7,15},{8,0},{9,1},... | collective-permute-start | bytes 1544 | tf_op jit(solution)/shard_map/ppermute | solution.py:26
  37.2 0.9 %collective-permute-start.9 = (f32[128]{0:T(128)S(1)}, f32[128]{0:T(128)S(1)}, u32[]{:S(2)}, u32[]{:S(2)}) collective-permute-start(f32[128]{0:T(128)S(1)} %multiply_reduce_fusion.1), channel_id=1, source_target_pairs={{0,12},{1,13},{2,14},{3,15},{4,8},{5,9},{6,10},{7,11},{8,4},{9,5},... | collective-permute-start | bytes 1544 | tf_op jit(solution)/shard_map/ppermute | solution.py:26
  38.1 0.2 multiply_reduce_fusion
  38.3 2.1 %collective-permute-start.4 = (f32[256]{0:T(256)S(1)}, f32[256]{0:T(256)S(1)}, u32[]{:S(2)}, u32[]{:S(2)}) collective-permute-start(f32[256]{0:T(256)S(1)} %multiply_reduce_fusion), channel_id=1, source_target_pairs={{0,1},{1,0},{2,3},{3,2},{4,5},{5,4},{6,7},{7,6},{8,9},{9,8},{10,11... | collective-permute-start | bytes 3080 | tf_op jit(solution)/shard_map/ppermute | solution.py:26
  40.4 2.4 %collective-permute-start.5 = (f32[256]{0:T(256)S(1)}, f32[256]{0:T(256)S(1)}, u32[]{:S(2)}, u32[]{:S(2)}) collective-permute-start(f32[256]{0:T(256)S(1)} %multiply_reduce_fusion), channel_id=1, source_target_pairs={{0,2},{1,3},{2,0},{3,1},{4,6},{5,7},{6,4},{7,5},{8,10},{9,11},{10,... | collective-permute-start | bytes 3080 | tf_op jit(solution)/shard_map/ppermute | solution.py:26
  42.7 0.1 collective-permute-start.6
  42.8 2.1 %collective-permute-done.4 = f32[256]{0:T(256)S(1)} collective-permute-done((f32[256]{0:T(256)S(1)}, f32[256]{0:T(256)S(1)}, u32[]{:S(2)}, u32[]{:S(2)}) %collective-permute-start.4) | collective-permute-done | bytes 1056 | tf_op jit(solution)/shard_map/ppermute | solution.py:26
  45.0 5.8 %collective-permute-done.5 = f32[256]{0:T(256)S(1)} collective-permute-done((f32[256]{0:T(256)S(1)}, f32[256]{0:T(256)S(1)}, u32[]{:S(2)}, u32[]{:S(2)}) %collective-permute-start.5) | collective-permute-done | bytes 1056 | tf_op jit(solution)/shard_map/ppermute | solution.py:26
  50.9 0.8 %multiply_multiply_fusion = f32[256,128]{1,0:T(8,128)} fusion(f32[256,128]{1,0:T(8,128)S(1)} %reduce_sum.27, f32[128]{0:T(128)S(1)} %add_rsqrt_fusion, f32[256]{0:T(256)S(1)} %rsqrt_multiply_fusion), kind=kLoop, calls=%fused_computation.8 | loop fusion | flops 65536 | bytes 263680 | tf_op jit(solution)/shard_map/mul | solution.py:32
  (15 shorter events, 0.2 us)
Async XLA Ops:
  0.0 24.5 %copy-start = (bf16[256,1024]{1,0:T(8,128)(2,1)S(1)}, bf16[256,1024]{1,0:T(8,128)(2,1)}, u32[]{:S(2)}) copy-start(bf16[256,1024]{1,0:T(8,128)(2,1)} %param.2) | copy-start | bytes 1572868
  0.0 22.6 %collective-permute-start.2 = (bf16[128,1024]{1,0:T(8,128)(2,1)}, bf16[128,1024]{1,0:T(8,128)(2,1)S(1)}, u32[]{:S(2)}, u32[]{:S(2)}) collective-permute-start(bf16[128,1024]{1,0:T(8,128)(2,1)} %param.3), channel_id=1, source_target_pairs={{0,8},{1,12},{2,0},{3,4},{4,9},{5,13},{6,1},{7,5},{8,10},{9,14},{1... | collective-permute-start | bytes 786440 | tf_op jit(solution)/shard_map/ppermute | solution.py:26
  2.9 19.7 %collective-permute-start = (bf16[128,1024]{1,0:T(8,128)(2,1)}, bf16[128,1024]{1,0:T(8,128)(2,1)S(1)}, u32[]{:S(2)}, u32[]{:S(2)}) collective-permute-start(bf16[128,1024]{1,0:T(8,128)(2,1)} %param.3), channel_id=1, source_target_pairs={{0,0},{1,4},{2,8},{3,12},{4,1},{5,5},{6,9},{7,13},{8,2},{9,6},{10,... | collective-permute-start | bytes 786440 | tf_op jit(solution)/shard_map/ppermute | solution.py:26
  22.6 2.2 %collective-permute-start.3 = (bf16[128,1024]{1,0:T(8,128)(2,1)S(1)}, bf16[128,1024]{1,0:T(8,128)(2,1)S(1)}, u32[]{:S(2)}, u32[]{:S(2)}) collective-permute-start(bf16[128,1024]{1,0:T(8,128)(2,1)S(1)} %collective-permute-done.2), channel_id=1, source_target_pairs={{0,4},{1,5},{2,6},{3,7},{4,0},{5,1},{6,2},{7,3},{8,12},{9,13},{10,... | collective-permute-start | bytes 786440 | tf_op jit(solution)/shard_map/ppermute | solution.py:26
  22.6 2.5 %collective-permute-start.1 = (bf16[128,1024]{1,0:T(8,128)(2,1)S(1)}, bf16[128,1024]{1,0:T(8,128)(2,1)S(1)}, u32[]{:S(2)}, u32[]{:S(2)}) collective-permute-start(bf16[128,1024]{1,0:T(8,128)(2,1)S(1)} %collective-permute-done), channel_id=1, source_target_pairs={{0,4},{1,5},{2,6},{3,7},{4,0},{5,1},{6,2},{7,3},{8,12},{9,13},{10,... | collective-permute-start | bytes 786440 | tf_op jit(solution)/shard_map/ppermute | solution.py:26
  26.4 9.6 %copy-start.1 = (bf16[128,1024]{1,0:T(8,128)(2,1)S(1)}, bf16[128,1024]{1,0:T(8,128)(2,1)}, u32[]{:S(2)}) copy-start(bf16[128,1024]{1,0:T(8,128)(2,1)} %param.3) | copy-start | bytes 786436
  26.4 24.4 %all-to-all-start = ((f32[4,256,128]{2,1,0:T(8,128)}), f32[4,256,128]{2,1,0:T(8,128)S(1)}, u32[]{:S(2)}, u32[]{:S(2)}) async-start(f32[4,256,128]{2,1,0:T(8,128)} %pad_maximum_fusion.1), calls=%async_computation | async-start | bytes 1048576 | tf_op jit(solution)/shard_map/all_to_all | solution.py:57
  36.2 6.6 %collective-permute-start.7 = (f32[128]{0:T(128)S(1)}, f32[128]{0:T(128)S(1)}, u32[]{:S(2)}, u32[]{:S(2)}) collective-permute-start(f32[128]{0:T(128)S(1)} %multiply_reduce_fusion.1), channel_id=1, source_target_pairs={{0,4},{1,5},{2,6},{3,7},{4,0},{5,1},{6,2},{7,3},{8,12},{9,13},{10,... | collective-permute-start | bytes 1544 | tf_op jit(solution)/shard_map/ppermute | solution.py:26
  36.2 6.6 %collective-permute-start.8 = (f32[128]{0:T(128)S(1)}, f32[128]{0:T(128)S(1)}, u32[]{:S(2)}, u32[]{:S(2)}) collective-permute-start(f32[128]{0:T(128)S(1)} %multiply_reduce_fusion.1), channel_id=1, source_target_pairs={{0,8},{1,9},{2,10},{3,11},{4,12},{5,13},{6,14},{7,15},{8,0},{9,1},... | collective-permute-start | bytes 1544 | tf_op jit(solution)/shard_map/ppermute | solution.py:26
  37.2 5.6 %collective-permute-start.9 = (f32[128]{0:T(128)S(1)}, f32[128]{0:T(128)S(1)}, u32[]{:S(2)}, u32[]{:S(2)}) collective-permute-start(f32[128]{0:T(128)S(1)} %multiply_reduce_fusion.1), channel_id=1, source_target_pairs={{0,12},{1,13},{2,14},{3,15},{4,8},{5,9},{6,10},{7,11},{8,4},{9,5},... | collective-permute-start | bytes 1544 | tf_op jit(solution)/shard_map/ppermute | solution.py:26
  38.3 6.7 %collective-permute-start.4 = (f32[256]{0:T(256)S(1)}, f32[256]{0:T(256)S(1)}, u32[]{:S(2)}, u32[]{:S(2)}) collective-permute-start(f32[256]{0:T(256)S(1)} %multiply_reduce_fusion), channel_id=1, source_target_pairs={{0,1},{1,0},{2,3},{3,2},{4,5},{5,4},{6,7},{7,6},{8,9},{9,8},{10,11... | collective-permute-start | bytes 3080 | tf_op jit(solution)/shard_map/ppermute | solution.py:26
  40.4 10.4 %collective-permute-start.5 = (f32[256]{0:T(256)S(1)}, f32[256]{0:T(256)S(1)}, u32[]{:S(2)}, u32[]{:S(2)}) collective-permute-start(f32[256]{0:T(256)S(1)} %multiply_reduce_fusion), channel_id=1, source_target_pairs={{0,2},{1,3},{2,0},{3,1},{4,6},{5,7},{6,4},{7,5},{8,10},{9,11},{10,... | collective-permute-start | bytes 3080 | tf_op jit(solution)/shard_map/ppermute | solution.py:26
  42.7 8.1 %collective-permute-start.6 = (f32[256]{0:T(256)S(1)}, f32[256]{0:T(256)S(1)}, u32[]{:S(2)}, u32[]{:S(2)}) collective-permute-start(f32[256]{0:T(256)S(1)} %multiply_reduce_fusion), channel_id=1, source_target_pairs={{0,3},{1,2},{2,1},{3,0},{4,7},{5,6},{6,5},{7,4},{8,11},{9,10},{10,... | collective-permute-start | bytes 3080 | tf_op jit(solution)/shard_map/ppermute | solution.py:26

commit v4 on v2

--- a/solution.py
+++ b/solution.py
@@ -1,6 +1,10 @@
+import functools
+
 import jax
 import jax.numpy as jnp
 from jax import lax
+from jax.experimental import pallas as pl
+from jax.experimental.pallas import tpu as pltpu
 from jax.sharding import PartitionSpec as P
 
 epsilon = 1e-06
@@ -21,8 +25,9 @@
     pairs = []
     for row in range(side):
         for col in range(side):
-            to_row, to_col = place(row, col)
-            pairs.append((row * side + col, to_row * side + to_col))
+            target = place(row, col)
+            if target is not None:
+                pairs.append((row * side + col, target[0] * side + target[1]))
     return lax.ppermute(value, ("row", "col"), pairs)
 
 
@@ -32,31 +37,104 @@
     return summed / feat_total * left_scale[:, None] * right_scale[None, :]
 
 
+def row_squares(block):
+    wide = block.astype(jnp.float32)
+    wide = wide * wide
+    high = wide.astype(jnp.bfloat16)
+    low = (wide - high.astype(jnp.float32)).astype(jnp.bfloat16)
+    ones = jnp.ones((8, block.shape[1]), jnp.bfloat16)
+    return contract(ones, high) + contract(ones, low)
+
+
+def multiply_kernel(turn, left, near, early_inner, late_inner, early_outer, late_outer, *messages):
+    rows, width = left.shape[0], early_inner.shape[0]
+    early = turn[0] == 1
+    line = lax.broadcasted_iota(jnp.int32, (8, width), 0)
+    lefts = [(block[...], row_squares(block[...])) for block in (left, near)]
+    for v, (one, other) in enumerate(((early_outer, late_outer), (early_inner, late_inner))):
+        right = jnp.where(early, one[...], other[...])
+        right_sq = row_squares(right)
+        for u, (block, left_sq) in enumerate(lefts):
+            gram = contract(block, right)
+            sums = right_sq
+            for part in range(rows // width):
+                sums = jnp.where(line == part + 1, left_sq[:, part * width:(part + 1) * width], sums)
+            number = 2 * (v ^ turn[2]) + (u ^ turn[1])
+            for n, message in enumerate(messages):
+                @pl.when(number == n)
+                def _(message=message, gram=gram, sums=sums):
+                    message[:rows] = gram
+                    message[rows:] = sums
+
+
+def multiply(turn, left, *others):
+    shape = (left.shape[0] + 8, others[-1].shape[0])
+    return pl.pallas_call(
+        multiply_kernel,
+        out_shape=[jax.ShapeDtypeStruct(shape, jnp.float32)] * 4,
+        in_specs=[pl.BlockSpec(memory_space=pltpu.SMEM)] + [pl.BlockSpec(memory_space=pltpu.VMEM)] * 6,
+        out_specs=[pl.BlockSpec(memory_space=pltpu.VMEM)] * 4,
+        compiler_params=pltpu.CompilerParams(vmem_limit_bytes=24 * 2**20),
+    )(turn, left, *others)
+
+
+def scale_kernel(feat_total, *refs):
+    messages, out = refs[:-1], refs[-1]
+    rows, width = out.shape
+    total = messages[0][...]
+    for message in messages[1:]:
+        total = total + message[...]
+    scales = lax.rsqrt(total[rows:] / feat_total + epsilon)
+    tile = (width, width)
+    diagonal = lax.broadcasted_iota(jnp.int32, tile, 0) == lax.broadcasted_iota(jnp.int32, tile, 1)
+    for part in range(rows // width):
+        along = jnp.broadcast_to(scales[part + 1:part + 2], tile)
+        down = jnp.sum(jnp.where(diagonal, along, 0.0), axis=1, keepdims=True)
+        here = slice(part * width, (part + 1) * width)
+        out[here] = total[here] / feat_total * down * scales[:1]
+
+
+def scale(feat_total, messages):
+    rows, width = messages[0].shape
+    return pl.pallas_call(
+        functools.partial(scale_kernel, feat_total),
+        out_shape=jax.ShapeDtypeStruct((rows - 8, width), jnp.float32),
+        in_specs=[pl.BlockSpec(memory_space=pltpu.VMEM)] * len(messages),
+        out_specs=pl.BlockSpec(memory_space=pltpu.VMEM),
+    )(*messages)
+
+
 def on_square_grid(left_docs, right_docs):
     side = lax.axis_size("col")
     feat_total = left_docs.shape[1] * side
     row, col = lax.axis_index("row"), lax.axis_index("col")
+    core = row & 1
+    early = (row >> 1) == (col >> 1)
 
-    def spread(c):
-        return 2 * (c & 1) + (c >> 1)
+    def inner(c):
+        return c in (1, 2)
 
-    held = moved(right_docs, side, lambda k, c: (spread(c), k))
-    far = moved(left_docs, side, lambda r, c: (r ^ 2, c))
+    def taker(r, c):
+        return (r & 2) + (c & 1)
+
+    crossed = moved(right_docs, side, lambda r, c: None if inner(c) else (r ^ 2, c))
+    early_inner = moved(right_docs, side, lambda r, c: (taker(r, c), r) if inner(c) else None)
+    early_outer = moved(right_docs, side, lambda r, c: None if inner(c) else (taker(r, c), r))
     near = moved(left_docs, side, lambda r, c: (r ^ 1, c))
-    lefts = [left_docs, near, far, moved(far, side, lambda r, c: (r ^ 1, c))]
-    partial = jnp.stack([contract(block, held) for block in lefts])
-
-    summed = 0.0
-    for m in range(side):
-        mine = lax.dynamic_index_in_dim(partial, row ^ col ^ m, 0, keepdims=False)
-        summed = summed + moved(mine, side, lambda i, k, m=m: (k ^ m, spread(i)))
-
-    left_sq, right_sq = squares(left_docs), squares(right_docs)
-    left_sq, right_sq, _ = lax.optimization_barrier((left_sq, right_sq, partial))
-    for step in (1, 2):
-        left_sq = left_sq + moved(left_sq, side, lambda r, c, d=step: (r, c ^ d))
-        right_sq = right_sq + moved(right_sq, side, lambda r, c, d=step: (r ^ d, c))
-    return finish(summed, left_sq, right_sq, feat_total)
+    late_outer = moved(crossed, side, lambda r, c: None if inner(c) else (taker(r, c), r ^ 2))
+    late_inner = moved(early_inner, side, lambda r, c: (r ^ 2, c) if r >> 1 == c >> 1 else None)
+    turn = jnp.stack([early.astype(jnp.int32), (col & 1) ^ core, (col >> 1) ^ core])
+    messages = multiply(turn, left_docs, near, early_inner, late_inner, early_outer, late_outer)
+    received = [
+        moved(
+            messages[2 * cross + flip],
+            side,
+            lambda r, k, g=cross, f=flip: ((r & 2) + ((k & 1) ^ f), (r & 1) + 2 * ((k >> 1) ^ g)),
+        )
+        for cross in (0, 1)
+        for flip in (0, 1)
+    ]
+    return scale(feat_total, received)
 
 
 def on_any_grid(left_docs, right_docs):

time: 49.1 us -> 48.4 us (0.986)
  the two profiles are of different devices: /device:TPU:0 before, /device:TPU:7 now
where the time goes in v4:
time: 48.4 us; the launch traced here: 48.1 us
  starting transfers between devices  23.2 us (48%)
  waiting for transfers between devices  18.3 us (38%)
  Pallas kernels  4.75 us (10%)
  local copies, waits for them, and re-layouts  1.7 us (4%)
    ppermute x10, starting transfers between devices, moved(): return lax.ppermute(value, ('row', 'col'), pairs)  23.2 us
    ppermute x10, waiting for transfers between devices, moved(): return lax.ppermute(value, ('row', 'col'), pairs)  18.3 us
    pallas_call x1, Pallas kernels, multiply(): pl.pallas_call(multiply_kernel, out_shape=[jax.ShapeDtypeStruct(shape, jn...  2.87 us
    pallas_call x1, Pallas kernels, scale(): pl.pallas_call(functools.partial(scale_kernel, feat_total), out_shape=jax...  1.88 us
    unnamed x10, local copies, waits for them, and re-layouts  1.7 us
  transfers between devices with their start and end apart: 10, of which 7 were waited for; matrix products, arithmetic and copies ran while one was open for 0% of the time, Pallas kernels for 0%

profile of v4, /device:TPU:7, one launch (start us, length us, event | category | flops | bytes accessed | tf_op | source)
XLA Modules:
  0.0 48.1 jit_solution(10156410028319873032)
XLA Ops:
  0.0 0.7 %collective-permute-start.1 = (bf16[128,1024]{1,0:T(8,128)(2,1)}, bf16[128,1024]{1,0:T(8,128)(2,1)S(1)}, u32[]{:S(2)}, u32[]{:S(2)}) collective-permute-start(bf16[128,1024]{1,0:T(8,128)(2,1)} %param.3), channel_id=1, source_target_pairs={{1,4},{2,0},{5,5},{6,1},{9,14},{10,10},{13,15},{14,11},{17,20},{18... | collective-permute-start | bytes 786440 | tf_op jit(solution)/shard_map/ppermute | solution.py:31
  0.7 2.8 %collective-permute-start.4 = (bf16[128,1024]{1,0:T(8,128)(2,1)}, bf16[128,1024]{1,0:T(8,128)(2,1)S(1)}, u32[]{:S(2)}, u32[]{:S(2)}) collective-permute-start(bf16[128,1024]{1,0:T(8,128)(2,1)} %param.3), channel_id=1, source_target_pairs={{0,8},{3,11},{4,12},{7,15},{8,0},{11,3},{12,4},{15,7},{16,24},{19,... | collective-permute-start | bytes 786440 | tf_op jit(solution)/shard_map/ppermute | solution.py:31
  3.5 1.0 %collective-permute-start = (bf16[256,1024]{1,0:T(8,128)(2,1)}, bf16[256,1024]{1,0:T(8,128)(2,1)S(1)}, u32[]{:S(2)}, u32[]{:S(2)}) collective-permute-start(bf16[256,1024]{1,0:T(8,128)(2,1)} %left.1), channel_id=1, source_target_pairs={{0,4},{1,5},{2,6},{3,7},{4,0},{5,1},{6,2},{7,3},{8,12},{9,13},{10,... | collective-permute-start | bytes 1572872 | tf_op jit(solution)/shard_map/ppermute | solution.py:31
  4.5 4.6 %collective-permute-start.3 = (bf16[128,1024]{1,0:T(8,128)(2,1)}, bf16[128,1024]{1,0:T(8,128)(2,1)S(1)}, u32[]{:S(2)}, u32[]{:S(2)}) collective-permute-start(bf16[128,1024]{1,0:T(8,128)(2,1)} %param.3), channel_id=1, source_target_pairs={{0,0},{3,4},{4,1},{7,5},{8,10},{11,14},{12,11},{15,15},{16,16},{19... | collective-permute-start | bytes 786440 | tf_op jit(solution)/shard_map/ppermute | solution.py:31
  9.1 0.0 collective-permute-done.1.early_inner
  9.1 1.3 %collective-permute-start.2 = (bf16[128,1024]{1,0:T(8,128)(2,1)S(1)}, bf16[128,1024]{1,0:T(8,128)(2,1)S(1)}, u32[]{:S(2)}, u32[]{:S(2)}) collective-permute-start(bf16[128,1024]{1,0:T(8,128)(2,1)S(1)} %collective-permute-done.1.early_inner), channel_id=1, source_target_pairs={{0,8},{1,9},{4,12},{5,13},{10,2},{11,3},{14,6},{15,7},{16,24},{17,... | collective-permute-start | bytes 786440 | tf_op jit(solution)/shard_map/ppermute | solution.py:31
  10.4 0.0 collective-permute-done.4
  10.4 4.4 %collective-permute-start.5 = (bf16[128,1024]{1,0:T(8,128)(2,1)S(1)}, bf16[128,1024]{1,0:T(8,128)(2,1)S(1)}, u32[]{:S(2)}, u32[]{:S(2)}) collective-permute-start(bf16[128,1024]{1,0:T(8,128)(2,1)S(1)} %collective-permute-done.4), channel_id=1, source_target_pairs={{0,2},{3,6},{4,3},{7,7},{8,8},{11,12},{12,9},{15,13},{16,18},{19,2... | collective-permute-start | bytes 786440 | tf_op jit(solution)/shard_map/ppermute | solution.py:31
  14.8 0.1 pad_add_fusion.turn
  14.9 0.1 collective-permute-done.3.early_outer
  15.0 1.2 %collective-permute-done.2.late_inner = bf16[128,1024]{1,0:T(8,128)(2,1)S(1)} collective-permute-done((bf16[128,1024]{1,0:T(8,128)(2,1)S(1)}, bf16[128,1024]{1,0:T(8,128)(2,1)S(1)}, u32[]{:S(2)}, u32[]{:S(2)}) %collective-permute-start.2) | collective-permute-done | bytes 262176 | tf_op jit(solution)/shard_map/ppermute | solution.py:31
  16.2 5.3 %collective-permute-done.5.late_outer = bf16[128,1024]{1,0:T(8,128)(2,1)S(1)} collective-permute-done((bf16[128,1024]{1,0:T(8,128)(2,1)S(1)}, bf16[128,1024]{1,0:T(8,128)(2,1)S(1)}, u32[]{:S(2)}, u32[]{:S(2)}) %collective-permute-start.5) | collective-permute-done | bytes 262176 | tf_op jit(solution)/shard_map/ppermute | solution.py:31
  21.6 1.0 %copy-done = bf16[256,1024]{1,0:T(8,128)(2,1)S(1)} copy-done((bf16[256,1024]{1,0:T(8,128)(2,1)S(1)}, bf16[256,1024]{1,0:T(8,128)(2,1)}, u32[]{:S(2)}) %copy-start) | copy-done | bytes 524312
  22.6 2.9 %shard_map.28 = (f32[264,128]{1,0:T(8,128)S(1)}, f32[264,128]{1,0:T(8,128)S(1)}, f32[264,128]{1,0:T(8,128)S(1)}, f32[264,128]{1,0:T(8,128)S(1)}) custom-call(s32[3]{0:T(128)S(1)} %pad_add_fusion.turn, bf16[256,1024]{1,0:T(8,128)(2,1)S(1)} %copy-done, bf16[256,1024]{1,0:T(8,128)(2,1)S(1)} %collective-permute-done.near, ...), custom_call_target="tpu_custom_call" | custom-call | tf_op jit(solution)/shard_map/pallas_call | solution.py:72
  25.5 6.2 %collective-permute-start.6 = (f32[264,128]{1,0:T(8,128)S(1)}, f32[264,128]{1,0:T(8,128)S(1)}, u32[]{:S(2)}, u32[]{:S(2)}) collective-permute-start(f32[264,128]{1,0:T(8,128)S(1)} %get-tuple-element.9), channel_id=1, source_target_pairs={{0,0},{1,4},{2,2},{3,6},{4,1},{5,5},{6,3},{7,7},{8,8},{9,12},{10,1... | collective-permute-start | bytes 405512 | tf_op jit(solution)/shard_map/ppermute | solution.py:31
  31.7 0.1 collective-permute-start.7
  31.8 0.1 collective-permute-start.8
  31.9 2.1 %collective-permute-start.9 = (f32[264,128]{1,0:T(8,128)S(1)}, f32[264,128]{1,0:T(8,128)S(1)}, u32[]{:S(2)}, u32[]{:S(2)}) collective-permute-start(f32[264,128]{1,0:T(8,128)S(1)} %get-tuple-element.12), channel_id=1, source_target_pairs={{0,6},{1,2},{2,4},{3,0},{4,7},{5,3},{6,5},{7,1},{8,14},{9,10},{10,... | collective-permute-start | bytes 405512 | tf_op jit(solution)/shard_map/ppermute | solution.py:31
  34.0 0.4 collective-permute-done.6.refs_0_
  34.4 2.9 %collective-permute-done.7.refs_1_ = f32[264,128]{1,0:T(8,128)S(1)} collective-permute-done((f32[264,128]{1,0:T(8,128)S(1)}, f32[264,128]{1,0:T(8,128)S(1)}, u32[]{:S(2)}, u32[]{:S(2)}) %collective-permute-start.7) | collective-permute-done | bytes 135200 | tf_op jit(solution)/shard_map/ppermute | solution.py:31
  37.2 2.2 %collective-permute-done.8.refs_2_ = f32[264,128]{1,0:T(8,128)S(1)} collective-permute-done((f32[264,128]{1,0:T(8,128)S(1)}, f32[264,128]{1,0:T(8,128)S(1)}, u32[]{:S(2)}, u32[]{:S(2)}) %collective-permute-start.8) | collective-permute-done | bytes 135200 | tf_op jit(solution)/shard_map/ppermute | solution.py:31
  39.4 6.1 %collective-permute-done.9.refs_3_ = f32[264,128]{1,0:T(8,128)S(1)} collective-permute-done((f32[264,128]{1,0:T(8,128)S(1)}, f32[264,128]{1,0:T(8,128)S(1)}, u32[]{:S(2)}, u32[]{:S(2)}) %collective-permute-start.9) | collective-permute-done | bytes 135200 | tf_op jit(solution)/shard_map/ppermute | solution.py:31
  45.6 0.6 %copy-done.4 = f32[264,128]{1,0:T(8,128)} copy-done((f32[264,128]{1,0:T(8,128)}, f32[264,128]{1,0:T(8,128)S(1)}, u32[]{:S(2)}) %copy-start.4) | copy-done | bytes 135192
  46.2 1.9 %shard_map.29 = f32[256,128]{1,0:T(8,128)} custom-call(f32[264,128]{1,0:T(8,128)} %copy-done.1, f32[264,128]{1,0:T(8,128)} %copy-done.2, f32[264,128]{1,0:T(8,128)} %copy-done.3, f32[264,128]{1,0:T(8,128)} %copy-done.4), custom_call_target="tpu_custom_call" | custom-call | tf_op jit(solution)/shard_map/pallas_call | solution.py:99
  (9 shorter events, 0.0 us)
Async XLA Ops:
  0.0 9.1 %collective-permute-start.1 = (bf16[128,1024]{1,0:T(8,128)(2,1)}, bf16[128,1024]{1,0:T(8,128)(2,1)S(1)}, u32[]{:S(2)}, u32[]{:S(2)}) collective-permute-start(bf16[128,1024]{1,0:T(8,128)(2,1)} %param.3), channel_id=1, source_target_pairs={{1,4},{2,0},{5,5},{6,1},{9,14},{10,10},{13,15},{14,11},{17,20},{18... | collective-permute-start | bytes 786440 | tf_op jit(solution)/shard_map/ppermute | solution.py:31
  0.7 9.7 %collective-permute-start.4 = (bf16[128,1024]{1,0:T(8,128)(2,1)}, bf16[128,1024]{1,0:T(8,128)(2,1)S(1)}, u32[]{:S(2)}, u32[]{:S(2)}) collective-permute-start(bf16[128,1024]{1,0:T(8,128)(2,1)} %param.3), channel_id=1, source_target_pairs={{0,8},{3,11},{4,12},{7,15},{8,0},{11,3},{12,4},{15,7},{16,24},{19,... | collective-permute-start | bytes 786440 | tf_op jit(solution)/shard_map/ppermute | solution.py:31
  3.5 18.1 %collective-permute-start = (bf16[256,1024]{1,0:T(8,128)(2,1)}, bf16[256,1024]{1,0:T(8,128)(2,1)S(1)}, u32[]{:S(2)}, u32[]{:S(2)}) collective-permute-start(bf16[256,1024]{1,0:T(8,128)(2,1)} %left.1), channel_id=1, source_target_pairs={{0,4},{1,5},{2,6},{3,7},{4,0},{5,1},{6,2},{7,3},{8,12},{9,13},{10,... | collective-permute-start | bytes 1572872 | tf_op jit(solution)/shard_map/ppermute | solution.py:31
  4.5 10.5 %collective-permute-start.3 = (bf16[128,1024]{1,0:T(8,128)(2,1)}, bf16[128,1024]{1,0:T(8,128)(2,1)S(1)}, u32[]{:S(2)}, u32[]{:S(2)}) collective-permute-start(bf16[128,1024]{1,0:T(8,128)(2,1)} %param.3), channel_id=1, source_target_pairs={{0,0},{3,4},{4,1},{7,5},{8,10},{11,14},{12,11},{15,15},{16,16},{19... | collective-permute-start | bytes 786440 | tf_op jit(solution)/shard_map/ppermute | solution.py:31
  9.1 7.1 %collective-permute-start.2 = (bf16[128,1024]{1,0:T(8,128)(2,1)S(1)}, bf16[128,1024]{1,0:T(8,128)(2,1)S(1)}, u32[]{:S(2)}, u32[]{:S(2)}) collective-permute-start(bf16[128,1024]{1,0:T(8,128)(2,1)S(1)} %collective-permute-done.1.early_inner), channel_id=1, source_target_pairs={{0,8},{1,9},{4,12},{5,13},{10,2},{11,3},{14,6},{15,7},{16,24},{17,... | collective-permute-start | bytes 786440 | tf_op jit(solution)/shard_map/ppermute | solution.py:31
  10.4 11.1 %collective-permute-start.5 = (bf16[128,1024]{1,0:T(8,128)(2,1)S(1)}, bf16[128,1024]{1,0:T(8,128)(2,1)S(1)}, u32[]{:S(2)}, u32[]{:S(2)}) collective-permute-start(bf16[128,1024]{1,0:T(8,128)(2,1)S(1)} %collective-permute-done.4), channel_id=1, source_target_pairs={{0,2},{3,6},{4,3},{7,7},{8,8},{11,12},{12,9},{15,13},{16,18},{19,2... | collective-permute-start | bytes 786440 | tf_op jit(solution)/shard_map/ppermute | solution.py:31
  21.6 1.0 %copy-start = (bf16[256,1024]{1,0:T(8,128)(2,1)S(1)}, bf16[256,1024]{1,0:T(8,128)(2,1)}, u32[]{:S(2)}) copy-start(bf16[256,1024]{1,0:T(8,128)(2,1)} %left.1) | copy-start | bytes 1572868
  25.5 8.9 %collective-permute-start.6 = (f32[264,128]{1,0:T(8,128)S(1)}, f32[264,128]{1,0:T(8,128)S(1)}, u32[]{:S(2)}, u32[]{:S(2)}) collective-permute-start(f32[264,128]{1,0:T(8,128)S(1)} %get-tuple-element.9), channel_id=1, source_target_pairs={{0,0},{1,4},{2,2},{3,6},{4,1},{5,5},{6,3},{7,7},{8,8},{9,12},{10,1... | collective-permute-start | bytes 405512 | tf_op jit(solution)/shard_map/ppermute | solution.py:31
  31.7 5.5 %collective-permute-start.7 = (f32[264,128]{1,0:T(8,128)S(1)}, f32[264,128]{1,0:T(8,128)S(1)}, u32[]{:S(2)}, u32[]{:S(2)}) collective-permute-start(f32[264,128]{1,0:T(8,128)S(1)} %get-tuple-element.10), channel_id=1, source_target_pairs={{0,4},{1,0},{2,6},{3,2},{4,5},{5,1},{6,7},{7,3},{8,12},{9,8},{10,1... | collective-permute-start | bytes 405512 | tf_op jit(solution)/shard_map/ppermute | solution.py:31
  31.8 7.7 %collective-permute-start.8 = (f32[264,128]{1,0:T(8,128)S(1)}, f32[264,128]{1,0:T(8,128)S(1)}, u32[]{:S(2)}, u32[]{:S(2)}) collective-permute-start(f32[264,128]{1,0:T(8,128)S(1)} %get-tuple-element.11), channel_id=1, source_target_pairs={{0,2},{1,6},{2,0},{3,4},{4,3},{5,7},{6,1},{7,5},{8,10},{9,14},{10,... | collective-permute-start | bytes 405512 | tf_op jit(solution)/shard_map/ppermute | solution.py:31
  31.9 13.7 %collective-permute-start.9 = (f32[264,128]{1,0:T(8,128)S(1)}, f32[264,128]{1,0:T(8,128)S(1)}, u32[]{:S(2)}, u32[]{:S(2)}) collective-permute-start(f32[264,128]{1,0:T(8,128)S(1)} %get-tuple-element.12), channel_id=1, source_target_pairs={{0,6},{1,2},{2,4},{3,0},{4,7},{5,3},{6,5},{7,1},{8,14},{9,10},{10,... | collective-permute-start | bytes 405512 | tf_op jit(solution)/shard_map/ppermute | solution.py:31
  34.4 11.2 %copy-start.1 = (f32[264,128]{1,0:T(8,128)}, f32[264,128]{1,0:T(8,128)S(1)}, u32[]{:S(2)}) copy-start(f32[264,128]{1,0:T(8,128)S(1)} %collective-permute-done.6.refs_0_) | copy-start | bytes 405508
  37.2 8.3 %copy-start.2 = (f32[264,128]{1,0:T(8,128)}, f32[264,128]{1,0:T(8,128)S(1)}, u32[]{:S(2)}) copy-start(f32[264,128]{1,0:T(8,128)S(1)} %collective-permute-done.7.refs_1_) | copy-start | bytes 405508
  39.4 6.1 %copy-start.3 = (f32[264,128]{1,0:T(8,128)}, f32[264,128]{1,0:T(8,128)S(1)}, u32[]{:S(2)}) copy-start(f32[264,128]{1,0:T(8,128)S(1)} %collective-permute-done.8.refs_2_) | copy-start | bytes 405508
  45.6 0.6 %copy-start.4 = (f32[264,128]{1,0:T(8,128)}, f32[264,128]{1,0:T(8,128)S(1)}, u32[]{:S(2)}) copy-start(f32[264,128]{1,0:T(8,128)S(1)} %collective-permute-done.9.refs_3_) | copy-start | bytes 405508

commit v5 on v2

--- a/solution.py
+++ b/solution.py
@@ -4,6 +4,11 @@
 from jax.sharding import PartitionSpec as P
 
 epsilon = 1e-06
+top = 2.0**15
+
+
+def inverse_norm(sum_of_squares):
+    return lax.rsqrt(jnp.maximum(sum_of_squares, 1e-36))
 
 
 def contract(left_part, right_part):
@@ -36,27 +41,37 @@
     side = lax.axis_size("col")
     feat_total = left_docs.shape[1] * side
     row, col = lax.axis_index("row"), lax.axis_index("col")
+    x, p = row >> 1, row & 1
 
-    def spread(c):
-        return 2 * (c & 1) + (c >> 1)
-
-    held = moved(right_docs, side, lambda k, c: (spread(c), k))
+    first = moved(right_docs, side, lambda k, c: (2 * (c & 1) + (c >> 1), k))
     far = moved(left_docs, side, lambda r, c: (r ^ 2, c))
-    near = moved(left_docs, side, lambda r, c: (r ^ 1, c))
-    lefts = [left_docs, near, far, moved(far, side, lambda r, c: (r ^ 1, c))]
-    partial = jnp.stack([contract(block, held) for block in lefts])
-
-    summed = 0.0
-    for m in range(side):
-        mine = lax.dynamic_index_in_dim(partial, row ^ col ^ m, 0, keepdims=False)
-        summed = summed + moved(mine, side, lambda i, k, m=m: (k ^ m, spread(i)))
 
     left_sq, right_sq = squares(left_docs), squares(right_docs)
-    left_sq, right_sq, _ = lax.optimization_barrier((left_sq, right_sq, partial))
-    for step in (1, 2):
-        left_sq = left_sq + moved(left_sq, side, lambda r, c, d=step: (r, c ^ d))
-        right_sq = right_sq + moved(right_sq, side, lambda r, c, d=step: (r ^ d, c))
-    return finish(summed, left_sq, right_sq, feat_total)
+    left_sqs = jnp.stack([left_sq] + [moved(left_sq, side, lambda r, c, d=d: (r, c ^ d)) for d in range(1, side)])
+    right_sqs = jnp.stack([right_sq] + [moved(right_sq, side, lambda r, c, d=d: (r ^ d, c)) for d in range(1, side)])
+
+    second = moved(first, side, lambda r, c: (r ^ 1, c))
+
+    def tile(left_block, right_block):
+        gram = contract(left_block, right_block)
+        down, along = inverse_norm(squares(left_block)), inverse_norm(squares(right_block))
+        return (gram * (down * top)[:, None] * along[None, :]).astype(jnp.float16)
+
+    tiles = jnp.stack([tile(l, r) for l in (left_docs, far) for r in (first, second)])
+    left_scale = lax.rsqrt(jnp.sum(left_sqs, axis=0) / feat_total + epsilon)
+    right_scale = lax.rsqrt(jnp.sum(right_sqs, axis=0) / feat_total + epsilon)
+    similarity = 0.0
+    for m in range(side):
+        index = 2 * ((col >> 1) ^ (m >> 1) ^ x) + ((col & 1) ^ (m & 1) ^ p)
+        mine = lax.dynamic_index_in_dim(tiles, index, 0, keepdims=False)
+        got = moved(mine, side, lambda r, k, m=m: (((k ^ m) & 2) + (r & 1), (r >> 1) + 2 * ((k ^ m) & 1)))
+        features = (2 * x + (col >> 1)) ^ m
+        down = lax.dynamic_index_in_dim(left_sqs, features ^ col, 0, keepdims=False)
+        along = lax.dynamic_index_in_dim(right_sqs, features ^ row, 0, keepdims=False)
+        down = left_scale / (top * feat_total * inverse_norm(down))
+        along = right_scale / inverse_norm(along)
+        similarity = similarity + got.astype(jnp.float32) * down[:, None] * along[None, :]
+    return similarity
 
 
 def on_any_grid(left_docs, right_docs):

time: 49.1 us -> 41.3 us (0.84)
  waiting for transfers between devices: 23.2 us -> 14.5 us
  other arithmetic: 3.13 us -> 3.87 us
    ppermute x12 -> x13, waiting for transfers between devices: 23.2 us -> 14.5 us  [moved(): return lax.ppermute(value, ('row', 'col'), pairs)]
    add x2 -> x1, other arithmetic: 0.01 us -> 0.86 us  [on_square_grid(): similarity + got.astype(jnp.float32) * down[:, None] * along[None, :]]
    mul x2 -> x4, other arithmetic: 0.76 us -> 0.07 us  [the longest x2 0.04 us: on_square_grid(): got.astype(jnp.float32) * down[:, None] * along[None, :]]
    reduce_sum x2 -> x5, other arithmetic: 2.31 us -> 2.79 us  [squares(): return jnp.sum(widened * widened, axis=1)]
    ppermute x12 -> x13, starting transfers between devices: 21.1 us -> 21.2 us  [moved(): return lax.ppermute(value, ('row', 'col'), pairs)]
  transfers between devices with their start and end apart: 12 -> 13, of which waited for: 4 -> 7; matrix products, arithmetic and copies ran while one was open for 7% -> 8% of each run, Pallas kernels for 0% -> 0%
where the time goes in v5:
time: 41.3 us; the launch traced here: 41.1 us
  starting transfers between devices  21.2 us (51%)
  waiting for transfers between devices  14.5 us (35%)
  other arithmetic  3.87 us (9%)
  matrix products  1.25 us (3%)
    ppermute x13, starting transfers between devices, moved(): return lax.ppermute(value, ('row', 'col'), pairs)  21.2 us
    ppermute x13, waiting for transfers between devices, moved(): return lax.ppermute(value, ('row', 'col'), pairs)  14.5 us
    reduce_sum x5, other arithmetic, squares(): return jnp.sum(widened * widened, axis=1)  2.79 us
    dot_general x4, matrix products, contract(): lax.dot_general(left_part, right_part, (((1,), (1,)), ((), ())), preferre...  1.25 us
    add x1, other arithmetic, on_square_grid(): similarity + got.astype(jnp.float32) * down[:, None] * along[None, :]  0.86 us
  transfers between devices with their start and end apart: 13, of which 7 were waited for; matrix products, arithmetic and copies ran while one was open for 8% of the time, Pallas kernels for 0%

profile of v5, /device:TPU:0, one launch (start us, length us, event | category | flops | bytes accessed | tf_op | source)
XLA Modules:
  0.0 41.1 jit_solution(3960735594055074343)
XLA Ops:
  0.0 1.6 %collective-permute-start = (bf16[128,1024]{1,0:T(8,128)(2,1)}, bf16[128,1024]{1,0:T(8,128)(2,1)S(1)}, u32[]{:S(2)}, u32[]{:S(2)}) collective-permute-start(bf16[128,1024]{1,0:T(8,128)(2,1)} %param.3), channel_id=1, source_target_pairs={{0,0},{1,8},{2,4},{3,12},{4,1},{5,9},{6,5},{7,13},{8,2},{9,10},{10... | collective-permute-start | bytes 786440 | tf_op jit(solution)/shard_map/ppermute | solution.py:31
  1.6 1.1 %multiply_reduce_fusion.2 = f32[128]{0:T(128)S(1)} fusion(bf16[128,1024]{1,0:T(8,128)(2,1)} %param.3), kind=kLoop, calls=%fused_computation.18 | loop fusion | flops 393088 | bytes 262656 | tf_op jit(solution)/shard_map/reduce_sum | solution.py:22
  2.7 6.6 %collective-permute-start.9 = (f32[128]{0:T(128)S(1)}, f32[128]{0:T(128)S(1)}, u32[]{:S(2)}, u32[]{:S(2)}) collective-permute-start(f32[128]{0:T(128)S(1)} %multiply_reduce_fusion.2), channel_id=1, source_target_pairs={{0,12},{1,13},{2,14},{3,15},{4,8},{5,9},{6,10},{7,11},{8,4},{9,5},... | collective-permute-start | bytes 1544 | tf_op jit(solution)/shard_map/ppermute | solution.py:31
  9.3 0.2 collective-permute-start.7
  9.5 1.8 %collective-permute-start.2 = (bf16[256,1024]{1,0:T(8,128)(2,1)}, bf16[256,1024]{1,0:T(8,128)(2,1)S(1)}, u32[]{:S(2)}, u32[]{:S(2)}) collective-permute-start(bf16[256,1024]{1,0:T(8,128)(2,1)} %param.2), channel_id=1, source_target_pairs={{0,8},{1,9},{2,10},{3,11},{4,12},{5,13},{6,14},{7,15},{8,0},{9,1},... | collective-permute-start | bytes 1572872 | tf_op jit(solution)/shard_map/ppermute | solution.py:31
  11.3 1.3 %multiply_reduce_fusion.1 = f32[256]{0:T(256)S(1)} fusion(bf16[256,1024]{1,0:T(8,128)(2,1)} %param.2), kind=kLoop, calls=%fused_computation.17 | loop fusion | flops 786176 | bytes 525312 | tf_op jit(solution)/shard_map/reduce_sum | solution.py:22
  12.7 0.2 collective-permute-start.6
  12.9 1.9 %collective-permute-start.5 = (f32[256]{0:T(256)S(1)}, f32[256]{0:T(256)S(1)}, u32[]{:S(2)}, u32[]{:S(2)}) collective-permute-start(f32[256]{0:T(256)S(1)} %multiply_reduce_fusion.1), channel_id=1, source_target_pairs={{0,2},{1,3},{2,0},{3,1},{4,6},{5,7},{6,4},{7,5},{8,10},{9,11},{10,... | collective-permute-start | bytes 3080 | tf_op jit(solution)/shard_map/ppermute | solution.py:31
  14.8 2.3 %collective-permute-start.4 = (f32[256]{0:T(256)S(1)}, f32[256]{0:T(256)S(1)}, u32[]{:S(2)}, u32[]{:S(2)}) collective-permute-start(f32[256]{0:T(256)S(1)} %multiply_reduce_fusion.1), channel_id=1, source_target_pairs={{0,1},{1,0},{2,3},{3,2},{4,5},{5,4},{6,7},{7,6},{8,9},{9,8},{10,11... | collective-permute-start | bytes 3080 | tf_op jit(solution)/shard_map/ppermute | solution.py:31
  17.2 0.9 %collective-permute-done.6 = f32[256]{0:T(256)S(1)} collective-permute-done((f32[256]{0:T(256)S(1)}, f32[256]{0:T(256)S(1)}, u32[]{:S(2)}, u32[]{:S(2)}) %collective-permute-start.6) | collective-permute-done | bytes 1056 | tf_op jit(solution)/shard_map/ppermute | solution.py:31
  18.3 0.4 collective-permute-done.4
  19.0 0.3 fusion.11
  19.3 5.1 %collective-permute-done.2 = bf16[256,1024]{1,0:T(8,128)(2,1)S(1)} collective-permute-done((bf16[256,1024]{1,0:T(8,128)(2,1)}, bf16[256,1024]{1,0:T(8,128)(2,1)S(1)}, u32[]{:S(2)}, u32[]{:S(2)}) %collective-permute-start.2) | collective-permute-done | bytes 524320 | tf_op jit(solution)/shard_map/ppermute | solution.py:31
  24.8 0.3 fusion.9
  25.1 0.3 fusion.8
  25.4 0.3 fusion.10
  25.9 2.8 %collective-permute-start.12 = (f16[256,128]{1,0:T(8,128)(2,1)S(1)}, f16[256,128]{1,0:T(8,128)(2,1)S(1)}, u32[]{:S(2)}, u32[]{:S(2)}) collective-permute-start(f16[256,128]{1,0:T(8,128)(2,1)S(1)} %get-tuple-element.10), channel_id=1, source_target_pairs={{0,10},{1,8},{2,2},{3,0},{4,14},{5,12},{6,6},{7,4},{8,11},{9,9},{1... | collective-permute-start | bytes 196616 | tf_op jit(solution)/shard_map/ppermute | solution.py:31
  28.7 2.0 %collective-permute-start.11 = (f16[256,128]{1,0:T(8,128)(2,1)S(1)}, f16[256,128]{1,0:T(8,128)(2,1)S(1)}, u32[]{:S(2)}, u32[]{:S(2)}) collective-permute-start(f16[256,128]{1,0:T(8,128)(2,1)S(1)} %get-tuple-element.11), channel_id=1, source_target_pairs={{0,8},{1,10},{2,0},{3,2},{4,12},{5,14},{6,4},{7,6},{8,9},{9,11},{1... | collective-permute-start | bytes 196616 | tf_op jit(solution)/shard_map/ppermute | solution.py:31
  30.7 0.9 %collective-permute-start.10 = (f16[256,128]{1,0:T(8,128)(2,1)S(1)}, f16[256,128]{1,0:T(8,128)(2,1)S(1)}, u32[]{:S(2)}, u32[]{:S(2)}) collective-permute-start(f16[256,128]{1,0:T(8,128)(2,1)S(1)} %get-tuple-element.12), channel_id=1, source_target_pairs={{0,2},{1,0},{2,10},{3,8},{4,6},{5,4},{6,14},{7,12},{8,3},{9,1},{10... | collective-permute-start | bytes 196616 | tf_op jit(solution)/shard_map/ppermute | solution.py:31
  31.7 0.7 %collective-permute-start.3 = (f16[256,128]{1,0:T(8,128)(2,1)S(1)}, f16[256,128]{1,0:T(8,128)(2,1)S(1)}, u32[]{:S(2)}, u32[]{:S(2)}) collective-permute-start(f16[256,128]{1,0:T(8,128)(2,1)S(1)} %get-tuple-element.9), channel_id=1, source_target_pairs={{0,0},{1,2},{2,8},{3,10},{4,4},{5,6},{6,12},{7,14},{8,1},{9,3},{10... | collective-permute-start | bytes 196616 | tf_op jit(solution)/shard_map/ppermute | solution.py:31
  32.4 2.0 %collective-permute-done.12 = f16[256,128]{1,0:T(8,128)(2,1)S(1)} collective-permute-done((f16[256,128]{1,0:T(8,128)(2,1)S(1)}, f16[256,128]{1,0:T(8,128)(2,1)S(1)}, u32[]{:S(2)}, u32[]{:S(2)}) %collective-permute-start.12) | collective-permute-done | bytes 65568 | tf_op jit(solution)/shard_map/ppermute | solution.py:31
  34.3 0.6 %collective-permute-done.11 = f16[256,128]{1,0:T(8,128)(2,1)S(1)} collective-permute-done((f16[256,128]{1,0:T(8,128)(2,1)S(1)}, f16[256,128]{1,0:T(8,128)(2,1)S(1)}, u32[]{:S(2)}, u32[]{:S(2)}) %collective-permute-start.11) | collective-permute-done | bytes 65568 | tf_op jit(solution)/shard_map/ppermute | solution.py:31
  34.9 5.3 %collective-permute-done.10 = f16[256,128]{1,0:T(8,128)(2,1)S(1)} collective-permute-done((f16[256,128]{1,0:T(8,128)(2,1)S(1)}, f16[256,128]{1,0:T(8,128)(2,1)S(1)}, u32[]{:S(2)}, u32[]{:S(2)}) %collective-permute-start.10) | collective-permute-done | bytes 65568 | tf_op jit(solution)/shard_map/ppermute | solution.py:31
  40.2 0.9 %multiply_add_fusion = f32[256,128]{1,0:T(8,128)} fusion(f16[256,128]{1,0:T(8,128)(2,1)S(1)} %collective-permute-done.12, f16[256,128]{1,0:T(8,128)(2,1)S(1)} %collective-permute-done.11, f16[256,128]{1,0:T(8,128)(2,1)S(1)} %collective-permute-done.10, f16[256,128]{1,0:T(8,128)(2,1)S(1)} %collective-permute-done.3, f32[128]{0:T(128)S(1)} %get-tuple-element.18, ...), kind=kLoop, calls=%fused_computation.22 | loop fusion | flops 491520 | bytes 399360 | tf_op jit(solution)/shard_map/add | solution.py:73
  (26 shorter events, 1.0 us)
Async XLA Ops:
  0.0 18.7 %collective-permute-start = (bf16[128,1024]{1,0:T(8,128)(2,1)}, bf16[128,1024]{1,0:T(8,128)(2,1)S(1)}, u32[]{:S(2)}, u32[]{:S(2)}) collective-permute-start(bf16[128,1024]{1,0:T(8,128)(2,1)} %param.3), channel_id=1, source_target_pairs={{0,0},{1,8},{2,4},{3,12},{4,1},{5,9},{6,5},{7,13},{8,2},{9,10},{10... | collective-permute-start | bytes 786440 | tf_op jit(solution)/shard_map/ppermute | solution.py:31
  2.7 16.3 %copy-start = (bf16[256,1024]{1,0:T(8,128)(2,1)S(1)}, bf16[256,1024]{1,0:T(8,128)(2,1)}, u32[]{:S(2)}) copy-start(bf16[256,1024]{1,0:T(8,128)(2,1)} %param.2) | copy-start | bytes 1572868
  2.7 10.0 %collective-permute-start.9 = (f32[128]{0:T(128)S(1)}, f32[128]{0:T(128)S(1)}, u32[]{:S(2)}, u32[]{:S(2)}) collective-permute-start(f32[128]{0:T(128)S(1)} %multiply_reduce_fusion.2), channel_id=1, source_target_pairs={{0,12},{1,13},{2,14},{3,15},{4,8},{5,9},{6,10},{7,11},{8,4},{9,5},... | collective-permute-start | bytes 1544 | tf_op jit(solution)/shard_map/ppermute | solution.py:31
  9.3 3.6 %collective-permute-start.8 = (f32[128]{0:T(128)S(1)}, f32[128]{0:T(128)S(1)}, u32[]{:S(2)}, u32[]{:S(2)}) collective-permute-start(f32[128]{0:T(128)S(1)} %multiply_reduce_fusion.2), channel_id=1, source_target_pairs={{0,8},{1,9},{2,10},{3,11},{4,12},{5,13},{6,14},{7,15},{8,0},{9,1},... | collective-permute-start | bytes 1544 | tf_op jit(solution)/shard_map/ppermute | solution.py:31
  9.3 5.5 %collective-permute-start.7 = (f32[128]{0:T(128)S(1)}, f32[128]{0:T(128)S(1)}, u32[]{:S(2)}, u32[]{:S(2)}) collective-permute-start(f32[128]{0:T(128)S(1)} %multiply_reduce_fusion.2), channel_id=1, source_target_pairs={{0,4},{1,5},{2,6},{3,7},{4,0},{5,1},{6,2},{7,3},{8,12},{9,13},{10,... | collective-permute-start | bytes 1544 | tf_op jit(solution)/shard_map/ppermute | solution.py:31
  9.5 14.9 %collective-permute-start.2 = (bf16[256,1024]{1,0:T(8,128)(2,1)}, bf16[256,1024]{1,0:T(8,128)(2,1)S(1)}, u32[]{:S(2)}, u32[]{:S(2)}) collective-permute-start(bf16[256,1024]{1,0:T(8,128)(2,1)} %param.2), channel_id=1, source_target_pairs={{0,8},{1,9},{2,10},{3,11},{4,12},{5,13},{6,14},{7,15},{8,0},{9,1},... | collective-permute-start | bytes 1572872 | tf_op jit(solution)/shard_map/ppermute | solution.py:31
  12.7 5.4 %collective-permute-start.6 = (f32[256]{0:T(256)S(1)}, f32[256]{0:T(256)S(1)}, u32[]{:S(2)}, u32[]{:S(2)}) collective-permute-start(f32[256]{0:T(256)S(1)} %multiply_reduce_fusion.1), channel_id=1, source_target_pairs={{0,3},{1,2},{2,1},{3,0},{4,7},{5,6},{6,5},{7,4},{8,11},{9,10},{10,... | collective-permute-start | bytes 3080 | tf_op jit(solution)/shard_map/ppermute | solution.py:31
  12.9 5.4 %collective-permute-start.5 = (f32[256]{0:T(256)S(1)}, f32[256]{0:T(256)S(1)}, u32[]{:S(2)}, u32[]{:S(2)}) collective-permute-start(f32[256]{0:T(256)S(1)} %multiply_reduce_fusion.1), channel_id=1, source_target_pairs={{0,2},{1,3},{2,0},{3,1},{4,6},{5,7},{6,4},{7,5},{8,10},{9,11},{10,... | collective-permute-start | bytes 3080 | tf_op jit(solution)/shard_map/ppermute | solution.py:31
  14.8 3.9 %collective-permute-start.4 = (f32[256]{0:T(256)S(1)}, f32[256]{0:T(256)S(1)}, u32[]{:S(2)}, u32[]{:S(2)}) collective-permute-start(f32[256]{0:T(256)S(1)} %multiply_reduce_fusion.1), channel_id=1, source_target_pairs={{0,1},{1,0},{2,3},{3,2},{4,5},{5,4},{6,7},{7,6},{8,9},{9,8},{10,11... | collective-permute-start | bytes 3080 | tf_op jit(solution)/shard_map/ppermute | solution.py:31
  18.7 5.9 %collective-permute-start.1 = (bf16[128,1024]{1,0:T(8,128)(2,1)S(1)}, bf16[128,1024]{1,0:T(8,128)(2,1)S(1)}, u32[]{:S(2)}, u32[]{:S(2)}) collective-permute-start(bf16[128,1024]{1,0:T(8,128)(2,1)S(1)} %collective-permute-done), channel_id=1, source_target_pairs={{0,4},{1,5},{2,6},{3,7},{4,0},{5,1},{6,2},{7,3},{8,12},{9,13},{10,... | collective-permute-start | bytes 786440 | tf_op jit(solution)/shard_map/ppermute | solution.py:31
  25.9 8.4 %collective-permute-start.12 = (f16[256,128]{1,0:T(8,128)(2,1)S(1)}, f16[256,128]{1,0:T(8,128)(2,1)S(1)}, u32[]{:S(2)}, u32[]{:S(2)}) collective-permute-start(f16[256,128]{1,0:T(8,128)(2,1)S(1)} %get-tuple-element.10), channel_id=1, source_target_pairs={{0,10},{1,8},{2,2},{3,0},{4,14},{5,12},{6,6},{7,4},{8,11},{9,9},{1... | collective-permute-start | bytes 196616 | tf_op jit(solution)/shard_map/ppermute | solution.py:31
  28.7 6.2 %collective-permute-start.11 = (f16[256,128]{1,0:T(8,128)(2,1)S(1)}, f16[256,128]{1,0:T(8,128)(2,1)S(1)}, u32[]{:S(2)}, u32[]{:S(2)}) collective-permute-start(f16[256,128]{1,0:T(8,128)(2,1)S(1)} %get-tuple-element.11), channel_id=1, source_target_pairs={{0,8},{1,10},{2,0},{3,2},{4,12},{5,14},{6,4},{7,6},{8,9},{9,11},{1... | collective-permute-start | bytes 196616 | tf_op jit(solution)/shard_map/ppermute | solution.py:31
  30.7 9.5 %collective-permute-start.10 = (f16[256,128]{1,0:T(8,128)(2,1)S(1)}, f16[256,128]{1,0:T(8,128)(2,1)S(1)}, u32[]{:S(2)}, u32[]{:S(2)}) collective-permute-start(f16[256,128]{1,0:T(8,128)(2,1)S(1)} %get-tuple-element.12), channel_id=1, source_target_pairs={{0,2},{1,0},{2,10},{3,8},{4,6},{5,4},{6,14},{7,12},{8,3},{9,1},{10... | collective-permute-start | bytes 196616 | tf_op jit(solution)/shard_map/ppermute | solution.py:31
  31.7 8.5 %collective-permute-start.3 = (f16[256,128]{1,0:T(8,128)(2,1)S(1)}, f16[256,128]{1,0:T(8,128)(2,1)S(1)}, u32[]{:S(2)}, u32[]{:S(2)}) collective-permute-start(f16[256,128]{1,0:T(8,128)(2,1)S(1)} %get-tuple-element.9), channel_id=1, source_target_pairs={{0,0},{1,2},{2,8},{3,10},{4,4},{5,6},{6,12},{7,14},{8,1},{9,3},{10... | collective-permute-start | bytes 196616 | tf_op jit(solution)/shard_map/ppermute | solution.py:31

commit v6 on v2

--- a/solution.py
+++ b/solution.py
@@ -4,6 +4,7 @@
 from jax.sharding import PartitionSpec as P
 
 epsilon = 1e-06
+top = 2.0**15
 
 
 def contract(left_part, right_part):
@@ -32,31 +33,64 @@
     return summed / feat_total * left_scale[:, None] * right_scale[None, :]
 
 
+def packed(sums):
+    root = 16.0 * jnp.sqrt(jnp.sqrt(jnp.sqrt(jnp.maximum(sums, 1e-36))))
+    high = lax.reduce_precision(root, 5, 10)
+    low = lax.reduce_precision((root - high) * 1024.0, 5, 10)
+    return high.astype(jnp.float16), low.astype(jnp.float16), unpacked(high, low)
+
+
+def unpacked(high, low):
+    root = (high + low / 1024.0) / 16.0
+    for _ in range(3):
+        root = root * root
+    return root
+
+
 def on_square_grid(left_docs, right_docs):
     side = lax.axis_size("col")
     feat_total = left_docs.shape[1] * side
-    row, col = lax.axis_index("row"), lax.axis_index("col")
+    rows, width = left_docs.shape[0], right_docs.shape[0]
 
-    def spread(c):
-        return 2 * (c & 1) + (c >> 1)
+    far = moved(left_docs, side, lambda r, c: (r ^ 2, c))
+    first = moved(right_docs, side, lambda k, c: (2 * ((k ^ c) & 1) + ((k ^ c) >> 1), k))
+    second = moved(first, side, lambda r, c: (r ^ 1, c))
 
-    held = moved(right_docs, side, lambda k, c: (spread(c), k))
-    far = moved(left_docs, side, lambda r, c: (r ^ 2, c))
-    near = moved(left_docs, side, lambda r, c: (r ^ 1, c))
-    lefts = [left_docs, near, far, moved(far, side, lambda r, c: (r ^ 1, c))]
-    partial = jnp.stack([contract(block, held) for block in lefts])
+    def message(left_block, left_sums, right_block, right_sums):
+        left_high, left_low, left_sq = left_sums
+        right_high, right_low, right_sq = right_sums
+        down, along = top * lax.rsqrt(left_sq), lax.rsqrt(right_sq)
+        tile = (contract(left_block, right_block) * down[:, None] * along[None, :]).astype(jnp.float16)
+        halves = (rows // width, width)
+        sums = [left_high.reshape(halves), left_low.reshape(halves), right_high[None], right_low[None]]
+        spare = -sum(part.shape[0] for part in sums) % 8
+        return jnp.concatenate([tile, *sums, jnp.zeros((spare, width), jnp.float16)])
 
-    summed = 0.0
-    for m in range(side):
-        mine = lax.dynamic_index_in_dim(partial, row ^ col ^ m, 0, keepdims=False)
-        summed = summed + moved(mine, side, lambda i, k, m=m: (k ^ m, spread(i)))
+    received = []
+    rights = [(block, packed(squares(block))) for block in (first, second)]
+    for g, left_block in enumerate((left_docs, far)):
+        left_sums = packed(squares(left_block))
+        for j, (right_block, right_sums) in enumerate(rights):
+            received.append(
+                moved(
+                    message(left_block, left_sums, right_block, right_sums),
+                    side,
+                    lambda r, k, g=g, j=j: (r ^ (2 * g), k ^ ((r >> 1) + 2 * ((r & 1) ^ j))),
+                )
+            )
 
-    left_sq, right_sq = squares(left_docs), squares(right_docs)
-    left_sq, right_sq, _ = lax.optimization_barrier((left_sq, right_sq, partial))
-    for step in (1, 2):
-        left_sq = left_sq + moved(left_sq, side, lambda r, c, d=step: (r, c ^ d))
-        right_sq = right_sq + moved(right_sq, side, lambda r, c, d=step: (r ^ d, c))
-    return finish(summed, left_sq, right_sq, feat_total)
+    parts = []
+    for got in received:
+        wide = got.astype(jnp.float32)
+        part = rows // width
+        left_high, left_low, right_high, right_low = jnp.split(wide[rows:rows + 2 * part + 2], (part, 2 * part, 2 * part + 1))
+        parts.append((wide[:rows], unpacked(left_high, left_low).reshape(rows), unpacked(right_high, right_low).reshape(width)))
+    left_scale = lax.rsqrt(sum(part[1] for part in parts) / feat_total + epsilon) / (feat_total * top)
+    right_scale = lax.rsqrt(sum(part[2] for part in parts) / feat_total + epsilon)
+    return sum(
+        tile * (left_scale * jnp.sqrt(left_sq))[:, None] * (right_scale * jnp.sqrt(right_sq))[None, :]
+        for tile, left_sq, right_sq in parts
+    )
 
 
 def on_any_grid(left_docs, right_docs):

time: 49.1 us -> 38.6 us (0.79)
  waiting for transfers between devices: 23.2 us -> 8.42 us
  starting transfers between devices: 21.1 us -> 25.3 us
    ppermute x12 -> x7, waiting for transfers between devices: 23.2 us -> 8.42 us  [moved(): return lax.ppermute(value, ('row', 'col'), pairs)]
    ppermute x12 -> x7, starting transfers between devices: 21.1 us -> 25.3 us  [moved(): return lax.ppermute(value, ('row', 'col'), pairs)]
    add x2 -> x1, other arithmetic: 0.01 us -> 0.86 us  [on_square_grid(): sum((tile * (left_scale * jnp.sqrt(left_sq))[:, None] * (right_scale * jn...]
    reduce_sum x2 -> x4, other arithmetic: 2.31 us -> 1.7 us  [squares(): return jnp.sum(widened * widened, axis=1)]
    mul x2 -> x6, other arithmetic: 0.76 us -> 0.17 us  [the longest x2 0.1 us: message(): down, along = (top * lax.rsqrt(left_sq), lax.rsqrt(right_sq))]
  transfers between devices with their start and end apart: 12 -> 7, of which waited for: 4 -> 4; matrix products, arithmetic and copies ran while one was open for 7% -> 9% of each run, Pallas kernels for 0% -> 0%
where the time goes in v6:
time: 38.6 us; the launch traced here: 38.4 us
  starting transfers between devices  25.3 us (66%)
  waiting for transfers between devices  8.42 us (22%)
  other arithmetic  3.06 us (8%)
  matrix products  1.23 us (3%)
    ppermute x7, starting transfers between devices, moved(): return lax.ppermute(value, ('row', 'col'), pairs)  25.3 us
    ppermute x7, waiting for transfers between devices, moved(): return lax.ppermute(value, ('row', 'col'), pairs)  8.42 us
    reduce_sum x4, other arithmetic, squares(): return jnp.sum(widened * widened, axis=1)  1.7 us
    dot_general x4, matrix products, contract(): lax.dot_general(left_part, right_part, (((1,), (1,)), ((), ())), preferre...  1.23 us
    add x1, other arithmetic, on_square_grid(): sum((tile * (left_scale * jnp.sqrt(left_sq))[:, None] * (right_scale * jn...  0.86 us
  transfers between devices with their start and end apart: 7, of which 4 were waited for; matrix products, arithmetic and copies ran while one was open for 9% of the time, Pallas kernels for 0%

profile of v6, /device:TPU:0, one launch (start us, length us, event | category | flops | bytes accessed | tf_op | source)
XLA Modules:
  0.0 38.4 jit_solution(12441387530952497400)
XLA Ops:
  0.0 1.7 %collective-permute-start = (bf16[128,1024]{1,0:T(8,128)(2,1)}, bf16[128,1024]{1,0:T(8,128)(2,1)S(1)}, u32[]{:S(2)}, u32[]{:S(2)}) collective-permute-start(bf16[128,1024]{1,0:T(8,128)(2,1)} %param.3), channel_id=1, source_target_pairs={{0,0},{1,8},{2,4},{3,12},{4,9},{5,1},{6,13},{7,5},{8,6},{9,14},{10... | collective-permute-start | bytes 786440 | tf_op jit(solution)/shard_map/ppermute | solution.py:27
  1.7 5.3 %collective-permute-start.4 = (bf16[256,1024]{1,0:T(8,128)(2,1)}, bf16[256,1024]{1,0:T(8,128)(2,1)S(1)}, u32[]{:S(2)}, u32[]{:S(2)}) collective-permute-start(bf16[256,1024]{1,0:T(8,128)(2,1)} %param.2), channel_id=1, source_target_pairs={{0,8},{1,9},{2,10},{3,11},{4,12},{5,13},{6,14},{7,15},{8,0},{9,1},... | collective-permute-start | bytes 1572872 | tf_op jit(solution)/shard_map/ppermute | solution.py:27
  7.0 1.3 %multiply_reduce_fusion.1 = f32[256]{0:T(256)S(1)} fusion(bf16[256,1024]{1,0:T(8,128)(2,1)} %param.2), kind=kLoop, calls=%fused_computation.13 | loop fusion | flops 786176 | bytes 525312 | tf_op jit(solution)/shard_map/reduce_sum | solution.py:18
  8.4 0.1 multiply_reduce_fusion.3
  8.6 10.3 %collective-permute-start.2 = (bf16[128,1024]{1,0:T(8,128)(2,1)S(1)}, bf16[128,1024]{1,0:T(8,128)(2,1)S(1)}, u32[]{:S(2)}, u32[]{:S(2)}) collective-permute-start(bf16[128,1024]{1,0:T(8,128)(2,1)S(1)} %collective-permute-done), channel_id=1, source_target_pairs={{0,4},{1,5},{2,6},{3,7},{4,0},{5,1},{6,2},{7,3},{8,12},{9,13},{10,... | collective-permute-start | bytes 786440 | tf_op jit(solution)/shard_map/ppermute | solution.py:27
  19.0 0.3 fusion.4
  19.3 0.1 concatenate.12
  19.3 0.7 %collective-permute-start.1 = (f16[264,128]{1,0:T(8,128)(2,1)S(1)}, f16[264,128]{1,0:T(8,128)(2,1)S(1)}, u32[]{:S(2)}, u32[]{:S(2)}) collective-permute-start(f16[264,128]{1,0:T(8,128)(2,1)S(1)} %concatenate.12), channel_id=1, source_target_pairs={{0,0},{1,1},{2,2},{3,3},{4,6},{5,7},{6,4},{7,5},{8,9},{9,8},{10,11... | collective-permute-start | bytes 202760 | tf_op jit(solution)/shard_map/ppermute | solution.py:27
  20.0 0.1 collective-permute-done.2
  20.1 0.1 multiply_reduce_fusion.2
  20.3 3.8 %collective-permute-done.4 = bf16[256,1024]{1,0:T(8,128)(2,1)S(1)} collective-permute-done((bf16[256,1024]{1,0:T(8,128)(2,1)}, bf16[256,1024]{1,0:T(8,128)(2,1)S(1)}, u32[]{:S(2)}, u32[]{:S(2)}) %collective-permute-start.4) | collective-permute-done | bytes 524320 | tf_op jit(solution)/shard_map/ppermute | solution.py:27
  24.1 0.2 multiply_reduce_fusion
  24.4 0.3 fusion.7
  24.7 0.1 concatenate.15
  24.8 1.7 %collective-permute-start.6 = (f16[264,128]{1,0:T(8,128)(2,1)S(1)}, f16[264,128]{1,0:T(8,128)(2,1)S(1)}, u32[]{:S(2)}, u32[]{:S(2)}) collective-permute-start(f16[264,128]{1,0:T(8,128)(2,1)S(1)} %concatenate.15), channel_id=1, source_target_pairs={{0,10},{1,11},{2,8},{3,9},{4,12},{5,13},{6,14},{7,15},{8,3},{9,2},... | collective-permute-start | bytes 202760 | tf_op jit(solution)/shard_map/ppermute | solution.py:27
  26.5 0.3 fusion.5
  26.8 0.1 concatenate.13
  26.9 5.0 %collective-permute-start.3 = (f16[264,128]{1,0:T(8,128)(2,1)S(1)}, f16[264,128]{1,0:T(8,128)(2,1)S(1)}, u32[]{:S(2)}, u32[]{:S(2)}) collective-permute-start(f16[264,128]{1,0:T(8,128)(2,1)S(1)} %concatenate.13), channel_id=1, source_target_pairs={{0,2},{1,3},{2,0},{3,1},{4,4},{5,5},{6,6},{7,7},{8,11},{9,10},{10,... | collective-permute-start | bytes 202760 | tf_op jit(solution)/shard_map/ppermute | solution.py:27
  31.8 0.3 fusion.6
  32.1 0.1 concatenate.14
  32.2 0.6 %collective-permute-start.5 = (f16[264,128]{1,0:T(8,128)(2,1)S(1)}, f16[264,128]{1,0:T(8,128)(2,1)S(1)}, u32[]{:S(2)}, u32[]{:S(2)}) collective-permute-start(f16[264,128]{1,0:T(8,128)(2,1)S(1)} %concatenate.14), channel_id=1, source_target_pairs={{0,8},{1,9},{2,10},{3,11},{4,14},{5,15},{6,12},{7,13},{8,1},{9,0},... | collective-permute-start | bytes 202760 | tf_op jit(solution)/shard_map/ppermute | solution.py:27
  32.9 3.1 %collective-permute-done.3 = f16[264,128]{1,0:T(8,128)(2,1)S(1)} collective-permute-done((f16[264,128]{1,0:T(8,128)(2,1)S(1)}, f16[264,128]{1,0:T(8,128)(2,1)S(1)}, u32[]{:S(2)}, u32[]{:S(2)}) %collective-permute-start.3) | collective-permute-done | bytes 67616 | tf_op jit(solution)/shard_map/ppermute | solution.py:27
  36.0 1.5 %collective-permute-done.5 = f16[264,128]{1,0:T(8,128)(2,1)S(1)} collective-permute-done((f16[264,128]{1,0:T(8,128)(2,1)S(1)}, f16[264,128]{1,0:T(8,128)(2,1)S(1)}, u32[]{:S(2)}, u32[]{:S(2)}) %collective-permute-start.5) | collective-permute-done | bytes 67616 | tf_op jit(solution)/shard_map/ppermute | solution.py:27
  37.6 0.9 %fusion.9 = f32[256,128]{1,0:T(8,128)} fusion(f32[264,128]{1,0:T(8,128)S(1)} %convert_element_type.111, f32[264,128]{1,0:T(8,128)S(1)} %convert_element_type.109, f32[264,128]{1,0:T(8,128)S(1)} %convert_element_type.104, f32[264,128]{1,0:T(8,128)S(1)} %convert_element_type.99, f32[128]{0:T(128)S(1)} %get-tuple-element.25, f32[256]{0:T(256)S(1)} %get-tuple-element.18, ...), kind=kLoop, calls=%fused_computation.18 | loop fusion | flops 360448 | bytes 661504 | tf_op jit(solution)/shard_map/add | solution.py:90
  (24 shorter events, 0.5 us)
Async XLA Ops:
  0.0 18.9 %copy-start = (bf16[256,1024]{1,0:T(8,128)(2,1)S(1)}, bf16[256,1024]{1,0:T(8,128)(2,1)}, u32[]{:S(2)}) copy-start(bf16[256,1024]{1,0:T(8,128)(2,1)} %param.2) | copy-start | bytes 1572868
  0.0 8.4 %collective-permute-start = (bf16[128,1024]{1,0:T(8,128)(2,1)}, bf16[128,1024]{1,0:T(8,128)(2,1)S(1)}, u32[]{:S(2)}, u32[]{:S(2)}) collective-permute-start(bf16[128,1024]{1,0:T(8,128)(2,1)} %param.3), channel_id=1, source_target_pairs={{0,0},{1,8},{2,4},{3,12},{4,9},{5,1},{6,13},{7,5},{8,6},{9,14},{10... | collective-permute-start | bytes 786440 | tf_op jit(solution)/shard_map/ppermute | solution.py:27
  1.7 22.4 %collective-permute-start.4 = (bf16[256,1024]{1,0:T(8,128)(2,1)}, bf16[256,1024]{1,0:T(8,128)(2,1)S(1)}, u32[]{:S(2)}, u32[]{:S(2)}) collective-permute-start(bf16[256,1024]{1,0:T(8,128)(2,1)} %param.2), channel_id=1, source_target_pairs={{0,8},{1,9},{2,10},{3,11},{4,12},{5,13},{6,14},{7,15},{8,0},{9,1},... | collective-permute-start | bytes 1572872 | tf_op jit(solution)/shard_map/ppermute | solution.py:27
  8.6 11.5 %collective-permute-start.2 = (bf16[128,1024]{1,0:T(8,128)(2,1)S(1)}, bf16[128,1024]{1,0:T(8,128)(2,1)S(1)}, u32[]{:S(2)}, u32[]{:S(2)}) collective-permute-start(bf16[128,1024]{1,0:T(8,128)(2,1)S(1)} %collective-permute-done), channel_id=1, source_target_pairs={{0,4},{1,5},{2,6},{3,7},{4,0},{5,1},{6,2},{7,3},{8,12},{9,13},{10,... | collective-permute-start | bytes 786440 | tf_op jit(solution)/shard_map/ppermute | solution.py:27
  19.3 13.5 %collective-permute-start.1 = (f16[264,128]{1,0:T(8,128)(2,1)S(1)}, f16[264,128]{1,0:T(8,128)(2,1)S(1)}, u32[]{:S(2)}, u32[]{:S(2)}) collective-permute-start(f16[264,128]{1,0:T(8,128)(2,1)S(1)} %concatenate.12), channel_id=1, source_target_pairs={{0,0},{1,1},{2,2},{3,3},{4,6},{5,7},{6,4},{7,5},{8,9},{9,8},{10,11... | collective-permute-start | bytes 202760 | tf_op jit(solution)/shard_map/ppermute | solution.py:27
  24.8 8.1 %collective-permute-start.6 = (f16[264,128]{1,0:T(8,128)(2,1)S(1)}, f16[264,128]{1,0:T(8,128)(2,1)S(1)}, u32[]{:S(2)}, u32[]{:S(2)}) collective-permute-start(f16[264,128]{1,0:T(8,128)(2,1)S(1)} %concatenate.15), channel_id=1, source_target_pairs={{0,10},{1,11},{2,8},{3,9},{4,12},{5,13},{6,14},{7,15},{8,3},{9,2},... | collective-permute-start | bytes 202760 | tf_op jit(solution)/shard_map/ppermute | solution.py:27
  26.9 9.1 %collective-permute-start.3 = (f16[264,128]{1,0:T(8,128)(2,1)S(1)}, f16[264,128]{1,0:T(8,128)(2,1)S(1)}, u32[]{:S(2)}, u32[]{:S(2)}) collective-permute-start(f16[264,128]{1,0:T(8,128)(2,1)S(1)} %concatenate.13), channel_id=1, source_target_pairs={{0,2},{1,3},{2,0},{3,1},{4,4},{5,5},{6,6},{7,7},{8,11},{9,10},{10,... | collective-permute-start | bytes 202760 | tf_op jit(solution)/shard_map/ppermute | solution.py:27
  32.2 5.2 %collective-permute-start.5 = (f16[264,128]{1,0:T(8,128)(2,1)S(1)}, f16[264,128]{1,0:T(8,128)(2,1)S(1)}, u32[]{:S(2)}, u32[]{:S(2)}) collective-permute-start(f16[264,128]{1,0:T(8,128)(2,1)S(1)} %concatenate.14), channel_id=1, source_target_pairs={{0,8},{1,9},{2,10},{3,11},{4,14},{5,15},{6,12},{7,13},{8,1},{9,0},... | collective-permute-start | bytes 202760 | tf_op jit(solution)/shard_map/ppermute | solution.py:27

commit v7 on v6

--- a/solution.py
+++ b/solution.py
@@ -66,31 +66,32 @@
         spare = -sum(part.shape[0] for part in sums) % 8
         return jnp.concatenate([tile, *sums, jnp.zeros((spare, width), jnp.float16)])
 
-    received = []
-    rights = [(block, packed(squares(block))) for block in (first, second)]
-    for g, left_block in enumerate((left_docs, far)):
-        left_sums = packed(squares(left_block))
-        for j, (right_block, right_sums) in enumerate(rights):
-            received.append(
-                moved(
-                    message(left_block, left_sums, right_block, right_sums),
-                    side,
-                    lambda r, k, g=g, j=j: (r ^ (2 * g), k ^ ((r >> 1) + 2 * ((r & 1) ^ j))),
-                )
-            )
+    def sent(value, g, j):
+        return moved(value, side, lambda r, k: (r ^ (2 * g), k ^ ((r >> 1) + 2 * ((r & 1) ^ j))))
 
-    parts = []
-    for got in received:
+    right_sums = [packed(squares(block)) for block in (first, second)]
+    own_sums = packed(squares(left_docs))
+    own = [message(left_docs, own_sums, block, sums) for block, sums in zip((first, second), right_sums)]
+    far, _ = lax.optimization_barrier((far, own[1]))
+    far_sums = packed(squares(far))
+    others = [message(far, far_sums, block, sums) for block, sums in zip((first, second), right_sums)]
+
+    def taken(got):
         wide = got.astype(jnp.float32)
         part = rows // width
         left_high, left_low, right_high, right_low = jnp.split(wide[rows:rows + 2 * part + 2], (part, 2 * part, 2 * part + 1))
-        parts.append((wide[:rows], unpacked(left_high, left_low).reshape(rows), unpacked(right_high, right_low).reshape(width)))
-    left_scale = lax.rsqrt(sum(part[1] for part in parts) / feat_total + epsilon) / (feat_total * top)
-    right_scale = lax.rsqrt(sum(part[2] for part in parts) / feat_total + epsilon)
-    return sum(
-        tile * (left_scale * jnp.sqrt(left_sq))[:, None] * (right_scale * jnp.sqrt(right_sq))[None, :]
-        for tile, left_sq, right_sq in parts
-    )
+        left_sq, right_sq = unpacked(left_high, left_low).reshape(rows), unpacked(right_high, right_low).reshape(width)
+        return wide[:rows] * jnp.sqrt(left_sq)[:, None] * jnp.sqrt(right_sq)[None, :], left_sq, right_sq
+
+    def added(one, other):
+        return [left + right for left, right in zip(one, other)]
+
+    own_got, _ = lax.optimization_barrier(([sent(value, 0, j) for j, value in enumerate(own)], others))
+    near_sum = added(*map(taken, own_got))
+    far_got = [sent(value, 1, j) for j, value in enumerate(others)]
+    near_sum, far_got = lax.optimization_barrier((near_sum, far_got))
+    summed, left_sq, right_sq = added(near_sum, added(*map(taken, far_got)))
+    return finish(summed / top, left_sq, right_sq, feat_total)
 
 
 def on_any_grid(left_docs, right_docs):

time: 38.6 us -> 35.4 us (0.917)
  waiting for transfers between devices: 8.42 us -> 5.77 us
  starting transfers between devices: 25.3 us -> 24.5 us
    ppermute x7, waiting for transfers between devices: 8.42 us -> 5.77 us  [moved(): return lax.ppermute(value, ('row', 'col'), pairs)]
    mul x4, other arithmetic: 0.07 us -> 0.88 us  [the longest x2 0.85 us: finish(): return summed / feat_total * left_scale[:, None] * right_scale[None, :]]
    ppermute x7, starting transfers between devices: 25.3 us -> 24.5 us  [moved(): return lax.ppermute(value, ('row', 'col'), pairs)]
    add x1 -> x3, other arithmetic: 0.86 us -> 0.16 us  [added(): return [left + right for left, right in zip(one, other)]]
  transfers between devices with their start and end apart: 7 -> 7, of which waited for: 4 -> 4; matrix products, arithmetic and copies ran while one was open for 9% -> 11% of each run, Pallas kernels for 0% -> 0%
where the time goes in v7:
time: 35.4 us; the launch traced here: 35.2 us
  starting transfers between devices  24.5 us (69%)
  waiting for transfers between devices  5.77 us (16%)
  other arithmetic  3.19 us (9%)
  matrix products  1.24 us (4%)
    ppermute x7, starting transfers between devices, moved(): return lax.ppermute(value, ('row', 'col'), pairs)  24.5 us
    ppermute x7, waiting for transfers between devices, moved(): return lax.ppermute(value, ('row', 'col'), pairs)  5.77 us
    reduce_sum x4, other arithmetic, squares(): return jnp.sum(widened * widened, axis=1)  1.7 us
    dot_general x4, matrix products, contract(): lax.dot_general(left_part, right_part, (((1,), (1,)), ((), ())), preferre...  1.24 us
    mul x2, other arithmetic, finish(): return summed / feat_total * left_scale[:, None] * right_scale[None, :]  0.85 us
  transfers between devices with their start and end apart: 7, of which 4 were waited for; matrix products, arithmetic and copies ran while one was open for 11% of the time, Pallas kernels for 0%

profile of v7, /device:TPU:0, one launch (start us, length us, event | category | flops | bytes accessed | tf_op | source)
XLA Modules:
  0.0 35.2 jit_solution(11048350063147460333)
XLA Ops:
  0.0 1.7 %collective-permute-start = (bf16[128,1024]{1,0:T(8,128)(2,1)}, bf16[128,1024]{1,0:T(8,128)(2,1)S(1)}, u32[]{:S(2)}, u32[]{:S(2)}) collective-permute-start(bf16[128,1024]{1,0:T(8,128)(2,1)} %param.3), channel_id=1, source_target_pairs={{0,0},{1,8},{2,4},{3,12},{4,9},{5,1},{6,13},{7,5},{8,6},{9,14},{10... | collective-permute-start | bytes 786440 | tf_op jit(solution)/shard_map/ppermute | solution.py:27
  1.7 5.3 %collective-permute-start.4 = (bf16[256,1024]{1,0:T(8,128)(2,1)}, bf16[256,1024]{1,0:T(8,128)(2,1)S(1)}, u32[]{:S(2)}, u32[]{:S(2)}) collective-permute-start(bf16[256,1024]{1,0:T(8,128)(2,1)} %param.2), channel_id=1, source_target_pairs={{0,8},{1,9},{2,10},{3,11},{4,12},{5,13},{6,14},{7,15},{8,0},{9,1},... | collective-permute-start | bytes 1572872 | tf_op jit(solution)/shard_map/ppermute | solution.py:27
  7.0 1.3 %multiply_reduce_fusion.1 = f32[256]{0:T(256)S(1)} fusion(bf16[256,1024]{1,0:T(8,128)(2,1)} %param.2), kind=kLoop, calls=%fused_computation.13 | loop fusion | flops 786176 | bytes 525312 | tf_op jit(solution)/shard_map/reduce_sum | solution.py:18
  8.4 0.1 multiply_reduce_fusion.3
  8.6 10.3 %collective-permute-start.2 = (bf16[128,1024]{1,0:T(8,128)(2,1)S(1)}, bf16[128,1024]{1,0:T(8,128)(2,1)S(1)}, u32[]{:S(2)}, u32[]{:S(2)}) collective-permute-start(bf16[128,1024]{1,0:T(8,128)(2,1)S(1)} %collective-permute-done), channel_id=1, source_target_pairs={{0,4},{1,5},{2,6},{3,7},{4,0},{5,1},{6,2},{7,3},{8,12},{9,13},{10,... | collective-permute-start | bytes 786440 | tf_op jit(solution)/shard_map/ppermute | solution.py:27
  19.0 0.3 fusion.4
  19.3 0.1 concatenate.12
  19.3 0.7 %collective-permute-start.1 = (f16[264,128]{1,0:T(8,128)(2,1)S(1)}, f16[264,128]{1,0:T(8,128)(2,1)S(1)}, u32[]{:S(2)}, u32[]{:S(2)}) collective-permute-start(f16[264,128]{1,0:T(8,128)(2,1)S(1)} %concatenate.12), channel_id=1, source_target_pairs={{0,0},{1,1},{2,2},{3,3},{4,6},{5,7},{6,4},{7,5},{8,9},{9,8},{10,11... | collective-permute-start | bytes 202760 | tf_op jit(solution)/shard_map/ppermute | solution.py:27
  20.0 0.1 collective-permute-done.2
  20.1 0.1 multiply_reduce_fusion.2
  20.3 0.3 fusion.5
  20.6 0.1 concatenate.13
  20.7 2.1 %collective-permute-start.3 = (f16[264,128]{1,0:T(8,128)(2,1)S(1)}, f16[264,128]{1,0:T(8,128)(2,1)S(1)}, u32[]{:S(2)}, u32[]{:S(2)}) collective-permute-start(f16[264,128]{1,0:T(8,128)(2,1)S(1)} %concatenate.13), channel_id=1, source_target_pairs={{0,2},{1,3},{2,0},{3,1},{4,4},{5,5},{6,6},{7,7},{8,11},{9,10},{10,... | collective-permute-start | bytes 202760 | tf_op jit(solution)/shard_map/ppermute | solution.py:27
  22.8 1.3 %collective-permute-done.4 = bf16[256,1024]{1,0:T(8,128)(2,1)S(1)} collective-permute-done((bf16[256,1024]{1,0:T(8,128)(2,1)}, bf16[256,1024]{1,0:T(8,128)(2,1)S(1)}, u32[]{:S(2)}, u32[]{:S(2)}) %collective-permute-start.4) | collective-permute-done | bytes 524320 | tf_op jit(solution)/shard_map/ppermute | solution.py:27
  24.1 0.2 multiply_reduce_fusion
  24.3 0.3 fusion.7
  24.6 0.3 fusion.6
  25.0 0.1 concatenate.15
  25.1 3.0 %collective-permute-start.6 = (f16[264,128]{1,0:T(8,128)(2,1)S(1)}, f16[264,128]{1,0:T(8,128)(2,1)S(1)}, u32[]{:S(2)}, u32[]{:S(2)}) collective-permute-start(f16[264,128]{1,0:T(8,128)(2,1)S(1)} %concatenate.15), channel_id=1, source_target_pairs={{0,10},{1,11},{2,8},{3,9},{4,12},{5,13},{6,14},{7,15},{8,3},{9,2},... | collective-permute-start | bytes 202760 | tf_op jit(solution)/shard_map/ppermute | solution.py:27
  28.2 1.4 %collective-permute-start.5 = (f16[264,128]{1,0:T(8,128)(2,1)S(1)}, f16[264,128]{1,0:T(8,128)(2,1)S(1)}, u32[]{:S(2)}, u32[]{:S(2)}) collective-permute-start(f16[264,128]{1,0:T(8,128)(2,1)S(1)} %concatenate.14), channel_id=1, source_target_pairs={{0,8},{1,9},{2,10},{3,11},{4,14},{5,15},{6,12},{7,13},{8,1},{9,0},... | collective-permute-start | bytes 202760 | tf_op jit(solution)/shard_map/ppermute | solution.py:27
  29.7 0.1 fusion.15
  29.8 3.0 %collective-permute-done.6 = f16[264,128]{1,0:T(8,128)(2,1)S(1)} collective-permute-done((f16[264,128]{1,0:T(8,128)(2,1)S(1)}, f16[264,128]{1,0:T(8,128)(2,1)S(1)}, u32[]{:S(2)}, u32[]{:S(2)}) %collective-permute-start.6) | collective-permute-done | bytes 67616 | tf_op jit(solution)/shard_map/ppermute | solution.py:27
  32.8 1.4 %collective-permute-done.5 = f16[264,128]{1,0:T(8,128)(2,1)S(1)} collective-permute-done((f16[264,128]{1,0:T(8,128)(2,1)S(1)}, f16[264,128]{1,0:T(8,128)(2,1)S(1)}, u32[]{:S(2)}, u32[]{:S(2)}) %collective-permute-start.5) | collective-permute-done | bytes 67616 | tf_op jit(solution)/shard_map/ppermute | solution.py:27
  34.4 0.8 %fusion.12 = f32[256,128]{1,0:T(8,128)} fusion(f32[256,128]{1,0:T(8,128)S(1)} %fusion.15, f32[264,128]{1,0:T(8,128)S(1)} %convert_element_type.111, f32[264,128]{1,0:T(8,128)S(1)} %convert_element_type.110, f32[128]{0:T(128)S(1)} %fusion.93, f32[256]{0:T(256)S(1)} %fusion.62, f32[128]{0:T(128)S(1)} %get-tuple-element.23, f32[256]{0:T(256)S(1)} %sqrt_bitcast_fusion, ...), kind=kLoop, calls=%fused_computation.21 | loop fusion | flops 262144 | bytes 528896 | tf_op jit(solution)/shard_map/mul | solution.py:33
  (31 shorter events, 0.6 us)
Async XLA Ops:
  0.0 18.9 %copy-start = (bf16[256,1024]{1,0:T(8,128)(2,1)S(1)}, bf16[256,1024]{1,0:T(8,128)(2,1)}, u32[]{:S(2)}) copy-start(bf16[256,1024]{1,0:T(8,128)(2,1)} %param.2) | copy-start | bytes 1572868
  0.0 8.4 %collective-permute-start = (bf16[128,1024]{1,0:T(8,128)(2,1)}, bf16[128,1024]{1,0:T(8,128)(2,1)S(1)}, u32[]{:S(2)}, u32[]{:S(2)}) collective-permute-start(bf16[128,1024]{1,0:T(8,128)(2,1)} %param.3), channel_id=1, source_target_pairs={{0,0},{1,8},{2,4},{3,12},{4,9},{5,1},{6,13},{7,5},{8,6},{9,14},{10... | collective-permute-start | bytes 786440 | tf_op jit(solution)/shard_map/ppermute | solution.py:27
  1.7 22.4 %collective-permute-start.4 = (bf16[256,1024]{1,0:T(8,128)(2,1)}, bf16[256,1024]{1,0:T(8,128)(2,1)S(1)}, u32[]{:S(2)}, u32[]{:S(2)}) collective-permute-start(bf16[256,1024]{1,0:T(8,128)(2,1)} %param.2), channel_id=1, source_target_pairs={{0,8},{1,9},{2,10},{3,11},{4,12},{5,13},{6,14},{7,15},{8,0},{9,1},... | collective-permute-start | bytes 1572872 | tf_op jit(solution)/shard_map/ppermute | solution.py:27
  8.6 11.5 %collective-permute-start.2 = (bf16[128,1024]{1,0:T(8,128)(2,1)S(1)}, bf16[128,1024]{1,0:T(8,128)(2,1)S(1)}, u32[]{:S(2)}, u32[]{:S(2)}) collective-permute-start(bf16[128,1024]{1,0:T(8,128)(2,1)S(1)} %collective-permute-done), channel_id=1, source_target_pairs={{0,4},{1,5},{2,6},{3,7},{4,0},{5,1},{6,2},{7,3},{8,12},{9,13},{10,... | collective-permute-start | bytes 786440 | tf_op jit(solution)/shard_map/ppermute | solution.py:27
  19.3 10.2 %collective-permute-start.1 = (f16[264,128]{1,0:T(8,128)(2,1)S(1)}, f16[264,128]{1,0:T(8,128)(2,1)S(1)}, u32[]{:S(2)}, u32[]{:S(2)}) collective-permute-start(f16[264,128]{1,0:T(8,128)(2,1)S(1)} %concatenate.12), channel_id=1, source_target_pairs={{0,0},{1,1},{2,2},{3,3},{4,6},{5,7},{6,4},{7,5},{8,9},{9,8},{10,11... | collective-permute-start | bytes 202760 | tf_op jit(solution)/shard_map/ppermute | solution.py:27
  20.7 8.8 %collective-permute-start.3 = (f16[264,128]{1,0:T(8,128)(2,1)S(1)}, f16[264,128]{1,0:T(8,128)(2,1)S(1)}, u32[]{:S(2)}, u32[]{:S(2)}) collective-permute-start(f16[264,128]{1,0:T(8,128)(2,1)S(1)} %concatenate.13), channel_id=1, source_target_pairs={{0,2},{1,3},{2,0},{3,1},{4,4},{5,5},{6,6},{7,7},{8,11},{9,10},{10,... | collective-permute-start | bytes 202760 | tf_op jit(solution)/shard_map/ppermute | solution.py:27
  25.1 7.6 %collective-permute-start.6 = (f16[264,128]{1,0:T(8,128)(2,1)S(1)}, f16[264,128]{1,0:T(8,128)(2,1)S(1)}, u32[]{:S(2)}, u32[]{:S(2)}) collective-permute-start(f16[264,128]{1,0:T(8,128)(2,1)S(1)} %concatenate.15), channel_id=1, source_target_pairs={{0,10},{1,11},{2,8},{3,9},{4,12},{5,13},{6,14},{7,15},{8,3},{9,2},... | collective-permute-start | bytes 202760 | tf_op jit(solution)/shard_map/ppermute | solution.py:27
  28.2 6.1 %collective-permute-start.5 = (f16[264,128]{1,0:T(8,128)(2,1)S(1)}, f16[264,128]{1,0:T(8,128)(2,1)S(1)}, u32[]{:S(2)}, u32[]{:S(2)}) collective-permute-start(f16[264,128]{1,0:T(8,128)(2,1)S(1)} %concatenate.14), channel_id=1, source_target_pairs={{0,8},{1,9},{2,10},{3,11},{4,14},{5,15},{6,12},{7,13},{8,1},{9,0},... | collective-permute-start | bytes 202760 | tf_op jit(solution)/shard_map/ppermute | solution.py:27

commit v8 on v7

--- a/solution.py
+++ b/solution.py
@@ -22,8 +22,9 @@
     pairs = []
     for row in range(side):
         for col in range(side):
-            to_row, to_col = place(row, col)
-            pairs.append((row * side + col, to_row * side + to_col))
+            target = place(row, col)
+            if target is not None:
+                pairs.append((row * side + col, target[0] * side + target[1]))
     return lax.ppermute(value, ("row", "col"), pairs)
 
 
@@ -52,8 +53,19 @@
     feat_total = left_docs.shape[1] * side
     rows, width = left_docs.shape[0], right_docs.shape[0]
 
+    def taker(k, c):
+        return 2 * ((k ^ c) & 1) + ((k ^ c) >> 1)
+
+    def turns(k, c):
+        return (k ^ c) >> 1 == 1 and (k ^ c) & 1 != k >> 1
+
+    turned = moved(right_docs, side, lambda k, c: (k ^ 2, c) if turns(k, c) else None)
     far = moved(left_docs, side, lambda r, c: (r ^ 2, c))
-    first = moved(right_docs, side, lambda k, c: (2 * ((k ^ c) & 1) + ((k ^ c) >> 1), k))
+    straight = moved(right_docs, side, lambda k, c: None if turns(k, c) else (taker(k, c), k))
+    turned = moved(turned, side, lambda r, c: (taker(r ^ 2, c), r ^ 2) if turns(r ^ 2, c) else None)
+    row, col = lax.axis_index("row"), lax.axis_index("col")
+    first = jnp.where(((row & 1) == 1) & ((row >> 1) != (col >> 1)), turned, straight)
+    first = lax.optimization_barrier(first)
     second = moved(first, side, lambda r, c: (r ^ 1, c))
 
     def message(left_block, left_sums, right_block, right_sums):

time: 35.4 us -> 36.2 us (1.023)
  waiting for transfers between devices: 5.77 us -> 10.3 us
  starting transfers between devices: 24.5 us -> 20.6 us
    ppermute x7 -> x9, waiting for transfers between devices: 5.77 us -> 10.3 us  [moved(): return lax.ppermute(value, ('row', 'col'), pairs)]
    ppermute x7 -> x9, starting transfers between devices: 24.5 us -> 20.6 us  [moved(): return lax.ppermute(value, ('row', 'col'), pairs)]
  transfers between devices with their start and end apart: 7 -> 9, of which waited for: 4 -> 5; matrix products, arithmetic and copies ran while one was open for 11% -> 11% of each run, Pallas kernels for 0% -> 0%
where the time goes in v8:
time: 36.2 us; the launch traced here: 35.9 us
  starting transfers between devices  20.6 us (57%)
  waiting for transfers between devices  10.3 us (28%)
  other arithmetic  3.21 us (9%)
  matrix products  1.24 us (3%)
    ppermute x9, starting transfers between devices, moved(): return lax.ppermute(value, ('row', 'col'), pairs)  20.6 us
    ppermute x9, waiting for transfers between devices, moved(): return lax.ppermute(value, ('row', 'col'), pairs)  10.3 us
    reduce_sum x4, other arithmetic, squares(): return jnp.sum(widened * widened, axis=1)  1.71 us
    dot_general x4, matrix products, contract(): lax.dot_general(left_part, right_part, (((1,), (1,)), ((), ())), preferre...  1.24 us
    mul x2, other arithmetic, finish(): return summed / feat_total * left_scale[:, None] * right_scale[None, :]  0.85 us
  transfers between devices with their start and end apart: 9, of which 5 were waited for; matrix products, arithmetic and copies ran while one was open for 11% of the time, Pallas kernels for 0%

profile of v8, /device:TPU:0, one launch (start us, length us, event | category | flops | bytes accessed | tf_op | source)
XLA Modules:
  0.0 35.9 jit_solution(10657880906411071706)
XLA Ops:
  0.0 1.3 %collective-permute-start = (bf16[128,1024]{1,0:T(8,128)(2,1)}, bf16[128,1024]{1,0:T(8,128)(2,1)S(1)}, u32[]{:S(2)}, u32[]{:S(2)}) collective-permute-start(bf16[128,1024]{1,0:T(8,128)(2,1)} %param.3), channel_id=1, source_target_pairs={{3,11},{6,14},{8,0},{13,5},{19,27},{22,30},{24,16},{29,21}} | collective-permute-start | bytes 786440 | tf_op jit(solution)/shard_map/ppermute | solution.py:28
  1.3 1.6 %collective-permute-start.2 = (bf16[128,1024]{1,0:T(8,128)(2,1)}, bf16[128,1024]{1,0:T(8,128)(2,1)S(1)}, u32[]{:S(2)}, u32[]{:S(2)}) collective-permute-start(bf16[128,1024]{1,0:T(8,128)(2,1)} %param.3), channel_id=1, source_target_pairs={{0,0},{1,8},{2,4},{4,9},{5,1},{7,5},{9,14},{10,2},{11,10},{12,15},... | collective-permute-start | bytes 786440 | tf_op jit(solution)/shard_map/ppermute | solution.py:28
  2.9 2.7 %collective-permute-start.6 = (bf16[256,1024]{1,0:T(8,128)(2,1)}, bf16[256,1024]{1,0:T(8,128)(2,1)S(1)}, u32[]{:S(2)}, u32[]{:S(2)}) collective-permute-start(bf16[256,1024]{1,0:T(8,128)(2,1)} %param.2), channel_id=1, source_target_pairs={{0,8},{1,9},{2,10},{3,11},{4,12},{5,13},{6,14},{7,15},{8,0},{9,1},... | collective-permute-start | bytes 1572872 | tf_op jit(solution)/shard_map/ppermute | solution.py:28
  5.6 1.3 %multiply_reduce_fusion.1 = f32[256]{0:T(256)S(1)} fusion(bf16[256,1024]{1,0:T(8,128)(2,1)} %param.2), kind=kLoop, calls=%fused_computation.15 | loop fusion | flops 786176 | bytes 525312 | tf_op jit(solution)/shard_map/reduce_sum | solution.py:18
  6.9 1.9 %collective-permute-done = bf16[128,1024]{1,0:T(8,128)(2,1)S(1)} collective-permute-done((bf16[128,1024]{1,0:T(8,128)(2,1)}, bf16[128,1024]{1,0:T(8,128)(2,1)S(1)}, u32[]{:S(2)}, u32[]{:S(2)}) %collective-permute-start) | collective-permute-done | bytes 262176 | tf_op jit(solution)/shard_map/ppermute | solution.py:28
  8.8 4.2 %collective-permute-start.1 = (bf16[128,1024]{1,0:T(8,128)(2,1)S(1)}, bf16[128,1024]{1,0:T(8,128)(2,1)S(1)}, u32[]{:S(2)}, u32[]{:S(2)}) collective-permute-start(bf16[128,1024]{1,0:T(8,128)(2,1)S(1)} %collective-permute-done), channel_id=1, source_target_pairs={{0,6},{5,7},{11,12},{14,13},{16,22},{21,23},{27,28},{30,29}} | collective-permute-start | bytes 786440 | tf_op jit(solution)/shard_map/ppermute | solution.py:28
  13.1 3.8 %collective-permute-done.1 = bf16[128,1024]{1,0:T(8,128)(2,1)S(1)} collective-permute-done((bf16[128,1024]{1,0:T(8,128)(2,1)S(1)}, bf16[128,1024]{1,0:T(8,128)(2,1)S(1)}, u32[]{:S(2)}, u32[]{:S(2)}) %collective-permute-start.1) | collective-permute-done | bytes 262176 | tf_op jit(solution)/shard_map/ppermute | solution.py:28
  16.9 0.1 collective-permute-start.4
  17.0 0.1 multiply_reduce_fusion.3
  17.3 0.3 fusion.9
  17.7 0.7 %collective-permute-start.3 = (f16[264,128]{1,0:T(8,128)(2,1)S(1)}, f16[264,128]{1,0:T(8,128)(2,1)S(1)}, u32[]{:S(2)}, u32[]{:S(2)}) collective-permute-start(f16[264,128]{1,0:T(8,128)(2,1)S(1)} %concatenate.12), channel_id=1, source_target_pairs={{0,0},{1,1},{2,2},{3,3},{4,6},{5,7},{6,4},{7,5},{8,9},{9,8},{10,11... | collective-permute-start | bytes 202760 | tf_op jit(solution)/shard_map/ppermute | solution.py:28
  18.3 0.2 collective-permute-done.4
  18.5 0.1 multiply_reduce_fusion.2
  18.8 0.3 fusion.8
  19.2 4.9 %collective-permute-start.5 = (f16[264,128]{1,0:T(8,128)(2,1)S(1)}, f16[264,128]{1,0:T(8,128)(2,1)S(1)}, u32[]{:S(2)}, u32[]{:S(2)}) collective-permute-start(f16[264,128]{1,0:T(8,128)(2,1)S(1)} %concatenate.13), channel_id=1, source_target_pairs={{0,2},{1,3},{2,0},{3,1},{4,4},{5,5},{6,6},{7,7},{8,11},{9,10},{10,... | collective-permute-start | bytes 202760 | tf_op jit(solution)/shard_map/ppermute | solution.py:28
  24.1 0.2 multiply_reduce_fusion
  24.4 0.3 fusion.6
  24.7 0.3 fusion.7
  25.2 4.6 %collective-permute-start.8 = (f16[264,128]{1,0:T(8,128)(2,1)S(1)}, f16[264,128]{1,0:T(8,128)(2,1)S(1)}, u32[]{:S(2)}, u32[]{:S(2)}) collective-permute-start(f16[264,128]{1,0:T(8,128)(2,1)S(1)} %concatenate.15), channel_id=1, source_target_pairs={{0,10},{1,11},{2,8},{3,9},{4,12},{5,13},{6,14},{7,15},{8,3},{9,2},... | collective-permute-start | bytes 202760 | tf_op jit(solution)/shard_map/ppermute | solution.py:28
  29.8 0.5 %collective-permute-start.7 = (f16[264,128]{1,0:T(8,128)(2,1)S(1)}, f16[264,128]{1,0:T(8,128)(2,1)S(1)}, u32[]{:S(2)}, u32[]{:S(2)}) collective-permute-start(f16[264,128]{1,0:T(8,128)(2,1)S(1)} %concatenate.14), channel_id=1, source_target_pairs={{0,8},{1,9},{2,10},{3,11},{4,14},{5,15},{6,12},{7,13},{8,1},{9,0},... | collective-permute-start | bytes 202760 | tf_op jit(solution)/shard_map/ppermute | solution.py:28
  30.4 0.1 fusion.17
  30.6 3.6 %collective-permute-done.8 = f16[264,128]{1,0:T(8,128)(2,1)S(1)} collective-permute-done((f16[264,128]{1,0:T(8,128)(2,1)S(1)}, f16[264,128]{1,0:T(8,128)(2,1)S(1)}, u32[]{:S(2)}, u32[]{:S(2)}) %collective-permute-start.8) | collective-permute-done | bytes 67616 | tf_op jit(solution)/shard_map/ppermute | solution.py:28
  34.2 0.8 %collective-permute-done.7 = f16[264,128]{1,0:T(8,128)(2,1)S(1)} collective-permute-done((f16[264,128]{1,0:T(8,128)(2,1)S(1)}, f16[264,128]{1,0:T(8,128)(2,1)S(1)}, u32[]{:S(2)}, u32[]{:S(2)}) %collective-permute-start.7) | collective-permute-done | bytes 67616 | tf_op jit(solution)/shard_map/ppermute | solution.py:28
  35.1 0.8 %fusion.14 = f32[256,128]{1,0:T(8,128)} fusion(f32[256,128]{1,0:T(8,128)S(1)} %fusion.17, f32[264,128]{1,0:T(8,128)S(1)} %convert_element_type.119, f32[264,128]{1,0:T(8,128)S(1)} %convert_element_type.118, f32[128]{0:T(128)S(1)} %fusion.95, f32[256]{0:T(256)S(1)} %fusion.64, f32[128]{0:T(128)S(1)} %get-tuple-element.23, f32[256]{0:T(256)S(1)} %sqrt_bitcast_fusion, ...), kind=kLoop, calls=%fused_computation.24 | loop fusion | flops 262144 | bytes 528896 | tf_op jit(solution)/shard_map/mul | solution.py:34
  (36 shorter events, 0.8 us)
Async XLA Ops:
  0.0 8.8 %collective-permute-start = (bf16[128,1024]{1,0:T(8,128)(2,1)}, bf16[128,1024]{1,0:T(8,128)(2,1)S(1)}, u32[]{:S(2)}, u32[]{:S(2)}) collective-permute-start(bf16[128,1024]{1,0:T(8,128)(2,1)} %param.3), channel_id=1, source_target_pairs={{3,11},{6,14},{8,0},{13,5},{19,27},{22,30},{24,16},{29,21}} | collective-permute-start | bytes 786440 | tf_op jit(solution)/shard_map/ppermute | solution.py:28
  1.3 11.8 %collective-permute-start.2 = (bf16[128,1024]{1,0:T(8,128)(2,1)}, bf16[128,1024]{1,0:T(8,128)(2,1)S(1)}, u32[]{:S(2)}, u32[]{:S(2)}) collective-permute-start(bf16[128,1024]{1,0:T(8,128)(2,1)} %param.3), channel_id=1, source_target_pairs={{0,0},{1,8},{2,4},{4,9},{5,1},{7,5},{9,14},{10,2},{11,10},{12,15},... | collective-permute-start | bytes 786440 | tf_op jit(solution)/shard_map/ppermute | solution.py:28
  2.9 21.2 %collective-permute-start.6 = (bf16[256,1024]{1,0:T(8,128)(2,1)}, bf16[256,1024]{1,0:T(8,128)(2,1)S(1)}, u32[]{:S(2)}, u32[]{:S(2)}) collective-permute-start(bf16[256,1024]{1,0:T(8,128)(2,1)} %param.2), channel_id=1, source_target_pairs={{0,8},{1,9},{2,10},{3,11},{4,12},{5,13},{6,14},{7,15},{8,0},{9,1},... | collective-permute-start | bytes 1572872 | tf_op jit(solution)/shard_map/ppermute | solution.py:28
  8.8 8.1 %collective-permute-start.1 = (bf16[128,1024]{1,0:T(8,128)(2,1)S(1)}, bf16[128,1024]{1,0:T(8,128)(2,1)S(1)}, u32[]{:S(2)}, u32[]{:S(2)}) collective-permute-start(bf16[128,1024]{1,0:T(8,128)(2,1)S(1)} %collective-permute-done), channel_id=1, source_target_pairs={{0,6},{5,7},{11,12},{14,13},{16,22},{21,23},{27,28},{30,29}} | collective-permute-start | bytes 786440 | tf_op jit(solution)/shard_map/ppermute | solution.py:28
  13.1 4.1 %copy-start = (bf16[256,1024]{1,0:T(8,128)(2,1)S(1)}, bf16[256,1024]{1,0:T(8,128)(2,1)}, u32[]{:S(2)}) copy-start(bf16[256,1024]{1,0:T(8,128)(2,1)} %param.2) | copy-start | bytes 1572868
  16.9 1.6 %collective-permute-start.4 = (bf16[128,1024]{1,0:T(8,128)(2,1)S(1)}, bf16[128,1024]{1,0:T(8,128)(2,1)S(1)}, u32[]{:S(2)}, u32[]{:S(2)}) collective-permute-start(bf16[128,1024]{1,0:T(8,128)(2,1)S(1)} %broadcast_select_fusion), channel_id=1, source_target_pairs={{0,4},{1,5},{2,6},{3,7},{4,0},{5,1},{6,2},{7,3},{8,12},{9,13},{10,... | collective-permute-start | bytes 786440 | tf_op jit(solution)/shard_map/ppermute | solution.py:28
  17.7 12.7 %collective-permute-start.3 = (f16[264,128]{1,0:T(8,128)(2,1)S(1)}, f16[264,128]{1,0:T(8,128)(2,1)S(1)}, u32[]{:S(2)}, u32[]{:S(2)}) collective-permute-start(f16[264,128]{1,0:T(8,128)(2,1)S(1)} %concatenate.12), channel_id=1, source_target_pairs={{0,0},{1,1},{2,2},{3,3},{4,6},{5,7},{6,4},{7,5},{8,9},{9,8},{10,11... | collective-permute-start | bytes 202760 | tf_op jit(solution)/shard_map/ppermute | solution.py:28
  19.2 11.2 %collective-permute-start.5 = (f16[264,128]{1,0:T(8,128)(2,1)S(1)}, f16[264,128]{1,0:T(8,128)(2,1)S(1)}, u32[]{:S(2)}, u32[]{:S(2)}) collective-permute-start(f16[264,128]{1,0:T(8,128)(2,1)S(1)} %concatenate.13), channel_id=1, source_target_pairs={{0,2},{1,3},{2,0},{3,1},{4,4},{5,5},{6,6},{7,7},{8,11},{9,10},{10,... | collective-permute-start | bytes 202760 | tf_op jit(solution)/shard_map/ppermute | solution.py:28
  25.2 9.0 %collective-permute-start.8 = (f16[264,128]{1,0:T(8,128)(2,1)S(1)}, f16[264,128]{1,0:T(8,128)(2,1)S(1)}, u32[]{:S(2)}, u32[]{:S(2)}) collective-permute-start(f16[264,128]{1,0:T(8,128)(2,1)S(1)} %concatenate.15), channel_id=1, source_target_pairs={{0,10},{1,11},{2,8},{3,9},{4,12},{5,13},{6,14},{7,15},{8,3},{9,2},... | collective-permute-start | bytes 202760 | tf_op jit(solution)/shard_map/ppermute | solution.py:28
  29.8 5.2 %collective-permute-start.7 = (f16[264,128]{1,0:T(8,128)(2,1)S(1)}, f16[264,128]{1,0:T(8,128)(2,1)S(1)}, u32[]{:S(2)}, u32[]{:S(2)}) collective-permute-start(f16[264,128]{1,0:T(8,128)(2,1)S(1)} %concatenate.14), channel_id=1, source_target_pairs={{0,8},{1,9},{2,10},{3,11},{4,14},{5,15},{6,12},{7,13},{8,1},{9,0},... | collective-permute-start | bytes 202760 | tf_op jit(solution)/shard_map/ppermute | solution.py:28

commit v9 on v7

--- a/solution.py
+++ b/solution.py
@@ -89,7 +89,6 @@
     own_got, _ = lax.optimization_barrier(([sent(value, 0, j) for j, value in enumerate(own)], others))
     near_sum = added(*map(taken, own_got))
     far_got = [sent(value, 1, j) for j, value in enumerate(others)]
-    near_sum, far_got = lax.optimization_barrier((near_sum, far_got))
     summed, left_sq, right_sq = added(near_sum, added(*map(taken, far_got)))
     return finish(summed / top, left_sq, right_sq, feat_total)
 

time: 35.4 us -> 39.2 us (1.11)
  starting transfers between devices: 24.5 us -> 27.8 us
  waiting for transfers between devices: 5.77 us -> 6.43 us
    ppermute x7, starting transfers between devices: 24.5 us -> 27.8 us  [moved(): return lax.ppermute(value, ('row', 'col'), pairs)]
    ppermute x7, waiting for transfers between devices: 5.77 us -> 6.43 us  [moved(): return lax.ppermute(value, ('row', 'col'), pairs)]
  transfers between devices with their start and end apart: 7 -> 7, of which waited for: 4 -> 3; matrix products, arithmetic and copies ran while one was open for 11% -> 9% of each run, Pallas kernels for 0% -> 0%
where the time goes in v9:
time: 39.2 us; the launch traced here: 39 us
  starting transfers between devices  27.8 us (71%)
  waiting for transfers between devices  6.43 us (16%)
  other arithmetic  3.07 us (8%)
  matrix products  1.23 us (3%)
    ppermute x7, starting transfers between devices, moved(): return lax.ppermute(value, ('row', 'col'), pairs)  27.8 us
    ppermute x7, waiting for transfers between devices, moved(): return lax.ppermute(value, ('row', 'col'), pairs)  6.43 us
    reduce_sum x4, other arithmetic, squares(): return jnp.sum(widened * widened, axis=1)  1.67 us
    dot_general x4, matrix products, contract(): lax.dot_general(left_part, right_part, (((1,), (1,)), ((), ())), preferre...  1.23 us
    mul x2, other arithmetic, finish(): return summed / feat_total * left_scale[:, None] * right_scale[None, :]  0.91 us
  transfers between devices with their start and end apart: 7, of which 3 were waited for; matrix products, arithmetic and copies ran while one was open for 9% of the time, Pallas kernels for 0%

profile of v9, /device:TPU:0, one launch (start us, length us, event | category | flops | bytes accessed | tf_op | source)
XLA Modules:
  0.0 39.0 jit_solution(2970536383800303784)
XLA Ops:
  0.0 2.9 %collective-permute-start.4 = (bf16[256,1024]{1,0:T(8,128)(2,1)}, bf16[256,1024]{1,0:T(8,128)(2,1)S(1)}, u32[]{:S(2)}, u32[]{:S(2)}) collective-permute-start(bf16[256,1024]{1,0:T(8,128)(2,1)} %param.2), channel_id=1, source_target_pairs={{0,8},{1,9},{2,10},{3,11},{4,12},{5,13},{6,14},{7,15},{8,0},{9,1},... | collective-permute-start | bytes 1572872 | tf_op jit(solution)/shard_map/ppermute | solution.py:27
  2.9 1.6 %collective-permute-start = (bf16[128,1024]{1,0:T(8,128)(2,1)}, bf16[128,1024]{1,0:T(8,128)(2,1)S(1)}, u32[]{:S(2)}, u32[]{:S(2)}) collective-permute-start(bf16[128,1024]{1,0:T(8,128)(2,1)} %param.3), channel_id=1, source_target_pairs={{0,0},{1,8},{2,4},{3,12},{4,9},{5,1},{6,13},{7,5},{8,6},{9,14},{10... | collective-permute-start | bytes 786440 | tf_op jit(solution)/shard_map/ppermute | solution.py:27
  4.5 1.2 %multiply_reduce_fusion.1 = f32[256]{0:T(256)S(1)} fusion(bf16[256,1024]{1,0:T(8,128)(2,1)} %param.2), kind=kLoop, calls=%fused_computation.13 | loop fusion | flops 786176 | bytes 525312 | tf_op jit(solution)/shard_map/reduce_sum | solution.py:18
  5.9 0.1 multiply_reduce_fusion.3
  6.1 13.4 %collective-permute-start.2 = (bf16[128,1024]{1,0:T(8,128)(2,1)S(1)}, bf16[128,1024]{1,0:T(8,128)(2,1)S(1)}, u32[]{:S(2)}, u32[]{:S(2)}) collective-permute-start(bf16[128,1024]{1,0:T(8,128)(2,1)S(1)} %collective-permute-done), channel_id=1, source_target_pairs={{0,4},{1,5},{2,6},{3,7},{4,0},{5,1},{6,2},{7,3},{8,12},{9,13},{10,... | collective-permute-start | bytes 786440 | tf_op jit(solution)/shard_map/ppermute | solution.py:27
  19.5 0.3 fusion.4
  19.9 0.1 concatenate.12
  19.9 0.7 %collective-permute-start.1 = (f16[264,128]{1,0:T(8,128)(2,1)S(1)}, f16[264,128]{1,0:T(8,128)(2,1)S(1)}, u32[]{:S(2)}, u32[]{:S(2)}) collective-permute-start(f16[264,128]{1,0:T(8,128)(2,1)S(1)} %concatenate.12), channel_id=1, source_target_pairs={{0,0},{1,1},{2,2},{3,3},{4,6},{5,7},{6,4},{7,5},{8,9},{9,8},{10,11... | collective-permute-start | bytes 202760 | tf_op jit(solution)/shard_map/ppermute | solution.py:27
  20.6 0.1 collective-permute-done.2
  20.7 0.1 multiply_reduce_fusion.2
  20.9 0.3 fusion.5
  21.2 0.1 concatenate.13
  21.3 0.2 multiply_reduce_fusion
  21.5 0.1 fusion.36
  21.6 6.6 %collective-permute-start.3 = (f16[264,128]{1,0:T(8,128)(2,1)S(1)}, f16[264,128]{1,0:T(8,128)(2,1)S(1)}, u32[]{:S(2)}, u32[]{:S(2)}) collective-permute-start(f16[264,128]{1,0:T(8,128)(2,1)S(1)} %concatenate.13), channel_id=1, source_target_pairs={{0,2},{1,3},{2,0},{3,1},{4,4},{5,5},{6,6},{7,7},{8,11},{9,10},{10,... | collective-permute-start | bytes 202760 | tf_op jit(solution)/shard_map/ppermute | solution.py:27
  28.2 0.3 fusion.6
  28.5 0.1 concatenate.14
  28.6 2.0 %collective-permute-start.5 = (f16[264,128]{1,0:T(8,128)(2,1)S(1)}, f16[264,128]{1,0:T(8,128)(2,1)S(1)}, u32[]{:S(2)}, u32[]{:S(2)}) collective-permute-start(f16[264,128]{1,0:T(8,128)(2,1)S(1)} %concatenate.14), channel_id=1, source_target_pairs={{0,8},{1,9},{2,10},{3,11},{4,14},{5,15},{6,12},{7,13},{8,1},{9,0},... | collective-permute-start | bytes 202760 | tf_op jit(solution)/shard_map/ppermute | solution.py:27
  30.5 0.3 fusion.7
  30.9 0.1 concatenate.15
  30.9 0.6 %collective-permute-start.6 = (f16[264,128]{1,0:T(8,128)(2,1)S(1)}, f16[264,128]{1,0:T(8,128)(2,1)S(1)}, u32[]{:S(2)}, u32[]{:S(2)}) collective-permute-start(f16[264,128]{1,0:T(8,128)(2,1)S(1)} %concatenate.15), channel_id=1, source_target_pairs={{0,10},{1,11},{2,8},{3,9},{4,12},{5,13},{6,14},{7,15},{8,3},{9,2},... | collective-permute-start | bytes 202760 | tf_op jit(solution)/shard_map/ppermute | solution.py:27
  31.5 3.3 %collective-permute-done.5 = f16[264,128]{1,0:T(8,128)(2,1)S(1)} collective-permute-done((f16[264,128]{1,0:T(8,128)(2,1)S(1)}, f16[264,128]{1,0:T(8,128)(2,1)S(1)}, u32[]{:S(2)}, u32[]{:S(2)}) %collective-permute-start.5) | collective-permute-done | bytes 67616 | tf_op jit(solution)/shard_map/ppermute | solution.py:27
  34.9 3.0 %collective-permute-done.6 = f16[264,128]{1,0:T(8,128)(2,1)S(1)} collective-permute-done((f16[264,128]{1,0:T(8,128)(2,1)S(1)}, f16[264,128]{1,0:T(8,128)(2,1)S(1)}, u32[]{:S(2)}, u32[]{:S(2)}) %collective-permute-start.6) | collective-permute-done | bytes 67616 | tf_op jit(solution)/shard_map/ppermute | solution.py:27
  38.1 0.9 %fusion.12 = f32[256,128]{1,0:T(8,128)} fusion(f32[264,128]{1,0:T(8,128)S(1)} %convert_element_type.111, f32[264,128]{1,0:T(8,128)S(1)} %convert_element_type.110, f32[264,128]{1,0:T(8,128)S(1)} %convert_element_type.109, f32[264,128]{1,0:T(8,128)S(1)} %convert_element_type.108, f32[128]{0:T(128)S(1)} %rsqrt_bitcast_fusion, f32[256]{0:T(256)S(1)} %get-tuple-element.24, ...), kind=kLoop, calls=%fused_computation.21 | loop fusion | flops 425984 | bytes 663040 | tf_op jit(solution)/shard_map/mul | solution.py:33
  (25 shorter events, 0.5 us)
Async XLA Ops:
  0.0 19.5 %copy-start = (bf16[256,1024]{1,0:T(8,128)(2,1)S(1)}, bf16[256,1024]{1,0:T(8,128)(2,1)}, u32[]{:S(2)}) copy-start(bf16[256,1024]{1,0:T(8,128)(2,1)} %param.2) | copy-start | bytes 1572868
  0.0 21.3 %collective-permute-start.4 = (bf16[256,1024]{1,0:T(8,128)(2,1)}, bf16[256,1024]{1,0:T(8,128)(2,1)S(1)}, u32[]{:S(2)}, u32[]{:S(2)}) collective-permute-start(bf16[256,1024]{1,0:T(8,128)(2,1)} %param.2), channel_id=1, source_target_pairs={{0,8},{1,9},{2,10},{3,11},{4,12},{5,13},{6,14},{7,15},{8,0},{9,1},... | collective-permute-start | bytes 1572872 | tf_op jit(solution)/shard_map/ppermute | solution.py:27
  2.9 2.9 %collective-permute-start = (bf16[128,1024]{1,0:T(8,128)(2,1)}, bf16[128,1024]{1,0:T(8,128)(2,1)S(1)}, u32[]{:S(2)}, u32[]{:S(2)}) collective-permute-start(bf16[128,1024]{1,0:T(8,128)(2,1)} %param.3), channel_id=1, source_target_pairs={{0,0},{1,8},{2,4},{3,12},{4,9},{5,1},{6,13},{7,5},{8,6},{9,14},{10... | collective-permute-start | bytes 786440 | tf_op jit(solution)/shard_map/ppermute | solution.py:27
  6.1 14.6 %collective-permute-start.2 = (bf16[128,1024]{1,0:T(8,128)(2,1)S(1)}, bf16[128,1024]{1,0:T(8,128)(2,1)S(1)}, u32[]{:S(2)}, u32[]{:S(2)}) collective-permute-start(bf16[128,1024]{1,0:T(8,128)(2,1)S(1)} %collective-permute-done), channel_id=1, source_target_pairs={{0,4},{1,5},{2,6},{3,7},{4,0},{5,1},{6,2},{7,3},{8,12},{9,13},{10,... | collective-permute-start | bytes 786440 | tf_op jit(solution)/shard_map/ppermute | solution.py:27
  19.9 14.9 %collective-permute-start.1 = (f16[264,128]{1,0:T(8,128)(2,1)S(1)}, f16[264,128]{1,0:T(8,128)(2,1)S(1)}, u32[]{:S(2)}, u32[]{:S(2)}) collective-permute-start(f16[264,128]{1,0:T(8,128)(2,1)S(1)} %concatenate.12), channel_id=1, source_target_pairs={{0,0},{1,1},{2,2},{3,3},{4,6},{5,7},{6,4},{7,5},{8,9},{9,8},{10,11... | collective-permute-start | bytes 202760 | tf_op jit(solution)/shard_map/ppermute | solution.py:27
  21.6 13.3 %collective-permute-start.3 = (f16[264,128]{1,0:T(8,128)(2,1)S(1)}, f16[264,128]{1,0:T(8,128)(2,1)S(1)}, u32[]{:S(2)}, u32[]{:S(2)}) collective-permute-start(f16[264,128]{1,0:T(8,128)(2,1)S(1)} %concatenate.13), channel_id=1, source_target_pairs={{0,2},{1,3},{2,0},{3,1},{4,4},{5,5},{6,6},{7,7},{8,11},{9,10},{10,... | collective-permute-start | bytes 202760 | tf_op jit(solution)/shard_map/ppermute | solution.py:27
  28.6 6.2 %collective-permute-start.5 = (f16[264,128]{1,0:T(8,128)(2,1)S(1)}, f16[264,128]{1,0:T(8,128)(2,1)S(1)}, u32[]{:S(2)}, u32[]{:S(2)}) collective-permute-start(f16[264,128]{1,0:T(8,128)(2,1)S(1)} %concatenate.14), channel_id=1, source_target_pairs={{0,8},{1,9},{2,10},{3,11},{4,14},{5,15},{6,12},{7,13},{8,1},{9,0},... | collective-permute-start | bytes 202760 | tf_op jit(solution)/shard_map/ppermute | solution.py:27
  30.9 7.0 %collective-permute-start.6 = (f16[264,128]{1,0:T(8,128)(2,1)S(1)}, f16[264,128]{1,0:T(8,128)(2,1)S(1)}, u32[]{:S(2)}, u32[]{:S(2)}) collective-permute-start(f16[264,128]{1,0:T(8,128)(2,1)S(1)} %concatenate.15), channel_id=1, source_target_pairs={{0,10},{1,11},{2,8},{3,9},{4,12},{5,13},{6,14},{7,15},{8,3},{9,2},... | collective-permute-start | bytes 202760 | tf_op jit(solution)/shard_map/ppermute | solution.py:27

commit v10 on v2

--- a/solution.py
+++ b/solution.py
@@ -21,8 +21,9 @@
     pairs = []
     for row in range(side):
         for col in range(side):
-            to_row, to_col = place(row, col)
-            pairs.append((row * side + col, to_row * side + to_col))
+            target = place(row, col)
+            if target is not None:
+                pairs.append((row * side + col, target[0] * side + target[1]))
     return lax.ppermute(value, ("row", "col"), pairs)
 
 
@@ -35,28 +36,36 @@
 def on_square_grid(left_docs, right_docs):
     side = lax.axis_size("col")
     feat_total = left_docs.shape[1] * side
+    rows, width = left_docs.shape[0], right_docs.shape[0]
     row, col = lax.axis_index("row"), lax.axis_index("col")
+    at_home = (row >> 1) == (col >> 1)
+    same = (row & 1) == (col & 1)
 
-    def spread(c):
-        return 2 * (c & 1) + (c >> 1)
+    def other_core(block):
+        return moved(block, side, lambda r, c: (r ^ 1, c))
 
-    held = moved(right_docs, side, lambda k, c: (spread(c), k))
-    far = moved(left_docs, side, lambda r, c: (r ^ 2, c))
-    near = moved(left_docs, side, lambda r, c: (r ^ 1, c))
-    lefts = [left_docs, near, far, moved(far, side, lambda r, c: (r ^ 1, c))]
-    partial = jnp.stack([contract(block, held) for block in lefts])
+    swapped = moved(right_docs, side, lambda r, c: (r ^ 2, c))
+    left_other = moved(left_docs, side, lambda r, c: (r, c ^ 1))
+    near, leaving = lax.optimization_barrier(
+        (jnp.where(at_home, right_docs, swapped), jnp.where(at_home, swapped, right_docs))
+    )
+    cross = moved(leaving, side, lambda r, c: (r, c ^ 2))
+    lefts = lax.optimization_barrier((jnp.where(same, left_docs, left_other), jnp.where(same, left_other, left_docs)))
 
-    summed = 0.0
-    for m in range(side):
-        mine = lax.dynamic_index_in_dim(partial, row ^ col ^ m, 0, keepdims=False)
-        summed = summed + moved(mine, side, lambda i, k, m=m: (k ^ m, spread(i)))
+    def half_sum(mine):
+        blocks = (mine, other_core(mine))
+        gram = sum(contract(left, right) for left, right in zip(lefts, blocks))
+        return gram, sum(squares(block) for block in blocks)
 
-    left_sq, right_sq = squares(left_docs), squares(right_docs)
-    left_sq, right_sq, _ = lax.optimization_barrier((left_sq, right_sq, partial))
-    for step in (1, 2):
-        left_sq = left_sq + moved(left_sq, side, lambda r, c, d=step: (r, c ^ d))
-        right_sq = right_sq + moved(right_sq, side, lambda r, c, d=step: (r ^ d, c))
-    return finish(summed, left_sq, right_sq, feat_total)
+    near_gram, near_sq = half_sum(near)
+    cross_gram, cross_sq = half_sum(cross)
+    left_sq = squares(left_docs) + squares(left_other)
+
+    parts = rows // width
+    sums = [cross_sq[None], left_sq.reshape(parts, width), jnp.zeros((-(parts + 1) % 8, width), jnp.float32)]
+    got = moved(jnp.concatenate([cross_gram, *sums]), side, lambda r, c: (r, c ^ 2))
+    left_sq = left_sq + got[rows + 1:rows + 1 + parts].reshape(rows)
+    return finish(near_gram + got[:rows], left_sq, near_sq + got[rows], feat_total)
 
 
 def on_any_grid(left_docs, right_docs):

time: 49.1 us -> 37.8 us (0.77)
  starting transfers between devices: 21.1 us -> 7.57 us
  waiting for transfers between devices: 23.2 us -> 25.8 us
  other arithmetic: 3.13 us -> 2.25 us
  matrix products: 1.21 us -> 1.87 us
    ppermute x12 -> x6, starting transfers between devices: 21.1 us -> 7.57 us  [moved(): return lax.ppermute(value, ('row', 'col'), pairs)]
    ppermute x12 -> x6, waiting for transfers between devices: 23.2 us -> 25.8 us  [moved(): return lax.ppermute(value, ('row', 'col'), pairs)]
    mul x2, other arithmetic: 0.76 us -> 0.02 us  [finish(): return summed / feat_total * left_scale[:, None] * right_scale[None, :]]
    dot_general x4, matrix products: 1.21 us -> 1.87 us  [contract(): lax.dot_general(left_part, right_part, (((1,), (1,)), ((), ())), preferre...]
    reduce_sum x2 -> x6, other arithmetic: 2.31 us -> 1.98 us  [squares(): return jnp.sum(widened * widened, axis=1)]
  transfers between devices with their start and end apart: 12 -> 6, of which waited for: 4 -> 5; matrix products, arithmetic and copies ran while one was open for 7% -> 9% of each run, Pallas kernels for 0% -> 0%
where the time goes in v10:
time: 37.8 us; the launch traced here: 37.7 us
  waiting for transfers between devices  25.8 us (68%)
  starting transfers between devices  7.57 us (20%)
  other arithmetic  2.25 us (6%)
  matrix products  1.87 us (5%)
    ppermute x6, waiting for transfers between devices, moved(): return lax.ppermute(value, ('row', 'col'), pairs)  25.8 us
    ppermute x6, starting transfers between devices, moved(): return lax.ppermute(value, ('row', 'col'), pairs)  7.57 us
    reduce_sum x6, other arithmetic, squares(): return jnp.sum(widened * widened, axis=1)  1.98 us
    dot_general x4, matrix products, contract(): lax.dot_general(left_part, right_part, (((1,), (1,)), ((), ())), preferre...  1.87 us
  transfers between devices with their start and end apart: 6, of which 5 were waited for; matrix products, arithmetic and copies ran while one was open for 9% of the time, Pallas kernels for 0%

profile of v10, /device:TPU:0, one launch (start us, length us, event | category | flops | bytes accessed | tf_op | source)
XLA Modules:
  0.0 37.7 jit_solution(4412115680954964699)
XLA Ops:
  0.0 2.9 %collective-permute-start.1 = (bf16[128,1024]{1,0:T(8,128)(2,1)}, bf16[128,1024]{1,0:T(8,128)(2,1)S(1)}, u32[]{:S(2)}, u32[]{:S(2)}) collective-permute-start(bf16[128,1024]{1,0:T(8,128)(2,1)} %param.3), channel_id=1, source_target_pairs={{0,8},{1,9},{2,10},{3,11},{4,12},{5,13},{6,14},{7,15},{8,0},{9,1},... | collective-permute-start | bytes 786440 | tf_op jit(solution)/shard_map/ppermute | solution.py:27
  2.9 1.6 %collective-permute-start = (bf16[256,1024]{1,0:T(8,128)(2,1)}, bf16[256,1024]{1,0:T(8,128)(2,1)S(1)}, u32[]{:S(2)}, u32[]{:S(2)}) collective-permute-start(bf16[256,1024]{1,0:T(8,128)(2,1)} %param.2), channel_id=1, source_target_pairs={{0,1},{1,0},{2,3},{3,2},{4,5},{5,4},{6,7},{7,6},{8,9},{9,8},{10,11... | collective-permute-start | bytes 1572872 | tf_op jit(solution)/shard_map/ppermute | solution.py:27
  4.5 0.1 pad.3.clone
  4.6 1.3 %multiply_reduce_fusion.1 = f32[256]{0:T(256)S(1)} fusion(bf16[256,1024]{1,0:T(8,128)(2,1)} %param.2), kind=kLoop, calls=%fused_computation.6 | loop fusion | flops 786176 | bytes 525312 | tf_op jit(solution)/shard_map/reduce_sum | solution.py:17
  5.9 3.6 %collective-permute-done.1 = bf16[128,1024]{1,0:T(8,128)(2,1)S(1)} collective-permute-done((bf16[128,1024]{1,0:T(8,128)(2,1)}, bf16[128,1024]{1,0:T(8,128)(2,1)S(1)}, u32[]{:S(2)}, u32[]{:S(2)}) %collective-permute-start.1) | collective-permute-done | bytes 262176 | tf_op jit(solution)/shard_map/ppermute | solution.py:27
  9.5 0.1 broadcast_select_fusion.2
  9.5 0.1 collective-permute-start.2
  9.6 2.9 %collective-permute-start.3 = (bf16[128,1024]{1,0:T(8,128)(2,1)S(1)}, bf16[128,1024]{1,0:T(8,128)(2,1)S(1)}, u32[]{:S(2)}, u32[]{:S(2)}) collective-permute-start(bf16[128,1024]{1,0:T(8,128)(2,1)S(1)} %get-tuple-element.12), channel_id=1, source_target_pairs={{0,2},{1,3},{2,0},{3,1},{4,6},{5,7},{6,4},{7,5},{8,10},{9,11},{10,... | collective-permute-start | bytes 786440 | tf_op jit(solution)/shard_map/ppermute | solution.py:27
  12.5 0.1 multiply_reduce_fusion.3
  12.7 8.7 %collective-permute-done = bf16[256,1024]{1,0:T(8,128)(2,1)S(1)} collective-permute-done((bf16[256,1024]{1,0:T(8,128)(2,1)}, bf16[256,1024]{1,0:T(8,128)(2,1)S(1)}, u32[]{:S(2)}, u32[]{:S(2)}) %collective-permute-start) | collective-permute-done | bytes 524320 | tf_op jit(solution)/shard_map/ppermute | solution.py:27
  21.4 0.2 multiply_reduce_fusion
  21.5 0.1 broadcast_select_fusion
  21.6 3.5 %collective-permute-done.3 = bf16[128,1024]{1,0:T(8,128)(2,1)S(1)} collective-permute-done((bf16[128,1024]{1,0:T(8,128)(2,1)S(1)}, bf16[128,1024]{1,0:T(8,128)(2,1)S(1)}, u32[]{:S(2)}, u32[]{:S(2)}) %collective-permute-start.3) | collective-permute-done | bytes 262176 | tf_op jit(solution)/shard_map/ppermute | solution.py:27
  25.1 0.1 multiply_reduce_fusion.5
  25.2 0.3 fusion.10
  25.5 1.1 %collective-permute-done.4 = bf16[128,1024]{1,0:T(8,128)(2,1)S(1)} collective-permute-done((bf16[128,1024]{1,0:T(8,128)(2,1)S(1)}, bf16[128,1024]{1,0:T(8,128)(2,1)S(1)}, u32[]{:S(2)}, u32[]{:S(2)}) %collective-permute-start.4) | collective-permute-done | bytes 262176 | tf_op jit(solution)/shard_map/ppermute | solution.py:27
  26.6 0.1 multiply_reduce_fusion.4
  26.8 0.3 convolution_add_fusion
  27.1 0.1 maximum_maximum_fusion
  27.2 0.1 collective-permute-start.5
  27.3 0.3 fusion.9
  27.6 0.1 multiply_reduce_fusion.2
  27.7 9.0 %collective-permute-done.5 = f32[264,128]{1,0:T(8,128)S(1)} collective-permute-done((f32[264,128]{1,0:T(8,128)S(1)}, f32[264,128]{1,0:T(8,128)S(1)}, u32[]{:S(2)}, u32[]{:S(2)}) %collective-permute-start.5) | collective-permute-done | bytes 135200 | tf_op jit(solution)/shard_map/ppermute | solution.py:27
  36.7 1.0 %fusion.2 = f32[256,128]{1,0:T(8,128)} fusion(f32[256,128]{1,0:T(8,128)S(1)} %fusion.9, bf16[256,1024]{1,0:T(8,128)(2,1)S(1)} %get-tuple-element.9, bf16[128,1024]{1,0:T(8,128)(2,1)S(1)} %get-tuple-element.10, f32[264,128]{1,0:T(8,128)S(1)} %collective-permute-done.5, f32[128]{0:T(128)S(1)} %rsqrt_bitcast_fusion, f32[256]{0:T(256)S(1)} %fusion.7), kind=kOutput, calls=%fused_computation.4 | convolution fusion | flops 67239936 | bytes 1181184 | tf_op jit(solution)/shard_map/dot_general | solution.py:10
  (11 shorter events, 0.0 us)
Async XLA Ops:
  0.0 9.5 %collective-permute-start.1 = (bf16[128,1024]{1,0:T(8,128)(2,1)}, bf16[128,1024]{1,0:T(8,128)(2,1)S(1)}, u32[]{:S(2)}, u32[]{:S(2)}) collective-permute-start(bf16[128,1024]{1,0:T(8,128)(2,1)} %param.3), channel_id=1, source_target_pairs={{0,8},{1,9},{2,10},{3,11},{4,12},{5,13},{6,14},{7,15},{8,0},{9,1},... | collective-permute-start | bytes 786440 | tf_op jit(solution)/shard_map/ppermute | solution.py:27
  2.9 18.4 %collective-permute-start = (bf16[256,1024]{1,0:T(8,128)(2,1)}, bf16[256,1024]{1,0:T(8,128)(2,1)S(1)}, u32[]{:S(2)}, u32[]{:S(2)}) collective-permute-start(bf16[256,1024]{1,0:T(8,128)(2,1)} %param.2), channel_id=1, source_target_pairs={{0,1},{1,0},{2,3},{3,2},{4,5},{5,4},{6,7},{7,6},{8,9},{9,8},{10,11... | collective-permute-start | bytes 1572872 | tf_op jit(solution)/shard_map/ppermute | solution.py:27
  4.6 4.9 %copy-start.1 = (bf16[128,1024]{1,0:T(8,128)(2,1)S(1)}, bf16[128,1024]{1,0:T(8,128)(2,1)}, u32[]{:S(2)}) copy-start(bf16[128,1024]{1,0:T(8,128)(2,1)} %param.3) | copy-start | bytes 786436
  9.5 12.0 %copy-start = (bf16[256,1024]{1,0:T(8,128)(2,1)S(1)}, bf16[256,1024]{1,0:T(8,128)(2,1)}, u32[]{:S(2)}) copy-start(bf16[256,1024]{1,0:T(8,128)(2,1)} %param.2) | copy-start | bytes 1572868
  9.5 17.7 %collective-permute-start.2 = (bf16[128,1024]{1,0:T(8,128)(2,1)S(1)}, bf16[128,1024]{1,0:T(8,128)(2,1)S(1)}, u32[]{:S(2)}, u32[]{:S(2)}) collective-permute-start(bf16[128,1024]{1,0:T(8,128)(2,1)S(1)} %get-tuple-element.10), channel_id=1, source_target_pairs={{0,4},{1,5},{2,6},{3,7},{4,0},{5,1},{6,2},{7,3},{8,12},{9,13},{10,... | collective-permute-start | bytes 786440 | tf_op jit(solution)/shard_map/ppermute | solution.py:27
  9.6 15.5 %collective-permute-start.3 = (bf16[128,1024]{1,0:T(8,128)(2,1)S(1)}, bf16[128,1024]{1,0:T(8,128)(2,1)S(1)}, u32[]{:S(2)}, u32[]{:S(2)}) collective-permute-start(bf16[128,1024]{1,0:T(8,128)(2,1)S(1)} %get-tuple-element.12), channel_id=1, source_target_pairs={{0,2},{1,3},{2,0},{3,1},{4,6},{5,7},{6,4},{7,5},{8,10},{9,11},{10,... | collective-permute-start | bytes 786440 | tf_op jit(solution)/shard_map/ppermute | solution.py:27
  25.1 1.5 %collective-permute-start.4 = (bf16[128,1024]{1,0:T(8,128)(2,1)S(1)}, bf16[128,1024]{1,0:T(8,128)(2,1)S(1)}, u32[]{:S(2)}, u32[]{:S(2)}) collective-permute-start(bf16[128,1024]{1,0:T(8,128)(2,1)S(1)} %collective-permute-done.3), channel_id=1, source_target_pairs={{0,4},{1,5},{2,6},{3,7},{4,0},{5,1},{6,2},{7,3},{8,12},{9,13},{10,... | collective-permute-start | bytes 786440 | tf_op jit(solution)/shard_map/ppermute | solution.py:27
  27.2 9.5 %collective-permute-start.5 = (f32[264,128]{1,0:T(8,128)S(1)}, f32[264,128]{1,0:T(8,128)S(1)}, u32[]{:S(2)}, u32[]{:S(2)}) collective-permute-start(f32[264,128]{1,0:T(8,128)S(1)} %maximum_maximum_fusion), channel_id=1, source_target_pairs={{0,2},{1,3},{2,0},{3,1},{4,6},{5,7},{6,4},{7,5},{8,10},{9,11},{10,... | collective-permute-start | bytes 405512 | tf_op jit(solution)/shard_map/ppermute | solution.py:27

commit v11 on v10

--- a/solution.py
+++ b/solution.py
@@ -44,12 +44,20 @@
     def other_core(block):
         return moved(block, side, lambda r, c: (r ^ 1, c))
 
-    swapped = moved(right_docs, side, lambda r, c: (r ^ 2, c))
+    def home(r, c):
+        return r >> 1 == c >> 1
+
+    first, second = right_docs[:width // 2], right_docs[width // 2:]
+    turned = moved(second, side, lambda r, c: None if home(r, c) else (r ^ 2, c))
+    straight = moved(first, side, lambda r, c: None if home(r, c) else (r, c ^ 2))
+    near = moved(right_docs, side, lambda r, c: (r ^ 2, c) if home(r, c) else None)
     left_other = moved(left_docs, side, lambda r, c: (r, c ^ 1))
-    near, leaving = lax.optimization_barrier(
-        (jnp.where(at_home, right_docs, swapped), jnp.where(at_home, swapped, right_docs))
-    )
-    cross = moved(leaving, side, lambda r, c: (r, c ^ 2))
+    turned = moved(turned, side, lambda r, c: (r, c ^ 2) if home(r, c) else None)
+    near = lax.optimization_barrier(jnp.where(at_home, right_docs, near))
+    mine = lax.optimization_barrier(jnp.where(at_home, straight, turned))
+    other = moved(mine, side, lambda r, c: (r ^ 2, c))
+    cross = jnp.concatenate([jnp.where(at_home, mine, other), jnp.where(at_home, other, mine)])
+    cross = lax.optimization_barrier(cross)
     lefts = lax.optimization_barrier((jnp.where(same, left_docs, left_other), jnp.where(same, left_other, left_docs)))
 
     def half_sum(mine):

time: 37.8 us -> 43.7 us (1.16)
  starting transfers between devices: 7.57 us -> 19.3 us
  waiting for transfers between devices: 25.8 us -> 19.8 us
  other arithmetic: 2.25 us -> 1.2 us
  local copies, waits for them, and re-layouts: 0.09 us -> 1.13 us
    ppermute x6 -> x9, starting transfers between devices: 7.57 us -> 19.3 us  [moved(): return lax.ppermute(value, ('row', 'col'), pairs)]
    ppermute x6 -> x9, waiting for transfers between devices: 25.8 us -> 19.8 us  [moved(): return lax.ppermute(value, ('row', 'col'), pairs)]
    reduce_sum x6, other arithmetic: 1.98 us -> 0.9 us  [squares(): return jnp.sum(widened * widened, axis=1)]
    slice x0 -> x1, local copies, waits for them, and re-layouts: none -> 1.04 us  [on_square_grid(): first, second = (right_docs[:width // 2], right_docs[width // 2:])]
  transfers between devices with their start and end apart: 6 -> 9, of which waited for: 5 -> 4; matrix products, arithmetic and copies ran while one was open for 9% -> 5% of each run, Pallas kernels for 0% -> 0%
where the time goes in v11:
time: 43.7 us; the launch traced here: 43.5 us
  waiting for transfers between devices  19.8 us (45%)
  starting transfers between devices  19.3 us (44%)
  matrix products  1.87 us (4%)
  other arithmetic  1.2 us (3%)
  local copies, waits for them, and re-layouts  1.13 us (3%)
    ppermute x9, waiting for transfers between devices, moved(): return lax.ppermute(value, ('row', 'col'), pairs)  19.8 us
    ppermute x9, starting transfers between devices, moved(): return lax.ppermute(value, ('row', 'col'), pairs)  19.3 us
    dot_general x4, matrix products, contract(): lax.dot_general(left_part, right_part, (((1,), (1,)), ((), ())), preferre...  1.87 us
    slice x1, local copies, waits for them, and re-layouts, on_square_grid(): first, second = (right_docs[:width // 2], right_docs[width // 2:])  1.04 us
    reduce_sum x6, other arithmetic, squares(): return jnp.sum(widened * widened, axis=1)  0.9 us
  transfers between devices with their start and end apart: 9, of which 4 were waited for; matrix products, arithmetic and copies ran while one was open for 5% of the time, Pallas kernels for 0%

profile of v11, /device:TPU:0, one launch (start us, length us, event | category | flops | bytes accessed | tf_op | source)
XLA Modules:
  0.0 43.5 jit_solution(17616129231027924666)
XLA Ops:
  0.0 1.0 %fusion.9 = (bf16[64,1024]{1,0:T(8,128)(2,1)S(1)}, bf16[64,1024]{1,0:T(8,128)(2,1)S(1)}) fusion(bf16[128,1024]{1,0:T(8,128)(2,1)} %param.3), kind=kLoop, calls=%fused_computation.29 | loop fusion | bytes 524288 | tf_op jit(solution)/shard_map/slice | solution.py:50
  1.0 1.3 %collective-permute-start.4 = (bf16[64,1024]{1,0:T(8,128)(2,1)S(1)}, bf16[64,1024]{1,0:T(8,128)(2,1)S(1)}, u32[]{:S(2)}, u32[]{:S(2)}) collective-permute-start(bf16[64,1024]{1,0:T(8,128)(2,1)S(1)} %get-tuple-element.13), channel_id=1, source_target_pairs={{2,10},{3,11},{6,14},{7,15},{8,0},{9,1},{12,4},{13,5},{18,26},{19,... | collective-permute-start | bytes 393224 | tf_op jit(solution)/shard_map/ppermute | solution.py:27
  2.3 4.9 %collective-permute-start.1 = (bf16[128,1024]{1,0:T(8,128)(2,1)}, bf16[128,1024]{1,0:T(8,128)(2,1)S(1)}, u32[]{:S(2)}, u32[]{:S(2)}) collective-permute-start(bf16[128,1024]{1,0:T(8,128)(2,1)} %param.3), channel_id=1, source_target_pairs={{0,8},{1,9},{4,12},{5,13},{10,2},{11,3},{14,6},{15,7},{16,24},{17,... | collective-permute-start | bytes 786440 | tf_op jit(solution)/shard_map/ppermute | solution.py:27
  7.2 1.3 %collective-permute-start.3 = (bf16[64,1024]{1,0:T(8,128)(2,1)S(1)}, bf16[64,1024]{1,0:T(8,128)(2,1)S(1)}, u32[]{:S(2)}, u32[]{:S(2)}) collective-permute-start(bf16[64,1024]{1,0:T(8,128)(2,1)S(1)} %get-tuple-element.14), channel_id=1, source_target_pairs={{2,0},{3,1},{6,4},{7,5},{8,10},{9,11},{12,14},{13,15},{18,16},{19,... | collective-permute-start | bytes 393224 | tf_op jit(solution)/shard_map/ppermute | solution.py:27
  8.5 2.8 %collective-permute-start = (bf16[256,1024]{1,0:T(8,128)(2,1)S(1)}, bf16[256,1024]{1,0:T(8,128)(2,1)S(1)}, u32[]{:S(2)}, u32[]{:S(2)}) collective-permute-start(bf16[256,1024]{1,0:T(8,128)(2,1)S(1)} %copy-done), channel_id=1, source_target_pairs={{0,1},{1,0},{2,3},{3,2},{4,5},{5,4},{6,7},{7,6},{8,9},{9,8},{10,11... | collective-permute-start | bytes 1572872 | tf_op jit(solution)/shard_map/ppermute | solution.py:27
  11.3 5.4 %collective-permute-start.5 = (bf16[64,1024]{1,0:T(8,128)(2,1)S(1)}, bf16[64,1024]{1,0:T(8,128)(2,1)S(1)}, u32[]{:S(2)}, u32[]{:S(2)}) collective-permute-start(bf16[64,1024]{1,0:T(8,128)(2,1)S(1)} %collective-permute-done.4), channel_id=1, source_target_pairs={{0,2},{1,3},{4,6},{5,7},{10,8},{11,9},{14,12},{15,13},{16,18},{17,... | collective-permute-start | bytes 393224 | tf_op jit(solution)/shard_map/ppermute | solution.py:27
  16.8 0.2 multiply_reduce_fusion.1
  17.0 0.1 pad.3.clone
  17.1 7.6 %collective-permute-done.5 = bf16[64,1024]{1,0:T(8,128)(2,1)S(1)} collective-permute-done((bf16[64,1024]{1,0:T(8,128)(2,1)S(1)}, bf16[64,1024]{1,0:T(8,128)(2,1)S(1)}, u32[]{:S(2)}, u32[]{:S(2)}) %collective-permute-start.5) | collective-permute-done | bytes 131104 | tf_op jit(solution)/shard_map/ppermute | solution.py:27
  25.0 0.1 multiply_reduce_fusion.3
  25.1 4.7 %collective-permute-done.6 = bf16[64,1024]{1,0:T(8,128)(2,1)S(1)} collective-permute-done((bf16[64,1024]{1,0:T(8,128)(2,1)S(1)}, bf16[64,1024]{1,0:T(8,128)(2,1)S(1)}, u32[]{:S(2)}, u32[]{:S(2)}) %collective-permute-start.6) | collective-permute-done | bytes 131104 | tf_op jit(solution)/shard_map/ppermute | solution.py:27
  29.9 0.1 multiply_reduce_fusion.5
  30.1 0.1 broadcast_select_fusion
  30.2 0.2 multiply_reduce_fusion
  30.4 1.1 %collective-permute-done.7 = bf16[128,1024]{1,0:T(8,128)(2,1)S(1)} collective-permute-done((bf16[128,1024]{1,0:T(8,128)(2,1)S(1)}, bf16[128,1024]{1,0:T(8,128)(2,1)S(1)}, u32[]{:S(2)}, u32[]{:S(2)}) %collective-permute-start.7) | collective-permute-done | bytes 262176 | tf_op jit(solution)/shard_map/ppermute | solution.py:27
  31.5 0.3 fusion.11
  31.8 0.3 convolution_add_fusion
  32.1 0.1 multiply_reduce_fusion.4
  32.2 0.1 maximum_maximum_fusion
  32.3 3.4 %collective-permute-start.8 = (f32[264,128]{1,0:T(8,128)S(1)}, f32[264,128]{1,0:T(8,128)S(1)}, u32[]{:S(2)}, u32[]{:S(2)}) collective-permute-start(f32[264,128]{1,0:T(8,128)S(1)} %maximum_maximum_fusion), channel_id=1, source_target_pairs={{0,2},{1,3},{2,0},{3,1},{4,6},{5,7},{6,4},{7,5},{8,10},{9,11},{10,... | collective-permute-start | bytes 405512 | tf_op jit(solution)/shard_map/ppermute | solution.py:27
  35.8 0.3 fusion.10
  36.1 0.1 multiply_reduce_fusion.2
  36.2 6.3 %collective-permute-done.8 = f32[264,128]{1,0:T(8,128)S(1)} collective-permute-done((f32[264,128]{1,0:T(8,128)S(1)}, f32[264,128]{1,0:T(8,128)S(1)}, u32[]{:S(2)}, u32[]{:S(2)}) %collective-permute-start.8) | collective-permute-done | bytes 135200 | tf_op jit(solution)/shard_map/ppermute | solution.py:27
  42.6 1.0 %fusion.2 = f32[256,128]{1,0:T(8,128)} fusion(f32[256,128]{1,0:T(8,128)S(1)} %fusion.10, bf16[256,1024]{1,0:T(8,128)(2,1)S(1)} %get-tuple-element.7, bf16[128,1024]{1,0:T(8,128)(2,1)S(1)} %broadcast_select_fusion.2, f32[264,128]{1,0:T(8,128)S(1)} %collective-permute-done.8, f32[128]{0:T(128)S(1)} %rsqrt_bitcast_fusion, f32[256]{0:T(256)S(1)} %fusion.7), kind=kOutput, calls=%fused_computation.4 | convolution fusion | flops 67239936 | bytes 1181184 | tf_op jit(solution)/shard_map/dot_general | solution.py:10
  (21 shorter events, 0.4 us)
Async XLA Ops:
  0.0 8.5 %copy-start = (bf16[256,1024]{1,0:T(8,128)(2,1)S(1)}, bf16[256,1024]{1,0:T(8,128)(2,1)}, u32[]{:S(2)}) copy-start(bf16[256,1024]{1,0:T(8,128)(2,1)} %param.2) | copy-start | bytes 1572868
  1.0 10.3 %collective-permute-start.4 = (bf16[64,1024]{1,0:T(8,128)(2,1)S(1)}, bf16[64,1024]{1,0:T(8,128)(2,1)S(1)}, u32[]{:S(2)}, u32[]{:S(2)}) collective-permute-start(bf16[64,1024]{1,0:T(8,128)(2,1)S(1)} %get-tuple-element.13), channel_id=1, source_target_pairs={{2,10},{3,11},{6,14},{7,15},{8,0},{9,1},{12,4},{13,5},{18,26},{19,... | collective-permute-start | bytes 393224 | tf_op jit(solution)/shard_map/ppermute | solution.py:27
  2.3 22.5 %collective-permute-start.1 = (bf16[128,1024]{1,0:T(8,128)(2,1)}, bf16[128,1024]{1,0:T(8,128)(2,1)S(1)}, u32[]{:S(2)}, u32[]{:S(2)}) collective-permute-start(bf16[128,1024]{1,0:T(8,128)(2,1)} %param.3), channel_id=1, source_target_pairs={{0,8},{1,9},{4,12},{5,13},{10,2},{11,3},{14,6},{15,7},{16,24},{17,... | collective-permute-start | bytes 786440 | tf_op jit(solution)/shard_map/ppermute | solution.py:27
  7.2 9.9 %collective-permute-start.3 = (bf16[64,1024]{1,0:T(8,128)(2,1)S(1)}, bf16[64,1024]{1,0:T(8,128)(2,1)S(1)}, u32[]{:S(2)}, u32[]{:S(2)}) collective-permute-start(bf16[64,1024]{1,0:T(8,128)(2,1)S(1)} %get-tuple-element.14), channel_id=1, source_target_pairs={{2,0},{3,1},{6,4},{7,5},{8,10},{9,11},{12,14},{13,15},{18,16},{19,... | collective-permute-start | bytes 393224 | tf_op jit(solution)/shard_map/ppermute | solution.py:27
  8.5 21.5 %collective-permute-start = (bf16[256,1024]{1,0:T(8,128)(2,1)S(1)}, bf16[256,1024]{1,0:T(8,128)(2,1)S(1)}, u32[]{:S(2)}, u32[]{:S(2)}) collective-permute-start(bf16[256,1024]{1,0:T(8,128)(2,1)S(1)} %copy-done), channel_id=1, source_target_pairs={{0,1},{1,0},{2,3},{3,2},{4,5},{5,4},{6,7},{7,6},{8,9},{9,8},{10,11... | collective-permute-start | bytes 1572872 | tf_op jit(solution)/shard_map/ppermute | solution.py:27
  11.3 13.4 %collective-permute-start.5 = (bf16[64,1024]{1,0:T(8,128)(2,1)S(1)}, bf16[64,1024]{1,0:T(8,128)(2,1)S(1)}, u32[]{:S(2)}, u32[]{:S(2)}) collective-permute-start(bf16[64,1024]{1,0:T(8,128)(2,1)S(1)} %collective-permute-done.4), channel_id=1, source_target_pairs={{0,2},{1,3},{4,6},{5,7},{10,8},{11,9},{14,12},{15,13},{16,18},{17,... | collective-permute-start | bytes 393224 | tf_op jit(solution)/shard_map/ppermute | solution.py:27
  17.0 7.9 %copy-start.1 = (bf16[128,1024]{1,0:T(8,128)(2,1)S(1)}, bf16[128,1024]{1,0:T(8,128)(2,1)}, u32[]{:S(2)}) copy-start(bf16[128,1024]{1,0:T(8,128)(2,1)} %param.3) | copy-start | bytes 786436
  24.8 5.0 %collective-permute-start.6 = (bf16[64,1024]{1,0:T(8,128)(2,1)S(1)}, bf16[64,1024]{1,0:T(8,128)(2,1)S(1)}, u32[]{:S(2)}, u32[]{:S(2)}) collective-permute-start(bf16[64,1024]{1,0:T(8,128)(2,1)S(1)} %broadcast_select_fusion.5), channel_id=1, source_target_pairs={{0,8},{1,9},{2,10},{3,11},{4,12},{5,13},{6,14},{7,15},{8,0},{9,1},... | collective-permute-start | bytes 393224 | tf_op jit(solution)/shard_map/ppermute | solution.py:27
  24.9 10.9 %collective-permute-start.2 = (bf16[128,1024]{1,0:T(8,128)(2,1)S(1)}, bf16[128,1024]{1,0:T(8,128)(2,1)S(1)}, u32[]{:S(2)}, u32[]{:S(2)}) collective-permute-start(bf16[128,1024]{1,0:T(8,128)(2,1)S(1)} %broadcast_select_fusion.2), channel_id=1, source_target_pairs={{0,4},{1,5},{2,6},{3,7},{4,0},{5,1},{6,2},{7,3},{8,12},{9,13},{10,... | collective-permute-start | bytes 786440 | tf_op jit(solution)/shard_map/ppermute | solution.py:27
  29.9 1.6 %collective-permute-start.7 = (bf16[128,1024]{1,0:T(8,128)(2,1)S(1)}, bf16[128,1024]{1,0:T(8,128)(2,1)S(1)}, u32[]{:S(2)}, u32[]{:S(2)}) collective-permute-start(bf16[128,1024]{1,0:T(8,128)(2,1)S(1)} %pad_maximum_fusion), channel_id=1, source_target_pairs={{0,4},{1,5},{2,6},{3,7},{4,0},{5,1},{6,2},{7,3},{8,12},{9,13},{10,... | collective-permute-start | bytes 786440 | tf_op jit(solution)/shard_map/ppermute | solution.py:27
  32.3 10.2 %collective-permute-start.8 = (f32[264,128]{1,0:T(8,128)S(1)}, f32[264,128]{1,0:T(8,128)S(1)}, u32[]{:S(2)}, u32[]{:S(2)}) collective-permute-start(f32[264,128]{1,0:T(8,128)S(1)} %maximum_maximum_fusion), channel_id=1, source_target_pairs={{0,2},{1,3},{2,0},{3,1},{4,6},{5,7},{6,4},{7,5},{8,10},{9,11},{10,... | collective-permute-start | bytes 405512 | tf_op jit(solution)/shard_map/ppermute | solution.py:27

commit v12 on v10

--- a/solution.py
+++ b/solution.py
@@ -44,12 +44,14 @@
     def other_core(block):
         return moved(block, side, lambda r, c: (r ^ 1, c))
 
-    swapped = moved(right_docs, side, lambda r, c: (r ^ 2, c))
+    nears, crosses = [], []
+    for half in (right_docs[:width // 2], right_docs[width // 2:]):
+        swapped = moved(half, side, lambda r, c: (r ^ 2, c))
+        near, leaving = lax.optimization_barrier((jnp.where(at_home, half, swapped), jnp.where(at_home, swapped, half)))
+        nears.append(near)
+        crosses.append(moved(leaving, side, lambda r, c: (r, c ^ 2)))
     left_other = moved(left_docs, side, lambda r, c: (r, c ^ 1))
-    near, leaving = lax.optimization_barrier(
-        (jnp.where(at_home, right_docs, swapped), jnp.where(at_home, swapped, right_docs))
-    )
-    cross = moved(leaving, side, lambda r, c: (r, c ^ 2))
+    near, cross = lax.optimization_barrier(jnp.concatenate(nears)), lax.optimization_barrier(jnp.concatenate(crosses))
     lefts = lax.optimization_barrier((jnp.where(same, left_docs, left_other), jnp.where(same, left_other, left_docs)))
 
     def half_sum(mine):

time: 37.8 us -> 36.3 us (0.960)
  waiting for transfers between devices: 25.8 us -> 16.3 us
  starting transfers between devices: 7.57 us -> 15.6 us
  other arithmetic: 2.25 us -> 1.2 us
  local copies, waits for them, and re-layouts: 0.09 us -> 1.07 us
    ppermute x6 -> x8, waiting for transfers between devices: 25.8 us -> 16.3 us  [moved(): return lax.ppermute(value, ('row', 'col'), pairs)]
    ppermute x6 -> x8, starting transfers between devices: 7.57 us -> 15.6 us  [moved(): return lax.ppermute(value, ('row', 'col'), pairs)]
    reduce_sum x6, other arithmetic: 1.98 us -> 0.9 us  [squares(): return jnp.sum(widened * widened, axis=1)]
    slice x0 -> x1, local copies, waits for them, and re-layouts: none -> 0.99 us  [on_square_grid(): right_docs[:width // 2]]
  transfers between devices with their start and end apart: 6 -> 8, of which waited for: 5 -> 7; matrix products, arithmetic and copies ran while one was open for 9% -> 6% of each run, Pallas kernels for 0% -> 0%
where the time goes in v12:
time: 36.3 us; the launch traced here: 36.1 us
  waiting for transfers between devices  16.3 us (45%)
  starting transfers between devices  15.6 us (43%)
  matrix products  1.87 us (5%)
  other arithmetic  1.2 us (3%)
  local copies, waits for them, and re-layouts  1.07 us (3%)
    ppermute x8, waiting for transfers between devices, moved(): return lax.ppermute(value, ('row', 'col'), pairs)  16.3 us
    ppermute x8, starting transfers between devices, moved(): return lax.ppermute(value, ('row', 'col'), pairs)  15.6 us
    dot_general x4, matrix products, contract(): lax.dot_general(left_part, right_part, (((1,), (1,)), ((), ())), preferre...  1.87 us
    slice x1, local copies, waits for them, and re-layouts, on_square_grid(): right_docs[:width // 2]  0.99 us
    reduce_sum x6, other arithmetic, squares(): return jnp.sum(widened * widened, axis=1)  0.9 us
  transfers between devices with their start and end apart: 8, of which 7 were waited for; matrix products, arithmetic and copies ran while one was open for 6% of the time, Pallas kernels for 0%

profile of v12, /device:TPU:0, one launch (start us, length us, event | category | flops | bytes accessed | tf_op | source)
XLA Modules:
  0.0 36.1 jit_solution(7640996222855215760)
XLA Ops:
  0.0 1.0 %slice.15 = bf16[64,1024]{1,0:T(8,128)(2,1)S(1)} slice(bf16[128,1024]{1,0:T(8,128)(2,1)} %param.3), slice={[0:64], [0:1024]} | slice | bytes 262144 | tf_op jit(solution)/shard_map/slice | solution.py:48
  1.0 3.0 %collective-permute-start.1 = (bf16[64,1024]{1,0:T(8,128)(2,1)S(1)}, bf16[64,1024]{1,0:T(8,128)(2,1)S(1)}, u32[]{:S(2)}, u32[]{:S(2)}) collective-permute-start(bf16[64,1024]{1,0:T(8,128)(2,1)S(1)} %slice.15), channel_id=1, source_target_pairs={{0,8},{1,9},{2,10},{3,11},{4,12},{5,13},{6,14},{7,15},{8,0},{9,1},... | collective-permute-start | bytes 393224 | tf_op jit(solution)/shard_map/ppermute | solution.py:27
  4.0 1.6 %collective-permute-start = (bf16[256,1024]{1,0:T(8,128)(2,1)}, bf16[256,1024]{1,0:T(8,128)(2,1)S(1)}, u32[]{:S(2)}, u32[]{:S(2)}) collective-permute-start(bf16[256,1024]{1,0:T(8,128)(2,1)} %param.2), channel_id=1, source_target_pairs={{0,1},{1,0},{2,3},{3,2},{4,5},{5,4},{6,7},{7,6},{8,9},{9,8},{10,11... | collective-permute-start | bytes 1572872 | tf_op jit(solution)/shard_map/ppermute | solution.py:27
  5.7 1.8 %collective-permute-done.1 = bf16[64,1024]{1,0:T(8,128)(2,1)S(1)} collective-permute-done((bf16[64,1024]{1,0:T(8,128)(2,1)S(1)}, bf16[64,1024]{1,0:T(8,128)(2,1)S(1)}, u32[]{:S(2)}, u32[]{:S(2)}) %collective-permute-start.1) | collective-permute-done | bytes 131104 | tf_op jit(solution)/shard_map/ppermute | solution.py:27
  7.5 1.8 %collective-permute-start.2 = (bf16[64,1024]{1,0:T(8,128)(2,1)S(1)}, bf16[64,1024]{1,0:T(8,128)(2,1)S(1)}, u32[]{:S(2)}, u32[]{:S(2)}) collective-permute-start(bf16[64,1024]{1,0:T(8,128)(2,1)S(1)} %get-tuple-element.23), channel_id=1, source_target_pairs={{0,8},{1,9},{2,10},{3,11},{4,12},{5,13},{6,14},{7,15},{8,0},{9,1},... | collective-permute-start | bytes 393224 | tf_op jit(solution)/shard_map/ppermute | solution.py:27
  9.3 0.2 multiply_reduce_fusion.1
  9.5 2.7 %collective-permute-start.4 = (bf16[64,1024]{1,0:T(8,128)(2,1)S(1)}, bf16[64,1024]{1,0:T(8,128)(2,1)S(1)}, u32[]{:S(2)}, u32[]{:S(2)}) collective-permute-start(bf16[64,1024]{1,0:T(8,128)(2,1)S(1)} %get-tuple-element.15), channel_id=1, source_target_pairs={{0,2},{1,3},{2,0},{3,1},{4,6},{5,7},{6,4},{7,5},{8,10},{9,11},{10,... | collective-permute-start | bytes 393224 | tf_op jit(solution)/shard_map/ppermute | solution.py:27
  12.2 0.4 %collective-permute-done.2 = bf16[64,1024]{1,0:T(8,128)(2,1)S(1)} collective-permute-done((bf16[64,1024]{1,0:T(8,128)(2,1)S(1)}, bf16[64,1024]{1,0:T(8,128)(2,1)S(1)}, u32[]{:S(2)}, u32[]{:S(2)}) %collective-permute-start.2) | collective-permute-done | bytes 131104 | tf_op jit(solution)/shard_map/ppermute | solution.py:27
  12.6 2.9 %collective-permute-start.5 = (bf16[64,1024]{1,0:T(8,128)(2,1)S(1)}, bf16[64,1024]{1,0:T(8,128)(2,1)S(1)}, u32[]{:S(2)}, u32[]{:S(2)}) collective-permute-start(bf16[64,1024]{1,0:T(8,128)(2,1)S(1)} %get-tuple-element.16), channel_id=1, source_target_pairs={{0,2},{1,3},{2,0},{3,1},{4,6},{5,7},{6,4},{7,5},{8,10},{9,11},{10,... | collective-permute-start | bytes 393224 | tf_op jit(solution)/shard_map/ppermute | solution.py:27
  15.6 0.1 multiply_reduce_fusion.3
  15.7 5.2 %collective-permute-done.4 = bf16[64,1024]{1,0:T(8,128)(2,1)S(1)} collective-permute-done((bf16[64,1024]{1,0:T(8,128)(2,1)S(1)}, bf16[64,1024]{1,0:T(8,128)(2,1)S(1)}, u32[]{:S(2)}, u32[]{:S(2)}) %collective-permute-start.4) | collective-permute-done | bytes 131104 | tf_op jit(solution)/shard_map/ppermute | solution.py:27
  21.0 1.4 %collective-permute-done.5 = bf16[64,1024]{1,0:T(8,128)(2,1)S(1)} collective-permute-done((bf16[64,1024]{1,0:T(8,128)(2,1)S(1)}, bf16[64,1024]{1,0:T(8,128)(2,1)S(1)}, u32[]{:S(2)}, u32[]{:S(2)}) %collective-permute-start.5) | collective-permute-done | bytes 131104 | tf_op jit(solution)/shard_map/ppermute | solution.py:27
  22.4 0.1 multiply_reduce_fusion.5
  22.6 0.6 %collective-permute-done = bf16[256,1024]{1,0:T(8,128)(2,1)S(1)} collective-permute-done((bf16[256,1024]{1,0:T(8,128)(2,1)}, bf16[256,1024]{1,0:T(8,128)(2,1)S(1)}, u32[]{:S(2)}, u32[]{:S(2)}) %collective-permute-start) | collective-permute-done | bytes 524320 | tf_op jit(solution)/shard_map/ppermute | solution.py:27
  23.3 0.2 multiply_reduce_fusion
  23.5 0.5 %collective-permute-done.6 = bf16[128,1024]{1,0:T(8,128)(2,1)S(1)} collective-permute-done((bf16[128,1024]{1,0:T(8,128)(2,1)S(1)}, bf16[128,1024]{1,0:T(8,128)(2,1)S(1)}, u32[]{:S(2)}, u32[]{:S(2)}) %collective-permute-start.6) | collective-permute-done | bytes 262176 | tf_op jit(solution)/shard_map/ppermute | solution.py:27
  24.0 0.3 fusion.10
  24.3 0.3 convolution_add_fusion
  24.6 0.1 multiply_reduce_fusion.4
  24.8 3.5 %collective-permute-start.7 = (f32[264,128]{1,0:T(8,128)S(1)}, f32[264,128]{1,0:T(8,128)S(1)}, u32[]{:S(2)}, u32[]{:S(2)}) collective-permute-start(f32[264,128]{1,0:T(8,128)S(1)} %maximum_maximum_fusion), channel_id=1, source_target_pairs={{0,2},{1,3},{2,0},{3,1},{4,6},{5,7},{6,4},{7,5},{8,10},{9,11},{10,... | collective-permute-start | bytes 405512 | tf_op jit(solution)/shard_map/ppermute | solution.py:27
  28.3 0.3 fusion.9
  28.6 0.1 multiply_reduce_fusion.2
  28.8 6.3 %collective-permute-done.7 = f32[264,128]{1,0:T(8,128)S(1)} collective-permute-done((f32[264,128]{1,0:T(8,128)S(1)}, f32[264,128]{1,0:T(8,128)S(1)}, u32[]{:S(2)}, u32[]{:S(2)}) %collective-permute-start.7) | collective-permute-done | bytes 135200 | tf_op jit(solution)/shard_map/ppermute | solution.py:27
  35.1 1.0 %fusion.2 = f32[256,128]{1,0:T(8,128)} fusion(f32[256,128]{1,0:T(8,128)S(1)} %fusion.9, bf16[256,1024]{1,0:T(8,128)(2,1)S(1)} %get-tuple-element.11, bf16[128,1024]{1,0:T(8,128)(2,1)S(1)} %pad_maximum_fusion, f32[264,128]{1,0:T(8,128)S(1)} %collective-permute-done.7, f32[128]{0:T(128)S(1)} %rsqrt_bitcast_fusion, f32[256]{0:T(256)S(1)} %fusion.7), kind=kOutput, calls=%fused_computation.4 | convolution fusion | flops 67239936 | bytes 1181184 | tf_op jit(solution)/shard_map/dot_general | solution.py:10
  (19 shorter events, 0.5 us)
Async XLA Ops:
  0.0 7.5 %copy-start.1 = (bf16[128,1024]{1,0:T(8,128)(2,1)S(1)}, bf16[128,1024]{1,0:T(8,128)(2,1)}, u32[]{:S(2)}) copy-start(bf16[128,1024]{1,0:T(8,128)(2,1)} %param.3) | copy-start | bytes 786436
  0.0 9.3 %copy-start = (bf16[256,1024]{1,0:T(8,128)(2,1)S(1)}, bf16[256,1024]{1,0:T(8,128)(2,1)}, u32[]{:S(2)}) copy-start(bf16[256,1024]{1,0:T(8,128)(2,1)} %param.2) | copy-start | bytes 1572868
  1.0 6.5 %collective-permute-start.1 = (bf16[64,1024]{1,0:T(8,128)(2,1)S(1)}, bf16[64,1024]{1,0:T(8,128)(2,1)S(1)}, u32[]{:S(2)}, u32[]{:S(2)}) collective-permute-start(bf16[64,1024]{1,0:T(8,128)(2,1)S(1)} %slice.15), channel_id=1, source_target_pairs={{0,8},{1,9},{2,10},{3,11},{4,12},{5,13},{6,14},{7,15},{8,0},{9,1},... | collective-permute-start | bytes 393224 | tf_op jit(solution)/shard_map/ppermute | solution.py:27
  4.0 19.2 %collective-permute-start = (bf16[256,1024]{1,0:T(8,128)(2,1)}, bf16[256,1024]{1,0:T(8,128)(2,1)S(1)}, u32[]{:S(2)}, u32[]{:S(2)}) collective-permute-start(bf16[256,1024]{1,0:T(8,128)(2,1)} %param.2), channel_id=1, source_target_pairs={{0,1},{1,0},{2,3},{3,2},{4,5},{5,4},{6,7},{7,6},{8,9},{9,8},{10,11... | collective-permute-start | bytes 1572872 | tf_op jit(solution)/shard_map/ppermute | solution.py:27
  7.5 5.0 %collective-permute-start.2 = (bf16[64,1024]{1,0:T(8,128)(2,1)S(1)}, bf16[64,1024]{1,0:T(8,128)(2,1)S(1)}, u32[]{:S(2)}, u32[]{:S(2)}) collective-permute-start(bf16[64,1024]{1,0:T(8,128)(2,1)S(1)} %get-tuple-element.23), channel_id=1, source_target_pairs={{0,8},{1,9},{2,10},{3,11},{4,12},{5,13},{6,14},{7,15},{8,0},{9,1},... | collective-permute-start | bytes 393224 | tf_op jit(solution)/shard_map/ppermute | solution.py:27
  9.5 11.4 %collective-permute-start.4 = (bf16[64,1024]{1,0:T(8,128)(2,1)S(1)}, bf16[64,1024]{1,0:T(8,128)(2,1)S(1)}, u32[]{:S(2)}, u32[]{:S(2)}) collective-permute-start(bf16[64,1024]{1,0:T(8,128)(2,1)S(1)} %get-tuple-element.15), channel_id=1, source_target_pairs={{0,2},{1,3},{2,0},{3,1},{4,6},{5,7},{6,4},{7,5},{8,10},{9,11},{10,... | collective-permute-start | bytes 393224 | tf_op jit(solution)/shard_map/ppermute | solution.py:27
  12.6 9.8 %collective-permute-start.5 = (bf16[64,1024]{1,0:T(8,128)(2,1)S(1)}, bf16[64,1024]{1,0:T(8,128)(2,1)S(1)}, u32[]{:S(2)}, u32[]{:S(2)}) collective-permute-start(bf16[64,1024]{1,0:T(8,128)(2,1)S(1)} %get-tuple-element.16), channel_id=1, source_target_pairs={{0,2},{1,3},{2,0},{3,1},{4,6},{5,7},{6,4},{7,5},{8,10},{9,11},{10,... | collective-permute-start | bytes 393224 | tf_op jit(solution)/shard_map/ppermute | solution.py:27
  15.5 12.8 %collective-permute-start.3 = (bf16[128,1024]{1,0:T(8,128)(2,1)S(1)}, bf16[128,1024]{1,0:T(8,128)(2,1)S(1)}, u32[]{:S(2)}, u32[]{:S(2)}) collective-permute-start(bf16[128,1024]{1,0:T(8,128)(2,1)S(1)} %pad_maximum_fusion), channel_id=1, source_target_pairs={{0,4},{1,5},{2,6},{3,7},{4,0},{5,1},{6,2},{7,3},{8,12},{9,13},{10,... | collective-permute-start | bytes 786440 | tf_op jit(solution)/shard_map/ppermute | solution.py:27
  22.4 1.6 %collective-permute-start.6 = (bf16[128,1024]{1,0:T(8,128)(2,1)S(1)}, bf16[128,1024]{1,0:T(8,128)(2,1)S(1)}, u32[]{:S(2)}, u32[]{:S(2)}) collective-permute-start(bf16[128,1024]{1,0:T(8,128)(2,1)S(1)} %pad_maximum_fusion.1), channel_id=1, source_target_pairs={{0,4},{1,5},{2,6},{3,7},{4,0},{5,1},{6,2},{7,3},{8,12},{9,13},{10,... | collective-permute-start | bytes 786440 | tf_op jit(solution)/shard_map/ppermute | solution.py:27
  24.8 10.3 %collective-permute-start.7 = (f32[264,128]{1,0:T(8,128)S(1)}, f32[264,128]{1,0:T(8,128)S(1)}, u32[]{:S(2)}, u32[]{:S(2)}) collective-permute-start(f32[264,128]{1,0:T(8,128)S(1)} %maximum_maximum_fusion), channel_id=1, source_target_pairs={{0,2},{1,3},{2,0},{3,1},{4,6},{5,7},{6,4},{7,5},{8,10},{9,11},{10,... | collective-permute-start | bytes 405512 | tf_op jit(solution)/shard_map/ppermute | solution.py:27

commit v13 on v12

--- a/solution.py
+++ b/solution.py
@@ -4,6 +4,7 @@
 from jax.sharding import PartitionSpec as P
 
 epsilon = 1e-06
+top = 2.0**15
 
 
 def contract(left_part, right_part):
@@ -31,6 +32,20 @@
     left_scale = lax.rsqrt(left_sq / feat_total + epsilon)
     right_scale = lax.rsqrt(right_sq / feat_total + epsilon)
     return summed / feat_total * left_scale[:, None] * right_scale[None, :]
+
+
+def packed(sums):
+    root = 16.0 * jnp.sqrt(jnp.sqrt(jnp.sqrt(jnp.maximum(sums, 1e-36))))
+    high = lax.reduce_precision(root, 5, 10)
+    low = lax.reduce_precision((root - high) * 1024.0, 5, 10)
+    return high.astype(jnp.float16), low.astype(jnp.float16), unpacked(high, low)
+
+
+def unpacked(high, low):
+    root = (high + low / 1024.0) / 16.0
+    for _ in range(3):
+        root = root * root
+    return root
 
 
 def on_square_grid(left_docs, right_docs):
@@ -63,11 +78,19 @@
     cross_gram, cross_sq = half_sum(cross)
     left_sq = squares(left_docs) + squares(left_other)
 
+    left_high, left_low, left_read = packed(left_sq)
+    right_high, right_low, right_read = packed(cross_sq)
+    tile = cross_gram * (top * lax.rsqrt(left_read))[:, None] * lax.rsqrt(right_read)[None, :]
     parts = rows // width
-    sums = [cross_sq[None], left_sq.reshape(parts, width), jnp.zeros((-(parts + 1) % 8, width), jnp.float32)]
-    got = moved(jnp.concatenate([cross_gram, *sums]), side, lambda r, c: (r, c ^ 2))
-    left_sq = left_sq + got[rows + 1:rows + 1 + parts].reshape(rows)
-    return finish(near_gram + got[:rows], left_sq, near_sq + got[rows], feat_total)
+    sums = [left_high.reshape(parts, width), left_low.reshape(parts, width), right_high[None], right_low[None]]
+    spare = jnp.zeros((-(2 * parts + 2) % 8, width), jnp.float16)
+    got = moved(jnp.concatenate([tile.astype(jnp.float16), *sums, spare]), side, lambda r, c: (r, c ^ 2))
+
+    got = got.astype(jnp.float32)
+    sums = jnp.split(got[rows:rows + 2 * parts + 2], (parts, 2 * parts, 2 * parts + 1))
+    left_got, right_got = unpacked(*sums[:2]).reshape(rows), unpacked(*sums[2:]).reshape(width)
+    far_gram = got[:rows] * (jnp.sqrt(left_got) / top)[:, None] * jnp.sqrt(right_got)[None, :]
+    return finish(near_gram + far_gram, left_sq + left_got, near_sq + right_got, feat_total)
 
 
 def on_any_grid(left_docs, right_docs):

time: 36.3 us -> 32.2 us (0.89)
  waiting for transfers between devices: 16.3 us -> 11.9 us
    ppermute x8, waiting for transfers between devices: 16.3 us -> 11.9 us  [moved(): return lax.ppermute(value, ('row', 'col'), pairs)]
  transfers between devices with their start and end apart: 8 -> 8, of which waited for: 7 -> 6; matrix products, arithmetic and copies ran while one was open for 6% -> 4% of each run, Pallas kernels for 0% -> 0%
where the time goes in v13:
time: 32.2 us; the launch traced here: 31.9 us
  starting transfers between devices  15.6 us (48%)
  waiting for transfers between devices  11.9 us (37%)
  matrix products  1.88 us (6%)
  other arithmetic  1.34 us (4%)
  local copies, waits for them, and re-layouts  1.07 us (3%)
    ppermute x8, starting transfers between devices, moved(): return lax.ppermute(value, ('row', 'col'), pairs)  15.6 us
    ppermute x8, waiting for transfers between devices, moved(): return lax.ppermute(value, ('row', 'col'), pairs)  11.9 us
    dot_general x4, matrix products, contract(): lax.dot_general(left_part, right_part, (((1,), (1,)), ((), ())), preferre...  1.88 us
    slice x1, local copies, waits for them, and re-layouts, on_square_grid(): right_docs[:width // 2]  0.99 us
    reduce_sum x6, other arithmetic, squares(): return jnp.sum(widened * widened, axis=1)  0.9 us
  transfers between devices with their start and end apart: 8, of which 6 were waited for; matrix products, arithmetic and copies ran while one was open for 4% of the time, Pallas kernels for 0%

profile of v13, /device:TPU:0, one launch (start us, length us, event | category | flops | bytes accessed | tf_op | source)
XLA Modules:
  0.0 31.9 jit_solution(14154731128282075878)
XLA Ops:
  0.0 1.0 %slice.14 = bf16[64,1024]{1,0:T(8,128)(2,1)S(1)} slice(bf16[128,1024]{1,0:T(8,128)(2,1)} %param.3), slice={[0:64], [0:1024]} | slice | bytes 262144 | tf_op jit(solution)/shard_map/slice | solution.py:63
  1.0 3.0 %collective-permute-start.1 = (bf16[64,1024]{1,0:T(8,128)(2,1)S(1)}, bf16[64,1024]{1,0:T(8,128)(2,1)S(1)}, u32[]{:S(2)}, u32[]{:S(2)}) collective-permute-start(bf16[64,1024]{1,0:T(8,128)(2,1)S(1)} %slice.14), channel_id=1, source_target_pairs={{0,8},{1,9},{2,10},{3,11},{4,12},{5,13},{6,14},{7,15},{8,0},{9,1},... | collective-permute-start | bytes 393224 | tf_op jit(solution)/shard_map/ppermute | solution.py:28
  4.0 1.6 %collective-permute-start = (bf16[256,1024]{1,0:T(8,128)(2,1)}, bf16[256,1024]{1,0:T(8,128)(2,1)S(1)}, u32[]{:S(2)}, u32[]{:S(2)}) collective-permute-start(bf16[256,1024]{1,0:T(8,128)(2,1)} %param.2), channel_id=1, source_target_pairs={{0,1},{1,0},{2,3},{3,2},{4,5},{5,4},{6,7},{7,6},{8,9},{9,8},{10,11... | collective-permute-start | bytes 1572872 | tf_op jit(solution)/shard_map/ppermute | solution.py:28
  5.6 1.9 %collective-permute-done.1 = bf16[64,1024]{1,0:T(8,128)(2,1)S(1)} collective-permute-done((bf16[64,1024]{1,0:T(8,128)(2,1)S(1)}, bf16[64,1024]{1,0:T(8,128)(2,1)S(1)}, u32[]{:S(2)}, u32[]{:S(2)}) %collective-permute-start.1) | collective-permute-done | bytes 131104 | tf_op jit(solution)/shard_map/ppermute | solution.py:28
  7.5 1.8 %collective-permute-start.2 = (bf16[64,1024]{1,0:T(8,128)(2,1)S(1)}, bf16[64,1024]{1,0:T(8,128)(2,1)S(1)}, u32[]{:S(2)}, u32[]{:S(2)}) collective-permute-start(bf16[64,1024]{1,0:T(8,128)(2,1)S(1)} %get-tuple-element.31), channel_id=1, source_target_pairs={{0,8},{1,9},{2,10},{3,11},{4,12},{5,13},{6,14},{7,15},{8,0},{9,1},... | collective-permute-start | bytes 393224 | tf_op jit(solution)/shard_map/ppermute | solution.py:28
  9.3 0.2 multiply_reduce_fusion.1
  9.5 2.7 %collective-permute-start.4 = (bf16[64,1024]{1,0:T(8,128)(2,1)S(1)}, bf16[64,1024]{1,0:T(8,128)(2,1)S(1)}, u32[]{:S(2)}, u32[]{:S(2)}) collective-permute-start(bf16[64,1024]{1,0:T(8,128)(2,1)S(1)} %get-tuple-element.15), channel_id=1, source_target_pairs={{0,2},{1,3},{2,0},{3,1},{4,6},{5,7},{6,4},{7,5},{8,10},{9,11},{10,... | collective-permute-start | bytes 393224 | tf_op jit(solution)/shard_map/ppermute | solution.py:28
  12.2 0.4 %collective-permute-done.2 = bf16[64,1024]{1,0:T(8,128)(2,1)S(1)} collective-permute-done((bf16[64,1024]{1,0:T(8,128)(2,1)S(1)}, bf16[64,1024]{1,0:T(8,128)(2,1)S(1)}, u32[]{:S(2)}, u32[]{:S(2)}) %collective-permute-start.2) | collective-permute-done | bytes 131104 | tf_op jit(solution)/shard_map/ppermute | solution.py:28
  12.6 2.9 %collective-permute-start.5 = (bf16[64,1024]{1,0:T(8,128)(2,1)S(1)}, bf16[64,1024]{1,0:T(8,128)(2,1)S(1)}, u32[]{:S(2)}, u32[]{:S(2)}) collective-permute-start(bf16[64,1024]{1,0:T(8,128)(2,1)S(1)} %get-tuple-element.16), channel_id=1, source_target_pairs={{0,2},{1,3},{2,0},{3,1},{4,6},{5,7},{6,4},{7,5},{8,10},{9,11},{10,... | collective-permute-start | bytes 393224 | tf_op jit(solution)/shard_map/ppermute | solution.py:28
  15.6 0.1 multiply_reduce_fusion.3
  15.7 5.2 %collective-permute-done.4 = bf16[64,1024]{1,0:T(8,128)(2,1)S(1)} collective-permute-done((bf16[64,1024]{1,0:T(8,128)(2,1)S(1)}, bf16[64,1024]{1,0:T(8,128)(2,1)S(1)}, u32[]{:S(2)}, u32[]{:S(2)}) %collective-permute-start.4) | collective-permute-done | bytes 131104 | tf_op jit(solution)/shard_map/ppermute | solution.py:28
  21.0 1.4 %collective-permute-done.5 = bf16[64,1024]{1,0:T(8,128)(2,1)S(1)} collective-permute-done((bf16[64,1024]{1,0:T(8,128)(2,1)S(1)}, bf16[64,1024]{1,0:T(8,128)(2,1)S(1)}, u32[]{:S(2)}, u32[]{:S(2)}) %collective-permute-start.5) | collective-permute-done | bytes 131104 | tf_op jit(solution)/shard_map/ppermute | solution.py:28
  22.4 0.1 multiply_reduce_fusion.5
  22.6 0.6 %collective-permute-done = bf16[256,1024]{1,0:T(8,128)(2,1)S(1)} collective-permute-done((bf16[256,1024]{1,0:T(8,128)(2,1)}, bf16[256,1024]{1,0:T(8,128)(2,1)S(1)}, u32[]{:S(2)}, u32[]{:S(2)}) %collective-permute-start) | collective-permute-done | bytes 524320 | tf_op jit(solution)/shard_map/ppermute | solution.py:28
  23.2 0.2 multiply_reduce_fusion
  23.4 0.1 broadcast_select_fusion
  23.6 0.3 fusion.44
  24.0 0.1 multiply_reduce_fusion.4
  24.2 0.3 fusion.45
  24.5 0.3 fusion.5
  24.9 3.5 %collective-permute-start.7 = (f16[264,128]{1,0:T(8,128)(2,1)S(1)}, f16[264,128]{1,0:T(8,128)(2,1)S(1)}, u32[]{:S(2)}, u32[]{:S(2)}) collective-permute-start(f16[264,128]{1,0:T(8,128)(2,1)S(1)} %concatenate.11), channel_id=1, source_target_pairs={{0,2},{1,3},{2,0},{3,1},{4,6},{5,7},{6,4},{7,5},{8,10},{9,11},{10,... | collective-permute-start | bytes 202760 | tf_op jit(solution)/shard_map/ppermute | solution.py:28
  28.4 0.1 multiply_reduce_fusion.2
  28.5 2.3 %collective-permute-done.7 = f16[264,128]{1,0:T(8,128)(2,1)S(1)} collective-permute-done((f16[264,128]{1,0:T(8,128)(2,1)S(1)}, f16[264,128]{1,0:T(8,128)(2,1)S(1)}, u32[]{:S(2)}, u32[]{:S(2)}) %collective-permute-start.7) | collective-permute-done | bytes 67616 | tf_op jit(solution)/shard_map/ppermute | solution.py:28
  30.9 1.0 %fusion.4 = f32[256,128]{1,0:T(8,128)} fusion(f32[256,128]{1,0:T(8,128)S(1)} %fusion.44, bf16[256,1024]{1,0:T(8,128)(2,1)S(1)} %get-tuple-element.11, bf16[128,1024]{1,0:T(8,128)(2,1)S(1)} %pad_maximum_fusion, f32[264,128]{1,0:T(8,128)S(1)} %convert_element_type.61, f32[128]{0:T(128)S(1)} %rsqrt_bitcast_fusion, f32[256]{0:T(256)S(1)} %fusion.27, ...), kind=kOutput, calls=%fused_computation.6 | convolution fusion | flops 67305472 | bytes 1182720 | tf_op jit(solution)/shard_map/dot_general | solution.py:11
  (25 shorter events, 0.6 us)
Async XLA Ops:
  0.0 7.5 %copy-start.1 = (bf16[128,1024]{1,0:T(8,128)(2,1)S(1)}, bf16[128,1024]{1,0:T(8,128)(2,1)}, u32[]{:S(2)}) copy-start(bf16[128,1024]{1,0:T(8,128)(2,1)} %param.3) | copy-start | bytes 786436
  0.0 9.3 %copy-start = (bf16[256,1024]{1,0:T(8,128)(2,1)S(1)}, bf16[256,1024]{1,0:T(8,128)(2,1)}, u32[]{:S(2)}) copy-start(bf16[256,1024]{1,0:T(8,128)(2,1)} %param.2) | copy-start | bytes 1572868
  1.0 6.5 %collective-permute-start.1 = (bf16[64,1024]{1,0:T(8,128)(2,1)S(1)}, bf16[64,1024]{1,0:T(8,128)(2,1)S(1)}, u32[]{:S(2)}, u32[]{:S(2)}) collective-permute-start(bf16[64,1024]{1,0:T(8,128)(2,1)S(1)} %slice.14), channel_id=1, source_target_pairs={{0,8},{1,9},{2,10},{3,11},{4,12},{5,13},{6,14},{7,15},{8,0},{9,1},... | collective-permute-start | bytes 393224 | tf_op jit(solution)/shard_map/ppermute | solution.py:28
  4.0 19.2 %collective-permute-start = (bf16[256,1024]{1,0:T(8,128)(2,1)}, bf16[256,1024]{1,0:T(8,128)(2,1)S(1)}, u32[]{:S(2)}, u32[]{:S(2)}) collective-permute-start(bf16[256,1024]{1,0:T(8,128)(2,1)} %param.2), channel_id=1, source_target_pairs={{0,1},{1,0},{2,3},{3,2},{4,5},{5,4},{6,7},{7,6},{8,9},{9,8},{10,11... | collective-permute-start | bytes 1572872 | tf_op jit(solution)/shard_map/ppermute | solution.py:28
  7.5 5.0 %collective-permute-start.2 = (bf16[64,1024]{1,0:T(8,128)(2,1)S(1)}, bf16[64,1024]{1,0:T(8,128)(2,1)S(1)}, u32[]{:S(2)}, u32[]{:S(2)}) collective-permute-start(bf16[64,1024]{1,0:T(8,128)(2,1)S(1)} %get-tuple-element.31), channel_id=1, source_target_pairs={{0,8},{1,9},{2,10},{3,11},{4,12},{5,13},{6,14},{7,15},{8,0},{9,1},... | collective-permute-start | bytes 393224 | tf_op jit(solution)/shard_map/ppermute | solution.py:28
  9.5 11.4 %collective-permute-start.4 = (bf16[64,1024]{1,0:T(8,128)(2,1)S(1)}, bf16[64,1024]{1,0:T(8,128)(2,1)S(1)}, u32[]{:S(2)}, u32[]{:S(2)}) collective-permute-start(bf16[64,1024]{1,0:T(8,128)(2,1)S(1)} %get-tuple-element.15), channel_id=1, source_target_pairs={{0,2},{1,3},{2,0},{3,1},{4,6},{5,7},{6,4},{7,5},{8,10},{9,11},{10,... | collective-permute-start | bytes 393224 | tf_op jit(solution)/shard_map/ppermute | solution.py:28
  12.6 9.8 %collective-permute-start.5 = (bf16[64,1024]{1,0:T(8,128)(2,1)S(1)}, bf16[64,1024]{1,0:T(8,128)(2,1)S(1)}, u32[]{:S(2)}, u32[]{:S(2)}) collective-permute-start(bf16[64,1024]{1,0:T(8,128)(2,1)S(1)} %get-tuple-element.16), channel_id=1, source_target_pairs={{0,2},{1,3},{2,0},{3,1},{4,6},{5,7},{6,4},{7,5},{8,10},{9,11},{10,... | collective-permute-start | bytes 393224 | tf_op jit(solution)/shard_map/ppermute | solution.py:28
  15.5 8.1 %collective-permute-start.3 = (bf16[128,1024]{1,0:T(8,128)(2,1)S(1)}, bf16[128,1024]{1,0:T(8,128)(2,1)S(1)}, u32[]{:S(2)}, u32[]{:S(2)}) collective-permute-start(bf16[128,1024]{1,0:T(8,128)(2,1)S(1)} %pad_maximum_fusion), channel_id=1, source_target_pairs={{0,4},{1,5},{2,6},{3,7},{4,0},{5,1},{6,2},{7,3},{8,12},{9,13},{10,... | collective-permute-start | bytes 786440 | tf_op jit(solution)/shard_map/ppermute | solution.py:28
  22.4 1.6 %collective-permute-start.6 = (bf16[128,1024]{1,0:T(8,128)(2,1)S(1)}, bf16[128,1024]{1,0:T(8,128)(2,1)S(1)}, u32[]{:S(2)}, u32[]{:S(2)}) collective-permute-start(bf16[128,1024]{1,0:T(8,128)(2,1)S(1)} %pad_maximum_fusion.1), channel_id=1, source_target_pairs={{0,4},{1,5},{2,6},{3,7},{4,0},{5,1},{6,2},{7,3},{8,12},{9,13},{10,... | collective-permute-start | bytes 786440 | tf_op jit(solution)/shard_map/ppermute | solution.py:28
  24.9 5.9 %collective-permute-start.7 = (f16[264,128]{1,0:T(8,128)(2,1)S(1)}, f16[264,128]{1,0:T(8,128)(2,1)S(1)}, u32[]{:S(2)}, u32[]{:S(2)}) collective-permute-start(f16[264,128]{1,0:T(8,128)(2,1)S(1)} %concatenate.11), channel_id=1, source_target_pairs={{0,2},{1,3},{2,0},{3,1},{4,6},{5,7},{6,4},{7,5},{8,10},{9,11},{10,... | collective-permute-start | bytes 202760 | tf_op jit(solution)/shard_map/ppermute | solution.py:28

commit v14 on v13

--- a/solution.py
+++ b/solution.py
@@ -59,14 +59,22 @@
     def other_core(block):
         return moved(block, side, lambda r, c: (r ^ 1, c))
 
-    nears, crosses = [], []
-    for half in (right_docs[:width // 2], right_docs[width // 2:]):
-        swapped = moved(half, side, lambda r, c: (r ^ 2, c))
-        near, leaving = lax.optimization_barrier((jnp.where(at_home, half, swapped), jnp.where(at_home, swapped, half)))
-        nears.append(near)
-        crosses.append(moved(leaving, side, lambda r, c: (r, c ^ 2)))
+    def over_x(block):
+        return moved(block, side, lambda r, c: (r ^ 2, c))
+
+    def over_middle(block):
+        return moved(block, side, lambda r, c: (r, c ^ 2))
+
+    part = width * 5 // 8
+    swapped = over_x(right_docs)
+    arrived = over_middle(right_docs[:part])
     left_other = moved(left_docs, side, lambda r, c: (r, c ^ 1))
-    near, cross = lax.optimization_barrier(jnp.concatenate(nears)), lax.optimization_barrier(jnp.concatenate(crosses))
+    near, leaving = lax.optimization_barrier(
+        (jnp.where(at_home, right_docs, swapped), jnp.where(at_home, swapped[part:], right_docs[part:]))
+    )
+    arrived, _ = lax.optimization_barrier((arrived, leaving))
+    cross = jnp.concatenate([jnp.where(at_home, arrived, over_x(arrived)), over_middle(leaving)])
+    cross = lax.optimization_barrier(cross)
     lefts = lax.optimization_barrier((jnp.where(same, left_docs, left_other), jnp.where(same, left_other, left_docs)))
 
     def half_sum(mine):

time: 32.2 us -> 34.2 us (1.062)
  waiting for transfers between devices: 11.9 us -> 18.3 us
  starting transfers between devices: 15.6 us -> 11.4 us
    ppermute x8, waiting for transfers between devices: 11.9 us -> 18.3 us  [moved(): return lax.ppermute(value, ('row', 'col'), pairs)]
    ppermute x8, starting transfers between devices: 15.6 us -> 11.4 us  [moved(): return lax.ppermute(value, ('row', 'col'), pairs)]
  transfers between devices with their start and end apart: 8 -> 8, of which waited for: 6 -> 6; matrix products, arithmetic and copies ran while one was open for 4% -> 7% of each run, Pallas kernels for 0% -> 0%
where the time goes in v14:
time: 34.2 us; the launch traced here: 34.1 us
  waiting for transfers between devices  18.3 us (54%)
  starting transfers between devices  11.4 us (33%)
  matrix products  1.88 us (5%)
  other arithmetic  1.33 us (4%)
  local copies, waits for them, and re-layouts  1.04 us (3%)
    ppermute x8, waiting for transfers between devices, moved(): return lax.ppermute(value, ('row', 'col'), pairs)  18.3 us
    ppermute x8, starting transfers between devices, moved(): return lax.ppermute(value, ('row', 'col'), pairs)  11.4 us
    dot_general x4, matrix products, contract(): lax.dot_general(left_part, right_part, (((1,), (1,)), ((), ())), preferre...  1.88 us
    slice x1, local copies, waits for them, and re-layouts, on_square_grid(): arrived = over_middle(right_docs[:part])  0.96 us
    reduce_sum x6, other arithmetic, squares(): return jnp.sum(widened * widened, axis=1)  0.9 us
  transfers between devices with their start and end apart: 8, of which 6 were waited for; matrix products, arithmetic and copies ran while one was open for 7% of the time, Pallas kernels for 0%

profile of v14, /device:TPU:0, one launch (start us, length us, event | category | flops | bytes accessed | tf_op | source)
XLA Modules:
  0.0 34.1 jit_solution(17125963556813229717)
XLA Ops:
  0.0 2.9 %collective-permute-start.1 = (bf16[128,1024]{1,0:T(8,128)(2,1)}, bf16[128,1024]{1,0:T(8,128)(2,1)S(1)}, u32[]{:S(2)}, u32[]{:S(2)}) collective-permute-start(bf16[128,1024]{1,0:T(8,128)(2,1)} %param.3), channel_id=1, source_target_pairs={{0,8},{1,9},{2,10},{3,11},{4,12},{5,13},{6,14},{7,15},{8,0},{9,1},... | collective-permute-start | bytes 786440 | tf_op jit(solution)/shard_map/ppermute | solution.py:28
  2.9 1.0 %slice.19 = bf16[80,1024]{1,0:T(8,128)(2,1)S(1)} slice(bf16[128,1024]{1,0:T(8,128)(2,1)} %param.3), slice={[0:80], [0:1024]} | slice | bytes 327680 | tf_op jit(solution)/shard_map/slice | solution.py:70
  3.9 2.7 %collective-permute-start.3 = (bf16[80,1024]{1,0:T(8,128)(2,1)S(1)}, bf16[80,1024]{1,0:T(8,128)(2,1)S(1)}, u32[]{:S(2)}, u32[]{:S(2)}) collective-permute-start(bf16[80,1024]{1,0:T(8,128)(2,1)S(1)} %slice.19), channel_id=1, source_target_pairs={{0,2},{1,3},{2,0},{3,1},{4,6},{5,7},{6,4},{7,5},{8,10},{9,11},{10,... | collective-permute-start | bytes 491528 | tf_op jit(solution)/shard_map/ppermute | solution.py:28
  6.6 1.6 %collective-permute-start = (bf16[256,1024]{1,0:T(8,128)(2,1)}, bf16[256,1024]{1,0:T(8,128)(2,1)S(1)}, u32[]{:S(2)}, u32[]{:S(2)}) collective-permute-start(bf16[256,1024]{1,0:T(8,128)(2,1)} %param.2), channel_id=1, source_target_pairs={{0,1},{1,0},{2,3},{3,2},{4,5},{5,4},{6,7},{7,6},{8,9},{9,8},{10,11... | collective-permute-start | bytes 1572872 | tf_op jit(solution)/shard_map/ppermute | solution.py:28
  8.1 1.4 %collective-permute-done.1 = bf16[128,1024]{1,0:T(8,128)(2,1)S(1)} collective-permute-done((bf16[128,1024]{1,0:T(8,128)(2,1)}, bf16[128,1024]{1,0:T(8,128)(2,1)S(1)}, u32[]{:S(2)}, u32[]{:S(2)}) %collective-permute-start.1) | collective-permute-done | bytes 262176 | tf_op jit(solution)/shard_map/ppermute | solution.py:28
  9.6 4.6 %collective-permute-done.3 = bf16[80,1024]{1,0:T(8,128)(2,1)S(1)} collective-permute-done((bf16[80,1024]{1,0:T(8,128)(2,1)S(1)}, bf16[80,1024]{1,0:T(8,128)(2,1)S(1)}, u32[]{:S(2)}, u32[]{:S(2)}) %collective-permute-start.3) | collective-permute-done | bytes 163872 | tf_op jit(solution)/shard_map/ppermute | solution.py:28
  14.1 0.5 %collective-permute-start.4 = (bf16[80,1024]{1,0:T(8,128)(2,1)S(1)}, bf16[80,1024]{1,0:T(8,128)(2,1)S(1)}, u32[]{:S(2)}, u32[]{:S(2)}) collective-permute-start(bf16[80,1024]{1,0:T(8,128)(2,1)S(1)} %collective-permute-done.3), channel_id=1, source_target_pairs={{0,8},{1,9},{2,10},{3,11},{4,12},{5,13},{6,14},{7,15},{8,0},{9,1},... | collective-permute-start | bytes 491528 | tf_op jit(solution)/shard_map/ppermute | solution.py:28
  14.6 0.2 multiply_reduce_fusion.1
  14.8 0.6 %collective-permute-start.5 = (bf16[48,1024]{1,0:T(8,128)(2,1)S(1)}, bf16[48,1024]{1,0:T(8,128)(2,1)S(1)}, u32[]{:S(2)}, u32[]{:S(2)}) collective-permute-start(bf16[48,1024]{1,0:T(8,128)(2,1)S(1)} %slice_select_fusion), channel_id=1, source_target_pairs={{0,2},{1,3},{2,0},{3,1},{4,6},{5,7},{6,4},{7,5},{8,10},{9,11},{10,... | collective-permute-start | bytes 294920 | tf_op jit(solution)/shard_map/ppermute | solution.py:28
  15.4 0.1 multiply_reduce_fusion.3
  15.6 3.9 %collective-permute-done.4 = bf16[80,1024]{1,0:T(8,128)(2,1)S(1)} collective-permute-done((bf16[80,1024]{1,0:T(8,128)(2,1)S(1)}, bf16[80,1024]{1,0:T(8,128)(2,1)S(1)}, u32[]{:S(2)}, u32[]{:S(2)}) %collective-permute-start.4) | collective-permute-done | bytes 163872 | tf_op jit(solution)/shard_map/ppermute | solution.py:28
  19.5 3.6 %collective-permute-done.5 = bf16[48,1024]{1,0:T(8,128)(2,1)S(1)} collective-permute-done((bf16[48,1024]{1,0:T(8,128)(2,1)S(1)}, bf16[48,1024]{1,0:T(8,128)(2,1)S(1)}, u32[]{:S(2)}, u32[]{:S(2)}) %collective-permute-start.5) | collective-permute-done | bytes 98336 | tf_op jit(solution)/shard_map/ppermute | solution.py:28
  23.2 0.1 multiply_reduce_fusion.5
  23.4 1.0 %collective-permute-done = bf16[256,1024]{1,0:T(8,128)(2,1)S(1)} collective-permute-done((bf16[256,1024]{1,0:T(8,128)(2,1)}, bf16[256,1024]{1,0:T(8,128)(2,1)S(1)}, u32[]{:S(2)}, u32[]{:S(2)}) %collective-permute-start) | collective-permute-done | bytes 524320 | tf_op jit(solution)/shard_map/ppermute | solution.py:28
  24.4 0.2 multiply_reduce_fusion
  24.6 0.1 broadcast_select_fusion
  24.8 0.3 fusion.44
  25.1 0.1 multiply_reduce_fusion.4
  25.4 0.3 fusion.45
  25.7 0.3 fusion.5
  26.1 3.1 %collective-permute-start.7 = (f16[264,128]{1,0:T(8,128)(2,1)S(1)}, f16[264,128]{1,0:T(8,128)(2,1)S(1)}, u32[]{:S(2)}, u32[]{:S(2)}) collective-permute-start(f16[264,128]{1,0:T(8,128)(2,1)S(1)} %concatenate.7), channel_id=1, source_target_pairs={{0,2},{1,3},{2,0},{3,1},{4,6},{5,7},{6,4},{7,5},{8,10},{9,11},{10,... | collective-permute-start | bytes 202760 | tf_op jit(solution)/shard_map/ppermute | solution.py:28
  29.1 0.1 multiply_reduce_fusion.2
  29.3 3.8 %collective-permute-done.7 = f16[264,128]{1,0:T(8,128)(2,1)S(1)} collective-permute-done((f16[264,128]{1,0:T(8,128)(2,1)S(1)}, f16[264,128]{1,0:T(8,128)(2,1)S(1)}, u32[]{:S(2)}, u32[]{:S(2)}) %collective-permute-start.7) | collective-permute-done | bytes 67616 | tf_op jit(solution)/shard_map/ppermute | solution.py:28
  33.1 1.0 %fusion.4 = f32[256,128]{1,0:T(8,128)} fusion(f32[256,128]{1,0:T(8,128)S(1)} %fusion.44, bf16[256,1024]{1,0:T(8,128)(2,1)S(1)} %get-tuple-element.10, bf16[128,1024]{1,0:T(8,128)(2,1)S(1)} %broadcast_select_fusion.2, f32[264,128]{1,0:T(8,128)S(1)} %convert_element_type.61, f32[128]{0:T(128)S(1)} %rsqrt_bitcast_fusion, f32[256]{0:T(256)S(1)} %fusion.27, ...), kind=kOutput, calls=%fused_computation.6 | convolution fusion | flops 67305472 | bytes 1182720 | tf_op jit(solution)/shard_map/dot_general | solution.py:11
  (25 shorter events, 0.5 us)
Async XLA Ops:
  0.0 9.5 %copy-start.1 = (bf16[128,1024]{1,0:T(8,128)(2,1)S(1)}, bf16[128,1024]{1,0:T(8,128)(2,1)}, u32[]{:S(2)}) copy-start(bf16[128,1024]{1,0:T(8,128)(2,1)} %param.3) | copy-start | bytes 786436
  0.0 9.5 %collective-permute-start.1 = (bf16[128,1024]{1,0:T(8,128)(2,1)}, bf16[128,1024]{1,0:T(8,128)(2,1)S(1)}, u32[]{:S(2)}, u32[]{:S(2)}) collective-permute-start(bf16[128,1024]{1,0:T(8,128)(2,1)} %param.3), channel_id=1, source_target_pairs={{0,8},{1,9},{2,10},{3,11},{4,12},{5,13},{6,14},{7,15},{8,0},{9,1},... | collective-permute-start | bytes 786440 | tf_op jit(solution)/shard_map/ppermute | solution.py:28
  3.9 10.2 %collective-permute-start.3 = (bf16[80,1024]{1,0:T(8,128)(2,1)S(1)}, bf16[80,1024]{1,0:T(8,128)(2,1)S(1)}, u32[]{:S(2)}, u32[]{:S(2)}) collective-permute-start(bf16[80,1024]{1,0:T(8,128)(2,1)S(1)} %slice.19), channel_id=1, source_target_pairs={{0,2},{1,3},{2,0},{3,1},{4,6},{5,7},{6,4},{7,5},{8,10},{9,11},{10,... | collective-permute-start | bytes 491528 | tf_op jit(solution)/shard_map/ppermute | solution.py:28
  6.6 17.8 %collective-permute-start = (bf16[256,1024]{1,0:T(8,128)(2,1)}, bf16[256,1024]{1,0:T(8,128)(2,1)S(1)}, u32[]{:S(2)}, u32[]{:S(2)}) collective-permute-start(bf16[256,1024]{1,0:T(8,128)(2,1)} %param.2), channel_id=1, source_target_pairs={{0,1},{1,0},{2,3},{3,2},{4,5},{5,4},{6,7},{7,6},{8,9},{9,8},{10,11... | collective-permute-start | bytes 1572872 | tf_op jit(solution)/shard_map/ppermute | solution.py:28
  8.1 6.5 %copy-start = (bf16[256,1024]{1,0:T(8,128)(2,1)S(1)}, bf16[256,1024]{1,0:T(8,128)(2,1)}, u32[]{:S(2)}) copy-start(bf16[256,1024]{1,0:T(8,128)(2,1)} %param.2) | copy-start | bytes 1572868
  14.1 5.3 %collective-permute-start.4 = (bf16[80,1024]{1,0:T(8,128)(2,1)S(1)}, bf16[80,1024]{1,0:T(8,128)(2,1)S(1)}, u32[]{:S(2)}, u32[]{:S(2)}) collective-permute-start(bf16[80,1024]{1,0:T(8,128)(2,1)S(1)} %collective-permute-done.3), channel_id=1, source_target_pairs={{0,8},{1,9},{2,10},{3,11},{4,12},{5,13},{6,14},{7,15},{8,0},{9,1},... | collective-permute-start | bytes 491528 | tf_op jit(solution)/shard_map/ppermute | solution.py:28
  14.8 8.3 %collective-permute-start.5 = (bf16[48,1024]{1,0:T(8,128)(2,1)S(1)}, bf16[48,1024]{1,0:T(8,128)(2,1)S(1)}, u32[]{:S(2)}, u32[]{:S(2)}) collective-permute-start(bf16[48,1024]{1,0:T(8,128)(2,1)S(1)} %slice_select_fusion), channel_id=1, source_target_pairs={{0,2},{1,3},{2,0},{3,1},{4,6},{5,7},{6,4},{7,5},{8,10},{9,11},{10,... | collective-permute-start | bytes 294920 | tf_op jit(solution)/shard_map/ppermute | solution.py:28
  15.4 9.4 %collective-permute-start.2 = (bf16[128,1024]{1,0:T(8,128)(2,1)S(1)}, bf16[128,1024]{1,0:T(8,128)(2,1)S(1)}, u32[]{:S(2)}, u32[]{:S(2)}) collective-permute-start(bf16[128,1024]{1,0:T(8,128)(2,1)S(1)} %broadcast_select_fusion.2), channel_id=1, source_target_pairs={{0,4},{1,5},{2,6},{3,7},{4,0},{5,1},{6,2},{7,3},{8,12},{9,13},{10,... | collective-permute-start | bytes 786440 | tf_op jit(solution)/shard_map/ppermute | solution.py:28
  23.1 2.0 %collective-permute-start.6 = (bf16[128,1024]{1,0:T(8,128)(2,1)S(1)}, bf16[128,1024]{1,0:T(8,128)(2,1)S(1)}, u32[]{:S(2)}, u32[]{:S(2)}) collective-permute-start(bf16[128,1024]{1,0:T(8,128)(2,1)S(1)} %pad_maximum_fusion), channel_id=1, source_target_pairs={{0,4},{1,5},{2,6},{3,7},{4,0},{5,1},{6,2},{7,3},{8,12},{9,13},{10,... | collective-permute-start | bytes 786440 | tf_op jit(solution)/shard_map/ppermute | solution.py:28
  26.1 6.9 %collective-permute-start.7 = (f16[264,128]{1,0:T(8,128)(2,1)S(1)}, f16[264,128]{1,0:T(8,128)(2,1)S(1)}, u32[]{:S(2)}, u32[]{:S(2)}) collective-permute-start(f16[264,128]{1,0:T(8,128)(2,1)S(1)} %concatenate.7), channel_id=1, source_target_pairs={{0,2},{1,3},{2,0},{3,1},{4,6},{5,7},{6,4},{7,5},{8,10},{9,11},{10,... | collective-permute-start | bytes 202760 | tf_op jit(solution)/shard_map/ppermute | solution.py:28

commit v15 on v14

--- a/solution.py
+++ b/solution.py
@@ -65,14 +65,14 @@
     def over_middle(block):
         return moved(block, side, lambda r, c: (r, c ^ 2))
 
-    part = width * 5 // 8
+    part = width * 3 // 8
     swapped = over_x(right_docs)
     arrived = over_middle(right_docs[:part])
     left_other = moved(left_docs, side, lambda r, c: (r, c ^ 1))
     near, leaving = lax.optimization_barrier(
         (jnp.where(at_home, right_docs, swapped), jnp.where(at_home, swapped[part:], right_docs[part:]))
     )
-    arrived, _ = lax.optimization_barrier((arrived, leaving))
+    arrived, left_other = lax.optimization_barrier((arrived, left_other))
     cross = jnp.concatenate([jnp.where(at_home, arrived, over_x(arrived)), over_middle(leaving)])
     cross = lax.optimization_barrier(cross)
     lefts = lax.optimization_barrier((jnp.where(same, left_docs, left_other), jnp.where(same, left_other, left_docs)))

time: 34.2 us -> 37.3 us (1.091)
  waiting for transfers between devices: 18.3 us -> 19.4 us
  other arithmetic: 1.33 us -> 2.41 us
  starting transfers between devices: 11.4 us -> 12.3 us
    ppermute x8, waiting for transfers between devices: 18.3 us -> 19.4 us  [moved(): return lax.ppermute(value, ('row', 'col'), pairs)]
    reduce_sum x6, other arithmetic: 0.9 us -> 1.98 us  [squares(): return jnp.sum(widened * widened, axis=1)]
    ppermute x8, starting transfers between devices: 11.4 us -> 12.3 us  [moved(): return lax.ppermute(value, ('row', 'col'), pairs)]
  transfers between devices with their start and end apart: 8 -> 8, of which waited for: 6 -> 6; matrix products, arithmetic and copies ran while one was open for 7% -> 9% of each run, Pallas kernels for 0% -> 0%
where the time goes in v15:
time: 37.3 us; the launch traced here: 37.1 us
  waiting for transfers between devices  19.4 us (52%)
  starting transfers between devices  12.3 us (33%)
  other arithmetic  2.41 us (6%)
  matrix products  1.88 us (5%)
  local copies, waits for them, and re-layouts  0.98 us (3%)
    ppermute x8, waiting for transfers between devices, moved(): return lax.ppermute(value, ('row', 'col'), pairs)  19.4 us
    ppermute x8, starting transfers between devices, moved(): return lax.ppermute(value, ('row', 'col'), pairs)  12.3 us
    reduce_sum x6, other arithmetic, squares(): return jnp.sum(widened * widened, axis=1)  1.98 us
    dot_general x4, matrix products, contract(): lax.dot_general(left_part, right_part, (((1,), (1,)), ((), ())), preferre...  1.88 us
    slice x1, local copies, waits for them, and re-layouts, on_square_grid(): arrived = over_middle(right_docs[:part])  0.9 us
  transfers between devices with their start and end apart: 8, of which 6 were waited for; matrix products, arithmetic and copies ran while one was open for 9% of the time, Pallas kernels for 0%

profile of v15, /device:TPU:0, one launch (start us, length us, event | category | flops | bytes accessed | tf_op | source)
XLA Modules:
  0.0 37.1 jit_solution(16120612990032201961)
XLA Ops:
  0.0 2.9 %collective-permute-start.2 = (bf16[128,1024]{1,0:T(8,128)(2,1)}, bf16[128,1024]{1,0:T(8,128)(2,1)S(1)}, u32[]{:S(2)}, u32[]{:S(2)}) collective-permute-start(bf16[128,1024]{1,0:T(8,128)(2,1)} %param.3), channel_id=1, source_target_pairs={{0,8},{1,9},{2,10},{3,11},{4,12},{5,13},{6,14},{7,15},{8,0},{9,1},... | collective-permute-start | bytes 786440 | tf_op jit(solution)/shard_map/ppermute | solution.py:28
  2.9 1.6 %collective-permute-start.1 = (bf16[256,1024]{1,0:T(8,128)(2,1)}, bf16[256,1024]{1,0:T(8,128)(2,1)S(1)}, u32[]{:S(2)}, u32[]{:S(2)}) collective-permute-start(bf16[256,1024]{1,0:T(8,128)(2,1)} %param.2), channel_id=1, source_target_pairs={{0,1},{1,0},{2,3},{3,2},{4,5},{5,4},{6,7},{7,6},{8,9},{9,8},{10,11... | collective-permute-start | bytes 1572872 | tf_op jit(solution)/shard_map/ppermute | solution.py:28
  4.5 0.9 %slice.17 = bf16[48,1024]{1,0:T(8,128)(2,1)S(1)} slice(bf16[128,1024]{1,0:T(8,128)(2,1)} %param.3), slice={[0:48], [0:1024]} | slice | bytes 196608 | tf_op jit(solution)/shard_map/slice | solution.py:70
  5.4 2.6 %collective-permute-start = (bf16[48,1024]{1,0:T(8,128)(2,1)S(1)}, bf16[48,1024]{1,0:T(8,128)(2,1)S(1)}, u32[]{:S(2)}, u32[]{:S(2)}) collective-permute-start(bf16[48,1024]{1,0:T(8,128)(2,1)S(1)} %slice.17), channel_id=1, source_target_pairs={{0,2},{1,3},{2,0},{3,1},{4,6},{5,7},{6,4},{7,5},{8,10},{9,11},{10,... | collective-permute-start | bytes 294920 | tf_op jit(solution)/shard_map/ppermute | solution.py:28
  8.0 1.3 %multiply_reduce_fusion.1 = f32[256]{0:T(256)S(1)} fusion(bf16[256,1024]{1,0:T(8,128)(2,1)} %param.2), kind=kLoop, calls=%fused_computation.9 | loop fusion | flops 786176 | bytes 525312 | tf_op jit(solution)/shard_map/reduce_sum | solution.py:18
  9.3 0.2 collective-permute-done.2
  9.5 2.9 %collective-permute-start.5 = (bf16[80,1024]{1,0:T(8,128)(2,1)S(1)}, bf16[80,1024]{1,0:T(8,128)(2,1)S(1)}, u32[]{:S(2)}, u32[]{:S(2)}) collective-permute-start(bf16[80,1024]{1,0:T(8,128)(2,1)S(1)} %slice_select_fusion), channel_id=1, source_target_pairs={{0,2},{1,3},{2,0},{3,1},{4,6},{5,7},{6,4},{7,5},{8,10},{9,11},{10,... | collective-permute-start | bytes 491528 | tf_op jit(solution)/shard_map/ppermute | solution.py:28
  12.4 0.1 multiply_reduce_fusion.3
  12.6 6.6 %collective-permute-done = bf16[48,1024]{1,0:T(8,128)(2,1)S(1)} collective-permute-done((bf16[48,1024]{1,0:T(8,128)(2,1)S(1)}, bf16[48,1024]{1,0:T(8,128)(2,1)S(1)}, u32[]{:S(2)}, u32[]{:S(2)}) %collective-permute-start) | collective-permute-done | bytes 98336 | tf_op jit(solution)/shard_map/ppermute | solution.py:28
  19.2 3.0 %collective-permute-done.1 = bf16[256,1024]{1,0:T(8,128)(2,1)S(1)} collective-permute-done((bf16[256,1024]{1,0:T(8,128)(2,1)}, bf16[256,1024]{1,0:T(8,128)(2,1)S(1)}, u32[]{:S(2)}, u32[]{:S(2)}) %collective-permute-start.1) | collective-permute-done | bytes 524320 | tf_op jit(solution)/shard_map/ppermute | solution.py:28
  22.2 0.4 collective-permute-start.4
  22.5 0.2 multiply_reduce_fusion
  22.7 0.1 broadcast_select_fusion
  22.9 0.3 fusion.44
  23.2 3.6 %collective-permute-done.4 = bf16[48,1024]{1,0:T(8,128)(2,1)S(1)} collective-permute-done((bf16[48,1024]{1,0:T(8,128)(2,1)S(1)}, bf16[48,1024]{1,0:T(8,128)(2,1)S(1)}, u32[]{:S(2)}, u32[]{:S(2)}) %collective-permute-start.4) | collective-permute-done | bytes 98336 | tf_op jit(solution)/shard_map/ppermute | solution.py:28
  26.9 0.1 multiply_reduce_fusion.5
  27.1 1.4 %collective-permute-done.6 = bf16[128,1024]{1,0:T(8,128)(2,1)S(1)} collective-permute-done((bf16[128,1024]{1,0:T(8,128)(2,1)S(1)}, bf16[128,1024]{1,0:T(8,128)(2,1)S(1)}, u32[]{:S(2)}, u32[]{:S(2)}) %collective-permute-start.6) | collective-permute-done | bytes 262176 | tf_op jit(solution)/shard_map/ppermute | solution.py:28
  28.4 0.1 multiply_reduce_fusion.4
  28.7 0.3 fusion.45
  29.0 0.3 fusion.5
  29.4 1.8 %collective-permute-start.7 = (f16[264,128]{1,0:T(8,128)(2,1)S(1)}, f16[264,128]{1,0:T(8,128)(2,1)S(1)}, u32[]{:S(2)}, u32[]{:S(2)}) collective-permute-start(f16[264,128]{1,0:T(8,128)(2,1)S(1)} %concatenate.7), channel_id=1, source_target_pairs={{0,2},{1,3},{2,0},{3,1},{4,6},{5,7},{6,4},{7,5},{8,10},{9,11},{10,... | collective-permute-start | bytes 202760 | tf_op jit(solution)/shard_map/ppermute | solution.py:28
  31.2 0.1 multiply_reduce_fusion.2
  31.3 4.7 %collective-permute-done.7 = f16[264,128]{1,0:T(8,128)(2,1)S(1)} collective-permute-done((f16[264,128]{1,0:T(8,128)(2,1)S(1)}, f16[264,128]{1,0:T(8,128)(2,1)S(1)}, u32[]{:S(2)}, u32[]{:S(2)}) %collective-permute-start.7) | collective-permute-done | bytes 67616 | tf_op jit(solution)/shard_map/ppermute | solution.py:28
  36.1 1.0 %fusion.4 = f32[256,128]{1,0:T(8,128)} fusion(f32[256,128]{1,0:T(8,128)S(1)} %fusion.44, bf16[256,1024]{1,0:T(8,128)(2,1)S(1)} %get-tuple-element.12, bf16[128,1024]{1,0:T(8,128)(2,1)S(1)} %broadcast_select_fusion.2, f32[264,128]{1,0:T(8,128)S(1)} %convert_element_type.61, f32[128]{0:T(128)S(1)} %rsqrt_bitcast_fusion, f32[256]{0:T(256)S(1)} %fusion.27, ...), kind=kOutput, calls=%fused_computation.6 | convolution fusion | flops 67305472 | bytes 1182720 | tf_op jit(solution)/shard_map/dot_general | solution.py:11
  (25 shorter events, 0.5 us)
Async XLA Ops:
  0.0 9.5 %collective-permute-start.2 = (bf16[128,1024]{1,0:T(8,128)(2,1)}, bf16[128,1024]{1,0:T(8,128)(2,1)S(1)}, u32[]{:S(2)}, u32[]{:S(2)}) collective-permute-start(bf16[128,1024]{1,0:T(8,128)(2,1)} %param.3), channel_id=1, source_target_pairs={{0,8},{1,9},{2,10},{3,11},{4,12},{5,13},{6,14},{7,15},{8,0},{9,1},... | collective-permute-start | bytes 786440 | tf_op jit(solution)/shard_map/ppermute | solution.py:28
  2.9 19.2 %collective-permute-start.1 = (bf16[256,1024]{1,0:T(8,128)(2,1)}, bf16[256,1024]{1,0:T(8,128)(2,1)S(1)}, u32[]{:S(2)}, u32[]{:S(2)}) collective-permute-start(bf16[256,1024]{1,0:T(8,128)(2,1)} %param.2), channel_id=1, source_target_pairs={{0,1},{1,0},{2,3},{3,2},{4,5},{5,4},{6,7},{7,6},{8,9},{9,8},{10,11... | collective-permute-start | bytes 1572872 | tf_op jit(solution)/shard_map/ppermute | solution.py:28
  5.4 13.8 %collective-permute-start = (bf16[48,1024]{1,0:T(8,128)(2,1)S(1)}, bf16[48,1024]{1,0:T(8,128)(2,1)S(1)}, u32[]{:S(2)}, u32[]{:S(2)}) collective-permute-start(bf16[48,1024]{1,0:T(8,128)(2,1)S(1)} %slice.17), channel_id=1, source_target_pairs={{0,2},{1,3},{2,0},{3,1},{4,6},{5,7},{6,4},{7,5},{8,10},{9,11},{10,... | collective-permute-start | bytes 294920 | tf_op jit(solution)/shard_map/ppermute | solution.py:28
  8.0 1.4 %copy-start.1 = (bf16[128,1024]{1,0:T(8,128)(2,1)S(1)}, bf16[128,1024]{1,0:T(8,128)(2,1)}, u32[]{:S(2)}) copy-start(bf16[128,1024]{1,0:T(8,128)(2,1)} %param.3) | copy-start | bytes 786436
  9.5 13.2 %copy-start = (bf16[256,1024]{1,0:T(8,128)(2,1)S(1)}, bf16[256,1024]{1,0:T(8,128)(2,1)}, u32[]{:S(2)}) copy-start(bf16[256,1024]{1,0:T(8,128)(2,1)} %param.2) | copy-start | bytes 1572868
  9.5 17.3 %collective-permute-start.5 = (bf16[80,1024]{1,0:T(8,128)(2,1)S(1)}, bf16[80,1024]{1,0:T(8,128)(2,1)S(1)}, u32[]{:S(2)}, u32[]{:S(2)}) collective-permute-start(bf16[80,1024]{1,0:T(8,128)(2,1)S(1)} %slice_select_fusion), channel_id=1, source_target_pairs={{0,2},{1,3},{2,0},{3,1},{4,6},{5,7},{6,4},{7,5},{8,10},{9,11},{10,... | collective-permute-start | bytes 491528 | tf_op jit(solution)/shard_map/ppermute | solution.py:28
  12.4 10.4 %collective-permute-start.3 = (bf16[128,1024]{1,0:T(8,128)(2,1)S(1)}, bf16[128,1024]{1,0:T(8,128)(2,1)S(1)}, u32[]{:S(2)}, u32[]{:S(2)}) collective-permute-start(bf16[128,1024]{1,0:T(8,128)(2,1)S(1)} %broadcast_select_fusion.2), channel_id=1, source_target_pairs={{0,4},{1,5},{2,6},{3,7},{4,0},{5,1},{6,2},{7,3},{8,12},{9,13},{10,... | collective-permute-start | bytes 786440 | tf_op jit(solution)/shard_map/ppermute | solution.py:28
  22.2 4.6 %collective-permute-start.4 = (bf16[48,1024]{1,0:T(8,128)(2,1)S(1)}, bf16[48,1024]{1,0:T(8,128)(2,1)S(1)}, u32[]{:S(2)}, u32[]{:S(2)}) collective-permute-start(bf16[48,1024]{1,0:T(8,128)(2,1)S(1)} %collective-permute-done), channel_id=1, source_target_pairs={{0,8},{1,9},{2,10},{3,11},{4,12},{5,13},{6,14},{7,15},{8,0},{9,1},... | collective-permute-start | bytes 294920 | tf_op jit(solution)/shard_map/ppermute | solution.py:28
  26.8 1.6 %collective-permute-start.6 = (bf16[128,1024]{1,0:T(8,128)(2,1)S(1)}, bf16[128,1024]{1,0:T(8,128)(2,1)S(1)}, u32[]{:S(2)}, u32[]{:S(2)}) collective-permute-start(bf16[128,1024]{1,0:T(8,128)(2,1)S(1)} %pad_maximum_fusion), channel_id=1, source_target_pairs={{0,4},{1,5},{2,6},{3,7},{4,0},{5,1},{6,2},{7,3},{8,12},{9,13},{10,... | collective-permute-start | bytes 786440 | tf_op jit(solution)/shard_map/ppermute | solution.py:28
  29.4 6.7 %collective-permute-start.7 = (f16[264,128]{1,0:T(8,128)(2,1)S(1)}, f16[264,128]{1,0:T(8,128)(2,1)S(1)}, u32[]{:S(2)}, u32[]{:S(2)}) collective-permute-start(f16[264,128]{1,0:T(8,128)(2,1)S(1)} %concatenate.7), channel_id=1, source_target_pairs={{0,2},{1,3},{2,0},{3,1},{4,6},{5,7},{6,4},{7,5},{8,10},{9,11},{10,... | collective-permute-start | bytes 202760 | tf_op jit(solution)/shard_map/ppermute | solution.py:28

commit v16 on v15

--- a/solution.py
+++ b/solution.py
@@ -59,21 +59,12 @@
     def other_core(block):
         return moved(block, side, lambda r, c: (r ^ 1, c))
 
-    def over_x(block):
-        return moved(block, side, lambda r, c: (r ^ 2, c))
-
-    def over_middle(block):
-        return moved(block, side, lambda r, c: (r, c ^ 2))
-
-    part = width * 3 // 8
-    swapped = over_x(right_docs)
-    arrived = over_middle(right_docs[:part])
+    swapped = moved(right_docs, side, lambda r, c: (r ^ 2, c))
     left_other = moved(left_docs, side, lambda r, c: (r, c ^ 1))
     near, leaving = lax.optimization_barrier(
-        (jnp.where(at_home, right_docs, swapped), jnp.where(at_home, swapped[part:], right_docs[part:]))
+        (jnp.where(at_home, right_docs, swapped), jnp.split(jnp.where(at_home, swapped, right_docs), 2))
     )
-    arrived, left_other = lax.optimization_barrier((arrived, left_other))
-    cross = jnp.concatenate([jnp.where(at_home, arrived, over_x(arrived)), over_middle(leaving)])
+    cross = jnp.concatenate([moved(part, side, lambda r, c: (r, c ^ 2)) for part in leaving])
     cross = lax.optimization_barrier(cross)
     lefts = lax.optimization_barrier((jnp.where(same, left_docs, left_other), jnp.where(same, left_other, left_docs)))
 

time: 37.3 us -> 35.2 us (0.944)
  starting transfers between devices: 12.3 us -> 7.71 us
  waiting for transfers between devices: 19.4 us -> 22.9 us
  local copies, waits for them, and re-layouts: 0.98 us -> 0.1 us
    ppermute x8 -> x7, starting transfers between devices: 12.3 us -> 7.71 us  [moved(): return lax.ppermute(value, ('row', 'col'), pairs)]
    ppermute x8 -> x7, waiting for transfers between devices: 19.4 us -> 22.9 us  [moved(): return lax.ppermute(value, ('row', 'col'), pairs)]
    reduce_sum x6, other arithmetic: 1.98 us -> 0.9 us  [squares(): return jnp.sum(widened * widened, axis=1)]
    select_n x3 -> x1, other arithmetic: 0.07 us -> 0.99 us  [on_square_grid(): jnp.where(at_home, swapped, right_docs)]
    slice x1 -> x0, local copies, waits for them, and re-layouts: 0.9 us -> none  [on_square_grid(): arrived = over_middle(right_docs[:part])]
  transfers between devices with their start and end apart: 8 -> 7, of which waited for: 6 -> 5; matrix products, arithmetic and copies ran while one was open for 9% -> 7% of each run, Pallas kernels for 0% -> 0%
where the time goes in v16:
time: 35.2 us; the launch traced here: 35 us
  waiting for transfers between devices  22.9 us (65%)
  starting transfers between devices  7.71 us (22%)
  other arithmetic  2.26 us (6%)
  matrix products  1.88 us (5%)
    ppermute x7, waiting for transfers between devices, moved(): return lax.ppermute(value, ('row', 'col'), pairs)  22.9 us
    ppermute x7, starting transfers between devices, moved(): return lax.ppermute(value, ('row', 'col'), pairs)  7.71 us
    dot_general x4, matrix products, contract(): lax.dot_general(left_part, right_part, (((1,), (1,)), ((), ())), preferre...  1.88 us
    select_n x1, other arithmetic, on_square_grid(): jnp.where(at_home, swapped, right_docs)  0.99 us
    reduce_sum x6, other arithmetic, squares(): return jnp.sum(widened * widened, axis=1)  0.9 us
  transfers between devices with their start and end apart: 7, of which 5 were waited for; matrix products, arithmetic and copies ran while one was open for 7% of the time, Pallas kernels for 0%

profile of v16, /device:TPU:0, one launch (start us, length us, event | category | flops | bytes accessed | tf_op | source)
XLA Modules:
  0.0 35.0 jit_solution(3381736910338130587)
XLA Ops:
  0.0 2.9 %collective-permute-start.1 = (bf16[128,1024]{1,0:T(8,128)(2,1)}, bf16[128,1024]{1,0:T(8,128)(2,1)S(1)}, u32[]{:S(2)}, u32[]{:S(2)}) collective-permute-start(bf16[128,1024]{1,0:T(8,128)(2,1)} %param.3), channel_id=1, source_target_pairs={{0,8},{1,9},{2,10},{3,11},{4,12},{5,13},{6,14},{7,15},{8,0},{9,1},... | collective-permute-start | bytes 786440 | tf_op jit(solution)/shard_map/ppermute | solution.py:28
  2.9 1.6 %collective-permute-start = (bf16[256,1024]{1,0:T(8,128)(2,1)}, bf16[256,1024]{1,0:T(8,128)(2,1)S(1)}, u32[]{:S(2)}, u32[]{:S(2)}) collective-permute-start(bf16[256,1024]{1,0:T(8,128)(2,1)} %param.2), channel_id=1, source_target_pairs={{0,1},{1,0},{2,3},{3,2},{4,5},{5,4},{6,7},{7,6},{8,9},{9,8},{10,11... | collective-permute-start | bytes 1572872 | tf_op jit(solution)/shard_map/ppermute | solution.py:28
  4.5 4.9 %collective-permute-done.1 = bf16[128,1024]{1,0:T(8,128)(2,1)S(1)} collective-permute-done((bf16[128,1024]{1,0:T(8,128)(2,1)}, bf16[128,1024]{1,0:T(8,128)(2,1)S(1)}, u32[]{:S(2)}, u32[]{:S(2)}) %collective-permute-start.1) | collective-permute-done | bytes 262176 | tf_op jit(solution)/shard_map/ppermute | solution.py:28
  9.5 1.0 %broadcast_select_fusion.2 = (bf16[128,1024]{1,0:T(8,128)(2,1)S(1)}, bf16[128,1024]{1,0:T(8,128)(2,1)S(1)}) fusion(bf16[128,1024]{1,0:T(8,128)(2,1)S(1)} %collective-permute-done.1, bf16[128,1024]{1,0:T(8,128)(2,1)} %param.3, pred[]{:T(512)S(6)} %eq.7), kind=kLoop, calls=%fused_computation.17 | loop fusion | flops 262144 | bytes 1048577 | tf_op jit(solution)/shard_map/jit(_where)/select_n | solution.py:65
  10.5 2.9 %collective-permute-start.3 = (bf16[64,1024]{1,0:T(8,128)(2,1)S(1)}, bf16[64,1024]{1,0:T(8,128)(2,1)S(1)}, u32[]{:S(2)}, u32[]{:S(2)}) collective-permute-start(bf16[64,1024]{1,0:T(8,128)(2,1)S(1)} %get-tuple-element.13), channel_id=1, source_target_pairs={{0,2},{1,3},{2,0},{3,1},{4,6},{5,7},{6,4},{7,5},{8,10},{9,11},{10,... | collective-permute-start | bytes 393224 | tf_op jit(solution)/shard_map/ppermute | solution.py:28
  13.4 0.1 collective-permute-start.4
  13.5 0.2 multiply_reduce_fusion.1
  13.7 0.1 collective-permute-start.2
  13.7 0.1 multiply_reduce_fusion.3
  13.9 6.0 %collective-permute-done.3 = bf16[64,1024]{1,0:T(8,128)(2,1)S(1)} collective-permute-done((bf16[64,1024]{1,0:T(8,128)(2,1)S(1)}, bf16[64,1024]{1,0:T(8,128)(2,1)S(1)}, u32[]{:S(2)}, u32[]{:S(2)}) %collective-permute-start.3) | collective-permute-done | bytes 131104 | tf_op jit(solution)/shard_map/ppermute | solution.py:28
  19.9 4.9 %collective-permute-done.4 = bf16[64,1024]{1,0:T(8,128)(2,1)S(1)} collective-permute-done((bf16[64,1024]{1,0:T(8,128)(2,1)S(1)}, bf16[64,1024]{1,0:T(8,128)(2,1)S(1)}, u32[]{:S(2)}, u32[]{:S(2)}) %collective-permute-start.4) | collective-permute-done | bytes 131104 | tf_op jit(solution)/shard_map/ppermute | solution.py:28
  24.9 0.1 collective-permute-start.5
  24.9 0.1 multiply_reduce_fusion.5
  25.1 0.2 multiply_reduce_fusion
  25.3 0.1 broadcast_select_fusion
  25.5 0.3 fusion.45
  25.8 0.6 %collective-permute-done.5 = bf16[128,1024]{1,0:T(8,128)(2,1)S(1)} collective-permute-done((bf16[128,1024]{1,0:T(8,128)(2,1)S(1)}, bf16[128,1024]{1,0:T(8,128)(2,1)S(1)}, u32[]{:S(2)}, u32[]{:S(2)}) %collective-permute-start.5) | collective-permute-done | bytes 262176 | tf_op jit(solution)/shard_map/ppermute | solution.py:28
  26.5 0.1 multiply_reduce_fusion.4
  26.7 0.3 fusion.46
  27.0 0.3 fusion.5
  27.3 0.1 concatenate.7
  27.5 0.1 multiply_reduce_fusion.2
  27.6 6.4 %collective-permute-done.6 = f16[264,128]{1,0:T(8,128)(2,1)S(1)} collective-permute-done((f16[264,128]{1,0:T(8,128)(2,1)S(1)}, f16[264,128]{1,0:T(8,128)(2,1)S(1)}, u32[]{:S(2)}, u32[]{:S(2)}) %collective-permute-start.6) | collective-permute-done | bytes 67616 | tf_op jit(solution)/shard_map/ppermute | solution.py:28
  34.1 1.0 %fusion.4 = f32[256,128]{1,0:T(8,128)} fusion(f32[256,128]{1,0:T(8,128)S(1)} %fusion.45, bf16[256,1024]{1,0:T(8,128)(2,1)S(1)} %get-tuple-element.10, bf16[128,1024]{1,0:T(8,128)(2,1)S(1)} %get-tuple-element.11, f32[264,128]{1,0:T(8,128)S(1)} %convert_element_type.61, f32[128]{0:T(128)S(1)} %rsqrt_bitcast_fusion, f32[256]{0:T(256)S(1)} %fusion.27, ...), kind=kOutput, calls=%fused_computation.6 | convolution fusion | flops 67305472 | bytes 1182720 | tf_op jit(solution)/shard_map/dot_general | solution.py:11
  (19 shorter events, 0.4 us)
Async XLA Ops:
  0.0 9.5 %collective-permute-start.1 = (bf16[128,1024]{1,0:T(8,128)(2,1)}, bf16[128,1024]{1,0:T(8,128)(2,1)S(1)}, u32[]{:S(2)}, u32[]{:S(2)}) collective-permute-start(bf16[128,1024]{1,0:T(8,128)(2,1)} %param.3), channel_id=1, source_target_pairs={{0,8},{1,9},{2,10},{3,11},{4,12},{5,13},{6,14},{7,15},{8,0},{9,1},... | collective-permute-start | bytes 786440 | tf_op jit(solution)/shard_map/ppermute | solution.py:28
  2.9 22.1 %collective-permute-start = (bf16[256,1024]{1,0:T(8,128)(2,1)}, bf16[256,1024]{1,0:T(8,128)(2,1)S(1)}, u32[]{:S(2)}, u32[]{:S(2)}) collective-permute-start(bf16[256,1024]{1,0:T(8,128)(2,1)} %param.2), channel_id=1, source_target_pairs={{0,1},{1,0},{2,3},{3,2},{4,5},{5,4},{6,7},{7,6},{8,9},{9,8},{10,11... | collective-permute-start | bytes 1572872 | tf_op jit(solution)/shard_map/ppermute | solution.py:28
  10.4 3.0 %copy-start = (bf16[256,1024]{1,0:T(8,128)(2,1)S(1)}, bf16[256,1024]{1,0:T(8,128)(2,1)}, u32[]{:S(2)}) copy-start(bf16[256,1024]{1,0:T(8,128)(2,1)} %param.2) | copy-start | bytes 1572868
  10.5 9.4 %collective-permute-start.3 = (bf16[64,1024]{1,0:T(8,128)(2,1)S(1)}, bf16[64,1024]{1,0:T(8,128)(2,1)S(1)}, u32[]{:S(2)}, u32[]{:S(2)}) collective-permute-start(bf16[64,1024]{1,0:T(8,128)(2,1)S(1)} %get-tuple-element.13), channel_id=1, source_target_pairs={{0,2},{1,3},{2,0},{3,1},{4,6},{5,7},{6,4},{7,5},{8,10},{9,11},{10,... | collective-permute-start | bytes 393224 | tf_op jit(solution)/shard_map/ppermute | solution.py:28
  13.4 11.5 %collective-permute-start.4 = (bf16[64,1024]{1,0:T(8,128)(2,1)S(1)}, bf16[64,1024]{1,0:T(8,128)(2,1)S(1)}, u32[]{:S(2)}, u32[]{:S(2)}) collective-permute-start(bf16[64,1024]{1,0:T(8,128)(2,1)S(1)} %get-tuple-element.14), channel_id=1, source_target_pairs={{0,2},{1,3},{2,0},{3,1},{4,6},{5,7},{6,4},{7,5},{8,10},{9,11},{10,... | collective-permute-start | bytes 393224 | tf_op jit(solution)/shard_map/ppermute | solution.py:28
  13.7 11.8 %collective-permute-start.2 = (bf16[128,1024]{1,0:T(8,128)(2,1)S(1)}, bf16[128,1024]{1,0:T(8,128)(2,1)S(1)}, u32[]{:S(2)}, u32[]{:S(2)}) collective-permute-start(bf16[128,1024]{1,0:T(8,128)(2,1)S(1)} %get-tuple-element.11), channel_id=1, source_target_pairs={{0,4},{1,5},{2,6},{3,7},{4,0},{5,1},{6,2},{7,3},{8,12},{9,13},{10,... | collective-permute-start | bytes 786440 | tf_op jit(solution)/shard_map/ppermute | solution.py:28
  24.9 1.6 %collective-permute-start.5 = (bf16[128,1024]{1,0:T(8,128)(2,1)S(1)}, bf16[128,1024]{1,0:T(8,128)(2,1)S(1)}, u32[]{:S(2)}, u32[]{:S(2)}) collective-permute-start(bf16[128,1024]{1,0:T(8,128)(2,1)S(1)} %pad_maximum_fusion), channel_id=1, source_target_pairs={{0,4},{1,5},{2,6},{3,7},{4,0},{5,1},{6,2},{7,3},{8,12},{9,13},{10,... | collective-permute-start | bytes 786440 | tf_op jit(solution)/shard_map/ppermute | solution.py:28
  27.4 6.6 %collective-permute-start.6 = (f16[264,128]{1,0:T(8,128)(2,1)S(1)}, f16[264,128]{1,0:T(8,128)(2,1)S(1)}, u32[]{:S(2)}, u32[]{:S(2)}) collective-permute-start(f16[264,128]{1,0:T(8,128)(2,1)S(1)} %concatenate.7), channel_id=1, source_target_pairs={{0,2},{1,3},{2,0},{3,1},{4,6},{5,7},{6,4},{7,5},{8,10},{9,11},{10,... | collective-permute-start | bytes 202760 | tf_op jit(solution)/shard_map/ppermute | solution.py:28

commit v17 on v13

--- a/solution.py
+++ b/solution.py
@@ -1,6 +1,8 @@
 import jax
 import jax.numpy as jnp
 from jax import lax
+from jax.experimental import pallas as pl
+from jax.experimental.pallas import tpu as pltpu
 from jax.sharding import PartitionSpec as P
 
 epsilon = 1e-06
@@ -48,6 +50,23 @@
     return root
 
 
+def halves_kernel(block, first, second):
+    half = first.shape[0]
+    first[...] = block[:half]
+    second[...] = block[half:]
+
+
+def halves_of(block):
+    half = jax.ShapeDtypeStruct((block.shape[0] // 2, block.shape[1]), block.dtype)
+    return pl.pallas_call(
+        halves_kernel,
+        out_shape=[half, half],
+        in_specs=[pl.BlockSpec(memory_space=pltpu.VMEM)],
+        out_specs=[pl.BlockSpec(memory_space=pltpu.VMEM)] * 2,
+        cost_estimate=pl.CostEstimate(flops=0, bytes_accessed=4 * block.size, transcendentals=0),
+    )(block)
+
+
 def on_square_grid(left_docs, right_docs):
     side = lax.axis_size("col")
     feat_total = left_docs.shape[1] * side
@@ -60,7 +79,7 @@
         return moved(block, side, lambda r, c: (r ^ 1, c))
 
     nears, crosses = [], []
-    for half in (right_docs[:width // 2], right_docs[width // 2:]):
+    for half in halves_of(right_docs):
         swapped = moved(half, side, lambda r, c: (r ^ 2, c))
         near, leaving = lax.optimization_barrier((jnp.where(at_home, half, swapped), jnp.where(at_home, swapped, half)))
         nears.append(near)

time: 32.2 us -> 33.2 us (1.031)
  starting transfers between devices: 15.6 us -> 12.6 us
  waiting for transfers between devices: 11.9 us -> 14.5 us
  Pallas kernels: 0 us -> 1.65 us
  local copies, waits for them, and re-layouts: 1.07 us -> 0.08 us
  other arithmetic: 1.34 us -> 2.24 us
    ppermute x8, starting transfers between devices: 15.6 us -> 12.6 us  [moved(): return lax.ppermute(value, ('row', 'col'), pairs)]
    ppermute x8, waiting for transfers between devices: 11.9 us -> 14.5 us  [moved(): return lax.ppermute(value, ('row', 'col'), pairs)]
    pallas_call x0 -> x1, Pallas kernels: none -> 1.65 us  [halves_of(): pl.pallas_call(halves_kernel, out_shape=[half, half], in_specs=[pl.BlockS...]
    slice x1 -> x0, local copies, waits for them, and re-layouts: 0.99 us -> none  [on_square_grid(): right_docs[:width // 2]]
    select_n x2, other arithmetic: 0.05 us -> 0.95 us  [on_square_grid(): jnp.where(at_home, swapped, half)]
  transfers between devices with their start and end apart: 8 -> 8, of which waited for: 6 -> 5; matrix products, arithmetic and copies ran while one was open for 4% -> 6% of each run, Pallas kernels for 0% -> 0%
where the time goes in v17:
time: 33.2 us; the launch traced here: 33.1 us
  waiting for transfers between devices  14.5 us (44%)
  starting transfers between devices  12.6 us (38%)
  other arithmetic  2.24 us (7%)
  matrix products  1.88 us (6%)
  Pallas kernels  1.65 us (5%)
    ppermute x8, waiting for transfers between devices, moved(): return lax.ppermute(value, ('row', 'col'), pairs)  14.5 us
    ppermute x8, starting transfers between devices, moved(): return lax.ppermute(value, ('row', 'col'), pairs)  12.6 us
    dot_general x4, matrix products, contract(): lax.dot_general(left_part, right_part, (((1,), (1,)), ((), ())), preferre...  1.88 us
    pallas_call x1, Pallas kernels, halves_of(): pl.pallas_call(halves_kernel, out_shape=[half, half], in_specs=[pl.BlockS...  1.65 us
    select_n x2, other arithmetic, on_square_grid(): jnp.where(at_home, swapped, half)  0.95 us
    reduce_sum x6, other arithmetic, squares(): return jnp.sum(widened * widened, axis=1)  0.9 us
  transfers between devices with their start and end apart: 8, of which 5 were waited for; matrix products, arithmetic and copies ran while one was open for 6% of the time, Pallas kernels for 0%

profile of v17, /device:TPU:0, one launch (start us, length us, event | category | flops | bytes accessed | tf_op | source)
XLA Modules:
  0.0 33.1 jit_solution(1954947863210185154)
XLA Ops:
  0.0 1.7 %shard_map.28 = (bf16[64,1024]{1,0:T(8,128)(2,1)}, bf16[64,1024]{1,0:T(8,128)(2,1)}) custom-call(bf16[128,1024]{1,0:T(8,128)(2,1)} %block.1), custom_call_target="tpu_custom_call" | custom-call | bytes 524288 | tf_op jit(solution)/shard_map/pallas_call | solution.py:61
  1.7 2.9 %collective-permute-start.1 = (bf16[64,1024]{1,0:T(8,128)(2,1)}, bf16[64,1024]{1,0:T(8,128)(2,1)S(1)}, u32[]{:S(2)}, u32[]{:S(2)}) collective-permute-start(bf16[64,1024]{1,0:T(8,128)(2,1)} %get-tuple-element.14), channel_id=1, source_target_pairs={{0,8},{1,9},{2,10},{3,11},{4,12},{5,13},{6,14},{7,15},{8,0},{9,1},... | collective-permute-start | bytes 393224 | tf_op jit(solution)/shard_map/ppermute | solution.py:30
  4.6 2.1 %collective-permute-start = (bf16[256,1024]{1,0:T(8,128)(2,1)}, bf16[256,1024]{1,0:T(8,128)(2,1)S(1)}, u32[]{:S(2)}, u32[]{:S(2)}) collective-permute-start(bf16[256,1024]{1,0:T(8,128)(2,1)} %param.2), channel_id=1, source_target_pairs={{0,1},{1,0},{2,3},{3,2},{4,5},{5,4},{6,7},{7,6},{8,9},{9,8},{10,11... | collective-permute-start | bytes 1572872 | tf_op jit(solution)/shard_map/ppermute | solution.py:30
  6.7 2.4 %collective-permute-done.1 = bf16[64,1024]{1,0:T(8,128)(2,1)S(1)} collective-permute-done((bf16[64,1024]{1,0:T(8,128)(2,1)}, bf16[64,1024]{1,0:T(8,128)(2,1)S(1)}, u32[]{:S(2)}, u32[]{:S(2)}) %collective-permute-start.1) | collective-permute-done | bytes 131104 | tf_op jit(solution)/shard_map/ppermute | solution.py:30
  9.1 0.9 %broadcast_select_fusion.4 = (bf16[64,1024]{1,0:T(8,128)(2,1)S(1)}, bf16[64,1024]{1,0:T(8,128)(2,1)S(1)}) fusion(bf16[64,1024]{1,0:T(8,128)(2,1)S(1)} %collective-permute-done.1, bf16[64,1024]{1,0:T(8,128)(2,1)} %get-tuple-element.14, pred[]{:T(512)S(6)} %eq.7), kind=kLoop, calls=%fused_computation.22 | loop fusion | flops 131072 | bytes 524289 | tf_op jit(solution)/shard_map/jit(_where)/select_n | solution.py:84
  10.1 3.2 %collective-permute-start.4 = (bf16[64,1024]{1,0:T(8,128)(2,1)S(1)}, bf16[64,1024]{1,0:T(8,128)(2,1)S(1)}, u32[]{:S(2)}, u32[]{:S(2)}) collective-permute-start(bf16[64,1024]{1,0:T(8,128)(2,1)S(1)} %get-tuple-element.19), channel_id=1, source_target_pairs={{0,2},{1,3},{2,0},{3,1},{4,6},{5,7},{6,4},{7,5},{8,10},{9,11},{10,... | collective-permute-start | bytes 393224 | tf_op jit(solution)/shard_map/ppermute | solution.py:30
  13.3 0.7 %collective-permute-start.5 = (bf16[64,1024]{1,0:T(8,128)(2,1)S(1)}, bf16[64,1024]{1,0:T(8,128)(2,1)S(1)}, u32[]{:S(2)}, u32[]{:S(2)}) collective-permute-start(bf16[64,1024]{1,0:T(8,128)(2,1)S(1)} %get-tuple-element.20), channel_id=1, source_target_pairs={{0,2},{1,3},{2,0},{3,1},{4,6},{5,7},{6,4},{7,5},{8,10},{9,11},{10,... | collective-permute-start | bytes 393224 | tf_op jit(solution)/shard_map/ppermute | solution.py:30
  14.0 0.2 multiply_reduce_fusion.1
  14.3 0.1 collective-permute-start.3
  14.3 7.4 %collective-permute-done.4 = bf16[64,1024]{1,0:T(8,128)(2,1)S(1)} collective-permute-done((bf16[64,1024]{1,0:T(8,128)(2,1)S(1)}, bf16[64,1024]{1,0:T(8,128)(2,1)S(1)}, u32[]{:S(2)}, u32[]{:S(2)}) %collective-permute-start.4) | collective-permute-done | bytes 131104 | tf_op jit(solution)/shard_map/ppermute | solution.py:30
  21.8 1.4 %collective-permute-done.5 = bf16[64,1024]{1,0:T(8,128)(2,1)S(1)} collective-permute-done((bf16[64,1024]{1,0:T(8,128)(2,1)S(1)}, bf16[64,1024]{1,0:T(8,128)(2,1)S(1)}, u32[]{:S(2)}, u32[]{:S(2)}) %collective-permute-start.5) | collective-permute-done | bytes 131104 | tf_op jit(solution)/shard_map/ppermute | solution.py:30
  23.3 0.1 multiply_reduce_fusion.3
  23.4 0.1 multiply_reduce_fusion.5
  23.5 0.1 multiply_reduce_fusion.2
  23.7 1.1 %collective-permute-done.6 = bf16[128,1024]{1,0:T(8,128)(2,1)S(1)} collective-permute-done((bf16[128,1024]{1,0:T(8,128)(2,1)S(1)}, bf16[128,1024]{1,0:T(8,128)(2,1)S(1)}, u32[]{:S(2)}, u32[]{:S(2)}) %collective-permute-start.6) | collective-permute-done | bytes 262176 | tf_op jit(solution)/shard_map/ppermute | solution.py:30
  24.8 0.1 multiply_reduce_fusion.4
  25.0 0.2 multiply_reduce_fusion
  25.4 0.1 broadcast_select_fusion
  25.4 0.3 fusion.45
  25.8 0.3 fusion.5
  26.2 3.4 %collective-permute-start.7 = (f16[264,128]{1,0:T(8,128)(2,1)S(1)}, f16[264,128]{1,0:T(8,128)(2,1)S(1)}, u32[]{:S(2)}, u32[]{:S(2)}) collective-permute-start(f16[264,128]{1,0:T(8,128)(2,1)S(1)} %concatenate.11), channel_id=1, source_target_pairs={{0,2},{1,3},{2,0},{3,1},{4,6},{5,7},{6,4},{7,5},{8,10},{9,11},{10,... | collective-permute-start | bytes 202760 | tf_op jit(solution)/shard_map/ppermute | solution.py:30
  29.6 0.3 fusion.44
  29.9 2.1 %collective-permute-done.7 = f16[264,128]{1,0:T(8,128)(2,1)S(1)} collective-permute-done((f16[264,128]{1,0:T(8,128)(2,1)S(1)}, f16[264,128]{1,0:T(8,128)(2,1)S(1)}, u32[]{:S(2)}, u32[]{:S(2)}) %collective-permute-start.7) | collective-permute-done | bytes 67616 | tf_op jit(solution)/shard_map/ppermute | solution.py:30
  32.1 1.0 %fusion.4 = f32[256,128]{1,0:T(8,128)} fusion(f32[256,128]{1,0:T(8,128)S(1)} %fusion.44, bf16[256,1024]{1,0:T(8,128)(2,1)S(1)} %get-tuple-element.13, bf16[128,1024]{1,0:T(8,128)(2,1)S(1)} %pad_maximum_fusion, f32[264,128]{1,0:T(8,128)S(1)} %convert_element_type.61, f32[128]{0:T(128)S(1)} %rsqrt_bitcast_fusion, f32[256]{0:T(256)S(1)} %fusion.27, ...), kind=kOutput, calls=%fused_computation.6 | convolution fusion | flops 67305472 | bytes 1182720 | tf_op jit(solution)/shard_map/dot_general | solution.py:13
  (25 shorter events, 0.5 us)
Async XLA Ops:
  1.7 7.5 %collective-permute-start.1 = (bf16[64,1024]{1,0:T(8,128)(2,1)}, bf16[64,1024]{1,0:T(8,128)(2,1)S(1)}, u32[]{:S(2)}, u32[]{:S(2)}) collective-permute-start(bf16[64,1024]{1,0:T(8,128)(2,1)} %get-tuple-element.14), channel_id=1, source_target_pairs={{0,8},{1,9},{2,10},{3,11},{4,12},{5,13},{6,14},{7,15},{8,0},{9,1},... | collective-permute-start | bytes 393224 | tf_op jit(solution)/shard_map/ppermute | solution.py:30
  4.6 8.7 %collective-permute-start.2 = (bf16[64,1024]{1,0:T(8,128)(2,1)}, bf16[64,1024]{1,0:T(8,128)(2,1)S(1)}, u32[]{:S(2)}, u32[]{:S(2)}) collective-permute-start(bf16[64,1024]{1,0:T(8,128)(2,1)} %get-tuple-element.16), channel_id=1, source_target_pairs={{0,8},{1,9},{2,10},{3,11},{4,12},{5,13},{6,14},{7,15},{8,0},{9,1},... | collective-permute-start | bytes 393224 | tf_op jit(solution)/shard_map/ppermute | solution.py:30
  4.6 20.4 %collective-permute-start = (bf16[256,1024]{1,0:T(8,128)(2,1)}, bf16[256,1024]{1,0:T(8,128)(2,1)S(1)}, u32[]{:S(2)}, u32[]{:S(2)}) collective-permute-start(bf16[256,1024]{1,0:T(8,128)(2,1)} %param.2), channel_id=1, source_target_pairs={{0,1},{1,0},{2,3},{3,2},{4,5},{5,4},{6,7},{7,6},{8,9},{9,8},{10,11... | collective-permute-start | bytes 1572872 | tf_op jit(solution)/shard_map/ppermute | solution.py:30
  6.7 6.6 %copy-start.1 = (bf16[64,1024]{1,0:T(8,128)(2,1)S(1)}, bf16[64,1024]{1,0:T(8,128)(2,1)}, u32[]{:S(2)}) copy-start(bf16[64,1024]{1,0:T(8,128)(2,1)} %get-tuple-element.16) | copy-start | bytes 393220
  6.7 7.3 %copy-start = (bf16[256,1024]{1,0:T(8,128)(2,1)S(1)}, bf16[256,1024]{1,0:T(8,128)(2,1)}, u32[]{:S(2)}) copy-start(bf16[256,1024]{1,0:T(8,128)(2,1)} %param.2) | copy-start | bytes 1572868
  10.1 11.7 %collective-permute-start.4 = (bf16[64,1024]{1,0:T(8,128)(2,1)S(1)}, bf16[64,1024]{1,0:T(8,128)(2,1)S(1)}, u32[]{:S(2)}, u32[]{:S(2)}) collective-permute-start(bf16[64,1024]{1,0:T(8,128)(2,1)S(1)} %get-tuple-element.19), channel_id=1, source_target_pairs={{0,2},{1,3},{2,0},{3,1},{4,6},{5,7},{6,4},{7,5},{8,10},{9,11},{10,... | collective-permute-start | bytes 393224 | tf_op jit(solution)/shard_map/ppermute | solution.py:30
  13.3 9.8 %collective-permute-start.5 = (bf16[64,1024]{1,0:T(8,128)(2,1)S(1)}, bf16[64,1024]{1,0:T(8,128)(2,1)S(1)}, u32[]{:S(2)}, u32[]{:S(2)}) collective-permute-start(bf16[64,1024]{1,0:T(8,128)(2,1)S(1)} %get-tuple-element.20), channel_id=1, source_target_pairs={{0,2},{1,3},{2,0},{3,1},{4,6},{5,7},{6,4},{7,5},{8,10},{9,11},{10,... | collective-permute-start | bytes 393224 | tf_op jit(solution)/shard_map/ppermute | solution.py:30
  14.3 9.3 %collective-permute-start.3 = (bf16[128,1024]{1,0:T(8,128)(2,1)S(1)}, bf16[128,1024]{1,0:T(8,128)(2,1)S(1)}, u32[]{:S(2)}, u32[]{:S(2)}) collective-permute-start(bf16[128,1024]{1,0:T(8,128)(2,1)S(1)} %pad_maximum_fusion), channel_id=1, source_target_pairs={{0,4},{1,5},{2,6},{3,7},{4,0},{5,1},{6,2},{7,3},{8,12},{9,13},{10,... | collective-permute-start | bytes 786440 | tf_op jit(solution)/shard_map/ppermute | solution.py:30
  23.2 1.6 %collective-permute-start.6 = (bf16[128,1024]{1,0:T(8,128)(2,1)S(1)}, bf16[128,1024]{1,0:T(8,128)(2,1)S(1)}, u32[]{:S(2)}, u32[]{:S(2)}) collective-permute-start(bf16[128,1024]{1,0:T(8,128)(2,1)S(1)} %pad_maximum_fusion.1), channel_id=1, source_target_pairs={{0,4},{1,5},{2,6},{3,7},{4,0},{5,1},{6,2},{7,3},{8,12},{9,13},{10,... | collective-permute-start | bytes 786440 | tf_op jit(solution)/shard_map/ppermute | solution.py:30
  26.2 5.9 %collective-permute-start.7 = (f16[264,128]{1,0:T(8,128)(2,1)S(1)}, f16[264,128]{1,0:T(8,128)(2,1)S(1)}, u32[]{:S(2)}, u32[]{:S(2)}) collective-permute-start(f16[264,128]{1,0:T(8,128)(2,1)S(1)} %concatenate.11), channel_id=1, source_target_pairs={{0,2},{1,3},{2,0},{3,1},{4,6},{5,7},{6,4},{7,5},{8,10},{9,11},{10,... | collective-permute-start | bytes 202760 | tf_op jit(solution)/shard_map/ppermute | solution.py:30

commit v18 on v13

--- a/solution.py
+++ b/solution.py
@@ -69,13 +69,15 @@
     near, cross = lax.optimization_barrier(jnp.concatenate(nears)), lax.optimization_barrier(jnp.concatenate(crosses))
     lefts = lax.optimization_barrier((jnp.where(same, left_docs, left_other), jnp.where(same, left_other, left_docs)))
 
-    def half_sum(mine):
-        blocks = (mine, other_core(mine))
-        gram = sum(contract(left, right) for left, right in zip(lefts, blocks))
-        return gram, sum(squares(block) for block in blocks)
+    def half_sum(mine, other):
+        gram = sum(contract(left, right) for left, right in zip(lefts, (mine, other)))
+        return gram, squares(mine) + squares(other)
 
-    near_gram, near_sq = half_sum(near)
-    cross_gram, cross_sq = half_sum(cross)
+    near_other = other_core(near)
+    cross_gram = contract(lefts[0], cross)
+    cross_other, cross_gram = lax.optimization_barrier((other_core(cross), cross_gram))
+    cross_gram = cross_gram + contract(lefts[1], cross_other)
+    cross_sq = squares(cross) + squares(cross_other)
     left_sq = squares(left_docs) + squares(left_other)
 
     left_high, left_low, left_read = packed(left_sq)
@@ -84,8 +86,12 @@
     parts = rows // width
     sums = [left_high.reshape(parts, width), left_low.reshape(parts, width), right_high[None], right_low[None]]
     spare = jnp.zeros((-(2 * parts + 2) % 8, width), jnp.float16)
-    got = moved(jnp.concatenate([tile.astype(jnp.float16), *sums, spare]), side, lambda r, c: (r, c ^ 2))
+    message = jnp.concatenate([tile.astype(jnp.float16), *sums, spare])
+    got = moved(message, side, lambda r, c: (r, c ^ 2))
 
+    near_other, _ = lax.optimization_barrier((near_other, message))
+    near_gram, near_sq = half_sum(near, near_other)
+    near_gram, got = lax.optimization_barrier((near_gram, got))
     got = got.astype(jnp.float32)
     sums = jnp.split(got[rows:rows + 2 * parts + 2], (parts, 2 * parts, 2 * parts + 1))
     left_got, right_got = unpacked(*sums[:2]).reshape(rows), unpacked(*sums[2:]).reshape(width)

time: 32.2 us -> 31.9 us (level)
  other arithmetic: 1.34 us -> 2.23 us
  matrix products: 1.88 us -> 1.21 us
  waiting for transfers between devices: 11.9 us -> 11.3 us
    mul x2 -> x3, other arithmetic: 0.02 us -> 0.81 us  [finish(): return summed / feat_total * left_scale[:, None] * right_scale[None, :]]
    dot_general x4, matrix products: 1.88 us -> 1.21 us  [contract(): lax.dot_general(left_part, right_part, (((1,), (1,)), ((), ())), preferre...]
    ppermute x8, waiting for transfers between devices: 11.9 us -> 11.3 us  [moved(): return lax.ppermute(value, ('row', 'col'), pairs)]
  transfers between devices with their start and end apart: 8 -> 8, of which waited for: 6 -> 6; matrix products, arithmetic and copies ran while one was open for 4% -> 8% of each run, Pallas kernels for 0% -> 0%
where the time goes in v18:
time: 31.9 us; the launch traced here: 31.5 us
  starting transfers between devices  15.6 us (49%)
  waiting for transfers between devices  11.3 us (35%)
  other arithmetic  2.23 us (7%)
  matrix products  1.21 us (4%)
  local copies, waits for them, and re-layouts  1.07 us (3%)
    ppermute x8, starting transfers between devices, moved(): return lax.ppermute(value, ('row', 'col'), pairs)  15.6 us
    ppermute x8, waiting for transfers between devices, moved(): return lax.ppermute(value, ('row', 'col'), pairs)  11.3 us
    dot_general x4, matrix products, contract(): lax.dot_general(left_part, right_part, (((1,), (1,)), ((), ())), preferre...  1.21 us
    slice x1, local copies, waits for them, and re-layouts, on_square_grid(): right_docs[:width // 2]  0.99 us
    reduce_sum x6, other arithmetic, squares(): return jnp.sum(widened * widened, axis=1)  0.9 us
    mul x3, other arithmetic, finish(): return summed / feat_total * left_scale[:, None] * right_scale[None, :]  0.81 us
  transfers between devices with their start and end apart: 8, of which 6 were waited for; matrix products, arithmetic and copies ran while one was open for 8% of the time, Pallas kernels for 0%

profile of v18, /device:TPU:0, one launch (start us, length us, event | category | flops | bytes accessed | tf_op | source)
XLA Modules:
  0.0 31.5 jit_solution(12814280249313717958)
XLA Ops:
  0.0 1.0 %slice.14 = bf16[64,1024]{1,0:T(8,128)(2,1)S(1)} slice(bf16[128,1024]{1,0:T(8,128)(2,1)} %param.3), slice={[0:64], [0:1024]} | slice | bytes 262144 | tf_op jit(solution)/shard_map/slice | solution.py:63
  1.0 3.0 %collective-permute-start.1 = (bf16[64,1024]{1,0:T(8,128)(2,1)S(1)}, bf16[64,1024]{1,0:T(8,128)(2,1)S(1)}, u32[]{:S(2)}, u32[]{:S(2)}) collective-permute-start(bf16[64,1024]{1,0:T(8,128)(2,1)S(1)} %slice.14), channel_id=1, source_target_pairs={{0,8},{1,9},{2,10},{3,11},{4,12},{5,13},{6,14},{7,15},{8,0},{9,1},... | collective-permute-start | bytes 393224 | tf_op jit(solution)/shard_map/ppermute | solution.py:28
  4.0 1.6 %collective-permute-start = (bf16[256,1024]{1,0:T(8,128)(2,1)}, bf16[256,1024]{1,0:T(8,128)(2,1)S(1)}, u32[]{:S(2)}, u32[]{:S(2)}) collective-permute-start(bf16[256,1024]{1,0:T(8,128)(2,1)} %param.2), channel_id=1, source_target_pairs={{0,1},{1,0},{2,3},{3,2},{4,5},{5,4},{6,7},{7,6},{8,9},{9,8},{10,11... | collective-permute-start | bytes 1572872 | tf_op jit(solution)/shard_map/ppermute | solution.py:28
  5.6 1.9 %collective-permute-done.1 = bf16[64,1024]{1,0:T(8,128)(2,1)S(1)} collective-permute-done((bf16[64,1024]{1,0:T(8,128)(2,1)S(1)}, bf16[64,1024]{1,0:T(8,128)(2,1)S(1)}, u32[]{:S(2)}, u32[]{:S(2)}) %collective-permute-start.1) | collective-permute-done | bytes 131104 | tf_op jit(solution)/shard_map/ppermute | solution.py:28
  7.5 1.8 %collective-permute-start.2 = (bf16[64,1024]{1,0:T(8,128)(2,1)S(1)}, bf16[64,1024]{1,0:T(8,128)(2,1)S(1)}, u32[]{:S(2)}, u32[]{:S(2)}) collective-permute-start(bf16[64,1024]{1,0:T(8,128)(2,1)S(1)} %get-tuple-element.41), channel_id=1, source_target_pairs={{0,8},{1,9},{2,10},{3,11},{4,12},{5,13},{6,14},{7,15},{8,0},{9,1},... | collective-permute-start | bytes 393224 | tf_op jit(solution)/shard_map/ppermute | solution.py:28
  9.3 0.2 multiply_reduce_fusion.1
  9.5 2.7 %collective-permute-start.4 = (bf16[64,1024]{1,0:T(8,128)(2,1)S(1)}, bf16[64,1024]{1,0:T(8,128)(2,1)S(1)}, u32[]{:S(2)}, u32[]{:S(2)}) collective-permute-start(bf16[64,1024]{1,0:T(8,128)(2,1)S(1)} %get-tuple-element.20), channel_id=1, source_target_pairs={{0,2},{1,3},{2,0},{3,1},{4,6},{5,7},{6,4},{7,5},{8,10},{9,11},{10,... | collective-permute-start | bytes 393224 | tf_op jit(solution)/shard_map/ppermute | solution.py:28
  12.2 0.4 %collective-permute-done.2 = bf16[64,1024]{1,0:T(8,128)(2,1)S(1)} collective-permute-done((bf16[64,1024]{1,0:T(8,128)(2,1)S(1)}, bf16[64,1024]{1,0:T(8,128)(2,1)S(1)}, u32[]{:S(2)}, u32[]{:S(2)}) %collective-permute-start.2) | collective-permute-done | bytes 131104 | tf_op jit(solution)/shard_map/ppermute | solution.py:28
  12.6 2.9 %collective-permute-start.5 = (bf16[64,1024]{1,0:T(8,128)(2,1)S(1)}, bf16[64,1024]{1,0:T(8,128)(2,1)S(1)}, u32[]{:S(2)}, u32[]{:S(2)}) collective-permute-start(bf16[64,1024]{1,0:T(8,128)(2,1)S(1)} %get-tuple-element.21), channel_id=1, source_target_pairs={{0,2},{1,3},{2,0},{3,1},{4,6},{5,7},{6,4},{7,5},{8,10},{9,11},{10,... | collective-permute-start | bytes 393224 | tf_op jit(solution)/shard_map/ppermute | solution.py:28
  15.6 0.1 multiply_reduce_fusion.3
  15.7 5.2 %collective-permute-done.4 = bf16[64,1024]{1,0:T(8,128)(2,1)S(1)} collective-permute-done((bf16[64,1024]{1,0:T(8,128)(2,1)S(1)}, bf16[64,1024]{1,0:T(8,128)(2,1)S(1)}, u32[]{:S(2)}, u32[]{:S(2)}) %collective-permute-start.4) | collective-permute-done | bytes 131104 | tf_op jit(solution)/shard_map/ppermute | solution.py:28
  21.0 1.4 %collective-permute-done.5 = bf16[64,1024]{1,0:T(8,128)(2,1)S(1)} collective-permute-done((bf16[64,1024]{1,0:T(8,128)(2,1)S(1)}, bf16[64,1024]{1,0:T(8,128)(2,1)S(1)}, u32[]{:S(2)}, u32[]{:S(2)}) %collective-permute-start.5) | collective-permute-done | bytes 131104 | tf_op jit(solution)/shard_map/ppermute | solution.py:28
  22.4 0.1 multiply_reduce_fusion.5
  22.6 0.6 %collective-permute-done = bf16[256,1024]{1,0:T(8,128)(2,1)S(1)} collective-permute-done((bf16[256,1024]{1,0:T(8,128)(2,1)}, bf16[256,1024]{1,0:T(8,128)(2,1)S(1)}, u32[]{:S(2)}, u32[]{:S(2)}) %collective-permute-start) | collective-permute-done | bytes 524320 | tf_op jit(solution)/shard_map/ppermute | solution.py:28
  23.2 0.2 multiply_reduce_fusion
  23.6 0.3 fusion.41
  24.0 0.1 multiply_reduce_fusion.4
  24.2 0.3 fusion.42
  24.7 3.5 %collective-permute-start.7 = (f16[264,128]{1,0:T(8,128)(2,1)S(1)}, f16[264,128]{1,0:T(8,128)(2,1)S(1)}, u32[]{:S(2)}, u32[]{:S(2)}) collective-permute-start(f16[264,128]{1,0:T(8,128)(2,1)S(1)} %concatenate.11), channel_id=1, source_target_pairs={{0,2},{1,3},{2,0},{3,1},{4,6},{5,7},{6,4},{7,5},{8,10},{9,11},{10,... | collective-permute-start | bytes 202760 | tf_op jit(solution)/shard_map/ppermute | solution.py:28
  28.2 0.3 fusion.43
  28.5 0.3 convolution_add_fusion
  28.8 0.1 multiply_reduce_fusion.2
  28.9 1.7 %collective-permute-done.7 = f16[264,128]{1,0:T(8,128)(2,1)S(1)} collective-permute-done((f16[264,128]{1,0:T(8,128)(2,1)S(1)}, f16[264,128]{1,0:T(8,128)(2,1)S(1)}, u32[]{:S(2)}, u32[]{:S(2)}) %collective-permute-start.7) | collective-permute-done | bytes 67616 | tf_op jit(solution)/shard_map/ppermute | solution.py:28
  30.7 0.8 %fusion.3 = f32[256,128]{1,0:T(8,128)} fusion(f32[256,128]{1,0:T(8,128)S(1)} %convolution_add_fusion, f32[264,128]{1,0:T(8,128)S(1)} %convert_element_type.61, f32[128]{0:T(128)S(1)} %rsqrt_bitcast_fusion, f32[256]{0:T(256)S(1)} %fusion.24, f32[128]{0:T(128)S(1)} %get-tuple-element.29, f32[256]{0:T(256)S(1)} %get-tuple-element.27), kind=kLoop, calls=%fused_computation.15 | loop fusion | flops 163840 | bytes 396288 | tf_op jit(solution)/shard_map/mul | solution.py:34
  (27 shorter events, 0.8 us)
Async XLA Ops:
  0.0 7.5 %copy-start.1 = (bf16[128,1024]{1,0:T(8,128)(2,1)S(1)}, bf16[128,1024]{1,0:T(8,128)(2,1)}, u32[]{:S(2)}) copy-start(bf16[128,1024]{1,0:T(8,128)(2,1)} %param.3) | copy-start | bytes 786436
  0.0 9.3 %copy-start = (bf16[256,1024]{1,0:T(8,128)(2,1)S(1)}, bf16[256,1024]{1,0:T(8,128)(2,1)}, u32[]{:S(2)}) copy-start(bf16[256,1024]{1,0:T(8,128)(2,1)} %param.2) | copy-start | bytes 1572868
  1.0 6.5 %collective-permute-start.1 = (bf16[64,1024]{1,0:T(8,128)(2,1)S(1)}, bf16[64,1024]{1,0:T(8,128)(2,1)S(1)}, u32[]{:S(2)}, u32[]{:S(2)}) collective-permute-start(bf16[64,1024]{1,0:T(8,128)(2,1)S(1)} %slice.14), channel_id=1, source_target_pairs={{0,8},{1,9},{2,10},{3,11},{4,12},{5,13},{6,14},{7,15},{8,0},{9,1},... | collective-permute-start | bytes 393224 | tf_op jit(solution)/shard_map/ppermute | solution.py:28
  4.0 19.2 %collective-permute-start = (bf16[256,1024]{1,0:T(8,128)(2,1)}, bf16[256,1024]{1,0:T(8,128)(2,1)S(1)}, u32[]{:S(2)}, u32[]{:S(2)}) collective-permute-start(bf16[256,1024]{1,0:T(8,128)(2,1)} %param.2), channel_id=1, source_target_pairs={{0,1},{1,0},{2,3},{3,2},{4,5},{5,4},{6,7},{7,6},{8,9},{9,8},{10,11... | collective-permute-start | bytes 1572872 | tf_op jit(solution)/shard_map/ppermute | solution.py:28
  7.5 5.0 %collective-permute-start.2 = (bf16[64,1024]{1,0:T(8,128)(2,1)S(1)}, bf16[64,1024]{1,0:T(8,128)(2,1)S(1)}, u32[]{:S(2)}, u32[]{:S(2)}) collective-permute-start(bf16[64,1024]{1,0:T(8,128)(2,1)S(1)} %get-tuple-element.41), channel_id=1, source_target_pairs={{0,8},{1,9},{2,10},{3,11},{4,12},{5,13},{6,14},{7,15},{8,0},{9,1},... | collective-permute-start | bytes 393224 | tf_op jit(solution)/shard_map/ppermute | solution.py:28
  9.5 11.4 %collective-permute-start.4 = (bf16[64,1024]{1,0:T(8,128)(2,1)S(1)}, bf16[64,1024]{1,0:T(8,128)(2,1)S(1)}, u32[]{:S(2)}, u32[]{:S(2)}) collective-permute-start(bf16[64,1024]{1,0:T(8,128)(2,1)S(1)} %get-tuple-element.20), channel_id=1, source_target_pairs={{0,2},{1,3},{2,0},{3,1},{4,6},{5,7},{6,4},{7,5},{8,10},{9,11},{10,... | collective-permute-start | bytes 393224 | tf_op jit(solution)/shard_map/ppermute | solution.py:28
  12.6 9.8 %collective-permute-start.5 = (bf16[64,1024]{1,0:T(8,128)(2,1)S(1)}, bf16[64,1024]{1,0:T(8,128)(2,1)S(1)}, u32[]{:S(2)}, u32[]{:S(2)}) collective-permute-start(bf16[64,1024]{1,0:T(8,128)(2,1)S(1)} %get-tuple-element.21), channel_id=1, source_target_pairs={{0,2},{1,3},{2,0},{3,1},{4,6},{5,7},{6,4},{7,5},{8,10},{9,11},{10,... | collective-permute-start | bytes 393224 | tf_op jit(solution)/shard_map/ppermute | solution.py:28
  15.5 12.7 %collective-permute-start.3 = (bf16[128,1024]{1,0:T(8,128)(2,1)S(1)}, bf16[128,1024]{1,0:T(8,128)(2,1)S(1)}, u32[]{:S(2)}, u32[]{:S(2)}) collective-permute-start(bf16[128,1024]{1,0:T(8,128)(2,1)S(1)} %pad_maximum_fusion), channel_id=1, source_target_pairs={{0,4},{1,5},{2,6},{3,7},{4,0},{5,1},{6,2},{7,3},{8,12},{9,13},{10,... | collective-permute-start | bytes 786440 | tf_op jit(solution)/shard_map/ppermute | solution.py:28
  22.4 1.6 %collective-permute-start.6 = (bf16[128,1024]{1,0:T(8,128)(2,1)S(1)}, bf16[128,1024]{1,0:T(8,128)(2,1)S(1)}, u32[]{:S(2)}, u32[]{:S(2)}) collective-permute-start(bf16[128,1024]{1,0:T(8,128)(2,1)S(1)} %pad_maximum_fusion.1), channel_id=1, source_target_pairs={{0,4},{1,5},{2,6},{3,7},{4,0},{5,1},{6,2},{7,3},{8,12},{9,13},{10,... | collective-permute-start | bytes 786440 | tf_op jit(solution)/shard_map/ppermute | solution.py:28
  24.7 5.9 %collective-permute-start.7 = (f16[264,128]{1,0:T(8,128)(2,1)S(1)}, f16[264,128]{1,0:T(8,128)(2,1)S(1)}, u32[]{:S(2)}, u32[]{:S(2)}) collective-permute-start(f16[264,128]{1,0:T(8,128)(2,1)S(1)} %concatenate.11), channel_id=1, source_target_pairs={{0,2},{1,3},{2,0},{3,1},{4,6},{5,7},{6,4},{7,5},{8,10},{9,11},{10,... | collective-permute-start | bytes 202760 | tf_op jit(solution)/shard_map/ppermute | solution.py:28

commit v19 on v18

--- a/solution.py
+++ b/solution.py
@@ -75,7 +75,7 @@
 
     near_other = other_core(near)
     cross_gram = contract(lefts[0], cross)
-    cross_other, cross_gram = lax.optimization_barrier((other_core(cross), cross_gram))
+    cross_other, cross_gram = lax.optimization_barrier((jnp.concatenate([other_core(part) for part in crosses]), cross_gram))
     cross_gram = cross_gram + contract(lefts[1], cross_other)
     cross_sq = squares(cross) + squares(cross_other)
     left_sq = squares(left_docs) + squares(left_other)

time: 31.9 us -> 31.8 us (level)
    ppermute x8 -> x9, starting transfers between devices: 15.6 us -> 15.4 us  [moved(): return lax.ppermute(value, ('row', 'col'), pairs)]
    ppermute x8 -> x9, waiting for transfers between devices: 11.3 us -> 11.4 us  [moved(): return lax.ppermute(value, ('row', 'col'), pairs)]
    reduce_sum x6 -> x5, other arithmetic: 0.9 us -> 0.82 us  [squares(): return jnp.sum(widened * widened, axis=1)]
  transfers between devices with their start and end apart: 8 -> 9, of which waited for: 6 -> 6; matrix products, arithmetic and copies ran while one was open for 8% -> 8% of each run, Pallas kernels for 0% -> 0%
where the time goes in v19:
time: 31.8 us; the launch traced here: 31.4 us
  starting transfers between devices  15.4 us (48%)
  waiting for transfers between devices  11.4 us (36%)
  other arithmetic  2.17 us (7%)
  matrix products  1.21 us (4%)
  local copies, waits for them, and re-layouts  1.07 us (3%)
    ppermute x9, starting transfers between devices, moved(): return lax.ppermute(value, ('row', 'col'), pairs)  15.4 us
    ppermute x9, waiting for transfers between devices, moved(): return lax.ppermute(value, ('row', 'col'), pairs)  11.4 us
    dot_general x4, matrix products, contract(): lax.dot_general(left_part, right_part, (((1,), (1,)), ((), ())), preferre...  1.21 us
    slice x1, local copies, waits for them, and re-layouts, on_square_grid(): right_docs[:width // 2]  0.99 us
    reduce_sum x5, other arithmetic, squares(): return jnp.sum(widened * widened, axis=1)  0.82 us
    mul x3, other arithmetic, finish(): return summed / feat_total * left_scale[:, None] * right_scale[None, :]  0.81 us
  transfers between devices with their start and end apart: 9, of which 6 were waited for; matrix products, arithmetic and copies ran while one was open for 8% of the time, Pallas kernels for 0%

profile of v19, /device:TPU:0, one launch (start us, length us, event | category | flops | bytes accessed | tf_op | source)
XLA Modules:
  0.0 31.4 jit_solution(15795237961563905084)
XLA Ops:
  0.0 1.0 %slice.14 = bf16[64,1024]{1,0:T(8,128)(2,1)S(1)} slice(bf16[128,1024]{1,0:T(8,128)(2,1)} %param.3), slice={[0:64], [0:1024]} | slice | bytes 262144 | tf_op jit(solution)/shard_map/slice | solution.py:63
  1.0 3.0 %collective-permute-start.1 = (bf16[64,1024]{1,0:T(8,128)(2,1)S(1)}, bf16[64,1024]{1,0:T(8,128)(2,1)S(1)}, u32[]{:S(2)}, u32[]{:S(2)}) collective-permute-start(bf16[64,1024]{1,0:T(8,128)(2,1)S(1)} %slice.14), channel_id=1, source_target_pairs={{0,8},{1,9},{2,10},{3,11},{4,12},{5,13},{6,14},{7,15},{8,0},{9,1},... | collective-permute-start | bytes 393224 | tf_op jit(solution)/shard_map/ppermute | solution.py:28
  4.0 1.6 %collective-permute-start = (bf16[256,1024]{1,0:T(8,128)(2,1)}, bf16[256,1024]{1,0:T(8,128)(2,1)S(1)}, u32[]{:S(2)}, u32[]{:S(2)}) collective-permute-start(bf16[256,1024]{1,0:T(8,128)(2,1)} %param.2), channel_id=1, source_target_pairs={{0,1},{1,0},{2,3},{3,2},{4,5},{5,4},{6,7},{7,6},{8,9},{9,8},{10,11... | collective-permute-start | bytes 1572872 | tf_op jit(solution)/shard_map/ppermute | solution.py:28
  5.6 1.9 %collective-permute-done.1 = bf16[64,1024]{1,0:T(8,128)(2,1)S(1)} collective-permute-done((bf16[64,1024]{1,0:T(8,128)(2,1)S(1)}, bf16[64,1024]{1,0:T(8,128)(2,1)S(1)}, u32[]{:S(2)}, u32[]{:S(2)}) %collective-permute-start.1) | collective-permute-done | bytes 131104 | tf_op jit(solution)/shard_map/ppermute | solution.py:28
  7.5 1.8 %collective-permute-start.2 = (bf16[64,1024]{1,0:T(8,128)(2,1)S(1)}, bf16[64,1024]{1,0:T(8,128)(2,1)S(1)}, u32[]{:S(2)}, u32[]{:S(2)}) collective-permute-start(bf16[64,1024]{1,0:T(8,128)(2,1)S(1)} %get-tuple-element.41), channel_id=1, source_target_pairs={{0,8},{1,9},{2,10},{3,11},{4,12},{5,13},{6,14},{7,15},{8,0},{9,1},... | collective-permute-start | bytes 393224 | tf_op jit(solution)/shard_map/ppermute | solution.py:28
  9.3 0.2 multiply_reduce_fusion.1
  9.5 2.7 %collective-permute-start.4 = (bf16[64,1024]{1,0:T(8,128)(2,1)S(1)}, bf16[64,1024]{1,0:T(8,128)(2,1)S(1)}, u32[]{:S(2)}, u32[]{:S(2)}) collective-permute-start(bf16[64,1024]{1,0:T(8,128)(2,1)S(1)} %get-tuple-element.20), channel_id=1, source_target_pairs={{0,2},{1,3},{2,0},{3,1},{4,6},{5,7},{6,4},{7,5},{8,10},{9,11},{10,... | collective-permute-start | bytes 393224 | tf_op jit(solution)/shard_map/ppermute | solution.py:28
  12.2 0.4 %collective-permute-done.2 = bf16[64,1024]{1,0:T(8,128)(2,1)S(1)} collective-permute-done((bf16[64,1024]{1,0:T(8,128)(2,1)S(1)}, bf16[64,1024]{1,0:T(8,128)(2,1)S(1)}, u32[]{:S(2)}, u32[]{:S(2)}) %collective-permute-start.2) | collective-permute-done | bytes 131104 | tf_op jit(solution)/shard_map/ppermute | solution.py:28
  12.6 2.9 %collective-permute-start.6 = (bf16[64,1024]{1,0:T(8,128)(2,1)S(1)}, bf16[64,1024]{1,0:T(8,128)(2,1)S(1)}, u32[]{:S(2)}, u32[]{:S(2)}) collective-permute-start(bf16[64,1024]{1,0:T(8,128)(2,1)S(1)} %get-tuple-element.21), channel_id=1, source_target_pairs={{0,2},{1,3},{2,0},{3,1},{4,6},{5,7},{6,4},{7,5},{8,10},{9,11},{10,... | collective-permute-start | bytes 393224 | tf_op jit(solution)/shard_map/ppermute | solution.py:28
  15.6 5.4 %collective-permute-done.4 = bf16[64,1024]{1,0:T(8,128)(2,1)S(1)} collective-permute-done((bf16[64,1024]{1,0:T(8,128)(2,1)S(1)}, bf16[64,1024]{1,0:T(8,128)(2,1)S(1)}, u32[]{:S(2)}, u32[]{:S(2)}) %collective-permute-start.4) | collective-permute-done | bytes 131104 | tf_op jit(solution)/shard_map/ppermute | solution.py:28
  21.0 0.1 multiply_reduce_fusion.3
  21.1 1.3 %collective-permute-done.6 = bf16[64,1024]{1,0:T(8,128)(2,1)S(1)} collective-permute-done((bf16[64,1024]{1,0:T(8,128)(2,1)S(1)}, bf16[64,1024]{1,0:T(8,128)(2,1)S(1)}, u32[]{:S(2)}, u32[]{:S(2)}) %collective-permute-start.6) | collective-permute-done | bytes 131104 | tf_op jit(solution)/shard_map/ppermute | solution.py:28
  22.4 0.8 %collective-permute-done = bf16[256,1024]{1,0:T(8,128)(2,1)S(1)} collective-permute-done((bf16[256,1024]{1,0:T(8,128)(2,1)}, bf16[256,1024]{1,0:T(8,128)(2,1)S(1)}, u32[]{:S(2)}, u32[]{:S(2)}) %collective-permute-start) | collective-permute-done | bytes 524320 | tf_op jit(solution)/shard_map/ppermute | solution.py:28
  23.2 0.2 multiply_reduce_fusion
  23.6 0.3 fusion.41
  24.0 0.2 multiply_reduce_fusion.4
  24.2 0.3 %fusion.42 = f32[256,128]{1,0:T(8,128)S(1)} fusion(bf16[256,1024]{1,0:T(8,128)(2,1)S(1)} %get-tuple-element.19, bf16[128,1024]{1,0:T(8,128)(2,1)S(1)} %pad_maximum_fusion.1), kind=kOutput, calls=%fused_computation.77 | convolution fusion | flops 67108864 | bytes 917504 | tf_op jit(solution)/shard_map/dot_general | solution.py:11
  24.6 0.1 multiply_convert_fusion
  24.8 3.3 %collective-permute-start.8 = (f16[264,128]{1,0:T(8,128)(2,1)S(1)}, f16[264,128]{1,0:T(8,128)(2,1)S(1)}, u32[]{:S(2)}, u32[]{:S(2)}) collective-permute-start(f16[264,128]{1,0:T(8,128)(2,1)S(1)} %concatenate.15), channel_id=1, source_target_pairs={{0,2},{1,3},{2,0},{3,1},{4,6},{5,7},{6,4},{7,5},{8,10},{9,11},{10,... | collective-permute-start | bytes 202760 | tf_op jit(solution)/shard_map/ppermute | solution.py:28
  28.1 0.3 fusion.43
  28.4 0.3 convolution_add_fusion
  28.7 0.1 multiply_reduce_fusion.2
  28.8 1.7 %collective-permute-done.8 = f16[264,128]{1,0:T(8,128)(2,1)S(1)} collective-permute-done((f16[264,128]{1,0:T(8,128)(2,1)S(1)}, f16[264,128]{1,0:T(8,128)(2,1)S(1)}, u32[]{:S(2)}, u32[]{:S(2)}) %collective-permute-start.8) | collective-permute-done | bytes 67616 | tf_op jit(solution)/shard_map/ppermute | solution.py:28
  30.6 0.8 %fusion.3 = f32[256,128]{1,0:T(8,128)} fusion(f32[256,128]{1,0:T(8,128)S(1)} %convolution_add_fusion, f32[264,128]{1,0:T(8,128)S(1)} %convert_element_type.61, f32[128]{0:T(128)S(1)} %rsqrt_bitcast_fusion, f32[256]{0:T(256)S(1)} %fusion.24, f32[128]{0:T(128)S(1)} %get-tuple-element.29, f32[256]{0:T(256)S(1)} %get-tuple-element.27), kind=kLoop, calls=%fused_computation.16 | loop fusion | flops 163840 | bytes 396288 | tf_op jit(solution)/shard_map/mul | solution.py:34
  (29 shorter events, 0.7 us)
Async XLA Ops:
  0.0 7.5 %copy-start.1 = (bf16[128,1024]{1,0:T(8,128)(2,1)S(1)}, bf16[128,1024]{1,0:T(8,128)(2,1)}, u32[]{:S(2)}) copy-start(bf16[128,1024]{1,0:T(8,128)(2,1)} %param.3) | copy-start | bytes 786436
  0.0 9.3 %copy-start = (bf16[256,1024]{1,0:T(8,128)(2,1)S(1)}, bf16[256,1024]{1,0:T(8,128)(2,1)}, u32[]{:S(2)}) copy-start(bf16[256,1024]{1,0:T(8,128)(2,1)} %param.2) | copy-start | bytes 1572868
  1.0 6.5 %collective-permute-start.1 = (bf16[64,1024]{1,0:T(8,128)(2,1)S(1)}, bf16[64,1024]{1,0:T(8,128)(2,1)S(1)}, u32[]{:S(2)}, u32[]{:S(2)}) collective-permute-start(bf16[64,1024]{1,0:T(8,128)(2,1)S(1)} %slice.14), channel_id=1, source_target_pairs={{0,8},{1,9},{2,10},{3,11},{4,12},{5,13},{6,14},{7,15},{8,0},{9,1},... | collective-permute-start | bytes 393224 | tf_op jit(solution)/shard_map/ppermute | solution.py:28
  4.0 19.2 %collective-permute-start = (bf16[256,1024]{1,0:T(8,128)(2,1)}, bf16[256,1024]{1,0:T(8,128)(2,1)S(1)}, u32[]{:S(2)}, u32[]{:S(2)}) collective-permute-start(bf16[256,1024]{1,0:T(8,128)(2,1)} %param.2), channel_id=1, source_target_pairs={{0,1},{1,0},{2,3},{3,2},{4,5},{5,4},{6,7},{7,6},{8,9},{9,8},{10,11... | collective-permute-start | bytes 1572872 | tf_op jit(solution)/shard_map/ppermute | solution.py:28
  7.5 5.0 %collective-permute-start.2 = (bf16[64,1024]{1,0:T(8,128)(2,1)S(1)}, bf16[64,1024]{1,0:T(8,128)(2,1)S(1)}, u32[]{:S(2)}, u32[]{:S(2)}) collective-permute-start(bf16[64,1024]{1,0:T(8,128)(2,1)S(1)} %get-tuple-element.41), channel_id=1, source_target_pairs={{0,8},{1,9},{2,10},{3,11},{4,12},{5,13},{6,14},{7,15},{8,0},{9,1},... | collective-permute-start | bytes 393224 | tf_op jit(solution)/shard_map/ppermute | solution.py:28
  9.5 11.4 %collective-permute-start.4 = (bf16[64,1024]{1,0:T(8,128)(2,1)S(1)}, bf16[64,1024]{1,0:T(8,128)(2,1)S(1)}, u32[]{:S(2)}, u32[]{:S(2)}) collective-permute-start(bf16[64,1024]{1,0:T(8,128)(2,1)S(1)} %get-tuple-element.20), channel_id=1, source_target_pairs={{0,2},{1,3},{2,0},{3,1},{4,6},{5,7},{6,4},{7,5},{8,10},{9,11},{10,... | collective-permute-start | bytes 393224 | tf_op jit(solution)/shard_map/ppermute | solution.py:28
  12.6 9.8 %collective-permute-start.6 = (bf16[64,1024]{1,0:T(8,128)(2,1)S(1)}, bf16[64,1024]{1,0:T(8,128)(2,1)S(1)}, u32[]{:S(2)}, u32[]{:S(2)}) collective-permute-start(bf16[64,1024]{1,0:T(8,128)(2,1)S(1)} %get-tuple-element.21), channel_id=1, source_target_pairs={{0,2},{1,3},{2,0},{3,1},{4,6},{5,7},{6,4},{7,5},{8,10},{9,11},{10,... | collective-permute-start | bytes 393224 | tf_op jit(solution)/shard_map/ppermute | solution.py:28
  15.5 12.6 %collective-permute-start.3 = (bf16[128,1024]{1,0:T(8,128)(2,1)S(1)}, bf16[128,1024]{1,0:T(8,128)(2,1)S(1)}, u32[]{:S(2)}, u32[]{:S(2)}) collective-permute-start(bf16[128,1024]{1,0:T(8,128)(2,1)S(1)} %pad_maximum_fusion), channel_id=1, source_target_pairs={{0,4},{1,5},{2,6},{3,7},{4,0},{5,1},{6,2},{7,3},{8,12},{9,13},{10,... | collective-permute-start | bytes 786440 | tf_op jit(solution)/shard_map/ppermute | solution.py:28
  21.0 3.0 %collective-permute-start.5 = (bf16[64,1024]{1,0:T(8,128)(2,1)S(1)}, bf16[64,1024]{1,0:T(8,128)(2,1)S(1)}, u32[]{:S(2)}, u32[]{:S(2)}) collective-permute-start(bf16[64,1024]{1,0:T(8,128)(2,1)S(1)} %collective-permute-done.4), channel_id=1, source_target_pairs={{0,4},{1,5},{2,6},{3,7},{4,0},{5,1},{6,2},{7,3},{8,12},{9,13},{10,... | collective-permute-start | bytes 393224 | tf_op jit(solution)/shard_map/ppermute | solution.py:28
  22.4 1.6 %collective-permute-start.7 = (bf16[64,1024]{1,0:T(8,128)(2,1)S(1)}, bf16[64,1024]{1,0:T(8,128)(2,1)S(1)}, u32[]{:S(2)}, u32[]{:S(2)}) collective-permute-start(bf16[64,1024]{1,0:T(8,128)(2,1)S(1)} %collective-permute-done.6), channel_id=1, source_target_pairs={{0,4},{1,5},{2,6},{3,7},{4,0},{5,1},{6,2},{7,3},{8,12},{9,13},{10,... | collective-permute-start | bytes 393224 | tf_op jit(solution)/shard_map/ppermute | solution.py:28
  24.8 5.8 %collective-permute-start.8 = (f16[264,128]{1,0:T(8,128)(2,1)S(1)}, f16[264,128]{1,0:T(8,128)(2,1)S(1)}, u32[]{:S(2)}, u32[]{:S(2)}) collective-permute-start(f16[264,128]{1,0:T(8,128)(2,1)S(1)} %concatenate.15), channel_id=1, source_target_pairs={{0,2},{1,3},{2,0},{3,1},{4,6},{5,7},{6,4},{7,5},{8,10},{9,11},{10,... | collective-permute-start | bytes 202760 | tf_op jit(solution)/shard_map/ppermute | solution.py:28

commit v20 on v19

--- a/solution.py
+++ b/solution.py
@@ -60,7 +60,7 @@
         return moved(block, side, lambda r, c: (r ^ 1, c))
 
     nears, crosses = [], []
-    for half in (right_docs[:width // 2], right_docs[width // 2:]):
+    for half in lax.optimization_barrier((right_docs[:width // 2], right_docs[width // 2:])):
         swapped = moved(half, side, lambda r, c: (r ^ 2, c))
         near, leaving = lax.optimization_barrier((jnp.where(at_home, half, swapped), jnp.where(at_home, swapped, half)))
         nears.append(near)

time: 31.8 us -> 32.2 us (1.013)
  waiting for transfers between devices: 11.4 us -> 13.4 us
  starting transfers between devices: 15.4 us -> 14 us
    ppermute x9, waiting for transfers between devices: 11.4 us -> 13.4 us  [moved(): return lax.ppermute(value, ('row', 'col'), pairs)]
    ppermute x9, starting transfers between devices: 15.4 us -> 14 us  [moved(): return lax.ppermute(value, ('row', 'col'), pairs)]
  transfers between devices with their start and end apart: 9 -> 9, of which waited for: 6 -> 5; matrix products, arithmetic and copies ran while one was open for 8% -> 8% of each run, Pallas kernels for 0% -> 0%
where the time goes in v20:
time: 32.2 us; the launch traced here: 32.1 us
  starting transfers between devices  14 us (43%)
  waiting for transfers between devices  13.4 us (42%)
  other arithmetic  2.16 us (7%)
  matrix products  1.2 us (4%)
  local copies, waits for them, and re-layouts  1.12 us (3%)
    ppermute x9, starting transfers between devices, moved(): return lax.ppermute(value, ('row', 'col'), pairs)  14 us
    ppermute x9, waiting for transfers between devices, moved(): return lax.ppermute(value, ('row', 'col'), pairs)  13.4 us
    dot_general x4, matrix products, contract(): lax.dot_general(left_part, right_part, (((1,), (1,)), ((), ())), preferre...  1.2 us
    slice x1, local copies, waits for them, and re-layouts, on_square_grid(): right_docs[width // 2:]  1.04 us
    reduce_sum x5, other arithmetic, squares(): return jnp.sum(widened * widened, axis=1)  0.81 us
    mul x3, other arithmetic, finish(): return summed / feat_total * left_scale[:, None] * right_scale[None, :]  0.81 us
  transfers between devices with their start and end apart: 9, of which 5 were waited for; matrix products, arithmetic and copies ran while one was open for 8% of the time, Pallas kernels for 0%

profile of v20, /device:TPU:0, one launch (start us, length us, event | category | flops | bytes accessed | tf_op | source)
XLA Modules:
  0.0 32.1 jit_solution(4035242905345407212)
XLA Ops:
  0.0 1.0 %fusion.41 = (bf16[64,1024]{1,0:T(8,128)(2,1)S(1)}, bf16[64,1024]{1,0:T(8,128)(2,1)S(1)}) fusion(bf16[128,1024]{1,0:T(8,128)(2,1)} %param.3), kind=kLoop, calls=%fused_computation.76 | loop fusion | bytes 524288 | tf_op jit(solution)/shard_map/slice | solution.py:63
  1.0 3.0 %collective-permute-start.1 = (bf16[64,1024]{1,0:T(8,128)(2,1)S(1)}, bf16[64,1024]{1,0:T(8,128)(2,1)S(1)}, u32[]{:S(2)}, u32[]{:S(2)}) collective-permute-start(bf16[64,1024]{1,0:T(8,128)(2,1)S(1)} %get-tuple-element.19), channel_id=1, source_target_pairs={{0,8},{1,9},{2,10},{3,11},{4,12},{5,13},{6,14},{7,15},{8,0},{9,1},... | collective-permute-start | bytes 393224 | tf_op jit(solution)/shard_map/ppermute | solution.py:28
  4.1 2.0 %collective-permute-start = (bf16[256,1024]{1,0:T(8,128)(2,1)S(1)}, bf16[256,1024]{1,0:T(8,128)(2,1)S(1)}, u32[]{:S(2)}, u32[]{:S(2)}) collective-permute-start(bf16[256,1024]{1,0:T(8,128)(2,1)S(1)} %copy-done), channel_id=1, source_target_pairs={{0,1},{1,0},{2,3},{3,2},{4,5},{5,4},{6,7},{7,6},{8,9},{9,8},{10,11... | collective-permute-start | bytes 1572872 | tf_op jit(solution)/shard_map/ppermute | solution.py:28
  6.2 2.2 %collective-permute-done.1 = bf16[64,1024]{1,0:T(8,128)(2,1)S(1)} collective-permute-done((bf16[64,1024]{1,0:T(8,128)(2,1)S(1)}, bf16[64,1024]{1,0:T(8,128)(2,1)S(1)}, u32[]{:S(2)}, u32[]{:S(2)}) %collective-permute-start.1) | collective-permute-done | bytes 131104 | tf_op jit(solution)/shard_map/ppermute | solution.py:28
  8.4 3.2 %collective-permute-start.4 = (bf16[64,1024]{1,0:T(8,128)(2,1)S(1)}, bf16[64,1024]{1,0:T(8,128)(2,1)S(1)}, u32[]{:S(2)}, u32[]{:S(2)}) collective-permute-start(bf16[64,1024]{1,0:T(8,128)(2,1)S(1)} %get-tuple-element.24), channel_id=1, source_target_pairs={{0,2},{1,3},{2,0},{3,1},{4,6},{5,7},{6,4},{7,5},{8,10},{9,11},{10,... | collective-permute-start | bytes 393224 | tf_op jit(solution)/shard_map/ppermute | solution.py:28
  11.7 1.6 %collective-permute-start.6 = (bf16[64,1024]{1,0:T(8,128)(2,1)S(1)}, bf16[64,1024]{1,0:T(8,128)(2,1)S(1)}, u32[]{:S(2)}, u32[]{:S(2)}) collective-permute-start(bf16[64,1024]{1,0:T(8,128)(2,1)S(1)} %get-tuple-element.25), channel_id=1, source_target_pairs={{0,2},{1,3},{2,0},{3,1},{4,6},{5,7},{6,4},{7,5},{8,10},{9,11},{10,... | collective-permute-start | bytes 393224 | tf_op jit(solution)/shard_map/ppermute | solution.py:28
  13.3 0.2 multiply_reduce_fusion.1
  13.5 7.5 %collective-permute-done.4 = bf16[64,1024]{1,0:T(8,128)(2,1)S(1)} collective-permute-done((bf16[64,1024]{1,0:T(8,128)(2,1)S(1)}, bf16[64,1024]{1,0:T(8,128)(2,1)S(1)}, u32[]{:S(2)}, u32[]{:S(2)}) %collective-permute-start.4) | collective-permute-done | bytes 131104 | tf_op jit(solution)/shard_map/ppermute | solution.py:28
  21.0 1.4 %collective-permute-done.6 = bf16[64,1024]{1,0:T(8,128)(2,1)S(1)} collective-permute-done((bf16[64,1024]{1,0:T(8,128)(2,1)S(1)}, bf16[64,1024]{1,0:T(8,128)(2,1)S(1)}, u32[]{:S(2)}, u32[]{:S(2)}) %collective-permute-start.6) | collective-permute-done | bytes 131104 | tf_op jit(solution)/shard_map/ppermute | solution.py:28
  22.4 0.1 multiply_reduce_fusion.3
  22.5 0.6 %collective-permute-start.3 = (bf16[128,1024]{1,0:T(8,128)(2,1)S(1)}, bf16[128,1024]{1,0:T(8,128)(2,1)S(1)}, u32[]{:S(2)}, u32[]{:S(2)}) collective-permute-start(bf16[128,1024]{1,0:T(8,128)(2,1)S(1)} %pad_maximum_fusion), channel_id=1, source_target_pairs={{0,4},{1,5},{2,6},{3,7},{4,0},{5,1},{6,2},{7,3},{8,12},{9,13},{10,... | collective-permute-start | bytes 786440 | tf_op jit(solution)/shard_map/ppermute | solution.py:28
  23.1 0.6 %collective-permute-done.7 = bf16[64,1024]{1,0:T(8,128)(2,1)S(1)} collective-permute-done((bf16[64,1024]{1,0:T(8,128)(2,1)S(1)}, bf16[64,1024]{1,0:T(8,128)(2,1)S(1)}, u32[]{:S(2)}, u32[]{:S(2)}) %collective-permute-start.7) | collective-permute-done | bytes 131104 | tf_op jit(solution)/shard_map/ppermute | solution.py:28
  23.8 0.2 multiply_reduce_fusion
  24.1 0.1 broadcast_select_fusion
  24.2 0.3 fusion.42
  24.5 0.2 multiply_reduce_fusion.4
  24.8 0.3 fusion.43
  25.1 0.1 multiply_convert_fusion
  25.3 3.4 %collective-permute-start.8 = (f16[264,128]{1,0:T(8,128)(2,1)S(1)}, f16[264,128]{1,0:T(8,128)(2,1)S(1)}, u32[]{:S(2)}, u32[]{:S(2)}) collective-permute-start(f16[264,128]{1,0:T(8,128)(2,1)S(1)} %concatenate.15), channel_id=1, source_target_pairs={{0,2},{1,3},{2,0},{3,1},{4,6},{5,7},{6,4},{7,5},{8,10},{9,11},{10,... | collective-permute-start | bytes 202760 | tf_op jit(solution)/shard_map/ppermute | solution.py:28
  28.7 0.3 fusion.44
  29.0 0.3 convolution_add_fusion
  29.3 0.1 multiply_reduce_fusion.2
  29.5 1.7 %collective-permute-done.8 = f16[264,128]{1,0:T(8,128)(2,1)S(1)} collective-permute-done((f16[264,128]{1,0:T(8,128)(2,1)S(1)}, f16[264,128]{1,0:T(8,128)(2,1)S(1)}, u32[]{:S(2)}, u32[]{:S(2)}) %collective-permute-start.8) | collective-permute-done | bytes 67616 | tf_op jit(solution)/shard_map/ppermute | solution.py:28
  31.3 0.8 %fusion.3 = f32[256,128]{1,0:T(8,128)} fusion(f32[256,128]{1,0:T(8,128)S(1)} %convolution_add_fusion, f32[264,128]{1,0:T(8,128)S(1)} %convert_element_type.61, f32[128]{0:T(128)S(1)} %rsqrt_bitcast_fusion, f32[256]{0:T(256)S(1)} %fusion.24, f32[128]{0:T(128)S(1)} %get-tuple-element.33, f32[256]{0:T(256)S(1)} %get-tuple-element.31), kind=kLoop, calls=%fused_computation.16 | loop fusion | flops 163840 | bytes 396288 | tf_op jit(solution)/shard_map/mul | solution.py:34
  (27 shorter events, 0.5 us)
Async XLA Ops:
  0.0 4.1 %copy-start = (bf16[256,1024]{1,0:T(8,128)(2,1)S(1)}, bf16[256,1024]{1,0:T(8,128)(2,1)}, u32[]{:S(2)}) copy-start(bf16[256,1024]{1,0:T(8,128)(2,1)} %param.2) | copy-start | bytes 1572868
  1.0 7.3 %collective-permute-start.1 = (bf16[64,1024]{1,0:T(8,128)(2,1)S(1)}, bf16[64,1024]{1,0:T(8,128)(2,1)S(1)}, u32[]{:S(2)}, u32[]{:S(2)}) collective-permute-start(bf16[64,1024]{1,0:T(8,128)(2,1)S(1)} %get-tuple-element.19), channel_id=1, source_target_pairs={{0,8},{1,9},{2,10},{3,11},{4,12},{5,13},{6,14},{7,15},{8,0},{9,1},... | collective-permute-start | bytes 393224 | tf_op jit(solution)/shard_map/ppermute | solution.py:28
  4.1 7.6 %collective-permute-start.2 = (bf16[64,1024]{1,0:T(8,128)(2,1)S(1)}, bf16[64,1024]{1,0:T(8,128)(2,1)S(1)}, u32[]{:S(2)}, u32[]{:S(2)}) collective-permute-start(bf16[64,1024]{1,0:T(8,128)(2,1)S(1)} %get-tuple-element.21), channel_id=1, source_target_pairs={{0,8},{1,9},{2,10},{3,11},{4,12},{5,13},{6,14},{7,15},{8,0},{9,1},... | collective-permute-start | bytes 393224 | tf_op jit(solution)/shard_map/ppermute | solution.py:28
  4.1 19.6 %collective-permute-start = (bf16[256,1024]{1,0:T(8,128)(2,1)S(1)}, bf16[256,1024]{1,0:T(8,128)(2,1)S(1)}, u32[]{:S(2)}, u32[]{:S(2)}) collective-permute-start(bf16[256,1024]{1,0:T(8,128)(2,1)S(1)} %copy-done), channel_id=1, source_target_pairs={{0,1},{1,0},{2,3},{3,2},{4,5},{5,4},{6,7},{7,6},{8,9},{9,8},{10,11... | collective-permute-start | bytes 1572872 | tf_op jit(solution)/shard_map/ppermute | solution.py:28
  8.4 12.6 %collective-permute-start.4 = (bf16[64,1024]{1,0:T(8,128)(2,1)S(1)}, bf16[64,1024]{1,0:T(8,128)(2,1)S(1)}, u32[]{:S(2)}, u32[]{:S(2)}) collective-permute-start(bf16[64,1024]{1,0:T(8,128)(2,1)S(1)} %get-tuple-element.24), channel_id=1, source_target_pairs={{0,2},{1,3},{2,0},{3,1},{4,6},{5,7},{6,4},{7,5},{8,10},{9,11},{10,... | collective-permute-start | bytes 393224 | tf_op jit(solution)/shard_map/ppermute | solution.py:28
  11.7 10.8 %collective-permute-start.6 = (bf16[64,1024]{1,0:T(8,128)(2,1)S(1)}, bf16[64,1024]{1,0:T(8,128)(2,1)S(1)}, u32[]{:S(2)}, u32[]{:S(2)}) collective-permute-start(bf16[64,1024]{1,0:T(8,128)(2,1)S(1)} %get-tuple-element.25), channel_id=1, source_target_pairs={{0,2},{1,3},{2,0},{3,1},{4,6},{5,7},{6,4},{7,5},{8,10},{9,11},{10,... | collective-permute-start | bytes 393224 | tf_op jit(solution)/shard_map/ppermute | solution.py:28
  21.0 2.1 %collective-permute-start.5 = (bf16[64,1024]{1,0:T(8,128)(2,1)S(1)}, bf16[64,1024]{1,0:T(8,128)(2,1)S(1)}, u32[]{:S(2)}, u32[]{:S(2)}) collective-permute-start(bf16[64,1024]{1,0:T(8,128)(2,1)S(1)} %collective-permute-done.4), channel_id=1, source_target_pairs={{0,4},{1,5},{2,6},{3,7},{4,0},{5,1},{6,2},{7,3},{8,12},{9,13},{10,... | collective-permute-start | bytes 393224 | tf_op jit(solution)/shard_map/ppermute | solution.py:28
  22.4 1.3 %collective-permute-start.7 = (bf16[64,1024]{1,0:T(8,128)(2,1)S(1)}, bf16[64,1024]{1,0:T(8,128)(2,1)S(1)}, u32[]{:S(2)}, u32[]{:S(2)}) collective-permute-start(bf16[64,1024]{1,0:T(8,128)(2,1)S(1)} %collective-permute-done.6), channel_id=1, source_target_pairs={{0,4},{1,5},{2,6},{3,7},{4,0},{5,1},{6,2},{7,3},{8,12},{9,13},{10,... | collective-permute-start | bytes 393224 | tf_op jit(solution)/shard_map/ppermute | solution.py:28
  22.5 6.2 %collective-permute-start.3 = (bf16[128,1024]{1,0:T(8,128)(2,1)S(1)}, bf16[128,1024]{1,0:T(8,128)(2,1)S(1)}, u32[]{:S(2)}, u32[]{:S(2)}) collective-permute-start(bf16[128,1024]{1,0:T(8,128)(2,1)S(1)} %pad_maximum_fusion), channel_id=1, source_target_pairs={{0,4},{1,5},{2,6},{3,7},{4,0},{5,1},{6,2},{7,3},{8,12},{9,13},{10,... | collective-permute-start | bytes 786440 | tf_op jit(solution)/shard_map/ppermute | solution.py:28
  25.3 5.9 %collective-permute-start.8 = (f16[264,128]{1,0:T(8,128)(2,1)S(1)}, f16[264,128]{1,0:T(8,128)(2,1)S(1)}, u32[]{:S(2)}, u32[]{:S(2)}) collective-permute-start(f16[264,128]{1,0:T(8,128)(2,1)S(1)} %concatenate.15), channel_id=1, source_target_pairs={{0,2},{1,3},{2,0},{3,1},{4,6},{5,7},{6,4},{7,5},{8,10},{9,11},{10,... | collective-permute-start | bytes 202760 | tf_op jit(solution)/shard_map/ppermute | solution.py:28

commit v21 on v20

--- a/solution.py
+++ b/solution.py
@@ -66,14 +66,16 @@
         nears.append(near)
         crosses.append(moved(leaving, side, lambda r, c: (r, c ^ 2)))
     left_other = moved(left_docs, side, lambda r, c: (r, c ^ 1))
-    near, cross = lax.optimization_barrier(jnp.concatenate(nears)), lax.optimization_barrier(jnp.concatenate(crosses))
+    near = lax.optimization_barrier(jnp.concatenate(nears))
+    near_other = other_core(near)
+    crosses[1], near_other = lax.optimization_barrier((crosses[1], near_other))
+    cross = lax.optimization_barrier(jnp.concatenate(crosses))
     lefts = lax.optimization_barrier((jnp.where(same, left_docs, left_other), jnp.where(same, left_other, left_docs)))
 
     def half_sum(mine, other):
         gram = sum(contract(left, right) for left, right in zip(lefts, (mine, other)))
         return gram, squares(mine) + squares(other)
 
-    near_other = other_core(near)
     cross_gram = contract(lefts[0], cross)
     cross_other, cross_gram = lax.optimization_barrier((jnp.concatenate([other_core(part) for part in crosses]), cross_gram))
     cross_gram = cross_gram + contract(lefts[1], cross_other)

time: 32.2 us -> 31.5 us (0.978)
  starting transfers between devices: 14 us -> 13.3 us
    ppermute x9, starting transfers between devices: 14 us -> 13.3 us  [moved(): return lax.ppermute(value, ('row', 'col'), pairs)]
  transfers between devices with their start and end apart: 9 -> 9, of which waited for: 5 -> 5; matrix products, arithmetic and copies ran while one was open for 8% -> 6% of each run, Pallas kernels for 0% -> 0%
where the time goes in v21:
time: 31.5 us; the launch traced here: 31.3 us
  waiting for transfers between devices  13.4 us (43%)
  starting transfers between devices  13.3 us (42%)
  other arithmetic  2.16 us (7%)
  matrix products  1.21 us (4%)
  local copies, waits for them, and re-layouts  1.12 us (4%)
    ppermute x9, waiting for transfers between devices, moved(): return lax.ppermute(value, ('row', 'col'), pairs)  13.4 us
    ppermute x9, starting transfers between devices, moved(): return lax.ppermute(value, ('row', 'col'), pairs)  13.3 us
    dot_general x4, matrix products, contract(): lax.dot_general(left_part, right_part, (((1,), (1,)), ((), ())), preferre...  1.21 us
    slice x1, local copies, waits for them, and re-layouts, on_square_grid(): right_docs[width // 2:]  1.04 us
    reduce_sum x5, other arithmetic, squares(): return jnp.sum(widened * widened, axis=1)  0.82 us
    mul x3, other arithmetic, finish(): return summed / feat_total * left_scale[:, None] * right_scale[None, :]  0.81 us
  transfers between devices with their start and end apart: 9, of which 5 were waited for; matrix products, arithmetic and copies ran while one was open for 6% of the time, Pallas kernels for 0%

profile of v21, /device:TPU:0, one launch (start us, length us, event | category | flops | bytes accessed | tf_op | source)
XLA Modules:
  0.0 31.3 jit_solution(9536228982384497922)
XLA Ops:
  0.0 1.0 %fusion.41 = (bf16[64,1024]{1,0:T(8,128)(2,1)S(1)}, bf16[64,1024]{1,0:T(8,128)(2,1)S(1)}) fusion(bf16[128,1024]{1,0:T(8,128)(2,1)} %param.3), kind=kLoop, calls=%fused_computation.76 | loop fusion | bytes 524288 | tf_op jit(solution)/shard_map/slice | solution.py:63
  1.0 3.0 %collective-permute-start.1 = (bf16[64,1024]{1,0:T(8,128)(2,1)S(1)}, bf16[64,1024]{1,0:T(8,128)(2,1)S(1)}, u32[]{:S(2)}, u32[]{:S(2)}) collective-permute-start(bf16[64,1024]{1,0:T(8,128)(2,1)S(1)} %get-tuple-element.21), channel_id=1, source_target_pairs={{0,8},{1,9},{2,10},{3,11},{4,12},{5,13},{6,14},{7,15},{8,0},{9,1},... | collective-permute-start | bytes 393224 | tf_op jit(solution)/shard_map/ppermute | solution.py:28
  4.1 0.1 collective-permute-start.2
  4.1 2.0 %collective-permute-start = (bf16[256,1024]{1,0:T(8,128)(2,1)S(1)}, bf16[256,1024]{1,0:T(8,128)(2,1)S(1)}, u32[]{:S(2)}, u32[]{:S(2)}) collective-permute-start(bf16[256,1024]{1,0:T(8,128)(2,1)S(1)} %copy-done), channel_id=1, source_target_pairs={{0,1},{1,0},{2,3},{3,2},{4,5},{5,4},{6,7},{7,6},{8,9},{9,8},{10,11... | collective-permute-start | bytes 1572872 | tf_op jit(solution)/shard_map/ppermute | solution.py:28
  6.2 2.2 %collective-permute-done.1 = bf16[64,1024]{1,0:T(8,128)(2,1)S(1)} collective-permute-done((bf16[64,1024]{1,0:T(8,128)(2,1)S(1)}, bf16[64,1024]{1,0:T(8,128)(2,1)S(1)}, u32[]{:S(2)}, u32[]{:S(2)}) %collective-permute-start.1) | collective-permute-done | bytes 131104 | tf_op jit(solution)/shard_map/ppermute | solution.py:28
  8.4 3.2 %collective-permute-start.5 = (bf16[64,1024]{1,0:T(8,128)(2,1)S(1)}, bf16[64,1024]{1,0:T(8,128)(2,1)S(1)}, u32[]{:S(2)}, u32[]{:S(2)}) collective-permute-start(bf16[64,1024]{1,0:T(8,128)(2,1)S(1)} %get-tuple-element.28), channel_id=1, source_target_pairs={{0,2},{1,3},{2,0},{3,1},{4,6},{5,7},{6,4},{7,5},{8,10},{9,11},{10,... | collective-permute-start | bytes 393224 | tf_op jit(solution)/shard_map/ppermute | solution.py:28
  11.7 1.6 %collective-permute-start.3 = (bf16[64,1024]{1,0:T(8,128)(2,1)S(1)}, bf16[64,1024]{1,0:T(8,128)(2,1)S(1)}, u32[]{:S(2)}, u32[]{:S(2)}) collective-permute-start(bf16[64,1024]{1,0:T(8,128)(2,1)S(1)} %get-tuple-element.26), channel_id=1, source_target_pairs={{0,2},{1,3},{2,0},{3,1},{4,6},{5,7},{6,4},{7,5},{8,10},{9,11},{10,... | collective-permute-start | bytes 393224 | tf_op jit(solution)/shard_map/ppermute | solution.py:28
  13.3 0.2 multiply_reduce_fusion.1
  13.5 0.1 multiply_reduce_fusion.3
  13.6 7.4 %collective-permute-done.5 = bf16[64,1024]{1,0:T(8,128)(2,1)S(1)} collective-permute-done((bf16[64,1024]{1,0:T(8,128)(2,1)S(1)}, bf16[64,1024]{1,0:T(8,128)(2,1)S(1)}, u32[]{:S(2)}, u32[]{:S(2)}) %collective-permute-start.5) | collective-permute-done | bytes 131104 | tf_op jit(solution)/shard_map/ppermute | solution.py:28
  21.0 1.4 %collective-permute-done.3 = bf16[64,1024]{1,0:T(8,128)(2,1)S(1)} collective-permute-done((bf16[64,1024]{1,0:T(8,128)(2,1)S(1)}, bf16[64,1024]{1,0:T(8,128)(2,1)S(1)}, u32[]{:S(2)}, u32[]{:S(2)}) %collective-permute-start.3) | collective-permute-done | bytes 131104 | tf_op jit(solution)/shard_map/ppermute | solution.py:28
  22.4 0.7 %collective-permute-done = bf16[256,1024]{1,0:T(8,128)(2,1)S(1)} collective-permute-done((bf16[256,1024]{1,0:T(8,128)(2,1)S(1)}, bf16[256,1024]{1,0:T(8,128)(2,1)S(1)}, u32[]{:S(2)}, u32[]{:S(2)}) %collective-permute-start) | collective-permute-done | bytes 524320 | tf_op jit(solution)/shard_map/ppermute | solution.py:28
  23.1 0.2 multiply_reduce_fusion
  23.4 0.1 broadcast_select_fusion
  23.5 0.3 fusion.42
  23.9 0.2 multiply_reduce_fusion.4
  24.2 0.3 fusion.43
  24.5 0.1 multiply_convert_fusion
  24.7 3.3 %collective-permute-start.8 = (f16[264,128]{1,0:T(8,128)(2,1)S(1)}, f16[264,128]{1,0:T(8,128)(2,1)S(1)}, u32[]{:S(2)}, u32[]{:S(2)}) collective-permute-start(f16[264,128]{1,0:T(8,128)(2,1)S(1)} %concatenate.15), channel_id=1, source_target_pairs={{0,2},{1,3},{2,0},{3,1},{4,6},{5,7},{6,4},{7,5},{8,10},{9,11},{10,... | collective-permute-start | bytes 202760 | tf_op jit(solution)/shard_map/ppermute | solution.py:28
  28.0 0.3 fusion.44
  28.3 0.3 convolution_add_fusion
  28.6 0.1 multiply_reduce_fusion.2
  28.8 1.7 %collective-permute-done.8 = f16[264,128]{1,0:T(8,128)(2,1)S(1)} collective-permute-done((f16[264,128]{1,0:T(8,128)(2,1)S(1)}, f16[264,128]{1,0:T(8,128)(2,1)S(1)}, u32[]{:S(2)}, u32[]{:S(2)}) %collective-permute-start.8) | collective-permute-done | bytes 67616 | tf_op jit(solution)/shard_map/ppermute | solution.py:28
  30.5 0.8 %fusion.3 = f32[256,128]{1,0:T(8,128)} fusion(f32[256,128]{1,0:T(8,128)S(1)} %convolution_add_fusion, f32[264,128]{1,0:T(8,128)S(1)} %convert_element_type.61, f32[128]{0:T(128)S(1)} %rsqrt_bitcast_fusion, f32[256]{0:T(256)S(1)} %fusion.24, f32[128]{0:T(128)S(1)} %get-tuple-element.37, f32[256]{0:T(256)S(1)} %get-tuple-element.35), kind=kLoop, calls=%fused_computation.16 | loop fusion | flops 163840 | bytes 396288 | tf_op jit(solution)/shard_map/mul | solution.py:34
  (27 shorter events, 0.5 us)
Async XLA Ops:
  0.0 4.1 %copy-start = (bf16[256,1024]{1,0:T(8,128)(2,1)S(1)}, bf16[256,1024]{1,0:T(8,128)(2,1)}, u32[]{:S(2)}) copy-start(bf16[256,1024]{1,0:T(8,128)(2,1)} %param.2) | copy-start | bytes 1572868
  1.0 7.3 %collective-permute-start.1 = (bf16[64,1024]{1,0:T(8,128)(2,1)S(1)}, bf16[64,1024]{1,0:T(8,128)(2,1)S(1)}, u32[]{:S(2)}, u32[]{:S(2)}) collective-permute-start(bf16[64,1024]{1,0:T(8,128)(2,1)S(1)} %get-tuple-element.21), channel_id=1, source_target_pairs={{0,8},{1,9},{2,10},{3,11},{4,12},{5,13},{6,14},{7,15},{8,0},{9,1},... | collective-permute-start | bytes 393224 | tf_op jit(solution)/shard_map/ppermute | solution.py:28
  4.1 7.6 %collective-permute-start.2 = (bf16[64,1024]{1,0:T(8,128)(2,1)S(1)}, bf16[64,1024]{1,0:T(8,128)(2,1)S(1)}, u32[]{:S(2)}, u32[]{:S(2)}) collective-permute-start(bf16[64,1024]{1,0:T(8,128)(2,1)S(1)} %get-tuple-element.23), channel_id=1, source_target_pairs={{0,8},{1,9},{2,10},{3,11},{4,12},{5,13},{6,14},{7,15},{8,0},{9,1},... | collective-permute-start | bytes 393224 | tf_op jit(solution)/shard_map/ppermute | solution.py:28
  4.1 19.0 %collective-permute-start = (bf16[256,1024]{1,0:T(8,128)(2,1)S(1)}, bf16[256,1024]{1,0:T(8,128)(2,1)S(1)}, u32[]{:S(2)}, u32[]{:S(2)}) collective-permute-start(bf16[256,1024]{1,0:T(8,128)(2,1)S(1)} %copy-done), channel_id=1, source_target_pairs={{0,1},{1,0},{2,3},{3,2},{4,5},{5,4},{6,7},{7,6},{8,9},{9,8},{10,11... | collective-permute-start | bytes 1572872 | tf_op jit(solution)/shard_map/ppermute | solution.py:28
  8.4 12.6 %collective-permute-start.5 = (bf16[64,1024]{1,0:T(8,128)(2,1)S(1)}, bf16[64,1024]{1,0:T(8,128)(2,1)S(1)}, u32[]{:S(2)}, u32[]{:S(2)}) collective-permute-start(bf16[64,1024]{1,0:T(8,128)(2,1)S(1)} %get-tuple-element.28), channel_id=1, source_target_pairs={{0,2},{1,3},{2,0},{3,1},{4,6},{5,7},{6,4},{7,5},{8,10},{9,11},{10,... | collective-permute-start | bytes 393224 | tf_op jit(solution)/shard_map/ppermute | solution.py:28
  11.7 10.7 %collective-permute-start.3 = (bf16[64,1024]{1,0:T(8,128)(2,1)S(1)}, bf16[64,1024]{1,0:T(8,128)(2,1)S(1)}, u32[]{:S(2)}, u32[]{:S(2)}) collective-permute-start(bf16[64,1024]{1,0:T(8,128)(2,1)S(1)} %get-tuple-element.26), channel_id=1, source_target_pairs={{0,2},{1,3},{2,0},{3,1},{4,6},{5,7},{6,4},{7,5},{8,10},{9,11},{10,... | collective-permute-start | bytes 393224 | tf_op jit(solution)/shard_map/ppermute | solution.py:28
  13.3 9.1 %collective-permute-start.4 = (bf16[128,1024]{1,0:T(8,128)(2,1)S(1)}, bf16[128,1024]{1,0:T(8,128)(2,1)S(1)}, u32[]{:S(2)}, u32[]{:S(2)}) collective-permute-start(bf16[128,1024]{1,0:T(8,128)(2,1)S(1)} %pad_maximum_fusion), channel_id=1, source_target_pairs={{0,4},{1,5},{2,6},{3,7},{4,0},{5,1},{6,2},{7,3},{8,12},{9,13},{10,... | collective-permute-start | bytes 786440 | tf_op jit(solution)/shard_map/ppermute | solution.py:28
  21.0 2.9 %collective-permute-start.6 = (bf16[64,1024]{1,0:T(8,128)(2,1)S(1)}, bf16[64,1024]{1,0:T(8,128)(2,1)S(1)}, u32[]{:S(2)}, u32[]{:S(2)}) collective-permute-start(bf16[64,1024]{1,0:T(8,128)(2,1)S(1)} %collective-permute-done.5), channel_id=1, source_target_pairs={{0,4},{1,5},{2,6},{3,7},{4,0},{5,1},{6,2},{7,3},{8,12},{9,13},{10,... | collective-permute-start | bytes 393224 | tf_op jit(solution)/shard_map/ppermute | solution.py:28
  22.4 1.5 %collective-permute-start.7 = (bf16[64,1024]{1,0:T(8,128)(2,1)S(1)}, bf16[64,1024]{1,0:T(8,128)(2,1)S(1)}, u32[]{:S(2)}, u32[]{:S(2)}) collective-permute-start(bf16[64,1024]{1,0:T(8,128)(2,1)S(1)} %collective-permute-done.3), channel_id=1, source_target_pairs={{0,4},{1,5},{2,6},{3,7},{4,0},{5,1},{6,2},{7,3},{8,12},{9,13},{10,... | collective-permute-start | bytes 393224 | tf_op jit(solution)/shard_map/ppermute | solution.py:28
  24.7 5.8 %collective-permute-start.8 = (f16[264,128]{1,0:T(8,128)(2,1)S(1)}, f16[264,128]{1,0:T(8,128)(2,1)S(1)}, u32[]{:S(2)}, u32[]{:S(2)}) collective-permute-start(f16[264,128]{1,0:T(8,128)(2,1)S(1)} %concatenate.15), channel_id=1, source_target_pairs={{0,2},{1,3},{2,0},{3,1},{4,6},{5,7},{6,4},{7,5},{8,10},{9,11},{10,... | collective-permute-start | bytes 202760 | tf_op jit(solution)/shard_map/ppermute | solution.py:28

commit v22 on v21

--- a/solution.py
+++ b/solution.py
@@ -67,8 +67,7 @@
         crosses.append(moved(leaving, side, lambda r, c: (r, c ^ 2)))
     left_other = moved(left_docs, side, lambda r, c: (r, c ^ 1))
     near = lax.optimization_barrier(jnp.concatenate(nears))
-    near_other = other_core(near)
-    crosses[1], near_other = lax.optimization_barrier((crosses[1], near_other))
+    crosses[1], left_other = lax.optimization_barrier((crosses[1], left_other))
     cross = lax.optimization_barrier(jnp.concatenate(crosses))
     lefts = lax.optimization_barrier((jnp.where(same, left_docs, left_other), jnp.where(same, left_other, left_docs)))
 
@@ -76,8 +75,9 @@
         gram = sum(contract(left, right) for left, right in zip(lefts, (mine, other)))
         return gram, squares(mine) + squares(other)
 
+    near_other = other_core(near)
     cross_gram = contract(lefts[0], cross)
-    cross_other, cross_gram = lax.optimization_barrier((jnp.concatenate([other_core(part) for part in crosses]), cross_gram))
+    cross_other, cross_gram = lax.optimization_barrier((other_core(cross), cross_gram))
     cross_gram = cross_gram + contract(lefts[1], cross_other)
     cross_sq = squares(cross) + squares(cross_other)
     left_sq = squares(left_docs) + squares(left_other)

time: 31.5 us -> 32.1 us (1.019)
  waiting for transfers between devices: 13.4 us -> 14.5 us
  starting transfers between devices: 13.3 us -> 12.7 us
    ppermute x9 -> x8, waiting for transfers between devices: 13.4 us -> 14.5 us  [moved(): return lax.ppermute(value, ('row', 'col'), pairs)]
    ppermute x9 -> x8, starting transfers between devices: 13.3 us -> 12.7 us  [moved(): return lax.ppermute(value, ('row', 'col'), pairs)]
    reduce_sum x5 -> x6, other arithmetic: 0.82 us -> 0.9 us  [squares(): return jnp.sum(widened * widened, axis=1)]
  transfers between devices with their start and end apart: 9 -> 8, of which waited for: 5 -> 5; matrix products, arithmetic and copies ran while one was open for 6% -> 8% of each run, Pallas kernels for 0% -> 0%
where the time goes in v22:
time: 32.1 us; the launch traced here: 32 us
  waiting for transfers between devices  14.5 us (45%)
  starting transfers between devices  12.7 us (40%)
  other arithmetic  2.22 us (7%)
  matrix products  1.23 us (4%)
  local copies, waits for them, and re-layouts  1.12 us (3%)
    ppermute x8, waiting for transfers between devices, moved(): return lax.ppermute(value, ('row', 'col'), pairs)  14.5 us
    ppermute x8, starting transfers between devices, moved(): return lax.ppermute(value, ('row', 'col'), pairs)  12.7 us
    dot_general x4, matrix products, contract(): lax.dot_general(left_part, right_part, (((1,), (1,)), ((), ())), preferre...  1.23 us
    slice x1, local copies, waits for them, and re-layouts, on_square_grid(): right_docs[width // 2:]  1.04 us
    reduce_sum x6, other arithmetic, squares(): return jnp.sum(widened * widened, axis=1)  0.9 us
    mul x3, other arithmetic, finish(): return summed / feat_total * left_scale[:, None] * right_scale[None, :]  0.81 us
  transfers between devices with their start and end apart: 8, of which 5 were waited for; matrix products, arithmetic and copies ran while one was open for 8% of the time, Pallas kernels for 0%

profile of v22, /device:TPU:0, one launch (start us, length us, event | category | flops | bytes accessed | tf_op | source)
XLA Modules:
  0.0 32.0 jit_solution(10936083329503645744)
XLA Ops:
  0.0 1.0 %fusion.41 = (bf16[64,1024]{1,0:T(8,128)(2,1)S(1)}, bf16[64,1024]{1,0:T(8,128)(2,1)S(1)}) fusion(bf16[128,1024]{1,0:T(8,128)(2,1)} %param.3), kind=kLoop, calls=%fused_computation.75 | loop fusion | bytes 524288 | tf_op jit(solution)/shard_map/slice | solution.py:63
  1.0 3.0 %collective-permute-start = (bf16[64,1024]{1,0:T(8,128)(2,1)S(1)}, bf16[64,1024]{1,0:T(8,128)(2,1)S(1)}, u32[]{:S(2)}, u32[]{:S(2)}) collective-permute-start(bf16[64,1024]{1,0:T(8,128)(2,1)S(1)} %get-tuple-element.20), channel_id=1, source_target_pairs={{0,8},{1,9},{2,10},{3,11},{4,12},{5,13},{6,14},{7,15},{8,0},{9,1},... | collective-permute-start | bytes 393224 | tf_op jit(solution)/shard_map/ppermute | solution.py:28
  4.1 1.6 %collective-permute-start.2 = (bf16[256,1024]{1,0:T(8,128)(2,1)S(1)}, bf16[256,1024]{1,0:T(8,128)(2,1)S(1)}, u32[]{:S(2)}, u32[]{:S(2)}) collective-permute-start(bf16[256,1024]{1,0:T(8,128)(2,1)S(1)} %copy-done), channel_id=1, source_target_pairs={{0,1},{1,0},{2,3},{3,2},{4,5},{5,4},{6,7},{7,6},{8,9},{9,8},{10,11... | collective-permute-start | bytes 1572872 | tf_op jit(solution)/shard_map/ppermute | solution.py:28
  5.6 0.5 %collective-permute-start.3 = (bf16[64,1024]{1,0:T(8,128)(2,1)S(1)}, bf16[64,1024]{1,0:T(8,128)(2,1)S(1)}, u32[]{:S(2)}, u32[]{:S(2)}) collective-permute-start(bf16[64,1024]{1,0:T(8,128)(2,1)S(1)} %get-tuple-element.24), channel_id=1, source_target_pairs={{0,8},{1,9},{2,10},{3,11},{4,12},{5,13},{6,14},{7,15},{8,0},{9,1},... | collective-permute-start | bytes 393224 | tf_op jit(solution)/shard_map/ppermute | solution.py:28
  6.2 0.2 multiply_reduce_fusion.1
  6.3 1.6 %collective-permute-done = bf16[64,1024]{1,0:T(8,128)(2,1)S(1)} collective-permute-done((bf16[64,1024]{1,0:T(8,128)(2,1)S(1)}, bf16[64,1024]{1,0:T(8,128)(2,1)S(1)}, u32[]{:S(2)}, u32[]{:S(2)}) %collective-permute-start) | collective-permute-done | bytes 131104 | tf_op jit(solution)/shard_map/ppermute | solution.py:28
  8.0 2.7 %collective-permute-start.1 = (bf16[64,1024]{1,0:T(8,128)(2,1)S(1)}, bf16[64,1024]{1,0:T(8,128)(2,1)S(1)}, u32[]{:S(2)}, u32[]{:S(2)}) collective-permute-start(bf16[64,1024]{1,0:T(8,128)(2,1)S(1)} %get-tuple-element.21), channel_id=1, source_target_pairs={{0,2},{1,3},{2,0},{3,1},{4,6},{5,7},{6,4},{7,5},{8,10},{9,11},{10,... | collective-permute-start | bytes 393224 | tf_op jit(solution)/shard_map/ppermute | solution.py:28
  10.8 2.5 %collective-permute-start.5 = (bf16[64,1024]{1,0:T(8,128)(2,1)S(1)}, bf16[64,1024]{1,0:T(8,128)(2,1)S(1)}, u32[]{:S(2)}, u32[]{:S(2)}) collective-permute-start(bf16[64,1024]{1,0:T(8,128)(2,1)S(1)} %get-tuple-element.28), channel_id=1, source_target_pairs={{0,2},{1,3},{2,0},{3,1},{4,6},{5,7},{6,4},{7,5},{8,10},{9,11},{10,... | collective-permute-start | bytes 393224 | tf_op jit(solution)/shard_map/ppermute | solution.py:28
  13.4 0.1 multiply_reduce_fusion.3
  13.5 7.3 %collective-permute-done.1 = bf16[64,1024]{1,0:T(8,128)(2,1)S(1)} collective-permute-done((bf16[64,1024]{1,0:T(8,128)(2,1)S(1)}, bf16[64,1024]{1,0:T(8,128)(2,1)S(1)}, u32[]{:S(2)}, u32[]{:S(2)}) %collective-permute-start.1) | collective-permute-done | bytes 131104 | tf_op jit(solution)/shard_map/ppermute | solution.py:28
  20.8 2.3 %collective-permute-done.2 = bf16[256,1024]{1,0:T(8,128)(2,1)S(1)} collective-permute-done((bf16[256,1024]{1,0:T(8,128)(2,1)S(1)}, bf16[256,1024]{1,0:T(8,128)(2,1)S(1)}, u32[]{:S(2)}, u32[]{:S(2)}) %collective-permute-start.2) | collective-permute-done | bytes 524320 | tf_op jit(solution)/shard_map/ppermute | solution.py:28
  23.1 0.2 multiply_reduce_fusion
  23.6 0.3 fusion.43
  23.9 0.1 multiply_reduce_fusion.5
  24.0 0.3 fusion.42
  24.4 0.8 %collective-permute-done.6 = bf16[128,1024]{1,0:T(8,128)(2,1)S(1)} collective-permute-done((bf16[128,1024]{1,0:T(8,128)(2,1)S(1)}, bf16[128,1024]{1,0:T(8,128)(2,1)S(1)}, u32[]{:S(2)}, u32[]{:S(2)}) %collective-permute-start.6) | collective-permute-done | bytes 262176 | tf_op jit(solution)/shard_map/ppermute | solution.py:28
  25.1 0.1 multiply_reduce_fusion.4
  25.3 0.3 fusion.44
  25.7 0.1 multiply_convert_fusion
  25.9 2.2 %collective-permute-start.7 = (f16[264,128]{1,0:T(8,128)(2,1)S(1)}, f16[264,128]{1,0:T(8,128)(2,1)S(1)}, u32[]{:S(2)}, u32[]{:S(2)}) collective-permute-start(f16[264,128]{1,0:T(8,128)(2,1)S(1)} %concatenate.11), channel_id=1, source_target_pairs={{0,2},{1,3},{2,0},{3,1},{4,6},{5,7},{6,4},{7,5},{8,10},{9,11},{10,... | collective-permute-start | bytes 202760 | tf_op jit(solution)/shard_map/ppermute | solution.py:28
  28.1 0.3 convolution_add_fusion
  28.4 0.1 multiply_reduce_fusion.2
  28.5 2.6 %collective-permute-done.7 = f16[264,128]{1,0:T(8,128)(2,1)S(1)} collective-permute-done((f16[264,128]{1,0:T(8,128)(2,1)S(1)}, f16[264,128]{1,0:T(8,128)(2,1)S(1)}, u32[]{:S(2)}, u32[]{:S(2)}) %collective-permute-start.7) | collective-permute-done | bytes 67616 | tf_op jit(solution)/shard_map/ppermute | solution.py:28
  31.2 0.8 %fusion.3 = f32[256,128]{1,0:T(8,128)} fusion(f32[256,128]{1,0:T(8,128)S(1)} %convolution_add_fusion, f32[264,128]{1,0:T(8,128)S(1)} %convert_element_type.61, f32[128]{0:T(128)S(1)} %rsqrt_bitcast_fusion, f32[256]{0:T(256)S(1)} %fusion.24, f32[128]{0:T(128)S(1)} %get-tuple-element.37, f32[256]{0:T(256)S(1)} %get-tuple-element.35), kind=kLoop, calls=%fused_computation.15 | loop fusion | flops 163840 | bytes 396288 | tf_op jit(solution)/shard_map/mul | solution.py:34
  (25 shorter events, 0.7 us)
Async XLA Ops:
  0.0 4.1 %copy-start = (bf16[256,1024]{1,0:T(8,128)(2,1)S(1)}, bf16[256,1024]{1,0:T(8,128)(2,1)}, u32[]{:S(2)}) copy-start(bf16[256,1024]{1,0:T(8,128)(2,1)} %param.2) | copy-start | bytes 1572868
  1.0 6.9 %collective-permute-start = (bf16[64,1024]{1,0:T(8,128)(2,1)S(1)}, bf16[64,1024]{1,0:T(8,128)(2,1)S(1)}, u32[]{:S(2)}, u32[]{:S(2)}) collective-permute-start(bf16[64,1024]{1,0:T(8,128)(2,1)S(1)} %get-tuple-element.20), channel_id=1, source_target_pairs={{0,8},{1,9},{2,10},{3,11},{4,12},{5,13},{6,14},{7,15},{8,0},{9,1},... | collective-permute-start | bytes 393224 | tf_op jit(solution)/shard_map/ppermute | solution.py:28
  4.1 19.0 %collective-permute-start.2 = (bf16[256,1024]{1,0:T(8,128)(2,1)S(1)}, bf16[256,1024]{1,0:T(8,128)(2,1)S(1)}, u32[]{:S(2)}, u32[]{:S(2)}) collective-permute-start(bf16[256,1024]{1,0:T(8,128)(2,1)S(1)} %copy-done), channel_id=1, source_target_pairs={{0,1},{1,0},{2,3},{3,2},{4,5},{5,4},{6,7},{7,6},{8,9},{9,8},{10,11... | collective-permute-start | bytes 1572872 | tf_op jit(solution)/shard_map/ppermute | solution.py:28
  5.6 5.1 %collective-permute-start.3 = (bf16[64,1024]{1,0:T(8,128)(2,1)S(1)}, bf16[64,1024]{1,0:T(8,128)(2,1)S(1)}, u32[]{:S(2)}, u32[]{:S(2)}) collective-permute-start(bf16[64,1024]{1,0:T(8,128)(2,1)S(1)} %get-tuple-element.24), channel_id=1, source_target_pairs={{0,8},{1,9},{2,10},{3,11},{4,12},{5,13},{6,14},{7,15},{8,0},{9,1},... | collective-permute-start | bytes 393224 | tf_op jit(solution)/shard_map/ppermute | solution.py:28
  8.0 12.8 %collective-permute-start.1 = (bf16[64,1024]{1,0:T(8,128)(2,1)S(1)}, bf16[64,1024]{1,0:T(8,128)(2,1)S(1)}, u32[]{:S(2)}, u32[]{:S(2)}) collective-permute-start(bf16[64,1024]{1,0:T(8,128)(2,1)S(1)} %get-tuple-element.21), channel_id=1, source_target_pairs={{0,2},{1,3},{2,0},{3,1},{4,6},{5,7},{6,4},{7,5},{8,10},{9,11},{10,... | collective-permute-start | bytes 393224 | tf_op jit(solution)/shard_map/ppermute | solution.py:28
  10.8 12.7 %collective-permute-start.5 = (bf16[64,1024]{1,0:T(8,128)(2,1)S(1)}, bf16[64,1024]{1,0:T(8,128)(2,1)S(1)}, u32[]{:S(2)}, u32[]{:S(2)}) collective-permute-start(bf16[64,1024]{1,0:T(8,128)(2,1)S(1)} %get-tuple-element.28), channel_id=1, source_target_pairs={{0,2},{1,3},{2,0},{3,1},{4,6},{5,7},{6,4},{7,5},{8,10},{9,11},{10,... | collective-permute-start | bytes 393224 | tf_op jit(solution)/shard_map/ppermute | solution.py:28
  13.3 14.7 %collective-permute-start.4 = (bf16[128,1024]{1,0:T(8,128)(2,1)S(1)}, bf16[128,1024]{1,0:T(8,128)(2,1)S(1)}, u32[]{:S(2)}, u32[]{:S(2)}) collective-permute-start(bf16[128,1024]{1,0:T(8,128)(2,1)S(1)} %pad_maximum_fusion), channel_id=1, source_target_pairs={{0,4},{1,5},{2,6},{3,7},{4,0},{5,1},{6,2},{7,3},{8,12},{9,13},{10,... | collective-permute-start | bytes 786440 | tf_op jit(solution)/shard_map/ppermute | solution.py:28
  23.5 1.6 %collective-permute-start.6 = (bf16[128,1024]{1,0:T(8,128)(2,1)S(1)}, bf16[128,1024]{1,0:T(8,128)(2,1)S(1)}, u32[]{:S(2)}, u32[]{:S(2)}) collective-permute-start(bf16[128,1024]{1,0:T(8,128)(2,1)S(1)} %pad_maximum_fusion.1), channel_id=1, source_target_pairs={{0,4},{1,5},{2,6},{3,7},{4,0},{5,1},{6,2},{7,3},{8,12},{9,13},{10,... | collective-permute-start | bytes 786440 | tf_op jit(solution)/shard_map/ppermute | solution.py:28
  25.9 5.2 %collective-permute-start.7 = (f16[264,128]{1,0:T(8,128)(2,1)S(1)}, f16[264,128]{1,0:T(8,128)(2,1)S(1)}, u32[]{:S(2)}, u32[]{:S(2)}) collective-permute-start(f16[264,128]{1,0:T(8,128)(2,1)S(1)} %concatenate.11), channel_id=1, source_target_pairs={{0,2},{1,3},{2,0},{3,1},{4,6},{5,7},{6,4},{7,5},{8,10},{9,11},{10,... | collective-permute-start | bytes 202760 | tf_op jit(solution)/shard_map/ppermute | solution.py:28

commit v23 on v21

--- a/solution.py
+++ b/solution.py
@@ -67,6 +67,7 @@
         crosses.append(moved(leaving, side, lambda r, c: (r, c ^ 2)))
     left_other = moved(left_docs, side, lambda r, c: (r, c ^ 1))
     near = lax.optimization_barrier(jnp.concatenate(nears))
+    near, left_other = lax.optimization_barrier((near, left_other))
     near_other = other_core(near)
     crosses[1], near_other = lax.optimization_barrier((crosses[1], near_other))
     cross = lax.optimization_barrier(jnp.concatenate(crosses))

time: 31.5 us -> 34.9 us (1.11)
  waiting for transfers between devices: 13.4 us -> 18 us
  starting transfers between devices: 13.3 us -> 12.1 us
    ppermute x9, waiting for transfers between devices: 13.4 us -> 18 us  [moved(): return lax.ppermute(value, ('row', 'col'), pairs)]
    ppermute x9, starting transfers between devices: 13.3 us -> 12.1 us  [moved(): return lax.ppermute(value, ('row', 'col'), pairs)]
  transfers between devices with their start and end apart: 9 -> 9, of which waited for: 5 -> 6; matrix products, arithmetic and copies ran while one was open for 6% -> 5% of each run, Pallas kernels for 0% -> 0%
where the time goes in v23:
time: 34.9 us; the launch traced here: 34.8 us
  waiting for transfers between devices  18 us (52%)
  starting transfers between devices  12.1 us (35%)
  other arithmetic  2.16 us (6%)
  matrix products  1.23 us (4%)
  local copies, waits for them, and re-layouts  1.12 us (3%)
    ppermute x9, waiting for transfers between devices, moved(): return lax.ppermute(value, ('row', 'col'), pairs)  18 us
    ppermute x9, starting transfers between devices, moved(): return lax.ppermute(value, ('row', 'col'), pairs)  12.1 us
    dot_general x4, matrix products, contract(): lax.dot_general(left_part, right_part, (((1,), (1,)), ((), ())), preferre...  1.23 us
    slice x1, local copies, waits for them, and re-layouts, on_square_grid(): right_docs[width // 2:]  1.04 us
    reduce_sum x5, other arithmetic, squares(): return jnp.sum(widened * widened, axis=1)  0.82 us
    mul x3, other arithmetic, finish(): return summed / feat_total * left_scale[:, None] * right_scale[None, :]  0.81 us
  transfers between devices with their start and end apart: 9, of which 6 were waited for; matrix products, arithmetic and copies ran while one was open for 5% of the time, Pallas kernels for 0%

profile of v23, /device:TPU:0, one launch (start us, length us, event | category | flops | bytes accessed | tf_op | source)
XLA Modules:
  0.0 34.8 jit_solution(5012012034340734719)
XLA Ops:
  0.0 1.0 %fusion.41 = (bf16[64,1024]{1,0:T(8,128)(2,1)S(1)}, bf16[64,1024]{1,0:T(8,128)(2,1)S(1)}) fusion(bf16[128,1024]{1,0:T(8,128)(2,1)} %param.3), kind=kLoop, calls=%fused_computation.76 | loop fusion | bytes 524288 | tf_op jit(solution)/shard_map/slice | solution.py:63
  1.0 3.0 %collective-permute-start = (bf16[64,1024]{1,0:T(8,128)(2,1)S(1)}, bf16[64,1024]{1,0:T(8,128)(2,1)S(1)}, u32[]{:S(2)}, u32[]{:S(2)}) collective-permute-start(bf16[64,1024]{1,0:T(8,128)(2,1)S(1)} %get-tuple-element.22), channel_id=1, source_target_pairs={{0,8},{1,9},{2,10},{3,11},{4,12},{5,13},{6,14},{7,15},{8,0},{9,1},... | collective-permute-start | bytes 393224 | tf_op jit(solution)/shard_map/ppermute | solution.py:28
  4.1 2.0 %collective-permute-start.2 = (bf16[256,1024]{1,0:T(8,128)(2,1)S(1)}, bf16[256,1024]{1,0:T(8,128)(2,1)S(1)}, u32[]{:S(2)}, u32[]{:S(2)}) collective-permute-start(bf16[256,1024]{1,0:T(8,128)(2,1)S(1)} %copy-done), channel_id=1, source_target_pairs={{0,1},{1,0},{2,3},{3,2},{4,5},{5,4},{6,7},{7,6},{8,9},{9,8},{10,11... | collective-permute-start | bytes 1572872 | tf_op jit(solution)/shard_map/ppermute | solution.py:28
  6.2 0.2 multiply_reduce_fusion.1
  6.3 2.0 %collective-permute-done = bf16[64,1024]{1,0:T(8,128)(2,1)S(1)} collective-permute-done((bf16[64,1024]{1,0:T(8,128)(2,1)S(1)}, bf16[64,1024]{1,0:T(8,128)(2,1)S(1)}, u32[]{:S(2)}, u32[]{:S(2)}) %collective-permute-start) | collective-permute-done | bytes 131104 | tf_op jit(solution)/shard_map/ppermute | solution.py:28
  8.4 3.2 %collective-permute-start.5 = (bf16[64,1024]{1,0:T(8,128)(2,1)S(1)}, bf16[64,1024]{1,0:T(8,128)(2,1)S(1)}, u32[]{:S(2)}, u32[]{:S(2)}) collective-permute-start(bf16[64,1024]{1,0:T(8,128)(2,1)S(1)} %get-tuple-element.32), channel_id=1, source_target_pairs={{0,2},{1,3},{2,0},{3,1},{4,6},{5,7},{6,4},{7,5},{8,10},{9,11},{10,... | collective-permute-start | bytes 393224 | tf_op jit(solution)/shard_map/ppermute | solution.py:28
  11.7 1.6 %collective-permute-start.3 = (bf16[64,1024]{1,0:T(8,128)(2,1)S(1)}, bf16[64,1024]{1,0:T(8,128)(2,1)S(1)}, u32[]{:S(2)}, u32[]{:S(2)}) collective-permute-start(bf16[64,1024]{1,0:T(8,128)(2,1)S(1)} %get-tuple-element.30), channel_id=1, source_target_pairs={{0,2},{1,3},{2,0},{3,1},{4,6},{5,7},{6,4},{7,5},{8,10},{9,11},{10,... | collective-permute-start | bytes 393224 | tf_op jit(solution)/shard_map/ppermute | solution.py:28
  13.3 7.7 %collective-permute-done.5 = bf16[64,1024]{1,0:T(8,128)(2,1)S(1)} collective-permute-done((bf16[64,1024]{1,0:T(8,128)(2,1)S(1)}, bf16[64,1024]{1,0:T(8,128)(2,1)S(1)}, u32[]{:S(2)}, u32[]{:S(2)}) %collective-permute-start.5) | collective-permute-done | bytes 131104 | tf_op jit(solution)/shard_map/ppermute | solution.py:28
  21.0 2.1 %collective-permute-done.2 = bf16[256,1024]{1,0:T(8,128)(2,1)S(1)} collective-permute-done((bf16[256,1024]{1,0:T(8,128)(2,1)S(1)}, bf16[256,1024]{1,0:T(8,128)(2,1)S(1)}, u32[]{:S(2)}, u32[]{:S(2)}) %collective-permute-start.2) | collective-permute-done | bytes 524320 | tf_op jit(solution)/shard_map/ppermute | solution.py:28
  23.1 0.2 multiply_reduce_fusion
  23.6 0.1 multiply_reduce_fusion.3
  23.8 1.3 %collective-permute-done.4 = bf16[128,1024]{1,0:T(8,128)(2,1)S(1)} collective-permute-done((bf16[128,1024]{1,0:T(8,128)(2,1)S(1)}, bf16[128,1024]{1,0:T(8,128)(2,1)S(1)}, u32[]{:S(2)}, u32[]{:S(2)}) %collective-permute-start.4) | collective-permute-done | bytes 262176 | tf_op jit(solution)/shard_map/ppermute | solution.py:28
  25.0 0.1 collective-permute-start.7
  25.2 0.3 fusion.42
  25.5 0.9 %collective-permute-done.7 = bf16[64,1024]{1,0:T(8,128)(2,1)S(1)} collective-permute-done((bf16[64,1024]{1,0:T(8,128)(2,1)S(1)}, bf16[64,1024]{1,0:T(8,128)(2,1)S(1)}, u32[]{:S(2)}, u32[]{:S(2)}) %collective-permute-start.7) | collective-permute-done | bytes 131104 | tf_op jit(solution)/shard_map/ppermute | solution.py:28
  26.4 0.2 multiply_reduce_fusion.4
  26.7 0.3 fusion.43
  27.0 0.1 multiply_convert_fusion
  27.2 1.9 %collective-permute-start.8 = (f16[264,128]{1,0:T(8,128)(2,1)S(1)}, f16[264,128]{1,0:T(8,128)(2,1)S(1)}, u32[]{:S(2)}, u32[]{:S(2)}) collective-permute-start(f16[264,128]{1,0:T(8,128)(2,1)S(1)} %concatenate.15), channel_id=1, source_target_pairs={{0,2},{1,3},{2,0},{3,1},{4,6},{5,7},{6,4},{7,5},{8,10},{9,11},{10,... | collective-permute-start | bytes 202760 | tf_op jit(solution)/shard_map/ppermute | solution.py:28
  29.1 0.3 fusion.44
  29.4 0.3 convolution_add_fusion
  29.7 0.1 multiply_reduce_fusion.2
  29.9 4.0 %collective-permute-done.8 = f16[264,128]{1,0:T(8,128)(2,1)S(1)} collective-permute-done((f16[264,128]{1,0:T(8,128)(2,1)S(1)}, f16[264,128]{1,0:T(8,128)(2,1)S(1)}, u32[]{:S(2)}, u32[]{:S(2)}) %collective-permute-start.8) | collective-permute-done | bytes 67616 | tf_op jit(solution)/shard_map/ppermute | solution.py:28
  34.0 0.8 %fusion.3 = f32[256,128]{1,0:T(8,128)} fusion(f32[256,128]{1,0:T(8,128)S(1)} %convolution_add_fusion, f32[264,128]{1,0:T(8,128)S(1)} %convert_element_type.61, f32[128]{0:T(128)S(1)} %rsqrt_bitcast_fusion, f32[256]{0:T(256)S(1)} %fusion.24, f32[128]{0:T(128)S(1)} %get-tuple-element.41, f32[256]{0:T(256)S(1)} %get-tuple-element.39), kind=kLoop, calls=%fused_computation.16 | loop fusion | flops 163840 | bytes 396288 | tf_op jit(solution)/shard_map/mul | solution.py:34
  (27 shorter events, 0.7 us)
Async XLA Ops:
  0.0 4.1 %copy-start = (bf16[256,1024]{1,0:T(8,128)(2,1)S(1)}, bf16[256,1024]{1,0:T(8,128)(2,1)}, u32[]{:S(2)}) copy-start(bf16[256,1024]{1,0:T(8,128)(2,1)} %param.2) | copy-start | bytes 1572868
  1.0 7.3 %collective-permute-start = (bf16[64,1024]{1,0:T(8,128)(2,1)S(1)}, bf16[64,1024]{1,0:T(8,128)(2,1)S(1)}, u32[]{:S(2)}, u32[]{:S(2)}) collective-permute-start(bf16[64,1024]{1,0:T(8,128)(2,1)S(1)} %get-tuple-element.22), channel_id=1, source_target_pairs={{0,8},{1,9},{2,10},{3,11},{4,12},{5,13},{6,14},{7,15},{8,0},{9,1},... | collective-permute-start | bytes 393224 | tf_op jit(solution)/shard_map/ppermute | solution.py:28
  4.1 7.6 %collective-permute-start.1 = (bf16[64,1024]{1,0:T(8,128)(2,1)S(1)}, bf16[64,1024]{1,0:T(8,128)(2,1)S(1)}, u32[]{:S(2)}, u32[]{:S(2)}) collective-permute-start(bf16[64,1024]{1,0:T(8,128)(2,1)S(1)} %get-tuple-element.24), channel_id=1, source_target_pairs={{0,8},{1,9},{2,10},{3,11},{4,12},{5,13},{6,14},{7,15},{8,0},{9,1},... | collective-permute-start | bytes 393224 | tf_op jit(solution)/shard_map/ppermute | solution.py:28
  4.1 19.0 %collective-permute-start.2 = (bf16[256,1024]{1,0:T(8,128)(2,1)S(1)}, bf16[256,1024]{1,0:T(8,128)(2,1)S(1)}, u32[]{:S(2)}, u32[]{:S(2)}) collective-permute-start(bf16[256,1024]{1,0:T(8,128)(2,1)S(1)} %copy-done), channel_id=1, source_target_pairs={{0,1},{1,0},{2,3},{3,2},{4,5},{5,4},{6,7},{7,6},{8,9},{9,8},{10,11... | collective-permute-start | bytes 1572872 | tf_op jit(solution)/shard_map/ppermute | solution.py:28
  8.4 12.6 %collective-permute-start.5 = (bf16[64,1024]{1,0:T(8,128)(2,1)S(1)}, bf16[64,1024]{1,0:T(8,128)(2,1)S(1)}, u32[]{:S(2)}, u32[]{:S(2)}) collective-permute-start(bf16[64,1024]{1,0:T(8,128)(2,1)S(1)} %get-tuple-element.32), channel_id=1, source_target_pairs={{0,2},{1,3},{2,0},{3,1},{4,6},{5,7},{6,4},{7,5},{8,10},{9,11},{10,... | collective-permute-start | bytes 393224 | tf_op jit(solution)/shard_map/ppermute | solution.py:28
  11.7 12.1 %collective-permute-start.3 = (bf16[64,1024]{1,0:T(8,128)(2,1)S(1)}, bf16[64,1024]{1,0:T(8,128)(2,1)S(1)}, u32[]{:S(2)}, u32[]{:S(2)}) collective-permute-start(bf16[64,1024]{1,0:T(8,128)(2,1)S(1)} %get-tuple-element.30), channel_id=1, source_target_pairs={{0,2},{1,3},{2,0},{3,1},{4,6},{5,7},{6,4},{7,5},{8,10},{9,11},{10,... | collective-permute-start | bytes 393224 | tf_op jit(solution)/shard_map/ppermute | solution.py:28
  21.0 4.5 %collective-permute-start.6 = (bf16[64,1024]{1,0:T(8,128)(2,1)S(1)}, bf16[64,1024]{1,0:T(8,128)(2,1)S(1)}, u32[]{:S(2)}, u32[]{:S(2)}) collective-permute-start(bf16[64,1024]{1,0:T(8,128)(2,1)S(1)} %collective-permute-done.5), channel_id=1, source_target_pairs={{0,4},{1,5},{2,6},{3,7},{4,0},{5,1},{6,2},{7,3},{8,12},{9,13},{10,... | collective-permute-start | bytes 393224 | tf_op jit(solution)/shard_map/ppermute | solution.py:28
  23.4 1.6 %collective-permute-start.4 = (bf16[128,1024]{1,0:T(8,128)(2,1)S(1)}, bf16[128,1024]{1,0:T(8,128)(2,1)S(1)}, u32[]{:S(2)}, u32[]{:S(2)}) collective-permute-start(bf16[128,1024]{1,0:T(8,128)(2,1)S(1)} %pad_maximum_fusion), channel_id=1, source_target_pairs={{0,4},{1,5},{2,6},{3,7},{4,0},{5,1},{6,2},{7,3},{8,12},{9,13},{10,... | collective-permute-start | bytes 786440 | tf_op jit(solution)/shard_map/ppermute | solution.py:28
  25.0 1.3 %collective-permute-start.7 = (bf16[64,1024]{1,0:T(8,128)(2,1)S(1)}, bf16[64,1024]{1,0:T(8,128)(2,1)S(1)}, u32[]{:S(2)}, u32[]{:S(2)}) collective-permute-start(bf16[64,1024]{1,0:T(8,128)(2,1)S(1)} %collective-permute-done.3), channel_id=1, source_target_pairs={{0,4},{1,5},{2,6},{3,7},{4,0},{5,1},{6,2},{7,3},{8,12},{9,13},{10,... | collective-permute-start | bytes 393224 | tf_op jit(solution)/shard_map/ppermute | solution.py:28
  27.2 6.7 %collective-permute-start.8 = (f16[264,128]{1,0:T(8,128)(2,1)S(1)}, f16[264,128]{1,0:T(8,128)(2,1)S(1)}, u32[]{:S(2)}, u32[]{:S(2)}) collective-permute-start(f16[264,128]{1,0:T(8,128)(2,1)S(1)} %concatenate.15), channel_id=1, source_target_pairs={{0,2},{1,3},{2,0},{3,1},{4,6},{5,7},{6,4},{7,5},{8,10},{9,11},{10,... | collective-permute-start | bytes 202760 | tf_op jit(solution)/shard_map/ppermute | solution.py:28

commit v24 on v21

--- a/solution.py
+++ b/solution.py
@@ -64,7 +64,7 @@
         swapped = moved(half, side, lambda r, c: (r ^ 2, c))
         near, leaving = lax.optimization_barrier((jnp.where(at_home, half, swapped), jnp.where(at_home, swapped, half)))
         nears.append(near)
-        crosses.append(moved(leaving, side, lambda r, c: (r, c ^ 2)))
+        crosses.append(moved(leaving, side, lambda r, c: (r, c ^ 3)))
     left_other = moved(left_docs, side, lambda r, c: (r, c ^ 1))
     near = lax.optimization_barrier(jnp.concatenate(nears))
     near_other = other_core(near)
@@ -89,7 +89,7 @@
     sums = [left_high.reshape(parts, width), left_low.reshape(parts, width), right_high[None], right_low[None]]
     spare = jnp.zeros((-(2 * parts + 2) % 8, width), jnp.float16)
     message = jnp.concatenate([tile.astype(jnp.float16), *sums, spare])
-    got = moved(message, side, lambda r, c: (r, c ^ 2))
+    got = moved(message, side, lambda r, c: (r, c ^ 3))
 
     near_other, _ = lax.optimization_barrier((near_other, message))
     near_gram, near_sq = half_sum(near, near_other)

time: 31.5 us -> 34.8 us (1.10)
  waiting for transfers between devices: 13.4 us -> 17.5 us
  starting transfers between devices: 13.3 us -> 12.5 us
    ppermute x9, waiting for transfers between devices: 13.4 us -> 17.5 us  [moved(): return lax.ppermute(value, ('row', 'col'), pairs)]
    ppermute x9, starting transfers between devices: 13.3 us -> 12.5 us  [moved(): return lax.ppermute(value, ('row', 'col'), pairs)]
  transfers between devices with their start and end apart: 9 -> 9, of which waited for: 5 -> 5; matrix products, arithmetic and copies ran while one was open for 6% -> 5% of each run, Pallas kernels for 0% -> 0%
where the time goes in v24:
time: 34.8 us; the launch traced here: 34.6 us
  waiting for transfers between devices  17.5 us (50%)
  starting transfers between devices  12.5 us (36%)
  other arithmetic  2.16 us (6%)
  matrix products  1.22 us (4%)
  local copies, waits for them, and re-layouts  1.12 us (3%)
    ppermute x9, waiting for transfers between devices, moved(): return lax.ppermute(value, ('row', 'col'), pairs)  17.5 us
    ppermute x9, starting transfers between devices, moved(): return lax.ppermute(value, ('row', 'col'), pairs)  12.5 us
    dot_general x4, matrix products, contract(): lax.dot_general(left_part, right_part, (((1,), (1,)), ((), ())), preferre...  1.22 us
    slice x1, local copies, waits for them, and re-layouts, on_square_grid(): right_docs[width // 2:]  1.04 us
    reduce_sum x5, other arithmetic, squares(): return jnp.sum(widened * widened, axis=1)  0.82 us
    mul x3, other arithmetic, finish(): return summed / feat_total * left_scale[:, None] * right_scale[None, :]  0.81 us
  transfers between devices with their start and end apart: 9, of which 5 were waited for; matrix products, arithmetic and copies ran while one was open for 5% of the time, Pallas kernels for 0%

profile of v24, /device:TPU:0, one launch (start us, length us, event | category | flops | bytes accessed | tf_op | source)
XLA Modules:
  0.0 34.6 jit_solution(17393110716262959597)
XLA Ops:
  0.0 1.0 %fusion.41 = (bf16[64,1024]{1,0:T(8,128)(2,1)S(1)}, bf16[64,1024]{1,0:T(8,128)(2,1)S(1)}) fusion(bf16[128,1024]{1,0:T(8,128)(2,1)} %param.3), kind=kLoop, calls=%fused_computation.76 | loop fusion | bytes 524288 | tf_op jit(solution)/shard_map/slice | solution.py:63
  1.0 3.0 %collective-permute-start.1 = (bf16[64,1024]{1,0:T(8,128)(2,1)S(1)}, bf16[64,1024]{1,0:T(8,128)(2,1)S(1)}, u32[]{:S(2)}, u32[]{:S(2)}) collective-permute-start(bf16[64,1024]{1,0:T(8,128)(2,1)S(1)} %get-tuple-element.21), channel_id=1, source_target_pairs={{0,8},{1,9},{2,10},{3,11},{4,12},{5,13},{6,14},{7,15},{8,0},{9,1},... | collective-permute-start | bytes 393224 | tf_op jit(solution)/shard_map/ppermute | solution.py:28
  4.1 0.1 collective-permute-start.2
  4.1 2.0 %collective-permute-start = (bf16[256,1024]{1,0:T(8,128)(2,1)S(1)}, bf16[256,1024]{1,0:T(8,128)(2,1)S(1)}, u32[]{:S(2)}, u32[]{:S(2)}) collective-permute-start(bf16[256,1024]{1,0:T(8,128)(2,1)S(1)} %copy-done), channel_id=1, source_target_pairs={{0,1},{1,0},{2,3},{3,2},{4,5},{5,4},{6,7},{7,6},{8,9},{9,8},{10,11... | collective-permute-start | bytes 1572872 | tf_op jit(solution)/shard_map/ppermute | solution.py:28
  6.2 2.2 %collective-permute-done.1 = bf16[64,1024]{1,0:T(8,128)(2,1)S(1)} collective-permute-done((bf16[64,1024]{1,0:T(8,128)(2,1)S(1)}, bf16[64,1024]{1,0:T(8,128)(2,1)S(1)}, u32[]{:S(2)}, u32[]{:S(2)}) %collective-permute-start.1) | collective-permute-done | bytes 131104 | tf_op jit(solution)/shard_map/ppermute | solution.py:28
  8.4 4.2 %collective-permute-start.5 = (bf16[64,1024]{1,0:T(8,128)(2,1)S(1)}, bf16[64,1024]{1,0:T(8,128)(2,1)S(1)}, u32[]{:S(2)}, u32[]{:S(2)}) collective-permute-start(bf16[64,1024]{1,0:T(8,128)(2,1)S(1)} %get-tuple-element.28), channel_id=1, source_target_pairs={{0,3},{1,2},{2,1},{3,0},{4,7},{5,6},{6,5},{7,4},{8,11},{9,10},{10,... | collective-permute-start | bytes 393224 | tf_op jit(solution)/shard_map/ppermute | solution.py:28
  12.7 1.6 %collective-permute-start.3 = (bf16[64,1024]{1,0:T(8,128)(2,1)S(1)}, bf16[64,1024]{1,0:T(8,128)(2,1)S(1)}, u32[]{:S(2)}, u32[]{:S(2)}) collective-permute-start(bf16[64,1024]{1,0:T(8,128)(2,1)S(1)} %get-tuple-element.26), channel_id=1, source_target_pairs={{0,3},{1,2},{2,1},{3,0},{4,7},{5,6},{6,5},{7,4},{8,11},{9,10},{10,... | collective-permute-start | bytes 393224 | tf_op jit(solution)/shard_map/ppermute | solution.py:28
  14.3 0.2 multiply_reduce_fusion.1
  14.5 0.1 multiply_reduce_fusion.3
  14.7 9.4 %collective-permute-done.5 = bf16[64,1024]{1,0:T(8,128)(2,1)S(1)} collective-permute-done((bf16[64,1024]{1,0:T(8,128)(2,1)S(1)}, bf16[64,1024]{1,0:T(8,128)(2,1)S(1)}, u32[]{:S(2)}, u32[]{:S(2)}) %collective-permute-start.5) | collective-permute-done | bytes 131104 | tf_op jit(solution)/shard_map/ppermute | solution.py:28
  24.0 1.4 %collective-permute-done.3 = bf16[64,1024]{1,0:T(8,128)(2,1)S(1)} collective-permute-done((bf16[64,1024]{1,0:T(8,128)(2,1)S(1)}, bf16[64,1024]{1,0:T(8,128)(2,1)S(1)}, u32[]{:S(2)}, u32[]{:S(2)}) %collective-permute-start.3) | collective-permute-done | bytes 131104 | tf_op jit(solution)/shard_map/ppermute | solution.py:28
  25.5 0.2 multiply_reduce_fusion
  25.8 0.1 broadcast_select_fusion
  25.9 0.3 fusion.42
  26.2 0.6 %collective-permute-done.7 = bf16[64,1024]{1,0:T(8,128)(2,1)S(1)} collective-permute-done((bf16[64,1024]{1,0:T(8,128)(2,1)S(1)}, bf16[64,1024]{1,0:T(8,128)(2,1)S(1)}, u32[]{:S(2)}, u32[]{:S(2)}) %collective-permute-start.7) | collective-permute-done | bytes 131104 | tf_op jit(solution)/shard_map/ppermute | solution.py:28
  26.8 0.2 multiply_reduce_fusion.4
  27.1 0.3 fusion.43
  27.4 0.1 multiply_convert_fusion
  27.6 1.5 %collective-permute-start.8 = (f16[264,128]{1,0:T(8,128)(2,1)S(1)}, f16[264,128]{1,0:T(8,128)(2,1)S(1)}, u32[]{:S(2)}, u32[]{:S(2)}) collective-permute-start(f16[264,128]{1,0:T(8,128)(2,1)S(1)} %concatenate.15), channel_id=1, source_target_pairs={{0,3},{1,2},{2,1},{3,0},{4,7},{5,6},{6,5},{7,4},{8,11},{9,10},{10,... | collective-permute-start | bytes 202760 | tf_op jit(solution)/shard_map/ppermute | solution.py:28
  29.1 0.3 fusion.44
  29.4 0.3 convolution_add_fusion
  29.7 0.1 multiply_reduce_fusion.2
  29.9 3.9 %collective-permute-done.8 = f16[264,128]{1,0:T(8,128)(2,1)S(1)} collective-permute-done((f16[264,128]{1,0:T(8,128)(2,1)S(1)}, f16[264,128]{1,0:T(8,128)(2,1)S(1)}, u32[]{:S(2)}, u32[]{:S(2)}) %collective-permute-start.8) | collective-permute-done | bytes 67616 | tf_op jit(solution)/shard_map/ppermute | solution.py:28
  33.8 0.8 %fusion.3 = f32[256,128]{1,0:T(8,128)} fusion(f32[256,128]{1,0:T(8,128)S(1)} %convolution_add_fusion, f32[264,128]{1,0:T(8,128)S(1)} %convert_element_type.61, f32[128]{0:T(128)S(1)} %rsqrt_bitcast_fusion, f32[256]{0:T(256)S(1)} %fusion.24, f32[128]{0:T(128)S(1)} %get-tuple-element.37, f32[256]{0:T(256)S(1)} %get-tuple-element.35), kind=kLoop, calls=%fused_computation.16 | loop fusion | flops 163840 | bytes 396288 | tf_op jit(solution)/shard_map/mul | solution.py:34
  (27 shorter events, 0.5 us)
Async XLA Ops:
  0.0 4.1 %copy-start = (bf16[256,1024]{1,0:T(8,128)(2,1)S(1)}, bf16[256,1024]{1,0:T(8,128)(2,1)}, u32[]{:S(2)}) copy-start(bf16[256,1024]{1,0:T(8,128)(2,1)} %param.2) | copy-start | bytes 1572868
  1.0 7.3 %collective-permute-start.1 = (bf16[64,1024]{1,0:T(8,128)(2,1)S(1)}, bf16[64,1024]{1,0:T(8,128)(2,1)S(1)}, u32[]{:S(2)}, u32[]{:S(2)}) collective-permute-start(bf16[64,1024]{1,0:T(8,128)(2,1)S(1)} %get-tuple-element.21), channel_id=1, source_target_pairs={{0,8},{1,9},{2,10},{3,11},{4,12},{5,13},{6,14},{7,15},{8,0},{9,1},... | collective-permute-start | bytes 393224 | tf_op jit(solution)/shard_map/ppermute | solution.py:28
  4.1 8.6 %collective-permute-start.2 = (bf16[64,1024]{1,0:T(8,128)(2,1)S(1)}, bf16[64,1024]{1,0:T(8,128)(2,1)S(1)}, u32[]{:S(2)}, u32[]{:S(2)}) collective-permute-start(bf16[64,1024]{1,0:T(8,128)(2,1)S(1)} %get-tuple-element.23), channel_id=1, source_target_pairs={{0,8},{1,9},{2,10},{3,11},{4,12},{5,13},{6,14},{7,15},{8,0},{9,1},... | collective-permute-start | bytes 393224 | tf_op jit(solution)/shard_map/ppermute | solution.py:28
  4.1 21.3 %collective-permute-start = (bf16[256,1024]{1,0:T(8,128)(2,1)S(1)}, bf16[256,1024]{1,0:T(8,128)(2,1)S(1)}, u32[]{:S(2)}, u32[]{:S(2)}) collective-permute-start(bf16[256,1024]{1,0:T(8,128)(2,1)S(1)} %copy-done), channel_id=1, source_target_pairs={{0,1},{1,0},{2,3},{3,2},{4,5},{5,4},{6,7},{7,6},{8,9},{9,8},{10,11... | collective-permute-start | bytes 1572872 | tf_op jit(solution)/shard_map/ppermute | solution.py:28
  8.4 15.6 %collective-permute-start.5 = (bf16[64,1024]{1,0:T(8,128)(2,1)S(1)}, bf16[64,1024]{1,0:T(8,128)(2,1)S(1)}, u32[]{:S(2)}, u32[]{:S(2)}) collective-permute-start(bf16[64,1024]{1,0:T(8,128)(2,1)S(1)} %get-tuple-element.28), channel_id=1, source_target_pairs={{0,3},{1,2},{2,1},{3,0},{4,7},{5,6},{6,5},{7,4},{8,11},{9,10},{10,... | collective-permute-start | bytes 393224 | tf_op jit(solution)/shard_map/ppermute | solution.py:28
  12.7 12.7 %collective-permute-start.3 = (bf16[64,1024]{1,0:T(8,128)(2,1)S(1)}, bf16[64,1024]{1,0:T(8,128)(2,1)S(1)}, u32[]{:S(2)}, u32[]{:S(2)}) collective-permute-start(bf16[64,1024]{1,0:T(8,128)(2,1)S(1)} %get-tuple-element.26), channel_id=1, source_target_pairs={{0,3},{1,2},{2,1},{3,0},{4,7},{5,6},{6,5},{7,4},{8,11},{9,10},{10,... | collective-permute-start | bytes 393224 | tf_op jit(solution)/shard_map/ppermute | solution.py:28
  14.3 11.1 %collective-permute-start.4 = (bf16[128,1024]{1,0:T(8,128)(2,1)S(1)}, bf16[128,1024]{1,0:T(8,128)(2,1)S(1)}, u32[]{:S(2)}, u32[]{:S(2)}) collective-permute-start(bf16[128,1024]{1,0:T(8,128)(2,1)S(1)} %pad_maximum_fusion), channel_id=1, source_target_pairs={{0,4},{1,5},{2,6},{3,7},{4,0},{5,1},{6,2},{7,3},{8,12},{9,13},{10,... | collective-permute-start | bytes 786440 | tf_op jit(solution)/shard_map/ppermute | solution.py:28
  24.0 2.2 %collective-permute-start.6 = (bf16[64,1024]{1,0:T(8,128)(2,1)S(1)}, bf16[64,1024]{1,0:T(8,128)(2,1)S(1)}, u32[]{:S(2)}, u32[]{:S(2)}) collective-permute-start(bf16[64,1024]{1,0:T(8,128)(2,1)S(1)} %collective-permute-done.5), channel_id=1, source_target_pairs={{0,4},{1,5},{2,6},{3,7},{4,0},{5,1},{6,2},{7,3},{8,12},{9,13},{10,... | collective-permute-start | bytes 393224 | tf_op jit(solution)/shard_map/ppermute | solution.py:28
  25.4 1.3 %collective-permute-start.7 = (bf16[64,1024]{1,0:T(8,128)(2,1)S(1)}, bf16[64,1024]{1,0:T(8,128)(2,1)S(1)}, u32[]{:S(2)}, u32[]{:S(2)}) collective-permute-start(bf16[64,1024]{1,0:T(8,128)(2,1)S(1)} %collective-permute-done.3), channel_id=1, source_target_pairs={{0,4},{1,5},{2,6},{3,7},{4,0},{5,1},{6,2},{7,3},{8,12},{9,13},{10,... | collective-permute-start | bytes 393224 | tf_op jit(solution)/shard_map/ppermute | solution.py:28
  27.6 6.1 %collective-permute-start.8 = (f16[264,128]{1,0:T(8,128)(2,1)S(1)}, f16[264,128]{1,0:T(8,128)(2,1)S(1)}, u32[]{:S(2)}, u32[]{:S(2)}) collective-permute-start(f16[264,128]{1,0:T(8,128)(2,1)S(1)} %concatenate.15), channel_id=1, source_target_pairs={{0,3},{1,2},{2,1},{3,0},{4,7},{5,6},{6,5},{7,4},{8,11},{9,10},{10,... | collective-permute-start | bytes 202760 | tf_op jit(solution)/shard_map/ppermute | solution.py:28

commit v25 on v21

--- a/solution.py
+++ b/solution.py
@@ -59,14 +59,14 @@
     def other_core(block):
         return moved(block, side, lambda r, c: (r ^ 1, c))
 
-    nears, crosses = [], []
-    for half in lax.optimization_barrier((right_docs[:width // 2], right_docs[width // 2:])):
-        swapped = moved(half, side, lambda r, c: (r ^ 2, c))
-        near, leaving = lax.optimization_barrier((jnp.where(at_home, half, swapped), jnp.where(at_home, swapped, half)))
-        nears.append(near)
-        crosses.append(moved(leaving, side, lambda r, c: (r, c ^ 2)))
+    swapped = moved(right_docs, side, lambda r, c: (r ^ 2, c))
+    own_sq = squares(left_docs)
+    swapped, own_sq = lax.optimization_barrier((swapped, own_sq))
+    near, *leaving = lax.optimization_barrier(
+        (jnp.where(at_home, right_docs, swapped), *jnp.split(jnp.where(at_home, swapped, right_docs), 2))
+    )
+    crosses = [moved(part, side, lambda r, c: (r, c ^ 2)) for part in leaving]
     left_other = moved(left_docs, side, lambda r, c: (r, c ^ 1))
-    near = lax.optimization_barrier(jnp.concatenate(nears))
     near_other = other_core(near)
     crosses[1], near_other = lax.optimization_barrier((crosses[1], near_other))
     cross = lax.optimization_barrier(jnp.concatenate(crosses))
@@ -80,7 +80,7 @@
     cross_other, cross_gram = lax.optimization_barrier((jnp.concatenate([other_core(part) for part in crosses]), cross_gram))
     cross_gram = cross_gram + contract(lefts[1], cross_other)
     cross_sq = squares(cross) + squares(cross_other)
-    left_sq = squares(left_docs) + squares(left_other)
+    left_sq = own_sq + squares(left_other)
 
     left_high, left_low, left_read = packed(left_sq)
     right_high, right_low, right_read = packed(cross_sq)

time: 31.5 us -> 35 us (1.11)
  waiting for transfers between devices: 13.4 us -> 22.5 us
  starting transfers between devices: 13.3 us -> 7.66 us
  other arithmetic: 2.16 us -> 3.22 us
  local copies, waits for them, and re-layouts: 1.12 us -> 0.1 us
    ppermute x9 -> x8, waiting for transfers between devices: 13.4 us -> 22.5 us  [moved(): return lax.ppermute(value, ('row', 'col'), pairs)]
    ppermute x9 -> x8, starting transfers between devices: 13.3 us -> 7.66 us  [moved(): return lax.ppermute(value, ('row', 'col'), pairs)]
    reduce_sum x5, other arithmetic: 0.82 us -> 1.93 us  [squares(): return jnp.sum(widened * widened, axis=1)]
    slice x1 -> x0, local copies, waits for them, and re-layouts: 1.04 us -> none  [on_square_grid(): right_docs[width // 2:]]
  transfers between devices with their start and end apart: 9 -> 8, of which waited for: 5 -> 5; matrix products, arithmetic and copies ran while one was open for 6% -> 8% of each run, Pallas kernels for 0% -> 0%
where the time goes in v25:
time: 35 us; the launch traced here: 34.8 us
  waiting for transfers between devices  22.5 us (64%)
  starting transfers between devices  7.66 us (22%)
  other arithmetic  3.22 us (9%)
  matrix products  1.22 us (3%)
    ppermute x8, waiting for transfers between devices, moved(): return lax.ppermute(value, ('row', 'col'), pairs)  22.5 us
    ppermute x8, starting transfers between devices, moved(): return lax.ppermute(value, ('row', 'col'), pairs)  7.66 us
    reduce_sum x5, other arithmetic, squares(): return jnp.sum(widened * widened, axis=1)  1.93 us
    dot_general x4, matrix products, contract(): lax.dot_general(left_part, right_part, (((1,), (1,)), ((), ())), preferre...  1.22 us
    mul x3, other arithmetic, finish(): return summed / feat_total * left_scale[:, None] * right_scale[None, :]  0.81 us
  transfers between devices with their start and end apart: 8, of which 5 were waited for; matrix products, arithmetic and copies ran while one was open for 8% of the time, Pallas kernels for 0%

profile of v25, /device:TPU:0, one launch (start us, length us, event | category | flops | bytes accessed | tf_op | source)
XLA Modules:
  0.0 34.8 jit_solution(16531859200391647464)
XLA Ops:
  0.0 2.9 %collective-permute-start.1 = (bf16[128,1024]{1,0:T(8,128)(2,1)}, bf16[128,1024]{1,0:T(8,128)(2,1)S(1)}, u32[]{:S(2)}, u32[]{:S(2)}) collective-permute-start(bf16[128,1024]{1,0:T(8,128)(2,1)} %param.3), channel_id=1, source_target_pairs={{0,8},{1,9},{2,10},{3,11},{4,12},{5,13},{6,14},{7,15},{8,0},{9,1},... | collective-permute-start | bytes 786440 | tf_op jit(solution)/shard_map/ppermute | solution.py:28
  2.9 1.6 %collective-permute-start = (bf16[256,1024]{1,0:T(8,128)(2,1)}, bf16[256,1024]{1,0:T(8,128)(2,1)S(1)}, u32[]{:S(2)}, u32[]{:S(2)}) collective-permute-start(bf16[256,1024]{1,0:T(8,128)(2,1)} %param.2), channel_id=1, source_target_pairs={{0,1},{1,0},{2,3},{3,2},{4,5},{5,4},{6,7},{7,6},{8,9},{9,8},{10,11... | collective-permute-start | bytes 1572872 | tf_op jit(solution)/shard_map/ppermute | solution.py:28
  4.5 1.3 %multiply_reduce_fusion.1 = f32[256]{0:T(256)S(1)} fusion(bf16[256,1024]{1,0:T(8,128)(2,1)} %param.2), kind=kLoop, calls=%fused_computation.2 | loop fusion | flops 786176 | bytes 525312 | tf_op jit(solution)/shard_map/reduce_sum | solution.py:18
  5.8 3.6 %collective-permute-done.1 = bf16[128,1024]{1,0:T(8,128)(2,1)S(1)} collective-permute-done((bf16[128,1024]{1,0:T(8,128)(2,1)}, bf16[128,1024]{1,0:T(8,128)(2,1)S(1)}, u32[]{:S(2)}, u32[]{:S(2)}) %collective-permute-start.1) | collective-permute-done | bytes 262176 | tf_op jit(solution)/shard_map/ppermute | solution.py:28
  9.5 0.1 collective-permute-start.3
  9.6 2.9 %collective-permute-start.4 = (bf16[64,1024]{1,0:T(8,128)(2,1)S(1)}, bf16[64,1024]{1,0:T(8,128)(2,1)S(1)}, u32[]{:S(2)}, u32[]{:S(2)}) collective-permute-start(bf16[64,1024]{1,0:T(8,128)(2,1)S(1)} %get-tuple-element.25), channel_id=1, source_target_pairs={{0,2},{1,3},{2,0},{3,1},{4,6},{5,7},{6,4},{7,5},{8,10},{9,11},{10,... | collective-permute-start | bytes 393224 | tf_op jit(solution)/shard_map/ppermute | solution.py:28
  12.5 0.1 collective-permute-start.2
  12.6 0.1 multiply_reduce_fusion.3
  12.8 7.1 %collective-permute-done.4 = bf16[64,1024]{1,0:T(8,128)(2,1)S(1)} collective-permute-done((bf16[64,1024]{1,0:T(8,128)(2,1)S(1)}, bf16[64,1024]{1,0:T(8,128)(2,1)S(1)}, u32[]{:S(2)}, u32[]{:S(2)}) %collective-permute-start.4) | collective-permute-done | bytes 131104 | tf_op jit(solution)/shard_map/ppermute | solution.py:28
  19.9 5.2 %collective-permute-done.2 = bf16[64,1024]{1,0:T(8,128)(2,1)S(1)} collective-permute-done((bf16[64,1024]{1,0:T(8,128)(2,1)S(1)}, bf16[64,1024]{1,0:T(8,128)(2,1)S(1)}, u32[]{:S(2)}, u32[]{:S(2)}) %collective-permute-start.2) | collective-permute-done | bytes 131104 | tf_op jit(solution)/shard_map/ppermute | solution.py:28
  25.1 0.1 broadcast_select_fusion
  25.2 0.2 multiply_reduce_fusion
  25.5 0.3 fusion.37
  25.8 0.6 %collective-permute-done.6 = bf16[64,1024]{1,0:T(8,128)(2,1)S(1)} collective-permute-done((bf16[64,1024]{1,0:T(8,128)(2,1)S(1)}, bf16[64,1024]{1,0:T(8,128)(2,1)S(1)}, u32[]{:S(2)}, u32[]{:S(2)}) %collective-permute-start.6) | collective-permute-done | bytes 131104 | tf_op jit(solution)/shard_map/ppermute | solution.py:28
  26.5 0.2 multiply_reduce_fusion.4
  26.7 0.3 fusion.38
  27.1 0.1 multiply_convert_fusion
  27.2 0.1 concatenate.11
  27.3 0.1 collective-permute-start.7
  27.3 0.3 fusion.39
  27.6 0.3 convolution_add_fusion
  27.9 0.1 multiply_reduce_fusion.2
  28.1 5.9 %collective-permute-done.7 = f16[264,128]{1,0:T(8,128)(2,1)S(1)} collective-permute-done((f16[264,128]{1,0:T(8,128)(2,1)S(1)}, f16[264,128]{1,0:T(8,128)(2,1)S(1)}, u32[]{:S(2)}, u32[]{:S(2)}) %collective-permute-start.7) | collective-permute-done | bytes 67616 | tf_op jit(solution)/shard_map/ppermute | solution.py:28
  34.0 0.8 %fusion.3 = f32[256,128]{1,0:T(8,128)} fusion(f32[256,128]{1,0:T(8,128)S(1)} %convolution_add_fusion, f32[264,128]{1,0:T(8,128)S(1)} %convert_element_type.59, f32[128]{0:T(128)S(1)} %rsqrt_bitcast_fusion, f32[256]{0:T(256)S(1)} %fusion.19, f32[128]{0:T(128)S(1)} %get-tuple-element.35, f32[256]{0:T(256)S(1)} %get-tuple-element.33), kind=kLoop, calls=%fused_computation.17 | loop fusion | flops 163840 | bytes 396288 | tf_op jit(solution)/shard_map/mul | solution.py:34
  (24 shorter events, 0.4 us)
Async XLA Ops:
  0.0 9.5 %collective-permute-start.1 = (bf16[128,1024]{1,0:T(8,128)(2,1)}, bf16[128,1024]{1,0:T(8,128)(2,1)S(1)}, u32[]{:S(2)}, u32[]{:S(2)}) collective-permute-start(bf16[128,1024]{1,0:T(8,128)(2,1)} %param.3), channel_id=1, source_target_pairs={{0,8},{1,9},{2,10},{3,11},{4,12},{5,13},{6,14},{7,15},{8,0},{9,1},... | collective-permute-start | bytes 786440 | tf_op jit(solution)/shard_map/ppermute | solution.py:28
  2.9 22.2 %collective-permute-start = (bf16[256,1024]{1,0:T(8,128)(2,1)}, bf16[256,1024]{1,0:T(8,128)(2,1)S(1)}, u32[]{:S(2)}, u32[]{:S(2)}) collective-permute-start(bf16[256,1024]{1,0:T(8,128)(2,1)} %param.2), channel_id=1, source_target_pairs={{0,1},{1,0},{2,3},{3,2},{4,5},{5,4},{6,7},{7,6},{8,9},{9,8},{10,11... | collective-permute-start | bytes 1572872 | tf_op jit(solution)/shard_map/ppermute | solution.py:28
  4.5 4.9 %copy-start.1 = (bf16[128,1024]{1,0:T(8,128)(2,1)S(1)}, bf16[128,1024]{1,0:T(8,128)(2,1)}, u32[]{:S(2)}) copy-start(bf16[128,1024]{1,0:T(8,128)(2,1)} %param.3) | copy-start | bytes 786436
  9.5 15.6 %copy-start = (bf16[256,1024]{1,0:T(8,128)(2,1)S(1)}, bf16[256,1024]{1,0:T(8,128)(2,1)}, u32[]{:S(2)}) copy-start(bf16[256,1024]{1,0:T(8,128)(2,1)} %param.2) | copy-start | bytes 1572868
  9.5 15.6 %collective-permute-start.3 = (bf16[128,1024]{1,0:T(8,128)(2,1)S(1)}, bf16[128,1024]{1,0:T(8,128)(2,1)S(1)}, u32[]{:S(2)}, u32[]{:S(2)}) collective-permute-start(bf16[128,1024]{1,0:T(8,128)(2,1)S(1)} %get-tuple-element.21), channel_id=1, source_target_pairs={{0,4},{1,5},{2,6},{3,7},{4,0},{5,1},{6,2},{7,3},{8,12},{9,13},{10,... | collective-permute-start | bytes 786440 | tf_op jit(solution)/shard_map/ppermute | solution.py:28
  9.6 10.2 %collective-permute-start.4 = (bf16[64,1024]{1,0:T(8,128)(2,1)S(1)}, bf16[64,1024]{1,0:T(8,128)(2,1)S(1)}, u32[]{:S(2)}, u32[]{:S(2)}) collective-permute-start(bf16[64,1024]{1,0:T(8,128)(2,1)S(1)} %get-tuple-element.25), channel_id=1, source_target_pairs={{0,2},{1,3},{2,0},{3,1},{4,6},{5,7},{6,4},{7,5},{8,10},{9,11},{10,... | collective-permute-start | bytes 393224 | tf_op jit(solution)/shard_map/ppermute | solution.py:28
  12.5 12.6 %collective-permute-start.2 = (bf16[64,1024]{1,0:T(8,128)(2,1)S(1)}, bf16[64,1024]{1,0:T(8,128)(2,1)S(1)}, u32[]{:S(2)}, u32[]{:S(2)}) collective-permute-start(bf16[64,1024]{1,0:T(8,128)(2,1)S(1)} %get-tuple-element.23), channel_id=1, source_target_pairs={{0,2},{1,3},{2,0},{3,1},{4,6},{5,7},{6,4},{7,5},{8,10},{9,11},{10,... | collective-permute-start | bytes 393224 | tf_op jit(solution)/shard_map/ppermute | solution.py:28
  19.9 6.0 %collective-permute-start.5 = (bf16[64,1024]{1,0:T(8,128)(2,1)S(1)}, bf16[64,1024]{1,0:T(8,128)(2,1)S(1)}, u32[]{:S(2)}, u32[]{:S(2)}) collective-permute-start(bf16[64,1024]{1,0:T(8,128)(2,1)S(1)} %collective-permute-done.4), channel_id=1, source_target_pairs={{0,4},{1,5},{2,6},{3,7},{4,0},{5,1},{6,2},{7,3},{8,12},{9,13},{10,... | collective-permute-start | bytes 393224 | tf_op jit(solution)/shard_map/ppermute | solution.py:28
  25.1 1.3 %collective-permute-start.6 = (bf16[64,1024]{1,0:T(8,128)(2,1)S(1)}, bf16[64,1024]{1,0:T(8,128)(2,1)S(1)}, u32[]{:S(2)}, u32[]{:S(2)}) collective-permute-start(bf16[64,1024]{1,0:T(8,128)(2,1)S(1)} %collective-permute-done.2), channel_id=1, source_target_pairs={{0,4},{1,5},{2,6},{3,7},{4,0},{5,1},{6,2},{7,3},{8,12},{9,13},{10,... | collective-permute-start | bytes 393224 | tf_op jit(solution)/shard_map/ppermute | solution.py:28
  27.3 6.7 %collective-permute-start.7 = (f16[264,128]{1,0:T(8,128)(2,1)S(1)}, f16[264,128]{1,0:T(8,128)(2,1)S(1)}, u32[]{:S(2)}, u32[]{:S(2)}) collective-permute-start(f16[264,128]{1,0:T(8,128)(2,1)S(1)} %concatenate.11), channel_id=1, source_target_pairs={{0,2},{1,3},{2,0},{3,1},{4,6},{5,7},{6,4},{7,5},{8,10},{9,11},{10,... | collective-permute-start | bytes 202760 | tf_op jit(solution)/shard_map/ppermute | solution.py:28

commit v26 on v21

--- a/solution.py
+++ b/solution.py
@@ -60,7 +60,10 @@
         return moved(block, side, lambda r, c: (r ^ 1, c))
 
     nears, crosses = [], []
-    for half in lax.optimization_barrier((right_docs[:width // 2], right_docs[width // 2:])):
+    first, second = lax.optimization_barrier((right_docs[:width // 2], right_docs[width // 2:]))
+    for half in (first, second):
+        if nears:
+            half, _ = lax.optimization_barrier((half, nears[0]))
         swapped = moved(half, side, lambda r, c: (r ^ 2, c))
         near, leaving = lax.optimization_barrier((jnp.where(at_home, half, swapped), jnp.where(at_home, swapped, half)))
         nears.append(near)

time: 31.5 us -> 35.7 us (1.13)
  waiting for transfers between devices: 13.4 us -> 16.8 us
  starting transfers between devices: 13.3 us -> 14.1 us
    ppermute x9, waiting for transfers between devices: 13.4 us -> 16.8 us  [moved(): return lax.ppermute(value, ('row', 'col'), pairs)]
    ppermute x9, starting transfers between devices: 13.3 us -> 14.1 us  [moved(): return lax.ppermute(value, ('row', 'col'), pairs)]
  transfers between devices with their start and end apart: 9 -> 9, of which waited for: 5 -> 5; matrix products, arithmetic and copies ran while one was open for 6% -> 5% of each run, Pallas kernels for 0% -> 0%
where the time goes in v26:
time: 35.7 us; the launch traced here: 35.5 us
  waiting for transfers between devices  16.8 us (47%)
  starting transfers between devices  14.1 us (39%)
  other arithmetic  2.16 us (6%)
  matrix products  1.21 us (3%)
  local copies, waits for them, and re-layouts  1.12 us (3%)
    ppermute x9, waiting for transfers between devices, moved(): return lax.ppermute(value, ('row', 'col'), pairs)  16.8 us
    ppermute x9, starting transfers between devices, moved(): return lax.ppermute(value, ('row', 'col'), pairs)  14.1 us
    dot_general x4, matrix products, contract(): lax.dot_general(left_part, right_part, (((1,), (1,)), ((), ())), preferre...  1.21 us
    slice x1, local copies, waits for them, and re-layouts, on_square_grid(): right_docs[width // 2:]  1.04 us
    reduce_sum x5, other arithmetic, squares(): return jnp.sum(widened * widened, axis=1)  0.82 us
    mul x3, other arithmetic, finish(): return summed / feat_total * left_scale[:, None] * right_scale[None, :]  0.81 us
  transfers between devices with their start and end apart: 9, of which 5 were waited for; matrix products, arithmetic and copies ran while one was open for 5% of the time, Pallas kernels for 0%

profile of v26, /device:TPU:0, one launch (start us, length us, event | category | flops | bytes accessed | tf_op | source)
XLA Modules:
  0.0 35.5 jit_solution(11419845674814768112)
XLA Ops:
  0.0 1.0 %fusion.41 = (bf16[64,1024]{1,0:T(8,128)(2,1)S(1)}, bf16[64,1024]{1,0:T(8,128)(2,1)S(1)}) fusion(bf16[128,1024]{1,0:T(8,128)(2,1)} %param.3), kind=kLoop, calls=%fused_computation.76 | loop fusion | bytes 524288 | tf_op jit(solution)/shard_map/slice | solution.py:63
  1.0 3.0 %collective-permute-start.1 = (bf16[64,1024]{1,0:T(8,128)(2,1)S(1)}, bf16[64,1024]{1,0:T(8,128)(2,1)S(1)}, u32[]{:S(2)}, u32[]{:S(2)}) collective-permute-start(bf16[64,1024]{1,0:T(8,128)(2,1)S(1)} %get-tuple-element.22), channel_id=1, source_target_pairs={{0,8},{1,9},{2,10},{3,11},{4,12},{5,13},{6,14},{7,15},{8,0},{9,1},... | collective-permute-start | bytes 393224 | tf_op jit(solution)/shard_map/ppermute | solution.py:28
  4.1 3.5 %collective-permute-done.1 = bf16[64,1024]{1,0:T(8,128)(2,1)S(1)} collective-permute-done((bf16[64,1024]{1,0:T(8,128)(2,1)S(1)}, bf16[64,1024]{1,0:T(8,128)(2,1)S(1)}, u32[]{:S(2)}, u32[]{:S(2)}) %collective-permute-start.1) | collective-permute-done | bytes 131104 | tf_op jit(solution)/shard_map/ppermute | solution.py:28
  7.6 1.8 %collective-permute-start.2 = (bf16[64,1024]{1,0:T(8,128)(2,1)S(1)}, bf16[64,1024]{1,0:T(8,128)(2,1)S(1)}, u32[]{:S(2)}, u32[]{:S(2)}) collective-permute-start(bf16[64,1024]{1,0:T(8,128)(2,1)S(1)} %get-tuple-element.25), channel_id=1, source_target_pairs={{0,8},{1,9},{2,10},{3,11},{4,12},{5,13},{6,14},{7,15},{8,0},{9,1},... | collective-permute-start | bytes 393224 | tf_op jit(solution)/shard_map/ppermute | solution.py:28
  9.4 1.6 %collective-permute-start = (bf16[256,1024]{1,0:T(8,128)(2,1)S(1)}, bf16[256,1024]{1,0:T(8,128)(2,1)S(1)}, u32[]{:S(2)}, u32[]{:S(2)}) collective-permute-start(bf16[256,1024]{1,0:T(8,128)(2,1)S(1)} %copy-done), channel_id=1, source_target_pairs={{0,1},{1,0},{2,3},{3,2},{4,5},{5,4},{6,7},{7,6},{8,9},{9,8},{10,11... | collective-permute-start | bytes 1572872 | tf_op jit(solution)/shard_map/ppermute | solution.py:28
  11.0 2.6 %collective-permute-start.5 = (bf16[64,1024]{1,0:T(8,128)(2,1)S(1)}, bf16[64,1024]{1,0:T(8,128)(2,1)S(1)}, u32[]{:S(2)}, u32[]{:S(2)}) collective-permute-start(bf16[64,1024]{1,0:T(8,128)(2,1)S(1)} %get-tuple-element.30), channel_id=1, source_target_pairs={{0,2},{1,3},{2,0},{3,1},{4,6},{5,7},{6,4},{7,5},{8,10},{9,11},{10,... | collective-permute-start | bytes 393224 | tf_op jit(solution)/shard_map/ppermute | solution.py:28
  13.6 2.0 %collective-permute-start.3 = (bf16[64,1024]{1,0:T(8,128)(2,1)S(1)}, bf16[64,1024]{1,0:T(8,128)(2,1)S(1)}, u32[]{:S(2)}, u32[]{:S(2)}) collective-permute-start(bf16[64,1024]{1,0:T(8,128)(2,1)S(1)} %get-tuple-element.28), channel_id=1, source_target_pairs={{0,2},{1,3},{2,0},{3,1},{4,6},{5,7},{6,4},{7,5},{8,10},{9,11},{10,... | collective-permute-start | bytes 393224 | tf_op jit(solution)/shard_map/ppermute | solution.py:28
  15.6 0.2 multiply_reduce_fusion.1
  15.8 9.4 %collective-permute-done.5 = bf16[64,1024]{1,0:T(8,128)(2,1)S(1)} collective-permute-done((bf16[64,1024]{1,0:T(8,128)(2,1)S(1)}, bf16[64,1024]{1,0:T(8,128)(2,1)S(1)}, u32[]{:S(2)}, u32[]{:S(2)}) %collective-permute-start.5) | collective-permute-done | bytes 131104 | tf_op jit(solution)/shard_map/ppermute | solution.py:28
  25.2 0.1 multiply_reduce_fusion.3
  25.3 1.3 %collective-permute-done.3 = bf16[64,1024]{1,0:T(8,128)(2,1)S(1)} collective-permute-done((bf16[64,1024]{1,0:T(8,128)(2,1)S(1)}, bf16[64,1024]{1,0:T(8,128)(2,1)S(1)}, u32[]{:S(2)}, u32[]{:S(2)}) %collective-permute-start.3) | collective-permute-done | bytes 131104 | tf_op jit(solution)/shard_map/ppermute | solution.py:28
  26.6 0.9 %collective-permute-done = bf16[256,1024]{1,0:T(8,128)(2,1)S(1)} collective-permute-done((bf16[256,1024]{1,0:T(8,128)(2,1)S(1)}, bf16[256,1024]{1,0:T(8,128)(2,1)S(1)}, u32[]{:S(2)}, u32[]{:S(2)}) %collective-permute-start) | collective-permute-done | bytes 524320 | tf_op jit(solution)/shard_map/ppermute | solution.py:28
  27.5 0.2 multiply_reduce_fusion
  27.8 0.1 broadcast_select_fusion
  27.9 0.3 fusion.42
  28.3 0.2 multiply_reduce_fusion.4
  28.6 0.3 fusion.43
  28.9 0.1 multiply_convert_fusion
  29.1 3.1 %collective-permute-start.8 = (f16[264,128]{1,0:T(8,128)(2,1)S(1)}, f16[264,128]{1,0:T(8,128)(2,1)S(1)}, u32[]{:S(2)}, u32[]{:S(2)}) collective-permute-start(f16[264,128]{1,0:T(8,128)(2,1)S(1)} %concatenate.15), channel_id=1, source_target_pairs={{0,2},{1,3},{2,0},{3,1},{4,6},{5,7},{6,4},{7,5},{8,10},{9,11},{10,... | collective-permute-start | bytes 202760 | tf_op jit(solution)/shard_map/ppermute | solution.py:28
  32.2 0.3 fusion.44
  32.5 0.3 convolution_add_fusion
  32.8 0.1 multiply_reduce_fusion.2
  33.0 1.7 %collective-permute-done.8 = f16[264,128]{1,0:T(8,128)(2,1)S(1)} collective-permute-done((f16[264,128]{1,0:T(8,128)(2,1)S(1)}, f16[264,128]{1,0:T(8,128)(2,1)S(1)}, u32[]{:S(2)}, u32[]{:S(2)}) %collective-permute-start.8) | collective-permute-done | bytes 67616 | tf_op jit(solution)/shard_map/ppermute | solution.py:28
  34.7 0.8 %fusion.3 = f32[256,128]{1,0:T(8,128)} fusion(f32[256,128]{1,0:T(8,128)S(1)} %convolution_add_fusion, f32[264,128]{1,0:T(8,128)S(1)} %convert_element_type.61, f32[128]{0:T(128)S(1)} %rsqrt_bitcast_fusion, f32[256]{0:T(256)S(1)} %fusion.24, f32[128]{0:T(128)S(1)} %get-tuple-element.39, f32[256]{0:T(256)S(1)} %get-tuple-element.37), kind=kLoop, calls=%fused_computation.16 | loop fusion | flops 163840 | bytes 396288 | tf_op jit(solution)/shard_map/mul | solution.py:34
  (27 shorter events, 0.5 us)
Async XLA Ops:
  0.0 9.4 %copy-start = (bf16[256,1024]{1,0:T(8,128)(2,1)S(1)}, bf16[256,1024]{1,0:T(8,128)(2,1)}, u32[]{:S(2)}) copy-start(bf16[256,1024]{1,0:T(8,128)(2,1)} %param.2) | copy-start | bytes 1572868
  1.0 6.5 %collective-permute-start.1 = (bf16[64,1024]{1,0:T(8,128)(2,1)S(1)}, bf16[64,1024]{1,0:T(8,128)(2,1)S(1)}, u32[]{:S(2)}, u32[]{:S(2)}) collective-permute-start(bf16[64,1024]{1,0:T(8,128)(2,1)S(1)} %get-tuple-element.22), channel_id=1, source_target_pairs={{0,8},{1,9},{2,10},{3,11},{4,12},{5,13},{6,14},{7,15},{8,0},{9,1},... | collective-permute-start | bytes 393224 | tf_op jit(solution)/shard_map/ppermute | solution.py:28
  7.6 6.0 %collective-permute-start.2 = (bf16[64,1024]{1,0:T(8,128)(2,1)S(1)}, bf16[64,1024]{1,0:T(8,128)(2,1)S(1)}, u32[]{:S(2)}, u32[]{:S(2)}) collective-permute-start(bf16[64,1024]{1,0:T(8,128)(2,1)S(1)} %get-tuple-element.25), channel_id=1, source_target_pairs={{0,8},{1,9},{2,10},{3,11},{4,12},{5,13},{6,14},{7,15},{8,0},{9,1},... | collective-permute-start | bytes 393224 | tf_op jit(solution)/shard_map/ppermute | solution.py:28
  9.4 18.1 %collective-permute-start = (bf16[256,1024]{1,0:T(8,128)(2,1)S(1)}, bf16[256,1024]{1,0:T(8,128)(2,1)S(1)}, u32[]{:S(2)}, u32[]{:S(2)}) collective-permute-start(bf16[256,1024]{1,0:T(8,128)(2,1)S(1)} %copy-done), channel_id=1, source_target_pairs={{0,1},{1,0},{2,3},{3,2},{4,5},{5,4},{6,7},{7,6},{8,9},{9,8},{10,11... | collective-permute-start | bytes 1572872 | tf_op jit(solution)/shard_map/ppermute | solution.py:28
  11.0 14.2 %collective-permute-start.5 = (bf16[64,1024]{1,0:T(8,128)(2,1)S(1)}, bf16[64,1024]{1,0:T(8,128)(2,1)S(1)}, u32[]{:S(2)}, u32[]{:S(2)}) collective-permute-start(bf16[64,1024]{1,0:T(8,128)(2,1)S(1)} %get-tuple-element.30), channel_id=1, source_target_pairs={{0,2},{1,3},{2,0},{3,1},{4,6},{5,7},{6,4},{7,5},{8,10},{9,11},{10,... | collective-permute-start | bytes 393224 | tf_op jit(solution)/shard_map/ppermute | solution.py:28
  13.6 13.0 %collective-permute-start.3 = (bf16[64,1024]{1,0:T(8,128)(2,1)S(1)}, bf16[64,1024]{1,0:T(8,128)(2,1)S(1)}, u32[]{:S(2)}, u32[]{:S(2)}) collective-permute-start(bf16[64,1024]{1,0:T(8,128)(2,1)S(1)} %get-tuple-element.28), channel_id=1, source_target_pairs={{0,2},{1,3},{2,0},{3,1},{4,6},{5,7},{6,4},{7,5},{8,10},{9,11},{10,... | collective-permute-start | bytes 393224 | tf_op jit(solution)/shard_map/ppermute | solution.py:28
  15.6 11.0 %collective-permute-start.4 = (bf16[128,1024]{1,0:T(8,128)(2,1)S(1)}, bf16[128,1024]{1,0:T(8,128)(2,1)S(1)}, u32[]{:S(2)}, u32[]{:S(2)}) collective-permute-start(bf16[128,1024]{1,0:T(8,128)(2,1)S(1)} %pad_maximum_fusion), channel_id=1, source_target_pairs={{0,4},{1,5},{2,6},{3,7},{4,0},{5,1},{6,2},{7,3},{8,12},{9,13},{10,... | collective-permute-start | bytes 786440 | tf_op jit(solution)/shard_map/ppermute | solution.py:28
  25.2 3.0 %collective-permute-start.6 = (bf16[64,1024]{1,0:T(8,128)(2,1)S(1)}, bf16[64,1024]{1,0:T(8,128)(2,1)S(1)}, u32[]{:S(2)}, u32[]{:S(2)}) collective-permute-start(bf16[64,1024]{1,0:T(8,128)(2,1)S(1)} %collective-permute-done.5), channel_id=1, source_target_pairs={{0,4},{1,5},{2,6},{3,7},{4,0},{5,1},{6,2},{7,3},{8,12},{9,13},{10,... | collective-permute-start | bytes 393224 | tf_op jit(solution)/shard_map/ppermute | solution.py:28
  26.6 1.6 %collective-permute-start.7 = (bf16[64,1024]{1,0:T(8,128)(2,1)S(1)}, bf16[64,1024]{1,0:T(8,128)(2,1)S(1)}, u32[]{:S(2)}, u32[]{:S(2)}) collective-permute-start(bf16[64,1024]{1,0:T(8,128)(2,1)S(1)} %collective-permute-done.3), channel_id=1, source_target_pairs={{0,4},{1,5},{2,6},{3,7},{4,0},{5,1},{6,2},{7,3},{8,12},{9,13},{10,... | collective-permute-start | bytes 393224 | tf_op jit(solution)/shard_map/ppermute | solution.py:28
  29.1 5.6 %collective-permute-start.8 = (f16[264,128]{1,0:T(8,128)(2,1)S(1)}, f16[264,128]{1,0:T(8,128)(2,1)S(1)}, u32[]{:S(2)}, u32[]{:S(2)}) collective-permute-start(f16[264,128]{1,0:T(8,128)(2,1)S(1)} %concatenate.15), channel_id=1, source_target_pairs={{0,2},{1,3},{2,0},{3,1},{4,6},{5,7},{6,4},{7,5},{8,10},{9,11},{10,... | collective-permute-start | bytes 202760 | tf_op jit(solution)/shard_map/ppermute | solution.py:28

commit v27 on v21

--- a/solution.py
+++ b/solution.py
@@ -62,9 +62,10 @@
     nears, crosses = [], []
     for half in lax.optimization_barrier((right_docs[:width // 2], right_docs[width // 2:])):
         swapped = moved(half, side, lambda r, c: (r ^ 2, c))
-        near, leaving = lax.optimization_barrier((jnp.where(at_home, half, swapped), jnp.where(at_home, swapped, half)))
+        pieces = jnp.split(jnp.where(at_home, swapped, half), 2)
+        near, *leaving = lax.optimization_barrier((jnp.where(at_home, half, swapped), *pieces))
         nears.append(near)
-        crosses.append(moved(leaving, side, lambda r, c: (r, c ^ 2)))
+        crosses.append(jnp.concatenate([moved(piece, side, lambda r, c: (r, c ^ 2)) for piece in leaving]))
     left_other = moved(left_docs, side, lambda r, c: (r, c ^ 1))
     near = lax.optimization_barrier(jnp.concatenate(nears))
     near_other = other_core(near)

time: 31.5 us -> 34.1 us (1.083)
  starting transfers between devices: 13.3 us -> 17.8 us
  waiting for transfers between devices: 13.4 us -> 11.4 us
    ppermute x9 -> x11, starting transfers between devices: 13.3 us -> 17.8 us  [moved(): return lax.ppermute(value, ('row', 'col'), pairs)]
    ppermute x9 -> x11, waiting for transfers between devices: 13.4 us -> 11.4 us  [moved(): return lax.ppermute(value, ('row', 'col'), pairs)]
  transfers between devices with their start and end apart: 9 -> 11, of which waited for: 5 -> 5; matrix products, arithmetic and copies ran while one was open for 6% -> 5% of each run, Pallas kernels for 0% -> 0%
where the time goes in v27:
time: 34.1 us; the launch traced here: 33.9 us
  starting transfers between devices  17.8 us (52%)
  waiting for transfers between devices  11.4 us (33%)
  other arithmetic  2.18 us (6%)
  matrix products  1.22 us (4%)
  local copies, waits for them, and re-layouts  1.14 us (3%)
    ppermute x11, starting transfers between devices, moved(): return lax.ppermute(value, ('row', 'col'), pairs)  17.8 us
    ppermute x11, waiting for transfers between devices, moved(): return lax.ppermute(value, ('row', 'col'), pairs)  11.4 us
    dot_general x4, matrix products, contract(): lax.dot_general(left_part, right_part, (((1,), (1,)), ((), ())), preferre...  1.22 us
    slice x1, local copies, waits for them, and re-layouts, on_square_grid(): right_docs[width // 2:]  1.04 us
    reduce_sum x5, other arithmetic, squares(): return jnp.sum(widened * widened, axis=1)  0.82 us
    mul x3, other arithmetic, finish(): return summed / feat_total * left_scale[:, None] * right_scale[None, :]  0.81 us
  transfers between devices with their start and end apart: 11, of which 5 were waited for; matrix products, arithmetic and copies ran while one was open for 5% of the time, Pallas kernels for 0%

profile of v27, /device:TPU:0, one launch (start us, length us, event | category | flops | bytes accessed | tf_op | source)
XLA Modules:
  0.0 33.9 jit_solution(9063954677861135294)
XLA Ops:
  0.0 1.0 %fusion.41 = (bf16[64,1024]{1,0:T(8,128)(2,1)S(1)}, bf16[64,1024]{1,0:T(8,128)(2,1)S(1)}) fusion(bf16[128,1024]{1,0:T(8,128)(2,1)} %param.3), kind=kLoop, calls=%fused_computation.78 | loop fusion | bytes 524288 | tf_op jit(solution)/shard_map/slice | solution.py:63
  1.0 3.0 %collective-permute-start.1 = (bf16[64,1024]{1,0:T(8,128)(2,1)S(1)}, bf16[64,1024]{1,0:T(8,128)(2,1)S(1)}, u32[]{:S(2)}, u32[]{:S(2)}) collective-permute-start(bf16[64,1024]{1,0:T(8,128)(2,1)S(1)} %get-tuple-element.23), channel_id=1, source_target_pairs={{0,8},{1,9},{2,10},{3,11},{4,12},{5,13},{6,14},{7,15},{8,0},{9,1},... | collective-permute-start | bytes 393224 | tf_op jit(solution)/shard_map/ppermute | solution.py:28
  4.1 2.0 %collective-permute-start = (bf16[256,1024]{1,0:T(8,128)(2,1)S(1)}, bf16[256,1024]{1,0:T(8,128)(2,1)S(1)}, u32[]{:S(2)}, u32[]{:S(2)}) collective-permute-start(bf16[256,1024]{1,0:T(8,128)(2,1)S(1)} %copy-done), channel_id=1, source_target_pairs={{0,1},{1,0},{2,3},{3,2},{4,5},{5,4},{6,7},{7,6},{8,9},{9,8},{10,11... | collective-permute-start | bytes 1572872 | tf_op jit(solution)/shard_map/ppermute | solution.py:28
  6.2 0.2 multiply_reduce_fusion.1
  6.3 2.0 %collective-permute-done.1 = bf16[64,1024]{1,0:T(8,128)(2,1)S(1)} collective-permute-done((bf16[64,1024]{1,0:T(8,128)(2,1)S(1)}, bf16[64,1024]{1,0:T(8,128)(2,1)S(1)}, u32[]{:S(2)}, u32[]{:S(2)}) %collective-permute-start.1) | collective-permute-done | bytes 131104 | tf_op jit(solution)/shard_map/ppermute | solution.py:28
  8.4 3.2 %collective-permute-start.6 = (bf16[32,1024]{1,0:T(8,128)(2,1)S(1)}, bf16[32,1024]{1,0:T(8,128)(2,1)S(1)}, u32[]{:S(2)}, u32[]{:S(2)}) collective-permute-start(bf16[32,1024]{1,0:T(8,128)(2,1)S(1)} %get-tuple-element.31), channel_id=1, source_target_pairs={{0,2},{1,3},{2,0},{3,1},{4,6},{5,7},{6,4},{7,5},{8,10},{9,11},{10,... | collective-permute-start | bytes 196616 | tf_op jit(solution)/shard_map/ppermute | solution.py:28
  11.9 0.1 multiply_reduce_fusion.3
  12.0 2.9 %collective-permute-start.3 = (bf16[32,1024]{1,0:T(8,128)(2,1)S(1)}, bf16[32,1024]{1,0:T(8,128)(2,1)S(1)}, u32[]{:S(2)}, u32[]{:S(2)}) collective-permute-start(bf16[32,1024]{1,0:T(8,128)(2,1)S(1)} %get-tuple-element.28), channel_id=1, source_target_pairs={{0,2},{1,3},{2,0},{3,1},{4,6},{5,7},{6,4},{7,5},{8,10},{9,11},{10,... | collective-permute-start | bytes 196616 | tf_op jit(solution)/shard_map/ppermute | solution.py:28
  14.9 4.7 %collective-permute-done.6 = bf16[32,1024]{1,0:T(8,128)(2,1)S(1)} collective-permute-done((bf16[32,1024]{1,0:T(8,128)(2,1)S(1)}, bf16[32,1024]{1,0:T(8,128)(2,1)S(1)}, u32[]{:S(2)}, u32[]{:S(2)}) %collective-permute-start.6) | collective-permute-done | bytes 65568 | tf_op jit(solution)/shard_map/ppermute | solution.py:28
  19.6 3.5 %collective-permute-start.4 = (bf16[32,1024]{1,0:T(8,128)(2,1)S(1)}, bf16[32,1024]{1,0:T(8,128)(2,1)S(1)}, u32[]{:S(2)}, u32[]{:S(2)}) collective-permute-start(bf16[32,1024]{1,0:T(8,128)(2,1)S(1)} %get-tuple-element.29), channel_id=1, source_target_pairs={{0,2},{1,3},{2,0},{3,1},{4,6},{5,7},{6,4},{7,5},{8,10},{9,11},{10,... | collective-permute-start | bytes 196616 | tf_op jit(solution)/shard_map/ppermute | solution.py:28
  23.2 2.4 %collective-permute-done.4 = bf16[32,1024]{1,0:T(8,128)(2,1)S(1)} collective-permute-done((bf16[32,1024]{1,0:T(8,128)(2,1)S(1)}, bf16[32,1024]{1,0:T(8,128)(2,1)S(1)}, u32[]{:S(2)}, u32[]{:S(2)}) %collective-permute-start.4) | collective-permute-done | bytes 65568 | tf_op jit(solution)/shard_map/ppermute | solution.py:28
  25.7 0.2 multiply_reduce_fusion
  26.0 0.1 broadcast_select_fusion
  26.1 0.3 fusion.44
  26.4 0.6 %collective-permute-done.9 = bf16[64,1024]{1,0:T(8,128)(2,1)S(1)} collective-permute-done((bf16[64,1024]{1,0:T(8,128)(2,1)S(1)}, bf16[64,1024]{1,0:T(8,128)(2,1)S(1)}, u32[]{:S(2)}, u32[]{:S(2)}) %collective-permute-start.9) | collective-permute-done | bytes 131104 | tf_op jit(solution)/shard_map/ppermute | solution.py:28
  27.0 0.2 multiply_reduce_fusion.4
  27.3 0.3 fusion.45
  27.6 0.1 multiply_convert_fusion
  27.8 2.8 %collective-permute-start.10 = (f16[264,128]{1,0:T(8,128)(2,1)S(1)}, f16[264,128]{1,0:T(8,128)(2,1)S(1)}, u32[]{:S(2)}, u32[]{:S(2)}) collective-permute-start(f16[264,128]{1,0:T(8,128)(2,1)S(1)} %concatenate.24), channel_id=1, source_target_pairs={{0,2},{1,3},{2,0},{3,1},{4,6},{5,7},{6,4},{7,5},{8,10},{9,11},{10,... | collective-permute-start | bytes 202760 | tf_op jit(solution)/shard_map/ppermute | solution.py:28
  30.6 0.3 fusion.46
  30.9 0.3 convolution_add_fusion
  31.2 0.1 multiply_reduce_fusion.2
  31.3 1.7 %collective-permute-done.10 = f16[264,128]{1,0:T(8,128)(2,1)S(1)} collective-permute-done((f16[264,128]{1,0:T(8,128)(2,1)S(1)}, f16[264,128]{1,0:T(8,128)(2,1)S(1)}, u32[]{:S(2)}, u32[]{:S(2)}) %collective-permute-start.10) | collective-permute-done | bytes 67616 | tf_op jit(solution)/shard_map/ppermute | solution.py:28
  33.1 0.8 %fusion.3 = f32[256,128]{1,0:T(8,128)} fusion(f32[256,128]{1,0:T(8,128)S(1)} %convolution_add_fusion, f32[264,128]{1,0:T(8,128)S(1)} %convert_element_type.61, f32[128]{0:T(128)S(1)} %rsqrt_bitcast_fusion, f32[256]{0:T(256)S(1)} %fusion.24, f32[128]{0:T(128)S(1)} %get-tuple-element.41, f32[256]{0:T(256)S(1)} %get-tuple-element.39), kind=kLoop, calls=%fused_computation.16 | loop fusion | flops 163840 | bytes 396288 | tf_op jit(solution)/shard_map/mul | solution.py:34
  (35 shorter events, 0.9 us)
Async XLA Ops:
  0.0 4.1 %copy-start = (bf16[256,1024]{1,0:T(8,128)(2,1)S(1)}, bf16[256,1024]{1,0:T(8,128)(2,1)}, u32[]{:S(2)}) copy-start(bf16[256,1024]{1,0:T(8,128)(2,1)} %param.2) | copy-start | bytes 1572868
  1.0 7.3 %collective-permute-start.1 = (bf16[64,1024]{1,0:T(8,128)(2,1)S(1)}, bf16[64,1024]{1,0:T(8,128)(2,1)S(1)}, u32[]{:S(2)}, u32[]{:S(2)}) collective-permute-start(bf16[64,1024]{1,0:T(8,128)(2,1)S(1)} %get-tuple-element.23), channel_id=1, source_target_pairs={{0,8},{1,9},{2,10},{3,11},{4,12},{5,13},{6,14},{7,15},{8,0},{9,1},... | collective-permute-start | bytes 393224 | tf_op jit(solution)/shard_map/ppermute | solution.py:28
  4.1 7.7 %collective-permute-start.2 = (bf16[64,1024]{1,0:T(8,128)(2,1)S(1)}, bf16[64,1024]{1,0:T(8,128)(2,1)S(1)}, u32[]{:S(2)}, u32[]{:S(2)}) collective-permute-start(bf16[64,1024]{1,0:T(8,128)(2,1)S(1)} %get-tuple-element.25), channel_id=1, source_target_pairs={{0,8},{1,9},{2,10},{3,11},{4,12},{5,13},{6,14},{7,15},{8,0},{9,1},... | collective-permute-start | bytes 393224 | tf_op jit(solution)/shard_map/ppermute | solution.py:28
  4.1 21.5 %collective-permute-start = (bf16[256,1024]{1,0:T(8,128)(2,1)S(1)}, bf16[256,1024]{1,0:T(8,128)(2,1)S(1)}, u32[]{:S(2)}, u32[]{:S(2)}) collective-permute-start(bf16[256,1024]{1,0:T(8,128)(2,1)S(1)} %copy-done), channel_id=1, source_target_pairs={{0,1},{1,0},{2,3},{3,2},{4,5},{5,4},{6,7},{7,6},{8,9},{9,8},{10,11... | collective-permute-start | bytes 1572872 | tf_op jit(solution)/shard_map/ppermute | solution.py:28
  8.4 11.2 %collective-permute-start.6 = (bf16[32,1024]{1,0:T(8,128)(2,1)S(1)}, bf16[32,1024]{1,0:T(8,128)(2,1)S(1)}, u32[]{:S(2)}, u32[]{:S(2)}) collective-permute-start(bf16[32,1024]{1,0:T(8,128)(2,1)S(1)} %get-tuple-element.31), channel_id=1, source_target_pairs={{0,2},{1,3},{2,0},{3,1},{4,6},{5,7},{6,4},{7,5},{8,10},{9,11},{10,... | collective-permute-start | bytes 196616 | tf_op jit(solution)/shard_map/ppermute | solution.py:28
  11.6 11.4 %collective-permute-start.7 = (bf16[32,1024]{1,0:T(8,128)(2,1)S(1)}, bf16[32,1024]{1,0:T(8,128)(2,1)S(1)}, u32[]{:S(2)}, u32[]{:S(2)}) collective-permute-start(bf16[32,1024]{1,0:T(8,128)(2,1)S(1)} %get-tuple-element.32), channel_id=1, source_target_pairs={{0,2},{1,3},{2,0},{3,1},{4,6},{5,7},{6,4},{7,5},{8,10},{9,11},{10,... | collective-permute-start | bytes 196616 | tf_op jit(solution)/shard_map/ppermute | solution.py:28
  11.8 13.8 %collective-permute-start.5 = (bf16[128,1024]{1,0:T(8,128)(2,1)S(1)}, bf16[128,1024]{1,0:T(8,128)(2,1)S(1)}, u32[]{:S(2)}, u32[]{:S(2)}) collective-permute-start(bf16[128,1024]{1,0:T(8,128)(2,1)S(1)} %pad_maximum_fusion), channel_id=1, source_target_pairs={{0,4},{1,5},{2,6},{3,7},{4,0},{5,1},{6,2},{7,3},{8,12},{9,13},{10,... | collective-permute-start | bytes 786440 | tf_op jit(solution)/shard_map/ppermute | solution.py:28
  12.0 11.2 %collective-permute-start.3 = (bf16[32,1024]{1,0:T(8,128)(2,1)S(1)}, bf16[32,1024]{1,0:T(8,128)(2,1)S(1)}, u32[]{:S(2)}, u32[]{:S(2)}) collective-permute-start(bf16[32,1024]{1,0:T(8,128)(2,1)S(1)} %get-tuple-element.28), channel_id=1, source_target_pairs={{0,2},{1,3},{2,0},{3,1},{4,6},{5,7},{6,4},{7,5},{8,10},{9,11},{10,... | collective-permute-start | bytes 196616 | tf_op jit(solution)/shard_map/ppermute | solution.py:28
  19.6 5.9 %collective-permute-start.4 = (bf16[32,1024]{1,0:T(8,128)(2,1)S(1)}, bf16[32,1024]{1,0:T(8,128)(2,1)S(1)}, u32[]{:S(2)}, u32[]{:S(2)}) collective-permute-start(bf16[32,1024]{1,0:T(8,128)(2,1)S(1)} %get-tuple-element.29), channel_id=1, source_target_pairs={{0,2},{1,3},{2,0},{3,1},{4,6},{5,7},{6,4},{7,5},{8,10},{9,11},{10,... | collective-permute-start | bytes 196616 | tf_op jit(solution)/shard_map/ppermute | solution.py:28
  23.1 3.3 %collective-permute-start.8 = (bf16[64,1024]{1,0:T(8,128)(2,1)S(1)}, bf16[64,1024]{1,0:T(8,128)(2,1)S(1)}, u32[]{:S(2)}, u32[]{:S(2)}) collective-permute-start(bf16[64,1024]{1,0:T(8,128)(2,1)S(1)} %pad_maximum_fusion.4), channel_id=1, source_target_pairs={{0,4},{1,5},{2,6},{3,7},{4,0},{5,1},{6,2},{7,3},{8,12},{9,13},{10,... | collective-permute-start | bytes 393224 | tf_op jit(solution)/shard_map/ppermute | solution.py:28
  25.6 1.4 %collective-permute-start.9 = (bf16[64,1024]{1,0:T(8,128)(2,1)S(1)}, bf16[64,1024]{1,0:T(8,128)(2,1)S(1)}, u32[]{:S(2)}, u32[]{:S(2)}) collective-permute-start(bf16[64,1024]{1,0:T(8,128)(2,1)S(1)} %pad_maximum_fusion.3), channel_id=1, source_target_pairs={{0,4},{1,5},{2,6},{3,7},{4,0},{5,1},{6,2},{7,3},{8,12},{9,13},{10,... | collective-permute-start | bytes 393224 | tf_op jit(solution)/shard_map/ppermute | solution.py:28
  27.8 5.2 %collective-permute-start.10 = (f16[264,128]{1,0:T(8,128)(2,1)S(1)}, f16[264,128]{1,0:T(8,128)(2,1)S(1)}, u32[]{:S(2)}, u32[]{:S(2)}) collective-permute-start(f16[264,128]{1,0:T(8,128)(2,1)S(1)} %concatenate.24), channel_id=1, source_target_pairs={{0,2},{1,3},{2,0},{3,1},{4,6},{5,7},{6,4},{7,5},{8,10},{9,11},{10,... | collective-permute-start | bytes 202760 | tf_op jit(solution)/shard_map/ppermute | solution.py:28

commit v28 on v22

--- a/solution.py
+++ b/solution.py
@@ -77,7 +77,7 @@
 
     near_other = other_core(near)
     cross_gram = contract(lefts[0], cross)
-    cross_other, cross_gram = lax.optimization_barrier((other_core(cross), cross_gram))
+    cross_other, cross_gram = lax.optimization_barrier((jnp.concatenate([other_core(part) for part in crosses]), cross_gram))
     cross_gram = cross_gram + contract(lefts[1], cross_other)
     cross_sq = squares(cross) + squares(cross_other)
     left_sq = squares(left_docs) + squares(left_other)
@@ -91,7 +91,7 @@
     message = jnp.concatenate([tile.astype(jnp.float16), *sums, spare])
     got = moved(message, side, lambda r, c: (r, c ^ 2))
 
-    near_other, _ = lax.optimization_barrier((near_other, message))
+    near, near_other, _ = lax.optimization_barrier((near, near_other, message))
     near_gram, near_sq = half_sum(near, near_other)
     near_gram, got = lax.optimization_barrier((near_gram, got))
     got = got.astype(jnp.float32)

time: 32.1 us -> 32.2 us (level)
    ppermute x8 -> x9, starting transfers between devices: 12.7 us -> 13 us  [moved(): return lax.ppermute(value, ('row', 'col'), pairs)]
    ppermute x8 -> x9, waiting for transfers between devices: 14.5 us -> 14.4 us  [moved(): return lax.ppermute(value, ('row', 'col'), pairs)]
    reduce_sum x6 -> x5, other arithmetic: 0.9 us -> 0.82 us  [squares(): return jnp.sum(widened * widened, axis=1)]
  transfers between devices with their start and end apart: 8 -> 9, of which waited for: 5 -> 5; matrix products, arithmetic and copies ran while one was open for 8% -> 8% of each run, Pallas kernels for 0% -> 0%
where the time goes in v28:
time: 32.2 us; the launch traced here: 32.1 us
  waiting for transfers between devices  14.4 us (45%)
  starting transfers between devices  13 us (40%)
  other arithmetic  2.16 us (7%)
  matrix products  1.21 us (4%)
  local copies, waits for them, and re-layouts  1.12 us (3%)
    ppermute x9, waiting for transfers between devices, moved(): return lax.ppermute(value, ('row', 'col'), pairs)  14.4 us
    ppermute x9, starting transfers between devices, moved(): return lax.ppermute(value, ('row', 'col'), pairs)  13 us
    dot_general x4, matrix products, contract(): lax.dot_general(left_part, right_part, (((1,), (1,)), ((), ())), preferre...  1.21 us
    slice x1, local copies, waits for them, and re-layouts, on_square_grid(): right_docs[width // 2:]  1.04 us
    reduce_sum x5, other arithmetic, squares(): return jnp.sum(widened * widened, axis=1)  0.82 us
    mul x3, other arithmetic, finish(): return summed / feat_total * left_scale[:, None] * right_scale[None, :]  0.81 us
  transfers between devices with their start and end apart: 9, of which 5 were waited for; matrix products, arithmetic and copies ran while one was open for 8% of the time, Pallas kernels for 0%

profile of v28, /device:TPU:0, one launch (start us, length us, event | category | flops | bytes accessed | tf_op | source)
XLA Modules:
  0.0 32.1 jit_solution(2056368329686649567)
XLA Ops:
  0.0 1.0 %fusion.41 = (bf16[64,1024]{1,0:T(8,128)(2,1)S(1)}, bf16[64,1024]{1,0:T(8,128)(2,1)S(1)}) fusion(bf16[128,1024]{1,0:T(8,128)(2,1)} %param.3), kind=kLoop, calls=%fused_computation.76 | loop fusion | bytes 524288 | tf_op jit(solution)/shard_map/slice | solution.py:63
  1.0 3.0 %collective-permute-start = (bf16[64,1024]{1,0:T(8,128)(2,1)S(1)}, bf16[64,1024]{1,0:T(8,128)(2,1)S(1)}, u32[]{:S(2)}, u32[]{:S(2)}) collective-permute-start(bf16[64,1024]{1,0:T(8,128)(2,1)S(1)} %get-tuple-element.21), channel_id=1, source_target_pairs={{0,8},{1,9},{2,10},{3,11},{4,12},{5,13},{6,14},{7,15},{8,0},{9,1},... | collective-permute-start | bytes 393224 | tf_op jit(solution)/shard_map/ppermute | solution.py:28
  4.1 0.1 collective-permute-start.3
  4.1 2.0 %collective-permute-start.2 = (bf16[256,1024]{1,0:T(8,128)(2,1)S(1)}, bf16[256,1024]{1,0:T(8,128)(2,1)S(1)}, u32[]{:S(2)}, u32[]{:S(2)}) collective-permute-start(bf16[256,1024]{1,0:T(8,128)(2,1)S(1)} %copy-done), channel_id=1, source_target_pairs={{0,1},{1,0},{2,3},{3,2},{4,5},{5,4},{6,7},{7,6},{8,9},{9,8},{10,11... | collective-permute-start | bytes 1572872 | tf_op jit(solution)/shard_map/ppermute | solution.py:28
  6.2 2.2 %collective-permute-done = bf16[64,1024]{1,0:T(8,128)(2,1)S(1)} collective-permute-done((bf16[64,1024]{1,0:T(8,128)(2,1)S(1)}, bf16[64,1024]{1,0:T(8,128)(2,1)S(1)}, u32[]{:S(2)}, u32[]{:S(2)}) %collective-permute-start) | collective-permute-done | bytes 131104 | tf_op jit(solution)/shard_map/ppermute | solution.py:28
  8.4 3.2 %collective-permute-start.1 = (bf16[64,1024]{1,0:T(8,128)(2,1)S(1)}, bf16[64,1024]{1,0:T(8,128)(2,1)S(1)}, u32[]{:S(2)}, u32[]{:S(2)}) collective-permute-start(bf16[64,1024]{1,0:T(8,128)(2,1)S(1)} %get-tuple-element.22), channel_id=1, source_target_pairs={{0,2},{1,3},{2,0},{3,1},{4,6},{5,7},{6,4},{7,5},{8,10},{9,11},{10,... | collective-permute-start | bytes 393224 | tf_op jit(solution)/shard_map/ppermute | solution.py:28
  11.7 1.6 %collective-permute-start.5 = (bf16[64,1024]{1,0:T(8,128)(2,1)S(1)}, bf16[64,1024]{1,0:T(8,128)(2,1)S(1)}, u32[]{:S(2)}, u32[]{:S(2)}) collective-permute-start(bf16[64,1024]{1,0:T(8,128)(2,1)S(1)} %get-tuple-element.28), channel_id=1, source_target_pairs={{0,2},{1,3},{2,0},{3,1},{4,6},{5,7},{6,4},{7,5},{8,10},{9,11},{10,... | collective-permute-start | bytes 393224 | tf_op jit(solution)/shard_map/ppermute | solution.py:28
  13.3 0.2 multiply_reduce_fusion.1
  13.6 8.8 %collective-permute-done.5 = bf16[64,1024]{1,0:T(8,128)(2,1)S(1)} collective-permute-done((bf16[64,1024]{1,0:T(8,128)(2,1)S(1)}, bf16[64,1024]{1,0:T(8,128)(2,1)S(1)}, u32[]{:S(2)}, u32[]{:S(2)}) %collective-permute-start.5) | collective-permute-done | bytes 131104 | tf_op jit(solution)/shard_map/ppermute | solution.py:28
  22.4 0.7 %collective-permute-done.2 = bf16[256,1024]{1,0:T(8,128)(2,1)S(1)} collective-permute-done((bf16[256,1024]{1,0:T(8,128)(2,1)S(1)}, bf16[256,1024]{1,0:T(8,128)(2,1)S(1)}, u32[]{:S(2)}, u32[]{:S(2)}) %collective-permute-start.2) | collective-permute-done | bytes 524320 | tf_op jit(solution)/shard_map/ppermute | solution.py:28
  23.1 0.2 multiply_reduce_fusion
  23.5 0.1 broadcast_select_fusion
  23.6 0.3 fusion.42
  24.0 0.9 %collective-permute-done.7 = bf16[64,1024]{1,0:T(8,128)(2,1)S(1)} collective-permute-done((bf16[64,1024]{1,0:T(8,128)(2,1)S(1)}, bf16[64,1024]{1,0:T(8,128)(2,1)S(1)}, u32[]{:S(2)}, u32[]{:S(2)}) %collective-permute-start.7) | collective-permute-done | bytes 131104 | tf_op jit(solution)/shard_map/ppermute | solution.py:28
  24.9 0.2 multiply_reduce_fusion.4
  25.1 0.3 fusion.43
  25.5 0.1 multiply_convert_fusion
  25.7 2.9 %collective-permute-start.8 = (f16[264,128]{1,0:T(8,128)(2,1)S(1)}, f16[264,128]{1,0:T(8,128)(2,1)S(1)}, u32[]{:S(2)}, u32[]{:S(2)}) collective-permute-start(f16[264,128]{1,0:T(8,128)(2,1)S(1)} %concatenate.15), channel_id=1, source_target_pairs={{0,2},{1,3},{2,0},{3,1},{4,6},{5,7},{6,4},{7,5},{8,10},{9,11},{10,... | collective-permute-start | bytes 202760 | tf_op jit(solution)/shard_map/ppermute | solution.py:28
  28.5 0.3 fusion.44
  28.8 0.1 multiply_reduce_fusion.3
  29.0 0.3 convolution_add_fusion
  29.3 0.1 multiply_reduce_fusion.2
  29.4 1.8 %collective-permute-done.8 = f16[264,128]{1,0:T(8,128)(2,1)S(1)} collective-permute-done((f16[264,128]{1,0:T(8,128)(2,1)S(1)}, f16[264,128]{1,0:T(8,128)(2,1)S(1)}, u32[]{:S(2)}, u32[]{:S(2)}) %collective-permute-start.8) | collective-permute-done | bytes 67616 | tf_op jit(solution)/shard_map/ppermute | solution.py:28
  31.3 0.8 %fusion.3 = f32[256,128]{1,0:T(8,128)} fusion(f32[256,128]{1,0:T(8,128)S(1)} %convolution_add_fusion, f32[264,128]{1,0:T(8,128)S(1)} %convert_element_type.61, f32[128]{0:T(128)S(1)} %rsqrt_bitcast_fusion, f32[256]{0:T(256)S(1)} %fusion.24, f32[128]{0:T(128)S(1)} %get-tuple-element.39, f32[256]{0:T(256)S(1)} %get-tuple-element.37), kind=kLoop, calls=%fused_computation.16 | loop fusion | flops 163840 | bytes 396288 | tf_op jit(solution)/shard_map/mul | solution.py:34
  (27 shorter events, 0.6 us)
Async XLA Ops:
  0.0 4.1 %copy-start = (bf16[256,1024]{1,0:T(8,128)(2,1)S(1)}, bf16[256,1024]{1,0:T(8,128)(2,1)}, u32[]{:S(2)}) copy-start(bf16[256,1024]{1,0:T(8,128)(2,1)} %param.2) | copy-start | bytes 1572868
  1.0 7.3 %collective-permute-start = (bf16[64,1024]{1,0:T(8,128)(2,1)S(1)}, bf16[64,1024]{1,0:T(8,128)(2,1)S(1)}, u32[]{:S(2)}, u32[]{:S(2)}) collective-permute-start(bf16[64,1024]{1,0:T(8,128)(2,1)S(1)} %get-tuple-element.21), channel_id=1, source_target_pairs={{0,8},{1,9},{2,10},{3,11},{4,12},{5,13},{6,14},{7,15},{8,0},{9,1},... | collective-permute-start | bytes 393224 | tf_op jit(solution)/shard_map/ppermute | solution.py:28
  4.1 7.6 %collective-permute-start.3 = (bf16[64,1024]{1,0:T(8,128)(2,1)S(1)}, bf16[64,1024]{1,0:T(8,128)(2,1)S(1)}, u32[]{:S(2)}, u32[]{:S(2)}) collective-permute-start(bf16[64,1024]{1,0:T(8,128)(2,1)S(1)} %get-tuple-element.25), channel_id=1, source_target_pairs={{0,8},{1,9},{2,10},{3,11},{4,12},{5,13},{6,14},{7,15},{8,0},{9,1},... | collective-permute-start | bytes 393224 | tf_op jit(solution)/shard_map/ppermute | solution.py:28
  4.1 19.0 %collective-permute-start.2 = (bf16[256,1024]{1,0:T(8,128)(2,1)S(1)}, bf16[256,1024]{1,0:T(8,128)(2,1)S(1)}, u32[]{:S(2)}, u32[]{:S(2)}) collective-permute-start(bf16[256,1024]{1,0:T(8,128)(2,1)S(1)} %copy-done), channel_id=1, source_target_pairs={{0,1},{1,0},{2,3},{3,2},{4,5},{5,4},{6,7},{7,6},{8,9},{9,8},{10,11... | collective-permute-start | bytes 1572872 | tf_op jit(solution)/shard_map/ppermute | solution.py:28
  8.4 14.0 %collective-permute-start.1 = (bf16[64,1024]{1,0:T(8,128)(2,1)S(1)}, bf16[64,1024]{1,0:T(8,128)(2,1)S(1)}, u32[]{:S(2)}, u32[]{:S(2)}) collective-permute-start(bf16[64,1024]{1,0:T(8,128)(2,1)S(1)} %get-tuple-element.22), channel_id=1, source_target_pairs={{0,2},{1,3},{2,0},{3,1},{4,6},{5,7},{6,4},{7,5},{8,10},{9,11},{10,... | collective-permute-start | bytes 393224 | tf_op jit(solution)/shard_map/ppermute | solution.py:28
  11.7 10.8 %collective-permute-start.5 = (bf16[64,1024]{1,0:T(8,128)(2,1)S(1)}, bf16[64,1024]{1,0:T(8,128)(2,1)S(1)}, u32[]{:S(2)}, u32[]{:S(2)}) collective-permute-start(bf16[64,1024]{1,0:T(8,128)(2,1)S(1)} %get-tuple-element.28), channel_id=1, source_target_pairs={{0,2},{1,3},{2,0},{3,1},{4,6},{5,7},{6,4},{7,5},{8,10},{9,11},{10,... | collective-permute-start | bytes 393224 | tf_op jit(solution)/shard_map/ppermute | solution.py:28
  13.5 15.0 %collective-permute-start.4 = (bf16[128,1024]{1,0:T(8,128)(2,1)S(1)}, bf16[128,1024]{1,0:T(8,128)(2,1)S(1)}, u32[]{:S(2)}, u32[]{:S(2)}) collective-permute-start(bf16[128,1024]{1,0:T(8,128)(2,1)S(1)} %pad_maximum_fusion), channel_id=1, source_target_pairs={{0,4},{1,5},{2,6},{3,7},{4,0},{5,1},{6,2},{7,3},{8,12},{9,13},{10,... | collective-permute-start | bytes 786440 | tf_op jit(solution)/shard_map/ppermute | solution.py:28
  22.4 1.6 %collective-permute-start.6 = (bf16[64,1024]{1,0:T(8,128)(2,1)S(1)}, bf16[64,1024]{1,0:T(8,128)(2,1)S(1)}, u32[]{:S(2)}, u32[]{:S(2)}) collective-permute-start(bf16[64,1024]{1,0:T(8,128)(2,1)S(1)} %collective-permute-done.5), channel_id=1, source_target_pairs={{0,4},{1,5},{2,6},{3,7},{4,0},{5,1},{6,2},{7,3},{8,12},{9,13},{10,... | collective-permute-start | bytes 393224 | tf_op jit(solution)/shard_map/ppermute | solution.py:28
  23.4 1.4 %collective-permute-start.7 = (bf16[64,1024]{1,0:T(8,128)(2,1)S(1)}, bf16[64,1024]{1,0:T(8,128)(2,1)S(1)}, u32[]{:S(2)}, u32[]{:S(2)}) collective-permute-start(bf16[64,1024]{1,0:T(8,128)(2,1)S(1)} %collective-permute-done.1), channel_id=1, source_target_pairs={{0,4},{1,5},{2,6},{3,7},{4,0},{5,1},{6,2},{7,3},{8,12},{9,13},{10,... | collective-permute-start | bytes 393224 | tf_op jit(solution)/shard_map/ppermute | solution.py:28
  25.7 5.5 %collective-permute-start.8 = (f16[264,128]{1,0:T(8,128)(2,1)S(1)}, f16[264,128]{1,0:T(8,128)(2,1)S(1)}, u32[]{:S(2)}, u32[]{:S(2)}) collective-permute-start(f16[264,128]{1,0:T(8,128)(2,1)S(1)} %concatenate.15), channel_id=1, source_target_pairs={{0,2},{1,3},{2,0},{3,1},{4,6},{5,7},{6,4},{7,5},{8,10},{9,11},{10,... | collective-permute-start | bytes 202760 | tf_op jit(solution)/shard_map/ppermute | solution.py:28

commit v29 on v21

--- a/solution.py
+++ b/solution.py
@@ -1,6 +1,8 @@
 import jax
 import jax.numpy as jnp
 from jax import lax
+from jax.experimental import pallas as pl
+from jax.experimental.pallas import tpu as pltpu
 from jax.sharding import PartitionSpec as P
 
 epsilon = 1e-06
@@ -48,6 +50,29 @@
     return root
 
 
+def parts_kernel(block, first, second, sems):
+    cut = first.shape[0]
+    copies = [
+        pltpu.make_async_copy(block.at[pl.ds(0, cut)], first, sems.at[0]),
+        pltpu.make_async_copy(block.at[pl.ds(cut, second.shape[0])], second, sems.at[1]),
+    ]
+    for copy in copies:
+        copy.start()
+    for copy in copies:
+        copy.wait()
+
+
+def parts_of(block, cut):
+    rows, depth = block.shape
+    return pl.pallas_call(
+        parts_kernel,
+        out_shape=[jax.ShapeDtypeStruct((part, depth), block.dtype) for part in (cut, rows - cut)],
+        in_specs=[pl.BlockSpec(memory_space=pl.ANY)],
+        out_specs=[pl.BlockSpec(memory_space=pltpu.VMEM)] * 2,
+        scratch_shapes=[pltpu.SemaphoreType.DMA((2,))],
+    )(block)
+
+
 def on_square_grid(left_docs, right_docs):
     side = lax.axis_size("col")
     feat_total = left_docs.shape[1] * side
@@ -60,9 +85,9 @@
         return moved(block, side, lambda r, c: (r ^ 1, c))
 
     nears, crosses = [], []
-    for half in lax.optimization_barrier((right_docs[:width // 2], right_docs[width // 2:])):
-        swapped = moved(half, side, lambda r, c: (r ^ 2, c))
-        near, leaving = lax.optimization_barrier((jnp.where(at_home, half, swapped), jnp.where(at_home, swapped, half)))
+    for part in parts_of(right_docs, width // 2):
+        swapped = moved(part, side, lambda r, c: (r ^ 2, c))
+        near, leaving = lax.optimization_barrier((jnp.where(at_home, part, swapped), jnp.where(at_home, swapped, part)))
         nears.append(near)
         crosses.append(moved(leaving, side, lambda r, c: (r, c ^ 2)))
     left_other = moved(left_docs, side, lambda r, c: (r, c ^ 1))

time: 31.5 us -> 32.3 us (1.025)
  Pallas kernels: 0 us -> 1.67 us
  local copies, waits for them, and re-layouts: 1.12 us -> 0.08 us
  other arithmetic: 2.16 us -> 3.07 us
  starting transfers between devices: 13.3 us -> 12.4 us
    pallas_call x0 -> x1, Pallas kernels: none -> 1.67 us  [parts_of(): pl.pallas_call(parts_kernel, out_shape=[jax.ShapeDtypeStruct((part, depth...]
    slice x1 -> x0, local copies, waits for them, and re-layouts: 1.04 us -> none  [on_square_grid(): right_docs[width // 2:]]
    ppermute x9, starting transfers between devices: 13.3 us -> 12.4 us  [moved(): return lax.ppermute(value, ('row', 'col'), pairs)]
    select_n x2, other arithmetic: 0.04 us -> 0.96 us  [on_square_grid(): jnp.where(at_home, swapped, part)]
  transfers between devices with their start and end apart: 9 -> 9, of which waited for: 5 -> 5; matrix products, arithmetic and copies ran while one was open for 6% -> 8% of each run, Pallas kernels for 0% -> 0%
where the time goes in v29:
time: 32.3 us; the launch traced here: 32.2 us
  waiting for transfers between devices  13.6 us (42%)
  starting transfers between devices  12.4 us (38%)
  other arithmetic  3.07 us (10%)
  Pallas kernels  1.67 us (5%)
  matrix products  1.22 us (4%)
    ppermute x9, waiting for transfers between devices, moved(): return lax.ppermute(value, ('row', 'col'), pairs)  13.6 us
    ppermute x9, starting transfers between devices, moved(): return lax.ppermute(value, ('row', 'col'), pairs)  12.4 us
    pallas_call x1, Pallas kernels, parts_of(): pl.pallas_call(parts_kernel, out_shape=[jax.ShapeDtypeStruct((part, depth...  1.67 us
    dot_general x4, matrix products, contract(): lax.dot_general(left_part, right_part, (((1,), (1,)), ((), ())), preferre...  1.22 us
    select_n x2, other arithmetic, on_square_grid(): jnp.where(at_home, swapped, part)  0.96 us
    reduce_sum x5, other arithmetic, squares(): return jnp.sum(widened * widened, axis=1)  0.82 us
    mul x3, other arithmetic, finish(): return summed / feat_total * left_scale[:, None] * right_scale[None, :]  0.81 us
  transfers between devices with their start and end apart: 9, of which 5 were waited for; matrix products, arithmetic and copies ran while one was open for 8% of the time, Pallas kernels for 0%

profile of v29, /device:TPU:0, one launch (start us, length us, event | category | flops | bytes accessed | tf_op | source)
XLA Modules:
  0.0 32.2 jit_solution(17680626706858463031)
XLA Ops:
  0.0 1.7 %shard_map.28 = (bf16[64,1024]{1,0:T(8,128)(2,1)}, bf16[64,1024]{1,0:T(8,128)(2,1)}) custom-call(bf16[128,1024]{1,0:T(8,128)(2,1)} %block.1), custom_call_target="tpu_custom_call" | custom-call | tf_op jit(solution)/shard_map/pallas_call | solution.py:67
  1.7 3.0 %collective-permute-start.1 = (bf16[64,1024]{1,0:T(8,128)(2,1)}, bf16[64,1024]{1,0:T(8,128)(2,1)S(1)}, u32[]{:S(2)}, u32[]{:S(2)}) collective-permute-start(bf16[64,1024]{1,0:T(8,128)(2,1)} %get-tuple-element.21), channel_id=1, source_target_pairs={{0,8},{1,9},{2,10},{3,11},{4,12},{5,13},{6,14},{7,15},{8,0},{9,1},... | collective-permute-start | bytes 393224 | tf_op jit(solution)/shard_map/ppermute | solution.py:30
  4.8 2.0 %collective-permute-start = (bf16[256,1024]{1,0:T(8,128)(2,1)}, bf16[256,1024]{1,0:T(8,128)(2,1)S(1)}, u32[]{:S(2)}, u32[]{:S(2)}) collective-permute-start(bf16[256,1024]{1,0:T(8,128)(2,1)} %param.2), channel_id=1, source_target_pairs={{0,1},{1,0},{2,3},{3,2},{4,5},{5,4},{6,7},{7,6},{8,9},{9,8},{10,11... | collective-permute-start | bytes 1572872 | tf_op jit(solution)/shard_map/ppermute | solution.py:30
  6.8 2.4 %collective-permute-done.1 = bf16[64,1024]{1,0:T(8,128)(2,1)S(1)} collective-permute-done((bf16[64,1024]{1,0:T(8,128)(2,1)}, bf16[64,1024]{1,0:T(8,128)(2,1)S(1)}, u32[]{:S(2)}, u32[]{:S(2)}) %collective-permute-start.1) | collective-permute-done | bytes 131104 | tf_op jit(solution)/shard_map/ppermute | solution.py:30
  9.2 0.9 %broadcast_select_fusion.4 = (bf16[64,1024]{1,0:T(8,128)(2,1)S(1)}, bf16[64,1024]{1,0:T(8,128)(2,1)S(1)}) fusion(bf16[64,1024]{1,0:T(8,128)(2,1)S(1)} %collective-permute-done.1, bf16[64,1024]{1,0:T(8,128)(2,1)} %get-tuple-element.21, pred[]{:T(512)S(6)} %eq.7), kind=kLoop, calls=%fused_computation.20 | loop fusion | flops 131072 | bytes 524289 | tf_op jit(solution)/shard_map/jit(_where)/select_n | solution.py:90
  10.2 3.2 %collective-permute-start.5 = (bf16[64,1024]{1,0:T(8,128)(2,1)S(1)}, bf16[64,1024]{1,0:T(8,128)(2,1)S(1)}, u32[]{:S(2)}, u32[]{:S(2)}) collective-permute-start(bf16[64,1024]{1,0:T(8,128)(2,1)S(1)} %get-tuple-element.28), channel_id=1, source_target_pairs={{0,2},{1,3},{2,0},{3,1},{4,6},{5,7},{6,4},{7,5},{8,10},{9,11},{10,... | collective-permute-start | bytes 393224 | tf_op jit(solution)/shard_map/ppermute | solution.py:30
  13.5 0.7 %collective-permute-start.3 = (bf16[64,1024]{1,0:T(8,128)(2,1)S(1)}, bf16[64,1024]{1,0:T(8,128)(2,1)S(1)}, u32[]{:S(2)}, u32[]{:S(2)}) collective-permute-start(bf16[64,1024]{1,0:T(8,128)(2,1)S(1)} %get-tuple-element.26), channel_id=1, source_target_pairs={{0,2},{1,3},{2,0},{3,1},{4,6},{5,7},{6,4},{7,5},{8,10},{9,11},{10,... | collective-permute-start | bytes 393224 | tf_op jit(solution)/shard_map/ppermute | solution.py:30
  14.2 0.2 multiply_reduce_fusion.1
  14.4 0.1 multiply_reduce_fusion.3
  14.5 7.3 %collective-permute-done.5 = bf16[64,1024]{1,0:T(8,128)(2,1)S(1)} collective-permute-done((bf16[64,1024]{1,0:T(8,128)(2,1)S(1)}, bf16[64,1024]{1,0:T(8,128)(2,1)S(1)}, u32[]{:S(2)}, u32[]{:S(2)}) %collective-permute-start.5) | collective-permute-done | bytes 131104 | tf_op jit(solution)/shard_map/ppermute | solution.py:30
  21.8 1.4 %collective-permute-done.3 = bf16[64,1024]{1,0:T(8,128)(2,1)S(1)} collective-permute-done((bf16[64,1024]{1,0:T(8,128)(2,1)S(1)}, bf16[64,1024]{1,0:T(8,128)(2,1)S(1)}, u32[]{:S(2)}, u32[]{:S(2)}) %collective-permute-start.3) | collective-permute-done | bytes 131104 | tf_op jit(solution)/shard_map/ppermute | solution.py:30
  23.3 0.7 %collective-permute-done = bf16[256,1024]{1,0:T(8,128)(2,1)S(1)} collective-permute-done((bf16[256,1024]{1,0:T(8,128)(2,1)}, bf16[256,1024]{1,0:T(8,128)(2,1)S(1)}, u32[]{:S(2)}, u32[]{:S(2)}) %collective-permute-start) | collective-permute-done | bytes 524320 | tf_op jit(solution)/shard_map/ppermute | solution.py:30
  24.0 0.2 multiply_reduce_fusion
  24.3 0.1 broadcast_select_fusion
  24.4 0.3 fusion.41
  24.8 0.2 multiply_reduce_fusion.4
  25.0 0.3 fusion.42
  25.4 0.1 multiply_convert_fusion
  25.6 3.3 %collective-permute-start.8 = (f16[264,128]{1,0:T(8,128)(2,1)S(1)}, f16[264,128]{1,0:T(8,128)(2,1)S(1)}, u32[]{:S(2)}, u32[]{:S(2)}) collective-permute-start(f16[264,128]{1,0:T(8,128)(2,1)S(1)} %concatenate.15), channel_id=1, source_target_pairs={{0,2},{1,3},{2,0},{3,1},{4,6},{5,7},{6,4},{7,5},{8,10},{9,11},{10,... | collective-permute-start | bytes 202760 | tf_op jit(solution)/shard_map/ppermute | solution.py:30
  28.9 0.3 fusion.43
  29.2 0.3 convolution_add_fusion
  29.5 0.1 multiply_reduce_fusion.2
  29.6 1.7 %collective-permute-done.8 = f16[264,128]{1,0:T(8,128)(2,1)S(1)} collective-permute-done((f16[264,128]{1,0:T(8,128)(2,1)S(1)}, f16[264,128]{1,0:T(8,128)(2,1)S(1)}, u32[]{:S(2)}, u32[]{:S(2)}) %collective-permute-start.8) | collective-permute-done | bytes 67616 | tf_op jit(solution)/shard_map/ppermute | solution.py:30
  31.4 0.8 %fusion.3 = f32[256,128]{1,0:T(8,128)} fusion(f32[256,128]{1,0:T(8,128)S(1)} %convolution_add_fusion, f32[264,128]{1,0:T(8,128)S(1)} %convert_element_type.61, f32[128]{0:T(128)S(1)} %rsqrt_bitcast_fusion, f32[256]{0:T(256)S(1)} %fusion.24, f32[128]{0:T(128)S(1)} %get-tuple-element.37, f32[256]{0:T(256)S(1)} %get-tuple-element.35), kind=kLoop, calls=%fused_computation.16 | loop fusion | flops 163840 | bytes 396288 | tf_op jit(solution)/shard_map/mul | solution.py:36
  (29 shorter events, 0.5 us)
Async XLA Ops:
  1.7 7.5 %collective-permute-start.1 = (bf16[64,1024]{1,0:T(8,128)(2,1)}, bf16[64,1024]{1,0:T(8,128)(2,1)S(1)}, u32[]{:S(2)}, u32[]{:S(2)}) collective-permute-start(bf16[64,1024]{1,0:T(8,128)(2,1)} %get-tuple-element.21), channel_id=1, source_target_pairs={{0,8},{1,9},{2,10},{3,11},{4,12},{5,13},{6,14},{7,15},{8,0},{9,1},... | collective-permute-start | bytes 393224 | tf_op jit(solution)/shard_map/ppermute | solution.py:30
  4.7 8.7 %collective-permute-start.2 = (bf16[64,1024]{1,0:T(8,128)(2,1)}, bf16[64,1024]{1,0:T(8,128)(2,1)S(1)}, u32[]{:S(2)}, u32[]{:S(2)}) collective-permute-start(bf16[64,1024]{1,0:T(8,128)(2,1)} %get-tuple-element.23), channel_id=1, source_target_pairs={{0,8},{1,9},{2,10},{3,11},{4,12},{5,13},{6,14},{7,15},{8,0},{9,1},... | collective-permute-start | bytes 393224 | tf_op jit(solution)/shard_map/ppermute | solution.py:30
  4.8 19.2 %collective-permute-start = (bf16[256,1024]{1,0:T(8,128)(2,1)}, bf16[256,1024]{1,0:T(8,128)(2,1)S(1)}, u32[]{:S(2)}, u32[]{:S(2)}) collective-permute-start(bf16[256,1024]{1,0:T(8,128)(2,1)} %param.2), channel_id=1, source_target_pairs={{0,1},{1,0},{2,3},{3,2},{4,5},{5,4},{6,7},{7,6},{8,9},{9,8},{10,11... | collective-permute-start | bytes 1572872 | tf_op jit(solution)/shard_map/ppermute | solution.py:30
  6.8 6.6 %copy-start.1 = (bf16[64,1024]{1,0:T(8,128)(2,1)S(1)}, bf16[64,1024]{1,0:T(8,128)(2,1)}, u32[]{:S(2)}) copy-start(bf16[64,1024]{1,0:T(8,128)(2,1)} %get-tuple-element.23) | copy-start | bytes 393220
  10.1 4.0 %copy-start = (bf16[256,1024]{1,0:T(8,128)(2,1)S(1)}, bf16[256,1024]{1,0:T(8,128)(2,1)}, u32[]{:S(2)}) copy-start(bf16[256,1024]{1,0:T(8,128)(2,1)} %param.2) | copy-start | bytes 1572868
  10.2 11.7 %collective-permute-start.5 = (bf16[64,1024]{1,0:T(8,128)(2,1)S(1)}, bf16[64,1024]{1,0:T(8,128)(2,1)S(1)}, u32[]{:S(2)}, u32[]{:S(2)}) collective-permute-start(bf16[64,1024]{1,0:T(8,128)(2,1)S(1)} %get-tuple-element.28), channel_id=1, source_target_pairs={{0,2},{1,3},{2,0},{3,1},{4,6},{5,7},{6,4},{7,5},{8,10},{9,11},{10,... | collective-permute-start | bytes 393224 | tf_op jit(solution)/shard_map/ppermute | solution.py:30
  13.5 9.8 %collective-permute-start.3 = (bf16[64,1024]{1,0:T(8,128)(2,1)S(1)}, bf16[64,1024]{1,0:T(8,128)(2,1)S(1)}, u32[]{:S(2)}, u32[]{:S(2)}) collective-permute-start(bf16[64,1024]{1,0:T(8,128)(2,1)S(1)} %get-tuple-element.26), channel_id=1, source_target_pairs={{0,2},{1,3},{2,0},{3,1},{4,6},{5,7},{6,4},{7,5},{8,10},{9,11},{10,... | collective-permute-start | bytes 393224 | tf_op jit(solution)/shard_map/ppermute | solution.py:30
  14.2 9.1 %collective-permute-start.4 = (bf16[128,1024]{1,0:T(8,128)(2,1)S(1)}, bf16[128,1024]{1,0:T(8,128)(2,1)S(1)}, u32[]{:S(2)}, u32[]{:S(2)}) collective-permute-start(bf16[128,1024]{1,0:T(8,128)(2,1)S(1)} %pad_maximum_fusion), channel_id=1, source_target_pairs={{0,4},{1,5},{2,6},{3,7},{4,0},{5,1},{6,2},{7,3},{8,12},{9,13},{10,... | collective-permute-start | bytes 786440 | tf_op jit(solution)/shard_map/ppermute | solution.py:30
  21.8 2.9 %collective-permute-start.6 = (bf16[64,1024]{1,0:T(8,128)(2,1)S(1)}, bf16[64,1024]{1,0:T(8,128)(2,1)S(1)}, u32[]{:S(2)}, u32[]{:S(2)}) collective-permute-start(bf16[64,1024]{1,0:T(8,128)(2,1)S(1)} %collective-permute-done.5), channel_id=1, source_target_pairs={{0,4},{1,5},{2,6},{3,7},{4,0},{5,1},{6,2},{7,3},{8,12},{9,13},{10,... | collective-permute-start | bytes 393224 | tf_op jit(solution)/shard_map/ppermute | solution.py:30
  23.3 1.5 %collective-permute-start.7 = (bf16[64,1024]{1,0:T(8,128)(2,1)S(1)}, bf16[64,1024]{1,0:T(8,128)(2,1)S(1)}, u32[]{:S(2)}, u32[]{:S(2)}) collective-permute-start(bf16[64,1024]{1,0:T(8,128)(2,1)S(1)} %collective-permute-done.3), channel_id=1, source_target_pairs={{0,4},{1,5},{2,6},{3,7},{4,0},{5,1},{6,2},{7,3},{8,12},{9,13},{10,... | collective-permute-start | bytes 393224 | tf_op jit(solution)/shard_map/ppermute | solution.py:30
  25.6 5.8 %collective-permute-start.8 = (f16[264,128]{1,0:T(8,128)(2,1)S(1)}, f16[264,128]{1,0:T(8,128)(2,1)S(1)}, u32[]{:S(2)}, u32[]{:S(2)}) collective-permute-start(f16[264,128]{1,0:T(8,128)(2,1)S(1)} %concatenate.15), channel_id=1, source_target_pairs={{0,2},{1,3},{2,0},{3,1},{4,6},{5,7},{6,4},{7,5},{8,10},{9,11},{10,... | collective-permute-start | bytes 202760 | tf_op jit(solution)/shard_map/ppermute | solution.py:30

commit v30 on v21

--- a/solution.py
+++ b/solution.py
@@ -77,7 +77,7 @@
         return gram, squares(mine) + squares(other)
 
     cross_gram = contract(lefts[0], cross)
-    cross_other, cross_gram = lax.optimization_barrier((jnp.concatenate([other_core(part) for part in crosses]), cross_gram))
+    cross_other, _ = lax.optimization_barrier((jnp.concatenate([other_core(part) for part in crosses]), cross_gram))
     cross_gram = cross_gram + contract(lefts[1], cross_other)
     cross_sq = squares(cross) + squares(cross_other)
     left_sq = squares(left_docs) + squares(left_other)

time: 31.5 us -> 31.4 us (level)
  no operation moved by 1% of the time
where the time goes in v30:
time: 31.4 us; the launch traced here: 31.2 us
  waiting for transfers between devices  13.4 us (43%)
  starting transfers between devices  13.3 us (42%)
  other arithmetic  2.06 us (7%)
  matrix products  1.21 us (4%)
  local copies, waits for them, and re-layouts  1.12 us (4%)
    ppermute x9, waiting for transfers between devices, moved(): return lax.ppermute(value, ('row', 'col'), pairs)  13.4 us
    ppermute x9, starting transfers between devices, moved(): return lax.ppermute(value, ('row', 'col'), pairs)  13.3 us
    dot_general x4, matrix products, contract(): lax.dot_general(left_part, right_part, (((1,), (1,)), ((), ())), preferre...  1.21 us
    slice x1, local copies, waits for them, and re-layouts, on_square_grid(): right_docs[width // 2:]  1.04 us
    reduce_sum x5, other arithmetic, squares(): return jnp.sum(widened * widened, axis=1)  0.82 us
    mul x3, other arithmetic, finish(): return summed / feat_total * left_scale[:, None] * right_scale[None, :]  0.81 us
  transfers between devices with their start and end apart: 9, of which 5 were waited for; matrix products, arithmetic and copies ran while one was open for 6% of the time, Pallas kernels for 0%

profile of v30, /device:TPU:0, one launch (start us, length us, event | category | flops | bytes accessed | tf_op | source)
XLA Modules:
  0.0 31.2 jit_solution(25391768926804561)
XLA Ops:
  0.0 1.0 %fusion.44 = (bf16[64,1024]{1,0:T(8,128)(2,1)S(1)}, bf16[64,1024]{1,0:T(8,128)(2,1)S(1)}) fusion(bf16[128,1024]{1,0:T(8,128)(2,1)} %param.3), kind=kLoop, calls=%fused_computation.79 | loop fusion | bytes 524288 | tf_op jit(solution)/shard_map/slice | solution.py:63
  1.0 3.0 %collective-permute-start.1 = (bf16[64,1024]{1,0:T(8,128)(2,1)S(1)}, bf16[64,1024]{1,0:T(8,128)(2,1)S(1)}, u32[]{:S(2)}, u32[]{:S(2)}) collective-permute-start(bf16[64,1024]{1,0:T(8,128)(2,1)S(1)} %get-tuple-element.20), channel_id=1, source_target_pairs={{0,8},{1,9},{2,10},{3,11},{4,12},{5,13},{6,14},{7,15},{8,0},{9,1},... | collective-permute-start | bytes 393224 | tf_op jit(solution)/shard_map/ppermute | solution.py:28
  4.1 0.1 collective-permute-start.2
  4.1 2.0 %collective-permute-start = (bf16[256,1024]{1,0:T(8,128)(2,1)S(1)}, bf16[256,1024]{1,0:T(8,128)(2,1)S(1)}, u32[]{:S(2)}, u32[]{:S(2)}) collective-permute-start(bf16[256,1024]{1,0:T(8,128)(2,1)S(1)} %copy-done), channel_id=1, source_target_pairs={{0,1},{1,0},{2,3},{3,2},{4,5},{5,4},{6,7},{7,6},{8,9},{9,8},{10,11... | collective-permute-start | bytes 1572872 | tf_op jit(solution)/shard_map/ppermute | solution.py:28
  6.2 2.2 %collective-permute-done.1 = bf16[64,1024]{1,0:T(8,128)(2,1)S(1)} collective-permute-done((bf16[64,1024]{1,0:T(8,128)(2,1)S(1)}, bf16[64,1024]{1,0:T(8,128)(2,1)S(1)}, u32[]{:S(2)}, u32[]{:S(2)}) %collective-permute-start.1) | collective-permute-done | bytes 131104 | tf_op jit(solution)/shard_map/ppermute | solution.py:28
  8.4 3.2 %collective-permute-start.5 = (bf16[64,1024]{1,0:T(8,128)(2,1)S(1)}, bf16[64,1024]{1,0:T(8,128)(2,1)S(1)}, u32[]{:S(2)}, u32[]{:S(2)}) collective-permute-start(bf16[64,1024]{1,0:T(8,128)(2,1)S(1)} %get-tuple-element.27), channel_id=1, source_target_pairs={{0,2},{1,3},{2,0},{3,1},{4,6},{5,7},{6,4},{7,5},{8,10},{9,11},{10,... | collective-permute-start | bytes 393224 | tf_op jit(solution)/shard_map/ppermute | solution.py:28
  11.7 1.6 %collective-permute-start.3 = (bf16[64,1024]{1,0:T(8,128)(2,1)S(1)}, bf16[64,1024]{1,0:T(8,128)(2,1)S(1)}, u32[]{:S(2)}, u32[]{:S(2)}) collective-permute-start(bf16[64,1024]{1,0:T(8,128)(2,1)S(1)} %get-tuple-element.25), channel_id=1, source_target_pairs={{0,2},{1,3},{2,0},{3,1},{4,6},{5,7},{6,4},{7,5},{8,10},{9,11},{10,... | collective-permute-start | bytes 393224 | tf_op jit(solution)/shard_map/ppermute | solution.py:28
  13.3 0.2 multiply_reduce_fusion.1
  13.5 0.1 multiply_reduce_fusion.3
  13.6 7.4 %collective-permute-done.5 = bf16[64,1024]{1,0:T(8,128)(2,1)S(1)} collective-permute-done((bf16[64,1024]{1,0:T(8,128)(2,1)S(1)}, bf16[64,1024]{1,0:T(8,128)(2,1)S(1)}, u32[]{:S(2)}, u32[]{:S(2)}) %collective-permute-start.5) | collective-permute-done | bytes 131104 | tf_op jit(solution)/shard_map/ppermute | solution.py:28
  21.0 1.4 %collective-permute-done.3 = bf16[64,1024]{1,0:T(8,128)(2,1)S(1)} collective-permute-done((bf16[64,1024]{1,0:T(8,128)(2,1)S(1)}, bf16[64,1024]{1,0:T(8,128)(2,1)S(1)}, u32[]{:S(2)}, u32[]{:S(2)}) %collective-permute-start.3) | collective-permute-done | bytes 131104 | tf_op jit(solution)/shard_map/ppermute | solution.py:28
  22.4 0.7 %collective-permute-done = bf16[256,1024]{1,0:T(8,128)(2,1)S(1)} collective-permute-done((bf16[256,1024]{1,0:T(8,128)(2,1)S(1)}, bf16[256,1024]{1,0:T(8,128)(2,1)S(1)}, u32[]{:S(2)}, u32[]{:S(2)}) %collective-permute-start) | collective-permute-done | bytes 524320 | tf_op jit(solution)/shard_map/ppermute | solution.py:28
  23.1 0.2 multiply_reduce_fusion
  23.4 0.1 broadcast_select_fusion
  23.5 0.3 fusion.45
  23.9 0.2 multiply_reduce_fusion.4
  24.2 0.3 %fusion.2 = f16[256,128]{1,0:T(8,128)(2,1)S(1)} fusion(f32[256,128]{1,0:T(8,128)S(1)} %fusion.45, bf16[256,1024]{1,0:T(8,128)(2,1)S(1)} %get-tuple-element.24, bf16[128,1024]{1,0:T(8,128)(2,1)S(1)} %pad_maximum_fusion.2, f32[128]{0:T(128)S(1)} %fusion.36, f32[256]{0:T(256)S(1)} %fusion.15), kind=kOutput, calls=%fused_computation.4 | convolution fusion | flops 67239936 | bytes 984576 | tf_op jit(solution)/shard_map/dot_general | solution.py:11
  24.5 0.1 concatenate.15
  24.6 3.3 %collective-permute-start.8 = (f16[264,128]{1,0:T(8,128)(2,1)S(1)}, f16[264,128]{1,0:T(8,128)(2,1)S(1)}, u32[]{:S(2)}, u32[]{:S(2)}) collective-permute-start(f16[264,128]{1,0:T(8,128)(2,1)S(1)} %concatenate.15), channel_id=1, source_target_pairs={{0,2},{1,3},{2,0},{3,1},{4,6},{5,7},{6,4},{7,5},{8,10},{9,11},{10,... | collective-permute-start | bytes 202760 | tf_op jit(solution)/shard_map/ppermute | solution.py:28
  27.9 0.3 fusion.46
  28.2 0.3 convolution_add_fusion.1
  28.5 0.1 multiply_reduce_fusion.2
  28.7 1.7 %collective-permute-done.8 = f16[264,128]{1,0:T(8,128)(2,1)S(1)} collective-permute-done((f16[264,128]{1,0:T(8,128)(2,1)S(1)}, f16[264,128]{1,0:T(8,128)(2,1)S(1)}, u32[]{:S(2)}, u32[]{:S(2)}) %collective-permute-start.8) | collective-permute-done | bytes 67616 | tf_op jit(solution)/shard_map/ppermute | solution.py:28
  30.4 0.8 %fusion.6 = f32[256,128]{1,0:T(8,128)} fusion(f32[256,128]{1,0:T(8,128)S(1)} %convolution_add_fusion.1, f32[264,128]{1,0:T(8,128)S(1)} %convert_element_type.61, f32[128]{0:T(128)S(1)} %rsqrt_bitcast_fusion, f32[256]{0:T(256)S(1)} %fusion.27, f32[128]{0:T(128)S(1)} %get-tuple-element.35, f32[256]{0:T(256)S(1)} %get-tuple-element.33), kind=kLoop, calls=%fused_computation.20 | loop fusion | flops 163840 | bytes 396288 | tf_op jit(solution)/shard_map/mul | solution.py:34
  (26 shorter events, 0.4 us)
Async XLA Ops:
  0.0 4.1 %copy-start = (bf16[256,1024]{1,0:T(8,128)(2,1)S(1)}, bf16[256,1024]{1,0:T(8,128)(2,1)}, u32[]{:S(2)}) copy-start(bf16[256,1024]{1,0:T(8,128)(2,1)} %param.2) | copy-start | bytes 1572868
  1.0 7.3 %collective-permute-start.1 = (bf16[64,1024]{1,0:T(8,128)(2,1)S(1)}, bf16[64,1024]{1,0:T(8,128)(2,1)S(1)}, u32[]{:S(2)}, u32[]{:S(2)}) collective-permute-start(bf16[64,1024]{1,0:T(8,128)(2,1)S(1)} %get-tuple-element.20), channel_id=1, source_target_pairs={{0,8},{1,9},{2,10},{3,11},{4,12},{5,13},{6,14},{7,15},{8,0},{9,1},... | collective-permute-start | bytes 393224 | tf_op jit(solution)/shard_map/ppermute | solution.py:28
  4.1 7.6 %collective-permute-start.2 = (bf16[64,1024]{1,0:T(8,128)(2,1)S(1)}, bf16[64,1024]{1,0:T(8,128)(2,1)S(1)}, u32[]{:S(2)}, u32[]{:S(2)}) collective-permute-start(bf16[64,1024]{1,0:T(8,128)(2,1)S(1)} %get-tuple-element.22), channel_id=1, source_target_pairs={{0,8},{1,9},{2,10},{3,11},{4,12},{5,13},{6,14},{7,15},{8,0},{9,1},... | collective-permute-start | bytes 393224 | tf_op jit(solution)/shard_map/ppermute | solution.py:28
  4.1 19.0 %collective-permute-start = (bf16[256,1024]{1,0:T(8,128)(2,1)S(1)}, bf16[256,1024]{1,0:T(8,128)(2,1)S(1)}, u32[]{:S(2)}, u32[]{:S(2)}) collective-permute-start(bf16[256,1024]{1,0:T(8,128)(2,1)S(1)} %copy-done), channel_id=1, source_target_pairs={{0,1},{1,0},{2,3},{3,2},{4,5},{5,4},{6,7},{7,6},{8,9},{9,8},{10,11... | collective-permute-start | bytes 1572872 | tf_op jit(solution)/shard_map/ppermute | solution.py:28
  8.4 12.6 %collective-permute-start.5 = (bf16[64,1024]{1,0:T(8,128)(2,1)S(1)}, bf16[64,1024]{1,0:T(8,128)(2,1)S(1)}, u32[]{:S(2)}, u32[]{:S(2)}) collective-permute-start(bf16[64,1024]{1,0:T(8,128)(2,1)S(1)} %get-tuple-element.27), channel_id=1, source_target_pairs={{0,2},{1,3},{2,0},{3,1},{4,6},{5,7},{6,4},{7,5},{8,10},{9,11},{10,... | collective-permute-start | bytes 393224 | tf_op jit(solution)/shard_map/ppermute | solution.py:28
  11.7 10.7 %collective-permute-start.3 = (bf16[64,1024]{1,0:T(8,128)(2,1)S(1)}, bf16[64,1024]{1,0:T(8,128)(2,1)S(1)}, u32[]{:S(2)}, u32[]{:S(2)}) collective-permute-start(bf16[64,1024]{1,0:T(8,128)(2,1)S(1)} %get-tuple-element.25), channel_id=1, source_target_pairs={{0,2},{1,3},{2,0},{3,1},{4,6},{5,7},{6,4},{7,5},{8,10},{9,11},{10,... | collective-permute-start | bytes 393224 | tf_op jit(solution)/shard_map/ppermute | solution.py:28
  13.3 9.1 %collective-permute-start.4 = (bf16[128,1024]{1,0:T(8,128)(2,1)S(1)}, bf16[128,1024]{1,0:T(8,128)(2,1)S(1)}, u32[]{:S(2)}, u32[]{:S(2)}) collective-permute-start(bf16[128,1024]{1,0:T(8,128)(2,1)S(1)} %pad_maximum_fusion), channel_id=1, source_target_pairs={{0,4},{1,5},{2,6},{3,7},{4,0},{5,1},{6,2},{7,3},{8,12},{9,13},{10,... | collective-permute-start | bytes 786440 | tf_op jit(solution)/shard_map/ppermute | solution.py:28
  21.0 2.9 %collective-permute-start.6 = (bf16[64,1024]{1,0:T(8,128)(2,1)S(1)}, bf16[64,1024]{1,0:T(8,128)(2,1)S(1)}, u32[]{:S(2)}, u32[]{:S(2)}) collective-permute-start(bf16[64,1024]{1,0:T(8,128)(2,1)S(1)} %collective-permute-done.5), channel_id=1, source_target_pairs={{0,4},{1,5},{2,6},{3,7},{4,0},{5,1},{6,2},{7,3},{8,12},{9,13},{10,... | collective-permute-start | bytes 393224 | tf_op jit(solution)/shard_map/ppermute | solution.py:28
  22.4 1.5 %collective-permute-start.7 = (bf16[64,1024]{1,0:T(8,128)(2,1)S(1)}, bf16[64,1024]{1,0:T(8,128)(2,1)S(1)}, u32[]{:S(2)}, u32[]{:S(2)}) collective-permute-start(bf16[64,1024]{1,0:T(8,128)(2,1)S(1)} %collective-permute-done.3), channel_id=1, source_target_pairs={{0,4},{1,5},{2,6},{3,7},{4,0},{5,1},{6,2},{7,3},{8,12},{9,13},{10,... | collective-permute-start | bytes 393224 | tf_op jit(solution)/shard_map/ppermute | solution.py:28
  24.6 5.8 %collective-permute-start.8 = (f16[264,128]{1,0:T(8,128)(2,1)S(1)}, f16[264,128]{1,0:T(8,128)(2,1)S(1)}, u32[]{:S(2)}, u32[]{:S(2)}) collective-permute-start(f16[264,128]{1,0:T(8,128)(2,1)S(1)} %concatenate.15), channel_id=1, source_target_pairs={{0,2},{1,3},{2,0},{3,1},{4,6},{5,7},{6,4},{7,5},{8,10},{9,11},{10,... | collective-permute-start | bytes 202760 | tf_op jit(solution)/shard_map/ppermute | solution.py:28

commit v31 on v30

--- a/solution.py
+++ b/solution.py
@@ -77,9 +77,11 @@
         return gram, squares(mine) + squares(other)
 
     cross_gram = contract(lefts[0], cross)
-    cross_other, _ = lax.optimization_barrier((jnp.concatenate([other_core(part) for part in crosses]), cross_gram))
+    others = [other_core(part) for part in crosses]
+    others[1], _ = lax.optimization_barrier((others[1], cross_gram))
+    cross_other = lax.optimization_barrier(jnp.concatenate(others))
     cross_gram = cross_gram + contract(lefts[1], cross_other)
-    cross_sq = squares(cross) + squares(cross_other)
+    cross_sq = squares(cross) + jnp.concatenate([squares(part) for part in others])
     left_sq = squares(left_docs) + squares(left_other)
 
     left_high, left_low, left_read = packed(left_sq)

time: 31.4 us -> 31.5 us (level)
  other arithmetic: 2.06 us -> 2.42 us
    reduce_sum x5 -> x7, other arithmetic: 0.82 us -> 1.02 us  [squares(): return jnp.sum(widened * widened, axis=1)]
  transfers between devices with their start and end apart: 9 -> 9, of which waited for: 5 -> 5; matrix products, arithmetic and copies ran while one was open for 6% -> 7% of each run, Pallas kernels for 0% -> 0%
where the time goes in v31:
time: 31.5 us; the launch traced here: 31.4 us
  starting transfers between devices  13.3 us (42%)
  waiting for transfers between devices  13.2 us (42%)
  other arithmetic  2.42 us (8%)
  matrix products  1.21 us (4%)
  local copies, waits for them, and re-layouts  1.12 us (4%)
    ppermute x9, starting transfers between devices, moved(): return lax.ppermute(value, ('row', 'col'), pairs)  13.3 us
    ppermute x9, waiting for transfers between devices, moved(): return lax.ppermute(value, ('row', 'col'), pairs)  13.2 us
    dot_general x4, matrix products, contract(): lax.dot_general(left_part, right_part, (((1,), (1,)), ((), ())), preferre...  1.21 us
    slice x1, local copies, waits for them, and re-layouts, on_square_grid(): right_docs[width // 2:]  1.04 us
    reduce_sum x7, other arithmetic, squares(): return jnp.sum(widened * widened, axis=1)  1.02 us
    mul x3, other arithmetic, finish(): return summed / feat_total * left_scale[:, None] * right_scale[None, :]  0.81 us
  transfers between devices with their start and end apart: 9, of which 5 were waited for; matrix products, arithmetic and copies ran while one was open for 7% of the time, Pallas kernels for 0%

profile of v31, /device:TPU:0, one launch (start us, length us, event | category | flops | bytes accessed | tf_op | source)
XLA Modules:
  0.0 31.4 jit_solution(5083761734625923428)
XLA Ops:
  0.0 1.0 %fusion.46 = (bf16[64,1024]{1,0:T(8,128)(2,1)S(1)}, bf16[64,1024]{1,0:T(8,128)(2,1)S(1)}) fusion(bf16[128,1024]{1,0:T(8,128)(2,1)} %param.3), kind=kLoop, calls=%fused_computation.84 | loop fusion | bytes 524288 | tf_op jit(solution)/shard_map/slice | solution.py:63
  1.0 3.0 %collective-permute-start.1 = (bf16[64,1024]{1,0:T(8,128)(2,1)S(1)}, bf16[64,1024]{1,0:T(8,128)(2,1)S(1)}, u32[]{:S(2)}, u32[]{:S(2)}) collective-permute-start(bf16[64,1024]{1,0:T(8,128)(2,1)S(1)} %get-tuple-element.20), channel_id=1, source_target_pairs={{0,8},{1,9},{2,10},{3,11},{4,12},{5,13},{6,14},{7,15},{8,0},{9,1},... | collective-permute-start | bytes 393224 | tf_op jit(solution)/shard_map/ppermute | solution.py:28
  4.1 2.0 %collective-permute-start = (bf16[256,1024]{1,0:T(8,128)(2,1)S(1)}, bf16[256,1024]{1,0:T(8,128)(2,1)S(1)}, u32[]{:S(2)}, u32[]{:S(2)}) collective-permute-start(bf16[256,1024]{1,0:T(8,128)(2,1)S(1)} %copy-done), channel_id=1, source_target_pairs={{0,1},{1,0},{2,3},{3,2},{4,5},{5,4},{6,7},{7,6},{8,9},{9,8},{10,11... | collective-permute-start | bytes 1572872 | tf_op jit(solution)/shard_map/ppermute | solution.py:28
  6.2 2.2 %collective-permute-done.1 = bf16[64,1024]{1,0:T(8,128)(2,1)S(1)} collective-permute-done((bf16[64,1024]{1,0:T(8,128)(2,1)S(1)}, bf16[64,1024]{1,0:T(8,128)(2,1)S(1)}, u32[]{:S(2)}, u32[]{:S(2)}) %collective-permute-start.1) | collective-permute-done | bytes 131104 | tf_op jit(solution)/shard_map/ppermute | solution.py:28
  8.4 3.2 %collective-permute-start.5 = (bf16[64,1024]{1,0:T(8,128)(2,1)S(1)}, bf16[64,1024]{1,0:T(8,128)(2,1)S(1)}, u32[]{:S(2)}, u32[]{:S(2)}) collective-permute-start(bf16[64,1024]{1,0:T(8,128)(2,1)S(1)} %get-tuple-element.27), channel_id=1, source_target_pairs={{0,2},{1,3},{2,0},{3,1},{4,6},{5,7},{6,4},{7,5},{8,10},{9,11},{10,... | collective-permute-start | bytes 393224 | tf_op jit(solution)/shard_map/ppermute | solution.py:28
  11.7 1.6 %collective-permute-start.3 = (bf16[64,1024]{1,0:T(8,128)(2,1)S(1)}, bf16[64,1024]{1,0:T(8,128)(2,1)S(1)}, u32[]{:S(2)}, u32[]{:S(2)}) collective-permute-start(bf16[64,1024]{1,0:T(8,128)(2,1)S(1)} %get-tuple-element.25), channel_id=1, source_target_pairs={{0,2},{1,3},{2,0},{3,1},{4,6},{5,7},{6,4},{7,5},{8,10},{9,11},{10,... | collective-permute-start | bytes 393224 | tf_op jit(solution)/shard_map/ppermute | solution.py:28
  13.3 0.2 multiply_reduce_fusion.1
  13.5 7.5 %collective-permute-done.5 = bf16[64,1024]{1,0:T(8,128)(2,1)S(1)} collective-permute-done((bf16[64,1024]{1,0:T(8,128)(2,1)S(1)}, bf16[64,1024]{1,0:T(8,128)(2,1)S(1)}, u32[]{:S(2)}, u32[]{:S(2)}) %collective-permute-start.5) | collective-permute-done | bytes 131104 | tf_op jit(solution)/shard_map/ppermute | solution.py:28
  21.0 0.1 multiply_reduce_fusion.3
  21.1 1.3 %collective-permute-done.3 = bf16[64,1024]{1,0:T(8,128)(2,1)S(1)} collective-permute-done((bf16[64,1024]{1,0:T(8,128)(2,1)S(1)}, bf16[64,1024]{1,0:T(8,128)(2,1)S(1)}, u32[]{:S(2)}, u32[]{:S(2)}) %collective-permute-start.3) | collective-permute-done | bytes 131104 | tf_op jit(solution)/shard_map/ppermute | solution.py:28
  22.4 0.1 multiply_reduce_fusion.6
  22.6 0.1 multiply_reduce_fusion.4
  22.7 0.4 %collective-permute-done = bf16[256,1024]{1,0:T(8,128)(2,1)S(1)} collective-permute-done((bf16[256,1024]{1,0:T(8,128)(2,1)S(1)}, bf16[256,1024]{1,0:T(8,128)(2,1)S(1)}, u32[]{:S(2)}, u32[]{:S(2)}) %collective-permute-start) | collective-permute-done | bytes 524320 | tf_op jit(solution)/shard_map/ppermute | solution.py:28
  23.1 0.2 multiply_reduce_fusion
  23.5 0.3 fusion.47
  23.9 0.1 multiply_reduce_fusion.5
  24.2 0.1 fusion.39
  24.3 0.3 fusion.2
  24.7 3.3 %collective-permute-start.8 = (f16[264,128]{1,0:T(8,128)(2,1)S(1)}, f16[264,128]{1,0:T(8,128)(2,1)S(1)}, u32[]{:S(2)}, u32[]{:S(2)}) collective-permute-start(f16[264,128]{1,0:T(8,128)(2,1)S(1)} %concatenate.42), channel_id=1, source_target_pairs={{0,2},{1,3},{2,0},{3,1},{4,6},{5,7},{6,4},{7,5},{8,10},{9,11},{10,... | collective-permute-start | bytes 202760 | tf_op jit(solution)/shard_map/ppermute | solution.py:28
  28.0 0.3 fusion.48
  28.3 0.3 convolution_add_fusion.1
  28.6 0.1 multiply_reduce_fusion.2
  28.8 1.7 %collective-permute-done.8 = f16[264,128]{1,0:T(8,128)(2,1)S(1)} collective-permute-done((f16[264,128]{1,0:T(8,128)(2,1)S(1)}, f16[264,128]{1,0:T(8,128)(2,1)S(1)}, u32[]{:S(2)}, u32[]{:S(2)}) %collective-permute-start.8) | collective-permute-done | bytes 67616 | tf_op jit(solution)/shard_map/ppermute | solution.py:28
  30.6 0.8 %fusion.6 = f32[256,128]{1,0:T(8,128)} fusion(f32[256,128]{1,0:T(8,128)S(1)} %convolution_add_fusion.1, f32[264,128]{1,0:T(8,128)S(1)} %convert_element_type.65, f32[128]{0:T(128)S(1)} %rsqrt_bitcast_fusion, f32[256]{0:T(256)S(1)} %fusion.27, f32[128]{0:T(128)S(1)} %get-tuple-element.35, f32[256]{0:T(256)S(1)} %get-tuple-element.33), kind=kLoop, calls=%fused_computation.21 | loop fusion | flops 163840 | bytes 396288 | tf_op jit(solution)/shard_map/mul | solution.py:34
  (28 shorter events, 0.7 us)
Async XLA Ops:
  0.0 4.1 %copy-start = (bf16[256,1024]{1,0:T(8,128)(2,1)S(1)}, bf16[256,1024]{1,0:T(8,128)(2,1)}, u32[]{:S(2)}) copy-start(bf16[256,1024]{1,0:T(8,128)(2,1)} %param.2) | copy-start | bytes 1572868
  1.0 7.3 %collective-permute-start.1 = (bf16[64,1024]{1,0:T(8,128)(2,1)S(1)}, bf16[64,1024]{1,0:T(8,128)(2,1)S(1)}, u32[]{:S(2)}, u32[]{:S(2)}) collective-permute-start(bf16[64,1024]{1,0:T(8,128)(2,1)S(1)} %get-tuple-element.20), channel_id=1, source_target_pairs={{0,8},{1,9},{2,10},{3,11},{4,12},{5,13},{6,14},{7,15},{8,0},{9,1},... | collective-permute-start | bytes 393224 | tf_op jit(solution)/shard_map/ppermute | solution.py:28
  4.1 7.6 %collective-permute-start.2 = (bf16[64,1024]{1,0:T(8,128)(2,1)S(1)}, bf16[64,1024]{1,0:T(8,128)(2,1)S(1)}, u32[]{:S(2)}, u32[]{:S(2)}) collective-permute-start(bf16[64,1024]{1,0:T(8,128)(2,1)S(1)} %get-tuple-element.22), channel_id=1, source_target_pairs={{0,8},{1,9},{2,10},{3,11},{4,12},{5,13},{6,14},{7,15},{8,0},{9,1},... | collective-permute-start | bytes 393224 | tf_op jit(solution)/shard_map/ppermute | solution.py:28
  4.1 19.0 %collective-permute-start = (bf16[256,1024]{1,0:T(8,128)(2,1)S(1)}, bf16[256,1024]{1,0:T(8,128)(2,1)S(1)}, u32[]{:S(2)}, u32[]{:S(2)}) collective-permute-start(bf16[256,1024]{1,0:T(8,128)(2,1)S(1)} %copy-done), channel_id=1, source_target_pairs={{0,1},{1,0},{2,3},{3,2},{4,5},{5,4},{6,7},{7,6},{8,9},{9,8},{10,11... | collective-permute-start | bytes 1572872 | tf_op jit(solution)/shard_map/ppermute | solution.py:28
  8.4 12.6 %collective-permute-start.5 = (bf16[64,1024]{1,0:T(8,128)(2,1)S(1)}, bf16[64,1024]{1,0:T(8,128)(2,1)S(1)}, u32[]{:S(2)}, u32[]{:S(2)}) collective-permute-start(bf16[64,1024]{1,0:T(8,128)(2,1)S(1)} %get-tuple-element.27), channel_id=1, source_target_pairs={{0,2},{1,3},{2,0},{3,1},{4,6},{5,7},{6,4},{7,5},{8,10},{9,11},{10,... | collective-permute-start | bytes 393224 | tf_op jit(solution)/shard_map/ppermute | solution.py:28
  11.7 10.7 %collective-permute-start.3 = (bf16[64,1024]{1,0:T(8,128)(2,1)S(1)}, bf16[64,1024]{1,0:T(8,128)(2,1)S(1)}, u32[]{:S(2)}, u32[]{:S(2)}) collective-permute-start(bf16[64,1024]{1,0:T(8,128)(2,1)S(1)} %get-tuple-element.25), channel_id=1, source_target_pairs={{0,2},{1,3},{2,0},{3,1},{4,6},{5,7},{6,4},{7,5},{8,10},{9,11},{10,... | collective-permute-start | bytes 393224 | tf_op jit(solution)/shard_map/ppermute | solution.py:28
  13.3 9.1 %collective-permute-start.4 = (bf16[128,1024]{1,0:T(8,128)(2,1)S(1)}, bf16[128,1024]{1,0:T(8,128)(2,1)S(1)}, u32[]{:S(2)}, u32[]{:S(2)}) collective-permute-start(bf16[128,1024]{1,0:T(8,128)(2,1)S(1)} %pad_maximum_fusion), channel_id=1, source_target_pairs={{0,4},{1,5},{2,6},{3,7},{4,0},{5,1},{6,2},{7,3},{8,12},{9,13},{10,... | collective-permute-start | bytes 786440 | tf_op jit(solution)/shard_map/ppermute | solution.py:28
  21.0 1.4 %collective-permute-start.6 = (bf16[64,1024]{1,0:T(8,128)(2,1)S(1)}, bf16[64,1024]{1,0:T(8,128)(2,1)S(1)}, u32[]{:S(2)}, u32[]{:S(2)}) collective-permute-start(bf16[64,1024]{1,0:T(8,128)(2,1)S(1)} %collective-permute-done.5), channel_id=1, source_target_pairs={{0,4},{1,5},{2,6},{3,7},{4,0},{5,1},{6,2},{7,3},{8,12},{9,13},{10,... | collective-permute-start | bytes 393224 | tf_op jit(solution)/shard_map/ppermute | solution.py:28
  22.4 1.5 %collective-permute-start.7 = (bf16[64,1024]{1,0:T(8,128)(2,1)S(1)}, bf16[64,1024]{1,0:T(8,128)(2,1)S(1)}, u32[]{:S(2)}, u32[]{:S(2)}) collective-permute-start(bf16[64,1024]{1,0:T(8,128)(2,1)S(1)} %collective-permute-done.3), channel_id=1, source_target_pairs={{0,4},{1,5},{2,6},{3,7},{4,0},{5,1},{6,2},{7,3},{8,12},{9,13},{10,... | collective-permute-start | bytes 393224 | tf_op jit(solution)/shard_map/ppermute | solution.py:28
  24.7 5.8 %collective-permute-start.8 = (f16[264,128]{1,0:T(8,128)(2,1)S(1)}, f16[264,128]{1,0:T(8,128)(2,1)S(1)}, u32[]{:S(2)}, u32[]{:S(2)}) collective-permute-start(f16[264,128]{1,0:T(8,128)(2,1)S(1)} %concatenate.42), channel_id=1, source_target_pairs={{0,2},{1,3},{2,0},{3,1},{4,6},{5,7},{6,4},{7,5},{8,10},{9,11},{10,... | collective-permute-start | bytes 202760 | tf_op jit(solution)/shard_map/ppermute | solution.py:28

commit v32 on v30

--- a/solution.py
+++ b/solution.py
@@ -77,7 +77,7 @@
         return gram, squares(mine) + squares(other)
 
     cross_gram = contract(lefts[0], cross)
-    cross_other, _ = lax.optimization_barrier((jnp.concatenate([other_core(part) for part in crosses]), cross_gram))
+    cross_other, _ = lax.optimization_barrier((other_core(cross), cross_gram))
     cross_gram = cross_gram + contract(lefts[1], cross_other)
     cross_sq = squares(cross) + squares(cross_other)
     left_sq = squares(left_docs) + squares(left_other)

time: 31.4 us -> 31.6 us (level)
    ppermute x9 -> x8, starting transfers between devices: 13.3 us -> 13.5 us  [moved(): return lax.ppermute(value, ('row', 'col'), pairs)]
    reduce_sum x5 -> x6, other arithmetic: 0.82 us -> 0.9 us  [squares(): return jnp.sum(widened * widened, axis=1)]
    ppermute x9 -> x8, waiting for transfers between devices: 13.4 us -> 13.3 us  [moved(): return lax.ppermute(value, ('row', 'col'), pairs)]
  transfers between devices with their start and end apart: 9 -> 8, of which waited for: 5 -> 5; matrix products, arithmetic and copies ran while one was open for 6% -> 6% of each run, Pallas kernels for 0% -> 0%
where the time goes in v32:
time: 31.6 us; the launch traced here: 31.4 us
  starting transfers between devices  13.5 us (43%)
  waiting for transfers between devices  13.3 us (42%)
  other arithmetic  2.12 us (7%)
  matrix products  1.21 us (4%)
  local copies, waits for them, and re-layouts  1.12 us (4%)
    ppermute x8, starting transfers between devices, moved(): return lax.ppermute(value, ('row', 'col'), pairs)  13.5 us
    ppermute x8, waiting for transfers between devices, moved(): return lax.ppermute(value, ('row', 'col'), pairs)  13.3 us
    dot_general x4, matrix products, contract(): lax.dot_general(left_part, right_part, (((1,), (1,)), ((), ())), preferre...  1.21 us
    slice x1, local copies, waits for them, and re-layouts, on_square_grid(): right_docs[width // 2:]  1.04 us
    reduce_sum x6, other arithmetic, squares(): return jnp.sum(widened * widened, axis=1)  0.9 us
    mul x3, other arithmetic, finish(): return summed / feat_total * left_scale[:, None] * right_scale[None, :]  0.81 us
  transfers between devices with their start and end apart: 8, of which 5 were waited for; matrix products, arithmetic and copies ran while one was open for 6% of the time, Pallas kernels for 0%

profile of v32, /device:TPU:0, one launch (start us, length us, event | category | flops | bytes accessed | tf_op | source)
XLA Modules:
  0.0 31.4 jit_solution(7632456039854491194)
XLA Ops:
  0.0 1.0 %fusion.44 = (bf16[64,1024]{1,0:T(8,128)(2,1)S(1)}, bf16[64,1024]{1,0:T(8,128)(2,1)S(1)}) fusion(bf16[128,1024]{1,0:T(8,128)(2,1)} %param.3), kind=kLoop, calls=%fused_computation.78 | loop fusion | bytes 524288 | tf_op jit(solution)/shard_map/slice | solution.py:63
  1.0 3.0 %collective-permute-start.1 = (bf16[64,1024]{1,0:T(8,128)(2,1)S(1)}, bf16[64,1024]{1,0:T(8,128)(2,1)S(1)}, u32[]{:S(2)}, u32[]{:S(2)}) collective-permute-start(bf16[64,1024]{1,0:T(8,128)(2,1)S(1)} %get-tuple-element.20), channel_id=1, source_target_pairs={{0,8},{1,9},{2,10},{3,11},{4,12},{5,13},{6,14},{7,15},{8,0},{9,1},... | collective-permute-start | bytes 393224 | tf_op jit(solution)/shard_map/ppermute | solution.py:28
  4.1 0.1 collective-permute-start.2
  4.1 2.0 %collective-permute-start = (bf16[256,1024]{1,0:T(8,128)(2,1)S(1)}, bf16[256,1024]{1,0:T(8,128)(2,1)S(1)}, u32[]{:S(2)}, u32[]{:S(2)}) collective-permute-start(bf16[256,1024]{1,0:T(8,128)(2,1)S(1)} %copy-done), channel_id=1, source_target_pairs={{0,1},{1,0},{2,3},{3,2},{4,5},{5,4},{6,7},{7,6},{8,9},{9,8},{10,11... | collective-permute-start | bytes 1572872 | tf_op jit(solution)/shard_map/ppermute | solution.py:28
  6.2 2.2 %collective-permute-done.1 = bf16[64,1024]{1,0:T(8,128)(2,1)S(1)} collective-permute-done((bf16[64,1024]{1,0:T(8,128)(2,1)S(1)}, bf16[64,1024]{1,0:T(8,128)(2,1)S(1)}, u32[]{:S(2)}, u32[]{:S(2)}) %collective-permute-start.1) | collective-permute-done | bytes 131104 | tf_op jit(solution)/shard_map/ppermute | solution.py:28
  8.4 3.2 %collective-permute-start.5 = (bf16[64,1024]{1,0:T(8,128)(2,1)S(1)}, bf16[64,1024]{1,0:T(8,128)(2,1)S(1)}, u32[]{:S(2)}, u32[]{:S(2)}) collective-permute-start(bf16[64,1024]{1,0:T(8,128)(2,1)S(1)} %get-tuple-element.27), channel_id=1, source_target_pairs={{0,2},{1,3},{2,0},{3,1},{4,6},{5,7},{6,4},{7,5},{8,10},{9,11},{10,... | collective-permute-start | bytes 393224 | tf_op jit(solution)/shard_map/ppermute | solution.py:28
  11.7 1.6 %collective-permute-start.3 = (bf16[64,1024]{1,0:T(8,128)(2,1)S(1)}, bf16[64,1024]{1,0:T(8,128)(2,1)S(1)}, u32[]{:S(2)}, u32[]{:S(2)}) collective-permute-start(bf16[64,1024]{1,0:T(8,128)(2,1)S(1)} %get-tuple-element.25), channel_id=1, source_target_pairs={{0,2},{1,3},{2,0},{3,1},{4,6},{5,7},{6,4},{7,5},{8,10},{9,11},{10,... | collective-permute-start | bytes 393224 | tf_op jit(solution)/shard_map/ppermute | solution.py:28
  13.3 0.2 multiply_reduce_fusion.1
  13.5 0.1 multiply_reduce_fusion.3
  13.6 8.8 %collective-permute-done.3 = bf16[64,1024]{1,0:T(8,128)(2,1)S(1)} collective-permute-done((bf16[64,1024]{1,0:T(8,128)(2,1)S(1)}, bf16[64,1024]{1,0:T(8,128)(2,1)S(1)}, u32[]{:S(2)}, u32[]{:S(2)}) %collective-permute-start.3) | collective-permute-done | bytes 131104 | tf_op jit(solution)/shard_map/ppermute | solution.py:28
  22.5 0.1 multiply_reduce_fusion.5
  22.7 0.5 %collective-permute-done = bf16[256,1024]{1,0:T(8,128)(2,1)S(1)} collective-permute-done((bf16[256,1024]{1,0:T(8,128)(2,1)S(1)}, bf16[256,1024]{1,0:T(8,128)(2,1)S(1)}, u32[]{:S(2)}, u32[]{:S(2)}) %collective-permute-start) | collective-permute-done | bytes 524320 | tf_op jit(solution)/shard_map/ppermute | solution.py:28
  23.1 0.2 multiply_reduce_fusion
  23.4 0.1 broadcast_select_fusion
  23.6 0.3 fusion.45
  23.9 0.2 collective-permute-done.6
  24.0 0.1 multiply_reduce_fusion.4
  24.3 0.3 fusion.2
  24.7 3.4 %collective-permute-start.7 = (f16[264,128]{1,0:T(8,128)(2,1)S(1)}, f16[264,128]{1,0:T(8,128)(2,1)S(1)}, u32[]{:S(2)}, u32[]{:S(2)}) collective-permute-start(f16[264,128]{1,0:T(8,128)(2,1)S(1)} %concatenate.11), channel_id=1, source_target_pairs={{0,2},{1,3},{2,0},{3,1},{4,6},{5,7},{6,4},{7,5},{8,10},{9,11},{10,... | collective-permute-start | bytes 202760 | tf_op jit(solution)/shard_map/ppermute | solution.py:28
  28.1 0.3 fusion.46
  28.4 0.3 convolution_add_fusion.1
  28.7 0.1 multiply_reduce_fusion.2
  28.9 1.7 %collective-permute-done.7 = f16[264,128]{1,0:T(8,128)(2,1)S(1)} collective-permute-done((f16[264,128]{1,0:T(8,128)(2,1)S(1)}, f16[264,128]{1,0:T(8,128)(2,1)S(1)}, u32[]{:S(2)}, u32[]{:S(2)}) %collective-permute-start.7) | collective-permute-done | bytes 67616 | tf_op jit(solution)/shard_map/ppermute | solution.py:28
  30.6 0.8 %fusion.6 = f32[256,128]{1,0:T(8,128)} fusion(f32[256,128]{1,0:T(8,128)S(1)} %convolution_add_fusion.1, f32[264,128]{1,0:T(8,128)S(1)} %convert_element_type.61, f32[128]{0:T(128)S(1)} %rsqrt_bitcast_fusion, f32[256]{0:T(256)S(1)} %fusion.27, f32[128]{0:T(128)S(1)} %get-tuple-element.35, f32[256]{0:T(256)S(1)} %get-tuple-element.33), kind=kLoop, calls=%fused_computation.19 | loop fusion | flops 163840 | bytes 396288 | tf_op jit(solution)/shard_map/mul | solution.py:34
  (24 shorter events, 0.5 us)
Async XLA Ops:
  0.0 4.1 %copy-start = (bf16[256,1024]{1,0:T(8,128)(2,1)S(1)}, bf16[256,1024]{1,0:T(8,128)(2,1)}, u32[]{:S(2)}) copy-start(bf16[256,1024]{1,0:T(8,128)(2,1)} %param.2) | copy-start | bytes 1572868
  1.0 7.3 %collective-permute-start.1 = (bf16[64,1024]{1,0:T(8,128)(2,1)S(1)}, bf16[64,1024]{1,0:T(8,128)(2,1)S(1)}, u32[]{:S(2)}, u32[]{:S(2)}) collective-permute-start(bf16[64,1024]{1,0:T(8,128)(2,1)S(1)} %get-tuple-element.20), channel_id=1, source_target_pairs={{0,8},{1,9},{2,10},{3,11},{4,12},{5,13},{6,14},{7,15},{8,0},{9,1},... | collective-permute-start | bytes 393224 | tf_op jit(solution)/shard_map/ppermute | solution.py:28
  4.1 7.6 %collective-permute-start.2 = (bf16[64,1024]{1,0:T(8,128)(2,1)S(1)}, bf16[64,1024]{1,0:T(8,128)(2,1)S(1)}, u32[]{:S(2)}, u32[]{:S(2)}) collective-permute-start(bf16[64,1024]{1,0:T(8,128)(2,1)S(1)} %get-tuple-element.22), channel_id=1, source_target_pairs={{0,8},{1,9},{2,10},{3,11},{4,12},{5,13},{6,14},{7,15},{8,0},{9,1},... | collective-permute-start | bytes 393224 | tf_op jit(solution)/shard_map/ppermute | solution.py:28
  4.1 19.0 %collective-permute-start = (bf16[256,1024]{1,0:T(8,128)(2,1)S(1)}, bf16[256,1024]{1,0:T(8,128)(2,1)S(1)}, u32[]{:S(2)}, u32[]{:S(2)}) collective-permute-start(bf16[256,1024]{1,0:T(8,128)(2,1)S(1)} %copy-done), channel_id=1, source_target_pairs={{0,1},{1,0},{2,3},{3,2},{4,5},{5,4},{6,7},{7,6},{8,9},{9,8},{10,11... | collective-permute-start | bytes 1572872 | tf_op jit(solution)/shard_map/ppermute | solution.py:28
  8.4 14.0 %collective-permute-start.5 = (bf16[64,1024]{1,0:T(8,128)(2,1)S(1)}, bf16[64,1024]{1,0:T(8,128)(2,1)S(1)}, u32[]{:S(2)}, u32[]{:S(2)}) collective-permute-start(bf16[64,1024]{1,0:T(8,128)(2,1)S(1)} %get-tuple-element.27), channel_id=1, source_target_pairs={{0,2},{1,3},{2,0},{3,1},{4,6},{5,7},{6,4},{7,5},{8,10},{9,11},{10,... | collective-permute-start | bytes 393224 | tf_op jit(solution)/shard_map/ppermute | solution.py:28
  11.7 10.7 %collective-permute-start.3 = (bf16[64,1024]{1,0:T(8,128)(2,1)S(1)}, bf16[64,1024]{1,0:T(8,128)(2,1)S(1)}, u32[]{:S(2)}, u32[]{:S(2)}) collective-permute-start(bf16[64,1024]{1,0:T(8,128)(2,1)S(1)} %get-tuple-element.25), channel_id=1, source_target_pairs={{0,2},{1,3},{2,0},{3,1},{4,6},{5,7},{6,4},{7,5},{8,10},{9,11},{10,... | collective-permute-start | bytes 393224 | tf_op jit(solution)/shard_map/ppermute | solution.py:28
  13.3 9.1 %collective-permute-start.4 = (bf16[128,1024]{1,0:T(8,128)(2,1)S(1)}, bf16[128,1024]{1,0:T(8,128)(2,1)S(1)}, u32[]{:S(2)}, u32[]{:S(2)}) collective-permute-start(bf16[128,1024]{1,0:T(8,128)(2,1)S(1)} %pad_maximum_fusion), channel_id=1, source_target_pairs={{0,4},{1,5},{2,6},{3,7},{4,0},{5,1},{6,2},{7,3},{8,12},{9,13},{10,... | collective-permute-start | bytes 786440 | tf_op jit(solution)/shard_map/ppermute | solution.py:28
  22.4 1.6 %collective-permute-start.6 = (bf16[128,1024]{1,0:T(8,128)(2,1)S(1)}, bf16[128,1024]{1,0:T(8,128)(2,1)S(1)}, u32[]{:S(2)}, u32[]{:S(2)}) collective-permute-start(bf16[128,1024]{1,0:T(8,128)(2,1)S(1)} %pad_maximum_fusion.1), channel_id=1, source_target_pairs={{0,4},{1,5},{2,6},{3,7},{4,0},{5,1},{6,2},{7,3},{8,12},{9,13},{10,... | collective-permute-start | bytes 786440 | tf_op jit(solution)/shard_map/ppermute | solution.py:28
  24.7 5.9 %collective-permute-start.7 = (f16[264,128]{1,0:T(8,128)(2,1)S(1)}, f16[264,128]{1,0:T(8,128)(2,1)S(1)}, u32[]{:S(2)}, u32[]{:S(2)}) collective-permute-start(f16[264,128]{1,0:T(8,128)(2,1)S(1)} %concatenate.11), channel_id=1, source_target_pairs={{0,2},{1,3},{2,0},{3,1},{4,6},{5,7},{6,4},{7,5},{8,10},{9,11},{10,... | collective-permute-start | bytes 202760 | tf_op jit(solution)/shard_map/ppermute | solution.py:28

commit v33 on v30

--- a/solution.py
+++ b/solution.py
@@ -77,10 +77,11 @@
         return gram, squares(mine) + squares(other)
 
     cross_gram = contract(lefts[0], cross)
+    left_late, _ = lax.optimization_barrier((left_other, cross_gram))
     cross_other, _ = lax.optimization_barrier((jnp.concatenate([other_core(part) for part in crosses]), cross_gram))
     cross_gram = cross_gram + contract(lefts[1], cross_other)
     cross_sq = squares(cross) + squares(cross_other)
-    left_sq = squares(left_docs) + squares(left_other)
+    left_sq = squares(left_docs) + squares(left_late)
 
     left_high, left_low, left_read = packed(left_sq)
     right_high, right_low, right_read = packed(cross_sq)

time: 31.4 us -> 36.3 us (1.16)
  waiting for transfers between devices: 13.4 us -> 22.9 us
  starting transfers between devices: 13.3 us -> 8.76 us
    ppermute x9, waiting for transfers between devices: 13.4 us -> 22.9 us  [moved(): return lax.ppermute(value, ('row', 'col'), pairs)]
    ppermute x9, starting transfers between devices: 13.3 us -> 8.76 us  [moved(): return lax.ppermute(value, ('row', 'col'), pairs)]
  transfers between devices with their start and end apart: 9 -> 9, of which waited for: 5 -> 6; matrix products, arithmetic and copies ran while one was open for 6% -> 4% of each run, Pallas kernels for 0% -> 0%
where the time goes in v33:
time: 36.3 us; the launch traced here: 36.2 us
  waiting for transfers between devices  22.9 us (63%)
  starting transfers between devices  8.76 us (24%)
  other arithmetic  2.07 us (6%)
  matrix products  1.22 us (3%)
  local copies, waits for them, and re-layouts  1.12 us (3%)
    ppermute x9, waiting for transfers between devices, moved(): return lax.ppermute(value, ('row', 'col'), pairs)  22.9 us
    ppermute x9, starting transfers between devices, moved(): return lax.ppermute(value, ('row', 'col'), pairs)  8.76 us
    dot_general x4, matrix products, contract(): lax.dot_general(left_part, right_part, (((1,), (1,)), ((), ())), preferre...  1.22 us
    slice x1, local copies, waits for them, and re-layouts, on_square_grid(): right_docs[width // 2:]  1.04 us
    reduce_sum x5, other arithmetic, squares(): return jnp.sum(widened * widened, axis=1)  0.82 us
    mul x3, other arithmetic, finish(): return summed / feat_total * left_scale[:, None] * right_scale[None, :]  0.81 us
  transfers between devices with their start and end apart: 9, of which 6 were waited for; matrix products, arithmetic and copies ran while one was open for 4% of the time, Pallas kernels for 0%

profile of v33, /device:TPU:0, one launch (start us, length us, event | category | flops | bytes accessed | tf_op | source)
XLA Modules:
  0.0 36.2 jit_solution(12093007901746910729)
XLA Ops:
  0.0 1.0 %fusion.44 = (bf16[64,1024]{1,0:T(8,128)(2,1)S(1)}, bf16[64,1024]{1,0:T(8,128)(2,1)S(1)}) fusion(bf16[128,1024]{1,0:T(8,128)(2,1)} %param.3), kind=kLoop, calls=%fused_computation.79 | loop fusion | bytes 524288 | tf_op jit(solution)/shard_map/slice | solution.py:63
  1.0 3.0 %collective-permute-start.1 = (bf16[64,1024]{1,0:T(8,128)(2,1)S(1)}, bf16[64,1024]{1,0:T(8,128)(2,1)S(1)}, u32[]{:S(2)}, u32[]{:S(2)}) collective-permute-start(bf16[64,1024]{1,0:T(8,128)(2,1)S(1)} %get-tuple-element.21), channel_id=1, source_target_pairs={{0,8},{1,9},{2,10},{3,11},{4,12},{5,13},{6,14},{7,15},{8,0},{9,1},... | collective-permute-start | bytes 393224 | tf_op jit(solution)/shard_map/ppermute | solution.py:28
  4.1 0.1 collective-permute-start.2
  4.1 2.0 %collective-permute-start = (bf16[256,1024]{1,0:T(8,128)(2,1)S(1)}, bf16[256,1024]{1,0:T(8,128)(2,1)S(1)}, u32[]{:S(2)}, u32[]{:S(2)}) collective-permute-start(bf16[256,1024]{1,0:T(8,128)(2,1)S(1)} %copy-done), channel_id=1, source_target_pairs={{0,1},{1,0},{2,3},{3,2},{4,5},{5,4},{6,7},{7,6},{8,9},{9,8},{10,11... | collective-permute-start | bytes 1572872 | tf_op jit(solution)/shard_map/ppermute | solution.py:28
  6.2 2.2 %collective-permute-done.1 = bf16[64,1024]{1,0:T(8,128)(2,1)S(1)} collective-permute-done((bf16[64,1024]{1,0:T(8,128)(2,1)S(1)}, bf16[64,1024]{1,0:T(8,128)(2,1)S(1)}, u32[]{:S(2)}, u32[]{:S(2)}) %collective-permute-start.1) | collective-permute-done | bytes 131104 | tf_op jit(solution)/shard_map/ppermute | solution.py:28
  8.4 2.0 %collective-permute-done.2 = bf16[64,1024]{1,0:T(8,128)(2,1)S(1)} collective-permute-done((bf16[64,1024]{1,0:T(8,128)(2,1)S(1)}, bf16[64,1024]{1,0:T(8,128)(2,1)S(1)}, u32[]{:S(2)}, u32[]{:S(2)}) %collective-permute-start.2) | collective-permute-done | bytes 131104 | tf_op jit(solution)/shard_map/ppermute | solution.py:28
  10.5 2.9 %collective-permute-start.3 = (bf16[64,1024]{1,0:T(8,128)(2,1)S(1)}, bf16[64,1024]{1,0:T(8,128)(2,1)S(1)}, u32[]{:S(2)}, u32[]{:S(2)}) collective-permute-start(bf16[64,1024]{1,0:T(8,128)(2,1)S(1)} %get-tuple-element.26), channel_id=1, source_target_pairs={{0,2},{1,3},{2,0},{3,1},{4,6},{5,7},{6,4},{7,5},{8,10},{9,11},{10,... | collective-permute-start | bytes 393224 | tf_op jit(solution)/shard_map/ppermute | solution.py:28
  13.4 0.1 collective-permute-start.5
  13.5 0.2 multiply_reduce_fusion.1
  13.7 0.1 multiply_reduce_fusion.3
  13.8 12.1 %collective-permute-done.5 = bf16[64,1024]{1,0:T(8,128)(2,1)S(1)} collective-permute-done((bf16[64,1024]{1,0:T(8,128)(2,1)S(1)}, bf16[64,1024]{1,0:T(8,128)(2,1)S(1)}, u32[]{:S(2)}, u32[]{:S(2)}) %collective-permute-start.5) | collective-permute-done | bytes 131104 | tf_op jit(solution)/shard_map/ppermute | solution.py:28
  26.0 0.5 %collective-permute-start.7 = (bf16[64,1024]{1,0:T(8,128)(2,1)S(1)}, bf16[64,1024]{1,0:T(8,128)(2,1)S(1)}, u32[]{:S(2)}, u32[]{:S(2)}) collective-permute-start(bf16[64,1024]{1,0:T(8,128)(2,1)S(1)} %collective-permute-done.3), channel_id=1, source_target_pairs={{0,4},{1,5},{2,6},{3,7},{4,0},{5,1},{6,2},{7,3},{8,12},{9,13},{10,... | collective-permute-start | bytes 393224 | tf_op jit(solution)/shard_map/ppermute | solution.py:28
  26.5 0.1 broadcast_select_fusion
  26.6 0.3 fusion.45
  26.9 0.4 %collective-permute-done.6 = bf16[64,1024]{1,0:T(8,128)(2,1)S(1)} collective-permute-done((bf16[64,1024]{1,0:T(8,128)(2,1)S(1)}, bf16[64,1024]{1,0:T(8,128)(2,1)S(1)}, u32[]{:S(2)}, u32[]{:S(2)}) %collective-permute-start.6) | collective-permute-done | bytes 131104 | tf_op jit(solution)/shard_map/ppermute | solution.py:28
  27.3 0.2 collective-permute-done.7
  27.5 0.2 multiply_reduce_fusion.4
  27.8 0.2 multiply_reduce_fusion
  28.1 0.3 fusion.2
  28.6 0.3 fusion.46
  28.9 0.3 convolution_add_fusion.1
  29.2 0.1 multiply_reduce_fusion.2
  29.4 6.0 %collective-permute-done.8 = f16[264,128]{1,0:T(8,128)(2,1)S(1)} collective-permute-done((f16[264,128]{1,0:T(8,128)(2,1)S(1)}, f16[264,128]{1,0:T(8,128)(2,1)S(1)}, u32[]{:S(2)}, u32[]{:S(2)}) %collective-permute-start.8) | collective-permute-done | bytes 67616 | tf_op jit(solution)/shard_map/ppermute | solution.py:28
  35.4 0.8 %fusion.6 = f32[256,128]{1,0:T(8,128)} fusion(f32[256,128]{1,0:T(8,128)S(1)} %convolution_add_fusion.1, f32[264,128]{1,0:T(8,128)S(1)} %convert_element_type.61, f32[128]{0:T(128)S(1)} %rsqrt_bitcast_fusion, f32[256]{0:T(256)S(1)} %fusion.27, f32[128]{0:T(128)S(1)} %get-tuple-element.37, f32[256]{0:T(256)S(1)} %get-tuple-element.35), kind=kLoop, calls=%fused_computation.20 | loop fusion | flops 163840 | bytes 396288 | tf_op jit(solution)/shard_map/mul | solution.py:34
  (26 shorter events, 0.6 us)
Async XLA Ops:
  0.0 4.1 %copy-start = (bf16[256,1024]{1,0:T(8,128)(2,1)S(1)}, bf16[256,1024]{1,0:T(8,128)(2,1)}, u32[]{:S(2)}) copy-start(bf16[256,1024]{1,0:T(8,128)(2,1)} %param.2) | copy-start | bytes 1572868
  1.0 7.3 %collective-permute-start.1 = (bf16[64,1024]{1,0:T(8,128)(2,1)S(1)}, bf16[64,1024]{1,0:T(8,128)(2,1)S(1)}, u32[]{:S(2)}, u32[]{:S(2)}) collective-permute-start(bf16[64,1024]{1,0:T(8,128)(2,1)S(1)} %get-tuple-element.21), channel_id=1, source_target_pairs={{0,8},{1,9},{2,10},{3,11},{4,12},{5,13},{6,14},{7,15},{8,0},{9,1},... | collective-permute-start | bytes 393224 | tf_op jit(solution)/shard_map/ppermute | solution.py:28
  4.1 6.3 %collective-permute-start.2 = (bf16[64,1024]{1,0:T(8,128)(2,1)S(1)}, bf16[64,1024]{1,0:T(8,128)(2,1)S(1)}, u32[]{:S(2)}, u32[]{:S(2)}) collective-permute-start(bf16[64,1024]{1,0:T(8,128)(2,1)S(1)} %get-tuple-element.23), channel_id=1, source_target_pairs={{0,8},{1,9},{2,10},{3,11},{4,12},{5,13},{6,14},{7,15},{8,0},{9,1},... | collective-permute-start | bytes 393224 | tf_op jit(solution)/shard_map/ppermute | solution.py:28
  4.1 22.4 %collective-permute-start = (bf16[256,1024]{1,0:T(8,128)(2,1)S(1)}, bf16[256,1024]{1,0:T(8,128)(2,1)S(1)}, u32[]{:S(2)}, u32[]{:S(2)}) collective-permute-start(bf16[256,1024]{1,0:T(8,128)(2,1)S(1)} %copy-done), channel_id=1, source_target_pairs={{0,1},{1,0},{2,3},{3,2},{4,5},{5,4},{6,7},{7,6},{8,9},{9,8},{10,11... | collective-permute-start | bytes 1572872 | tf_op jit(solution)/shard_map/ppermute | solution.py:28
  10.4 15.6 %collective-permute-start.4 = (bf16[128,1024]{1,0:T(8,128)(2,1)S(1)}, bf16[128,1024]{1,0:T(8,128)(2,1)S(1)}, u32[]{:S(2)}, u32[]{:S(2)}) collective-permute-start(bf16[128,1024]{1,0:T(8,128)(2,1)S(1)} %pad_maximum_fusion), channel_id=1, source_target_pairs={{0,4},{1,5},{2,6},{3,7},{4,0},{5,1},{6,2},{7,3},{8,12},{9,13},{10,... | collective-permute-start | bytes 786440 | tf_op jit(solution)/shard_map/ppermute | solution.py:28
  10.5 15.5 %collective-permute-start.3 = (bf16[64,1024]{1,0:T(8,128)(2,1)S(1)}, bf16[64,1024]{1,0:T(8,128)(2,1)S(1)}, u32[]{:S(2)}, u32[]{:S(2)}) collective-permute-start(bf16[64,1024]{1,0:T(8,128)(2,1)S(1)} %get-tuple-element.26), channel_id=1, source_target_pairs={{0,2},{1,3},{2,0},{3,1},{4,6},{5,7},{6,4},{7,5},{8,10},{9,11},{10,... | collective-permute-start | bytes 393224 | tf_op jit(solution)/shard_map/ppermute | solution.py:28
  13.4 12.6 %collective-permute-start.5 = (bf16[64,1024]{1,0:T(8,128)(2,1)S(1)}, bf16[64,1024]{1,0:T(8,128)(2,1)S(1)}, u32[]{:S(2)}, u32[]{:S(2)}) collective-permute-start(bf16[64,1024]{1,0:T(8,128)(2,1)S(1)} %get-tuple-element.28), channel_id=1, source_target_pairs={{0,2},{1,3},{2,0},{3,1},{4,6},{5,7},{6,4},{7,5},{8,10},{9,11},{10,... | collective-permute-start | bytes 393224 | tf_op jit(solution)/shard_map/ppermute | solution.py:28
  26.0 1.3 %collective-permute-start.6 = (bf16[64,1024]{1,0:T(8,128)(2,1)S(1)}, bf16[64,1024]{1,0:T(8,128)(2,1)S(1)}, u32[]{:S(2)}, u32[]{:S(2)}) collective-permute-start(bf16[64,1024]{1,0:T(8,128)(2,1)S(1)} %collective-permute-done.5), channel_id=1, source_target_pairs={{0,4},{1,5},{2,6},{3,7},{4,0},{5,1},{6,2},{7,3},{8,12},{9,13},{10,... | collective-permute-start | bytes 393224 | tf_op jit(solution)/shard_map/ppermute | solution.py:28
  26.0 1.5 %collective-permute-start.7 = (bf16[64,1024]{1,0:T(8,128)(2,1)S(1)}, bf16[64,1024]{1,0:T(8,128)(2,1)S(1)}, u32[]{:S(2)}, u32[]{:S(2)}) collective-permute-start(bf16[64,1024]{1,0:T(8,128)(2,1)S(1)} %collective-permute-done.3), channel_id=1, source_target_pairs={{0,4},{1,5},{2,6},{3,7},{4,0},{5,1},{6,2},{7,3},{8,12},{9,13},{10,... | collective-permute-start | bytes 393224 | tf_op jit(solution)/shard_map/ppermute | solution.py:28
  28.5 6.8 %collective-permute-start.8 = (f16[264,128]{1,0:T(8,128)(2,1)S(1)}, f16[264,128]{1,0:T(8,128)(2,1)S(1)}, u32[]{:S(2)}, u32[]{:S(2)}) collective-permute-start(f16[264,128]{1,0:T(8,128)(2,1)S(1)} %concatenate.15), channel_id=1, source_target_pairs={{0,2},{1,3},{2,0},{3,1},{4,6},{5,7},{6,4},{7,5},{8,10},{9,11},{10,... | collective-permute-start | bytes 202760 | tf_op jit(solution)/shard_map/ppermute | solution.py:28

commit v34 on v30

--- a/solution.py
+++ b/solution.py
@@ -68,7 +68,7 @@
     left_other = moved(left_docs, side, lambda r, c: (r, c ^ 1))
     near = lax.optimization_barrier(jnp.concatenate(nears))
     near_other = other_core(near)
-    crosses[1], near_other = lax.optimization_barrier((crosses[1], near_other))
+    crosses[1], near_other, left_other = lax.optimization_barrier((crosses[1], near_other, left_other))
     cross = lax.optimization_barrier(jnp.concatenate(crosses))
     lefts = lax.optimization_barrier((jnp.where(same, left_docs, left_other), jnp.where(same, left_other, left_docs)))
 

time: 31.4 us -> 32.1 us (1.022)
  waiting for transfers between devices: 13.4 us -> 14.5 us
  starting transfers between devices: 13.3 us -> 12.9 us
    ppermute x9, waiting for transfers between devices: 13.4 us -> 14.5 us  [moved(): return lax.ppermute(value, ('row', 'col'), pairs)]
    ppermute x9, starting transfers between devices: 13.3 us -> 12.9 us  [moved(): return lax.ppermute(value, ('row', 'col'), pairs)]
where the time goes in v34:
time: 32.1 us; the launch traced here: 32 us
  waiting for transfers between devices  14.5 us (45%)
  starting transfers between devices  12.9 us (40%)
  other arithmetic  2.06 us (6%)
  matrix products  1.21 us (4%)
  local copies, waits for them, and re-layouts  1.12 us (3%)
    ppermute x9, waiting for transfers between devices, moved(): return lax.ppermute(value, ('row', 'col'), pairs)  14.5 us
    ppermute x9, starting transfers between devices, moved(): return lax.ppermute(value, ('row', 'col'), pairs)  12.9 us
    dot_general x4, matrix products, contract(): lax.dot_general(left_part, right_part, (((1,), (1,)), ((), ())), preferre...  1.21 us
    slice x1, local copies, waits for them, and re-layouts, on_square_grid(): right_docs[width // 2:]  1.04 us
    reduce_sum x5, other arithmetic, squares(): return jnp.sum(widened * widened, axis=1)  0.82 us
    mul x3, other arithmetic, finish(): return summed / feat_total * left_scale[:, None] * right_scale[None, :]  0.81 us
  transfers between devices with their start and end apart: 9, of which 5 were waited for; matrix products, arithmetic and copies ran while one was open for 6% of the time, Pallas kernels for 0%

profile of v34, /device:TPU:0, one launch (start us, length us, event | category | flops | bytes accessed | tf_op | source)
XLA Modules:
  0.0 32.0 jit_solution(7971384922292952677)
XLA Ops:
  0.0 1.0 %fusion.44 = (bf16[64,1024]{1,0:T(8,128)(2,1)S(1)}, bf16[64,1024]{1,0:T(8,128)(2,1)S(1)}) fusion(bf16[128,1024]{1,0:T(8,128)(2,1)} %param.3), kind=kLoop, calls=%fused_computation.79 | loop fusion | bytes 524288 | tf_op jit(solution)/shard_map/slice | solution.py:63
  1.0 3.0 %collective-permute-start = (bf16[64,1024]{1,0:T(8,128)(2,1)S(1)}, bf16[64,1024]{1,0:T(8,128)(2,1)S(1)}, u32[]{:S(2)}, u32[]{:S(2)}) collective-permute-start(bf16[64,1024]{1,0:T(8,128)(2,1)S(1)} %get-tuple-element.20), channel_id=1, source_target_pairs={{0,8},{1,9},{2,10},{3,11},{4,12},{5,13},{6,14},{7,15},{8,0},{9,1},... | collective-permute-start | bytes 393224 | tf_op jit(solution)/shard_map/ppermute | solution.py:28
  4.1 0.1 collective-permute-start.2
  4.1 2.0 %collective-permute-start.4 = (bf16[256,1024]{1,0:T(8,128)(2,1)S(1)}, bf16[256,1024]{1,0:T(8,128)(2,1)S(1)}, u32[]{:S(2)}, u32[]{:S(2)}) collective-permute-start(bf16[256,1024]{1,0:T(8,128)(2,1)S(1)} %copy-done), channel_id=1, source_target_pairs={{0,1},{1,0},{2,3},{3,2},{4,5},{5,4},{6,7},{7,6},{8,9},{9,8},{10,11... | collective-permute-start | bytes 1572872 | tf_op jit(solution)/shard_map/ppermute | solution.py:28
  6.2 2.2 %collective-permute-done = bf16[64,1024]{1,0:T(8,128)(2,1)S(1)} collective-permute-done((bf16[64,1024]{1,0:T(8,128)(2,1)S(1)}, bf16[64,1024]{1,0:T(8,128)(2,1)S(1)}, u32[]{:S(2)}, u32[]{:S(2)}) %collective-permute-start) | collective-permute-done | bytes 131104 | tf_op jit(solution)/shard_map/ppermute | solution.py:28
  8.4 3.2 %collective-permute-start.1 = (bf16[64,1024]{1,0:T(8,128)(2,1)S(1)}, bf16[64,1024]{1,0:T(8,128)(2,1)S(1)}, u32[]{:S(2)}, u32[]{:S(2)}) collective-permute-start(bf16[64,1024]{1,0:T(8,128)(2,1)S(1)} %get-tuple-element.21), channel_id=1, source_target_pairs={{0,2},{1,3},{2,0},{3,1},{4,6},{5,7},{6,4},{7,5},{8,10},{9,11},{10,... | collective-permute-start | bytes 393224 | tf_op jit(solution)/shard_map/ppermute | solution.py:28
  11.7 1.6 %collective-permute-start.5 = (bf16[64,1024]{1,0:T(8,128)(2,1)S(1)}, bf16[64,1024]{1,0:T(8,128)(2,1)S(1)}, u32[]{:S(2)}, u32[]{:S(2)}) collective-permute-start(bf16[64,1024]{1,0:T(8,128)(2,1)S(1)} %get-tuple-element.29), channel_id=1, source_target_pairs={{0,2},{1,3},{2,0},{3,1},{4,6},{5,7},{6,4},{7,5},{8,10},{9,11},{10,... | collective-permute-start | bytes 393224 | tf_op jit(solution)/shard_map/ppermute | solution.py:28
  13.3 0.2 multiply_reduce_fusion.1
  13.5 0.1 multiply_reduce_fusion.3
  13.6 8.8 %collective-permute-done.5 = bf16[64,1024]{1,0:T(8,128)(2,1)S(1)} collective-permute-done((bf16[64,1024]{1,0:T(8,128)(2,1)S(1)}, bf16[64,1024]{1,0:T(8,128)(2,1)S(1)}, u32[]{:S(2)}, u32[]{:S(2)}) %collective-permute-start.5) | collective-permute-done | bytes 131104 | tf_op jit(solution)/shard_map/ppermute | solution.py:28
  22.4 0.7 %collective-permute-done.4 = bf16[256,1024]{1,0:T(8,128)(2,1)S(1)} collective-permute-done((bf16[256,1024]{1,0:T(8,128)(2,1)S(1)}, bf16[256,1024]{1,0:T(8,128)(2,1)S(1)}, u32[]{:S(2)}, u32[]{:S(2)}) %collective-permute-start.4) | collective-permute-done | bytes 524320 | tf_op jit(solution)/shard_map/ppermute | solution.py:28
  23.1 0.2 multiply_reduce_fusion
  23.4 0.1 collective-permute-start.7
  23.5 0.1 broadcast_select_fusion
  23.6 0.3 fusion.45
  23.9 0.3 fusion.46
  24.3 0.6 %collective-permute-done.7 = bf16[64,1024]{1,0:T(8,128)(2,1)S(1)} collective-permute-done((bf16[64,1024]{1,0:T(8,128)(2,1)S(1)}, bf16[64,1024]{1,0:T(8,128)(2,1)S(1)}, u32[]{:S(2)}, u32[]{:S(2)}) %collective-permute-start.7) | collective-permute-done | bytes 131104 | tf_op jit(solution)/shard_map/ppermute | solution.py:28
  24.9 0.2 multiply_reduce_fusion.4
  25.2 0.3 fusion.2
  25.6 2.9 %collective-permute-start.8 = (f16[264,128]{1,0:T(8,128)(2,1)S(1)}, f16[264,128]{1,0:T(8,128)(2,1)S(1)}, u32[]{:S(2)}, u32[]{:S(2)}) collective-permute-start(f16[264,128]{1,0:T(8,128)(2,1)S(1)} %concatenate.15), channel_id=1, source_target_pairs={{0,2},{1,3},{2,0},{3,1},{4,6},{5,7},{6,4},{7,5},{8,10},{9,11},{10,... | collective-permute-start | bytes 202760 | tf_op jit(solution)/shard_map/ppermute | solution.py:28
  28.4 0.3 convolution_add_fusion
  28.7 0.1 multiply_reduce_fusion.2
  28.9 2.2 %collective-permute-done.8 = f16[264,128]{1,0:T(8,128)(2,1)S(1)} collective-permute-done((f16[264,128]{1,0:T(8,128)(2,1)S(1)}, f16[264,128]{1,0:T(8,128)(2,1)S(1)}, u32[]{:S(2)}, u32[]{:S(2)}) %collective-permute-start.8) | collective-permute-done | bytes 67616 | tf_op jit(solution)/shard_map/ppermute | solution.py:28
  31.2 0.8 %fusion.6 = f32[256,128]{1,0:T(8,128)} fusion(f32[256,128]{1,0:T(8,128)S(1)} %convolution_add_fusion, f32[264,128]{1,0:T(8,128)S(1)} %convert_element_type.61, f32[128]{0:T(128)S(1)} %rsqrt_bitcast_fusion, f32[256]{0:T(256)S(1)} %fusion.27, f32[128]{0:T(128)S(1)} %get-tuple-element.37, f32[256]{0:T(256)S(1)} %get-tuple-element.35), kind=kLoop, calls=%fused_computation.20 | loop fusion | flops 163840 | bytes 396288 | tf_op jit(solution)/shard_map/mul | solution.py:34
  (26 shorter events, 0.5 us)
Async XLA Ops:
  0.0 4.1 %copy-start = (bf16[256,1024]{1,0:T(8,128)(2,1)S(1)}, bf16[256,1024]{1,0:T(8,128)(2,1)}, u32[]{:S(2)}) copy-start(bf16[256,1024]{1,0:T(8,128)(2,1)} %param.2) | copy-start | bytes 1572868
  1.0 7.3 %collective-permute-start = (bf16[64,1024]{1,0:T(8,128)(2,1)S(1)}, bf16[64,1024]{1,0:T(8,128)(2,1)S(1)}, u32[]{:S(2)}, u32[]{:S(2)}) collective-permute-start(bf16[64,1024]{1,0:T(8,128)(2,1)S(1)} %get-tuple-element.20), channel_id=1, source_target_pairs={{0,8},{1,9},{2,10},{3,11},{4,12},{5,13},{6,14},{7,15},{8,0},{9,1},... | collective-permute-start | bytes 393224 | tf_op jit(solution)/shard_map/ppermute | solution.py:28
  4.1 7.6 %collective-permute-start.2 = (bf16[64,1024]{1,0:T(8,128)(2,1)S(1)}, bf16[64,1024]{1,0:T(8,128)(2,1)S(1)}, u32[]{:S(2)}, u32[]{:S(2)}) collective-permute-start(bf16[64,1024]{1,0:T(8,128)(2,1)S(1)} %get-tuple-element.22), channel_id=1, source_target_pairs={{0,8},{1,9},{2,10},{3,11},{4,12},{5,13},{6,14},{7,15},{8,0},{9,1},... | collective-permute-start | bytes 393224 | tf_op jit(solution)/shard_map/ppermute | solution.py:28
  4.1 19.0 %collective-permute-start.4 = (bf16[256,1024]{1,0:T(8,128)(2,1)S(1)}, bf16[256,1024]{1,0:T(8,128)(2,1)S(1)}, u32[]{:S(2)}, u32[]{:S(2)}) collective-permute-start(bf16[256,1024]{1,0:T(8,128)(2,1)S(1)} %copy-done), channel_id=1, source_target_pairs={{0,1},{1,0},{2,3},{3,2},{4,5},{5,4},{6,7},{7,6},{8,9},{9,8},{10,11... | collective-permute-start | bytes 1572872 | tf_op jit(solution)/shard_map/ppermute | solution.py:28
  8.4 14.0 %collective-permute-start.1 = (bf16[64,1024]{1,0:T(8,128)(2,1)S(1)}, bf16[64,1024]{1,0:T(8,128)(2,1)S(1)}, u32[]{:S(2)}, u32[]{:S(2)}) collective-permute-start(bf16[64,1024]{1,0:T(8,128)(2,1)S(1)} %get-tuple-element.21), channel_id=1, source_target_pairs={{0,2},{1,3},{2,0},{3,1},{4,6},{5,7},{6,4},{7,5},{8,10},{9,11},{10,... | collective-permute-start | bytes 393224 | tf_op jit(solution)/shard_map/ppermute | solution.py:28
  11.7 10.7 %collective-permute-start.5 = (bf16[64,1024]{1,0:T(8,128)(2,1)S(1)}, bf16[64,1024]{1,0:T(8,128)(2,1)S(1)}, u32[]{:S(2)}, u32[]{:S(2)}) collective-permute-start(bf16[64,1024]{1,0:T(8,128)(2,1)S(1)} %get-tuple-element.29), channel_id=1, source_target_pairs={{0,2},{1,3},{2,0},{3,1},{4,6},{5,7},{6,4},{7,5},{8,10},{9,11},{10,... | collective-permute-start | bytes 393224 | tf_op jit(solution)/shard_map/ppermute | solution.py:28
  13.3 9.1 %collective-permute-start.3 = (bf16[128,1024]{1,0:T(8,128)(2,1)S(1)}, bf16[128,1024]{1,0:T(8,128)(2,1)S(1)}, u32[]{:S(2)}, u32[]{:S(2)}) collective-permute-start(bf16[128,1024]{1,0:T(8,128)(2,1)S(1)} %pad_maximum_fusion), channel_id=1, source_target_pairs={{0,4},{1,5},{2,6},{3,7},{4,0},{5,1},{6,2},{7,3},{8,12},{9,13},{10,... | collective-permute-start | bytes 786440 | tf_op jit(solution)/shard_map/ppermute | solution.py:28
  22.4 1.9 %collective-permute-start.6 = (bf16[64,1024]{1,0:T(8,128)(2,1)S(1)}, bf16[64,1024]{1,0:T(8,128)(2,1)S(1)}, u32[]{:S(2)}, u32[]{:S(2)}) collective-permute-start(bf16[64,1024]{1,0:T(8,128)(2,1)S(1)} %collective-permute-done.5), channel_id=1, source_target_pairs={{0,4},{1,5},{2,6},{3,7},{4,0},{5,1},{6,2},{7,3},{8,12},{9,13},{10,... | collective-permute-start | bytes 393224 | tf_op jit(solution)/shard_map/ppermute | solution.py:28
  23.4 1.4 %collective-permute-start.7 = (bf16[64,1024]{1,0:T(8,128)(2,1)S(1)}, bf16[64,1024]{1,0:T(8,128)(2,1)S(1)}, u32[]{:S(2)}, u32[]{:S(2)}) collective-permute-start(bf16[64,1024]{1,0:T(8,128)(2,1)S(1)} %collective-permute-done.1), channel_id=1, source_target_pairs={{0,4},{1,5},{2,6},{3,7},{4,0},{5,1},{6,2},{7,3},{8,12},{9,13},{10,... | collective-permute-start | bytes 393224 | tf_op jit(solution)/shard_map/ppermute | solution.py:28
  25.6 5.5 %collective-permute-start.8 = (f16[264,128]{1,0:T(8,128)(2,1)S(1)}, f16[264,128]{1,0:T(8,128)(2,1)S(1)}, u32[]{:S(2)}, u32[]{:S(2)}) collective-permute-start(f16[264,128]{1,0:T(8,128)(2,1)S(1)} %concatenate.15), channel_id=1, source_target_pairs={{0,2},{1,3},{2,0},{3,1},{4,6},{5,7},{6,4},{7,5},{8,10},{9,11},{10,... | collective-permute-start | bytes 202760 | tf_op jit(solution)/shard_map/ppermute | solution.py:28

commit v35 on v30

--- a/solution.py
+++ b/solution.py
@@ -79,7 +79,7 @@
     cross_gram = contract(lefts[0], cross)
     cross_other, _ = lax.optimization_barrier((jnp.concatenate([other_core(part) for part in crosses]), cross_gram))
     cross_gram = cross_gram + contract(lefts[1], cross_other)
-    cross_sq = squares(cross) + squares(cross_other)
+    cross_sq = jnp.concatenate([squares(part) for part in crosses]) + squares(cross_other)
     left_sq = squares(left_docs) + squares(left_other)
 
     left_high, left_low, left_read = packed(left_sq)

time: 31.4 us -> 31.7 us (level)
  other arithmetic: 2.06 us -> 2.43 us
    ppermute x9, waiting for transfers between devices: 13.4 us -> 13.1 us  [moved(): return lax.ppermute(value, ('row', 'col'), pairs)]
    reduce_sum x5 -> x7, other arithmetic: 0.82 us -> 1.02 us  [squares(): return jnp.sum(widened * widened, axis=1)]
  transfers between devices with their start and end apart: 9 -> 9, of which waited for: 5 -> 5; matrix products, arithmetic and copies ran while one was open for 6% -> 7% of each run, Pallas kernels for 0% -> 0%
where the time goes in v35:
time: 31.7 us; the launch traced here: 31.5 us
  starting transfers between devices  13.5 us (43%)
  waiting for transfers between devices  13.1 us (41%)
  other arithmetic  2.43 us (8%)
  matrix products  1.21 us (4%)
  local copies, waits for them, and re-layouts  1.12 us (4%)
    ppermute x9, starting transfers between devices, moved(): return lax.ppermute(value, ('row', 'col'), pairs)  13.5 us
    ppermute x9, waiting for transfers between devices, moved(): return lax.ppermute(value, ('row', 'col'), pairs)  13.1 us
    dot_general x4, matrix products, contract(): lax.dot_general(left_part, right_part, (((1,), (1,)), ((), ())), preferre...  1.21 us
    slice x1, local copies, waits for them, and re-layouts, on_square_grid(): right_docs[width // 2:]  1.04 us
    reduce_sum x7, other arithmetic, squares(): return jnp.sum(widened * widened, axis=1)  1.02 us
    mul x3, other arithmetic, finish(): return summed / feat_total * left_scale[:, None] * right_scale[None, :]  0.81 us
  transfers between devices with their start and end apart: 9, of which 5 were waited for; matrix products, arithmetic and copies ran while one was open for 7% of the time, Pallas kernels for 0%

profile of v35, /device:TPU:0, one launch (start us, length us, event | category | flops | bytes accessed | tf_op | source)
XLA Modules:
  0.0 31.5 jit_solution(14559053099351565597)
XLA Ops:
  0.0 1.0 %fusion.46 = (bf16[64,1024]{1,0:T(8,128)(2,1)S(1)}, bf16[64,1024]{1,0:T(8,128)(2,1)S(1)}) fusion(bf16[128,1024]{1,0:T(8,128)(2,1)} %param.3), kind=kLoop, calls=%fused_computation.84 | loop fusion | bytes 524288 | tf_op jit(solution)/shard_map/slice | solution.py:63
  1.0 3.0 %collective-permute-start.1 = (bf16[64,1024]{1,0:T(8,128)(2,1)S(1)}, bf16[64,1024]{1,0:T(8,128)(2,1)S(1)}, u32[]{:S(2)}, u32[]{:S(2)}) collective-permute-start(bf16[64,1024]{1,0:T(8,128)(2,1)S(1)} %get-tuple-element.20), channel_id=1, source_target_pairs={{0,8},{1,9},{2,10},{3,11},{4,12},{5,13},{6,14},{7,15},{8,0},{9,1},... | collective-permute-start | bytes 393224 | tf_op jit(solution)/shard_map/ppermute | solution.py:28
  4.1 2.0 %collective-permute-start = (bf16[256,1024]{1,0:T(8,128)(2,1)S(1)}, bf16[256,1024]{1,0:T(8,128)(2,1)S(1)}, u32[]{:S(2)}, u32[]{:S(2)}) collective-permute-start(bf16[256,1024]{1,0:T(8,128)(2,1)S(1)} %copy-done), channel_id=1, source_target_pairs={{0,1},{1,0},{2,3},{3,2},{4,5},{5,4},{6,7},{7,6},{8,9},{9,8},{10,11... | collective-permute-start | bytes 1572872 | tf_op jit(solution)/shard_map/ppermute | solution.py:28
  6.2 2.2 %collective-permute-done.1 = bf16[64,1024]{1,0:T(8,128)(2,1)S(1)} collective-permute-done((bf16[64,1024]{1,0:T(8,128)(2,1)S(1)}, bf16[64,1024]{1,0:T(8,128)(2,1)S(1)}, u32[]{:S(2)}, u32[]{:S(2)}) %collective-permute-start.1) | collective-permute-done | bytes 131104 | tf_op jit(solution)/shard_map/ppermute | solution.py:28
  8.4 3.2 %collective-permute-start.5 = (bf16[64,1024]{1,0:T(8,128)(2,1)S(1)}, bf16[64,1024]{1,0:T(8,128)(2,1)S(1)}, u32[]{:S(2)}, u32[]{:S(2)}) collective-permute-start(bf16[64,1024]{1,0:T(8,128)(2,1)S(1)} %get-tuple-element.27), channel_id=1, source_target_pairs={{0,2},{1,3},{2,0},{3,1},{4,6},{5,7},{6,4},{7,5},{8,10},{9,11},{10,... | collective-permute-start | bytes 393224 | tf_op jit(solution)/shard_map/ppermute | solution.py:28
  11.8 0.2 multiply_reduce_fusion.1
  12.0 1.6 %collective-permute-start.3 = (bf16[64,1024]{1,0:T(8,128)(2,1)S(1)}, bf16[64,1024]{1,0:T(8,128)(2,1)S(1)}, u32[]{:S(2)}, u32[]{:S(2)}) collective-permute-start(bf16[64,1024]{1,0:T(8,128)(2,1)S(1)} %get-tuple-element.25), channel_id=1, source_target_pairs={{0,2},{1,3},{2,0},{3,1},{4,6},{5,7},{6,4},{7,5},{8,10},{9,11},{10,... | collective-permute-start | bytes 393224 | tf_op jit(solution)/shard_map/ppermute | solution.py:28
  13.6 0.1 multiply_reduce_fusion.3
  13.7 7.3 %collective-permute-done.5 = bf16[64,1024]{1,0:T(8,128)(2,1)S(1)} collective-permute-done((bf16[64,1024]{1,0:T(8,128)(2,1)S(1)}, bf16[64,1024]{1,0:T(8,128)(2,1)S(1)}, u32[]{:S(2)}, u32[]{:S(2)}) %collective-permute-start.5) | collective-permute-done | bytes 131104 | tf_op jit(solution)/shard_map/ppermute | solution.py:28
  21.1 0.1 multiply_reduce_fusion.6
  21.2 1.3 %collective-permute-done.3 = bf16[64,1024]{1,0:T(8,128)(2,1)S(1)} collective-permute-done((bf16[64,1024]{1,0:T(8,128)(2,1)S(1)}, bf16[64,1024]{1,0:T(8,128)(2,1)S(1)}, u32[]{:S(2)}, u32[]{:S(2)}) %collective-permute-start.3) | collective-permute-done | bytes 131104 | tf_op jit(solution)/shard_map/ppermute | solution.py:28
  22.5 0.1 multiply_reduce_fusion.5
  22.6 0.5 %collective-permute-done = bf16[256,1024]{1,0:T(8,128)(2,1)S(1)} collective-permute-done((bf16[256,1024]{1,0:T(8,128)(2,1)S(1)}, bf16[256,1024]{1,0:T(8,128)(2,1)S(1)}, u32[]{:S(2)}, u32[]{:S(2)}) %collective-permute-start) | collective-permute-done | bytes 524320 | tf_op jit(solution)/shard_map/ppermute | solution.py:28
  23.1 0.2 multiply_reduce_fusion
  23.5 0.3 fusion.47
  23.9 0.1 multiply_reduce_fusion.4
  24.0 0.1 fusion.36
  24.3 0.3 fusion.2
  24.7 3.4 %collective-permute-start.8 = (f16[264,128]{1,0:T(8,128)(2,1)S(1)}, f16[264,128]{1,0:T(8,128)(2,1)S(1)}, u32[]{:S(2)}, u32[]{:S(2)}) collective-permute-start(f16[264,128]{1,0:T(8,128)(2,1)S(1)} %concatenate.42), channel_id=1, source_target_pairs={{0,2},{1,3},{2,0},{3,1},{4,6},{5,7},{6,4},{7,5},{8,10},{9,11},{10,... | collective-permute-start | bytes 202760 | tf_op jit(solution)/shard_map/ppermute | solution.py:28
  28.1 0.3 fusion.48
  28.4 0.3 convolution_add_fusion.1
  28.7 0.1 multiply_reduce_fusion.2
  28.9 1.7 %collective-permute-done.8 = f16[264,128]{1,0:T(8,128)(2,1)S(1)} collective-permute-done((f16[264,128]{1,0:T(8,128)(2,1)S(1)}, f16[264,128]{1,0:T(8,128)(2,1)S(1)}, u32[]{:S(2)}, u32[]{:S(2)}) %collective-permute-start.8) | collective-permute-done | bytes 67616 | tf_op jit(solution)/shard_map/ppermute | solution.py:28
  30.7 0.8 %fusion.6 = f32[256,128]{1,0:T(8,128)} fusion(f32[256,128]{1,0:T(8,128)S(1)} %convolution_add_fusion.1, f32[264,128]{1,0:T(8,128)S(1)} %convert_element_type.65, f32[128]{0:T(128)S(1)} %rsqrt_bitcast_fusion, f32[256]{0:T(256)S(1)} %fusion.27, f32[128]{0:T(128)S(1)} %get-tuple-element.35, f32[256]{0:T(256)S(1)} %get-tuple-element.33), kind=kLoop, calls=%fused_computation.21 | loop fusion | flops 163840 | bytes 396288 | tf_op jit(solution)/shard_map/mul | solution.py:34
  (28 shorter events, 0.7 us)
Async XLA Ops:
  0.0 4.1 %copy-start = (bf16[256,1024]{1,0:T(8,128)(2,1)S(1)}, bf16[256,1024]{1,0:T(8,128)(2,1)}, u32[]{:S(2)}) copy-start(bf16[256,1024]{1,0:T(8,128)(2,1)} %param.2) | copy-start | bytes 1572868
  1.0 7.3 %collective-permute-start.1 = (bf16[64,1024]{1,0:T(8,128)(2,1)S(1)}, bf16[64,1024]{1,0:T(8,128)(2,1)S(1)}, u32[]{:S(2)}, u32[]{:S(2)}) collective-permute-start(bf16[64,1024]{1,0:T(8,128)(2,1)S(1)} %get-tuple-element.20), channel_id=1, source_target_pairs={{0,8},{1,9},{2,10},{3,11},{4,12},{5,13},{6,14},{7,15},{8,0},{9,1},... | collective-permute-start | bytes 393224 | tf_op jit(solution)/shard_map/ppermute | solution.py:28
  4.1 7.6 %collective-permute-start.2 = (bf16[64,1024]{1,0:T(8,128)(2,1)S(1)}, bf16[64,1024]{1,0:T(8,128)(2,1)S(1)}, u32[]{:S(2)}, u32[]{:S(2)}) collective-permute-start(bf16[64,1024]{1,0:T(8,128)(2,1)S(1)} %get-tuple-element.22), channel_id=1, source_target_pairs={{0,8},{1,9},{2,10},{3,11},{4,12},{5,13},{6,14},{7,15},{8,0},{9,1},... | collective-permute-start | bytes 393224 | tf_op jit(solution)/shard_map/ppermute | solution.py:28
  4.1 19.0 %collective-permute-start = (bf16[256,1024]{1,0:T(8,128)(2,1)S(1)}, bf16[256,1024]{1,0:T(8,128)(2,1)S(1)}, u32[]{:S(2)}, u32[]{:S(2)}) collective-permute-start(bf16[256,1024]{1,0:T(8,128)(2,1)S(1)} %copy-done), channel_id=1, source_target_pairs={{0,1},{1,0},{2,3},{3,2},{4,5},{5,4},{6,7},{7,6},{8,9},{9,8},{10,11... | collective-permute-start | bytes 1572872 | tf_op jit(solution)/shard_map/ppermute | solution.py:28
  8.4 12.6 %collective-permute-start.5 = (bf16[64,1024]{1,0:T(8,128)(2,1)S(1)}, bf16[64,1024]{1,0:T(8,128)(2,1)S(1)}, u32[]{:S(2)}, u32[]{:S(2)}) collective-permute-start(bf16[64,1024]{1,0:T(8,128)(2,1)S(1)} %get-tuple-element.27), channel_id=1, source_target_pairs={{0,2},{1,3},{2,0},{3,1},{4,6},{5,7},{6,4},{7,5},{8,10},{9,11},{10,... | collective-permute-start | bytes 393224 | tf_op jit(solution)/shard_map/ppermute | solution.py:28
  11.7 10.8 %collective-permute-start.4 = (bf16[128,1024]{1,0:T(8,128)(2,1)S(1)}, bf16[128,1024]{1,0:T(8,128)(2,1)S(1)}, u32[]{:S(2)}, u32[]{:S(2)}) collective-permute-start(bf16[128,1024]{1,0:T(8,128)(2,1)S(1)} %pad_maximum_fusion), channel_id=1, source_target_pairs={{0,4},{1,5},{2,6},{3,7},{4,0},{5,1},{6,2},{7,3},{8,12},{9,13},{10,... | collective-permute-start | bytes 786440 | tf_op jit(solution)/shard_map/ppermute | solution.py:28
  12.0 10.5 %collective-permute-start.3 = (bf16[64,1024]{1,0:T(8,128)(2,1)S(1)}, bf16[64,1024]{1,0:T(8,128)(2,1)S(1)}, u32[]{:S(2)}, u32[]{:S(2)}) collective-permute-start(bf16[64,1024]{1,0:T(8,128)(2,1)S(1)} %get-tuple-element.25), channel_id=1, source_target_pairs={{0,2},{1,3},{2,0},{3,1},{4,6},{5,7},{6,4},{7,5},{8,10},{9,11},{10,... | collective-permute-start | bytes 393224 | tf_op jit(solution)/shard_map/ppermute | solution.py:28
  21.0 2.8 %collective-permute-start.6 = (bf16[64,1024]{1,0:T(8,128)(2,1)S(1)}, bf16[64,1024]{1,0:T(8,128)(2,1)S(1)}, u32[]{:S(2)}, u32[]{:S(2)}) collective-permute-start(bf16[64,1024]{1,0:T(8,128)(2,1)S(1)} %collective-permute-done.5), channel_id=1, source_target_pairs={{0,4},{1,5},{2,6},{3,7},{4,0},{5,1},{6,2},{7,3},{8,12},{9,13},{10,... | collective-permute-start | bytes 393224 | tf_op jit(solution)/shard_map/ppermute | solution.py:28
  22.5 1.4 %collective-permute-start.7 = (bf16[64,1024]{1,0:T(8,128)(2,1)S(1)}, bf16[64,1024]{1,0:T(8,128)(2,1)S(1)}, u32[]{:S(2)}, u32[]{:S(2)}) collective-permute-start(bf16[64,1024]{1,0:T(8,128)(2,1)S(1)} %collective-permute-done.3), channel_id=1, source_target_pairs={{0,4},{1,5},{2,6},{3,7},{4,0},{5,1},{6,2},{7,3},{8,12},{9,13},{10,... | collective-permute-start | bytes 393224 | tf_op jit(solution)/shard_map/ppermute | solution.py:28
  24.7 5.9 %collective-permute-start.8 = (f16[264,128]{1,0:T(8,128)(2,1)S(1)}, f16[264,128]{1,0:T(8,128)(2,1)S(1)}, u32[]{:S(2)}, u32[]{:S(2)}) collective-permute-start(f16[264,128]{1,0:T(8,128)(2,1)S(1)} %concatenate.42), channel_id=1, source_target_pairs={{0,2},{1,3},{2,0},{3,1},{4,6},{5,7},{6,4},{7,5},{8,10},{9,11},{10,... | collective-permute-start | bytes 202760 | tf_op jit(solution)/shard_map/ppermute | solution.py:28
